TPU v7x, 32 devices: a whole 2x2x4 slice. The times are simulated.
32 devices in a mesh: segment: 2 (over y), slot: 16 (over z, x, core).
Axes of the slice: x: 2, y: 2, z: 4, core: 2. Of those that a mesh axis runs over, the one named last changes fastest.
Arguments:
- hidden_rows: bfloat16 [2, 4, 16, 8192], P('segment', None, None, 'slot'), may hold values from -6 to 6
- norm_gain: bfloat16 [2, 8192], P('segment', 'slot'), may hold values from 0.099609375 to 1.8984375
- qkv_weight: bfloat16 [2, 8192, 5120], P('segment', None, 'slot'), may hold values from -0.0625 to 0.0625
- out_weight: bfloat16 [2, 4096, 8192], P('segment', None, 'slot'), may hold values from -0.5 to 0.5
- cache_kv: bfloat16 [2, 2, 4, 16, 16, 1024], P('segment', None, None, 'slot'), may hold values from -86 to 86
- cache_len: int32 [2, 2, 4, 16], P('segment', None, None, 'slot'), may hold values from 1 to 16, as said below
- page_kv: bfloat16 [2, 16, 16, 8, 1024], P('segment', 'slot'), may hold values from -6 to 6
- page_dest: int32 [2, 16, 16], P('segment'), may hold values from 0 to 15, as said below
- page_row: int32 [2, 16, 16], P('segment'), may hold values from 0 to 7
- page_count: int32 [2, 16, 16], P('segment'), may hold values from 1 to 8, as said below
Outputs:
- final_rows: bfloat16 [2, 4, 16, 8192], P('segment', None, None, 'slot')
Inputs may be any that keep to these rules, and one draw needn't show every extreme that they name: `cache_len`: positions of a row's cache from its length on are not part of it. `page_dest`: the 16 pages of one source device go to distinct slot indices, so every slot index receives one page from every source. `page_count`: tokens of a page from its count on are not part of it.
All inputs are finite; a program needn't handle non-finite values.
Results may differ from a plain program's by a relative error of at most 0.015.
Values may be sent and summed in bfloat16 or wider, within the bound.
No kernel may reach another device: no remote copies, remote signals or barrier semaphores. Data moves between devices by JAX's collectives and lax.ppermute only.
A program may use at most 64 MiB of HBM per device.

v0:
```python
import jax
import jax.numpy as jnp
from jax import lax
from jax.sharding import PartitionSpec as P

QUERY_HEADS = 32
KEY_VALUE_HEADS = 4
HEAD_SIZE = 128
CYCLE_STEPS = 2


norm_eps = 1e-06


def shifted(block, axis, distance):
    devices = range(lax.axis_size(axis))
    route = [((i - distance) % len(devices), i) for i in devices]
    return lax.ppermute(block, axis, route)


def shards(
    hidden_rows,
    norm_gain,
    qkv_weight,
    out_weight,
    cache_kv,
    cache_len,
    page_kv,
    page_dest,
    page_row,
    page_count,
):
    slot_indices = lax.axis_size("slot")
    own_slot = lax.axis_index("slot")
    row_count = hidden_rows.shape[1]
    local_width = hidden_rows.shape[3]
    model_width = local_width * slot_indices
    kv_width = cache_kv.shape[5]
    cache_extent = cache_kv.shape[4]
    page_extent = page_kv.shape[3]
    page_total = page_kv.shape[2]
    width_of_keys = KEY_VALUE_HEADS * HEAD_SIZE
    query_group_width = QUERY_HEADS // KEY_VALUE_HEADS
    score_scale = HEAD_SIZE ** (-0.5)
    slot_ids = jnp.arange(slot_indices, dtype=jnp.int32)
    dest_all = page_dest[0]
    own_dest = lax.dynamic_index_in_dim(dest_all, own_slot, 0, keepdims=False)
    selector = (own_dest[None, :] == slot_ids[:, None]).astype(jnp.bfloat16)
    flat_pages = page_kv[0, 0].reshape(page_total, page_extent * kv_width)
    outgoing = jnp.dot(selector, flat_pages, preferred_element_type=jnp.float32).astype(
        jnp.bfloat16
    )
    outgoing = outgoing.reshape(slot_indices, page_extent, kv_width)
    incoming = lax.all_to_all(outgoing, "slot", split_axis=0, concat_axis=0, tiled=True)
    arriving = dest_all == own_slot
    present = jnp.any(arriving, axis=1)
    owner_row = jnp.sum(jnp.where(arriving, page_row[0], 0), axis=1)
    live_count = jnp.sum(jnp.where(arriving, page_count[0], 0), axis=1)
    token_ids = jnp.arange(page_extent, dtype=jnp.int32)
    page_live = present[:, None] & (token_ids[None, :] < live_count[:, None])
    page_flattened = incoming.reshape(slot_indices * page_extent, kv_width)
    cropped_page_keys = page_flattened[:, :width_of_keys].reshape(
        slot_indices * page_extent, KEY_VALUE_HEADS, HEAD_SIZE
    )
    cropped_page_values = page_flattened[:, width_of_keys:].reshape(
        slot_indices * page_extent, KEY_VALUE_HEADS, HEAD_SIZE
    )
    gain_piece = norm_gain.reshape(1, 1, local_width)
    weight_in = qkv_weight[0]
    weight_out = out_weight[0]
    current = hidden_rows[0]
    for visit_idx in range(CYCLE_STEPS):
        rows_of_block = current.shape[0]
        feature_piece = lax.all_gather(current, "slot", axis=2, tiled=True)
        gain_part = lax.all_gather(gain_piece, "slot", axis=2, tiled=True)
        as_float = feature_piece.astype(jnp.float32)
        scaled = (as_float * gain_part.astype(jnp.float32)).astype(jnp.bfloat16)
        product = jnp.einsum("bnk,kc->bnc", scaled, weight_in, preferred_element_type=jnp.float32)
        square_sum = jnp.sum(as_float * as_float, axis=2)
        query_key_value_rows = (
            product * lax.rsqrt(square_sum / model_width + norm_eps)[..., None]
        ).astype(jnp.bfloat16)
        section_own_rows = lax.all_to_all(
            query_key_value_rows, "slot", split_axis=1, concat_axis=2, tiled=True
        )[:, 0]
        query_rows = section_own_rows[:, : QUERY_HEADS * HEAD_SIZE].reshape(
            rows_of_block, KEY_VALUE_HEADS, query_group_width, HEAD_SIZE
        )
        fresh_key = section_own_rows[
            :, QUERY_HEADS * HEAD_SIZE : QUERY_HEADS * HEAD_SIZE + width_of_keys
        ].reshape(rows_of_block, KEY_VALUE_HEADS, HEAD_SIZE)
        fresh_value = section_own_rows[:, QUERY_HEADS * HEAD_SIZE + width_of_keys :].reshape(
            rows_of_block, KEY_VALUE_HEADS, HEAD_SIZE
        )
        block_of_cache = cache_kv[0, visit_idx, 0 : 0 + rows_of_block, 0]
        lengths = cache_len[0, visit_idx, 0 : 0 + rows_of_block, 0]
        resident_key_rows = block_of_cache[..., :width_of_keys].reshape(
            rows_of_block, cache_extent, KEY_VALUE_HEADS, HEAD_SIZE
        )
        resident_value_rows = block_of_cache[..., width_of_keys:].reshape(
            rows_of_block, cache_extent, KEY_VALUE_HEADS, HEAD_SIZE
        )
        score_cache = jnp.einsum(
            "bhgx,bchx->bhgc", query_rows, resident_key_rows, preferred_element_type=jnp.float32
        )
        score_pages = jnp.einsum(
            "bhgx,phx->bhgp", query_rows, cropped_page_keys, preferred_element_type=jnp.float32
        )
        score_self = jnp.einsum(
            "bhgx,bhx->bhg", query_rows, fresh_key, preferred_element_type=jnp.float32
        )[..., None]
        scores = jnp.concatenate([score_cache, score_pages, score_self], axis=-1) * score_scale
        row_ids = visit_idx * row_count + 0 + jnp.arange(rows_of_block, dtype=jnp.int32)
        visible_cache = jnp.arange(cache_extent, dtype=jnp.int32)[None, :] < lengths[:, None]
        visible_pages = page_live[None] & (owner_row[None, :, None] == row_ids[:, None, None])
        visible_pages = visible_pages.reshape(rows_of_block, slot_indices * page_extent)
        visible = jnp.concatenate(
            [visible_cache, visible_pages, jnp.ones((rows_of_block, 1), dtype=bool)], axis=-1
        )
        scores = jnp.where(visible[:, None, None, :], scores, -1e30)
        row_max = jnp.max(scores, axis=-1, keepdims=True)
        expd = jnp.exp(scores - row_max)
        denominator = jnp.sum(expd, axis=-1, keepdims=True)
        weights = (expd / denominator).astype(jnp.bfloat16)
        context = jnp.einsum(
            "bhgc,bchx->bhgx",
            weights[..., :cache_extent],
            resident_value_rows,
            preferred_element_type=jnp.float32,
        )
        context = context + jnp.einsum(
            "bhgp,phx->bhgx",
            weights[..., cache_extent : cache_extent + slot_indices * page_extent],
            cropped_page_values,
            preferred_element_type=jnp.float32,
        )
        context = context + jnp.einsum(
            "bhg,bhx->bhgx", weights[..., -1], fresh_value, preferred_element_type=jnp.float32
        )
        context = context.astype(jnp.bfloat16).reshape(rows_of_block, 1, QUERY_HEADS * HEAD_SIZE)
        output = jnp.einsum(
            "bnh,hc->bnc",
            lax.all_gather(context, "slot", axis=1, tiled=True),
            weight_out,
            preferred_element_type=jnp.float32,
        )
        updated = (current.astype(jnp.float32) + output).astype(jnp.bfloat16)
        current = shifted(updated, "segment", 1)
    return current[None]


def solution(mesh):
    return jax.shard_map(
        shards,
        mesh=mesh,
        in_specs=(
            P("segment", None, None, "slot"),
            P("segment", "slot"),
            P("segment", None, "slot"),
            P("segment", None, "slot"),
            P("segment", None, None, "slot", None, None),
            P("segment", None, None, "slot"),
            P("segment", "slot", None, None, None),
            P("segment", None, None),
            P("segment", None, None),
            P("segment", None, None),
        ),
        out_specs=P("segment", None, None, "slot"),
        check_vma=False,
    )
```

profile of v0, /device:TPU:0, one launch (start us, length us, event | category | flops | bytes accessed | tf_op | source)
XLA Modules:
  0.0 193.1 jit_solution(1255550048329797405)
XLA Ops:
  6.5 0.7 all-gather.7.cloned.1.call-update
  7.3 1.1 copy.221
  8.4 0.7 dynamic-slice_bitcast_fusion
  9.3 0.8 copy.222
  10.1 7.4 %all-to-all-start.1 = ((bf16[16,8,1024]{2,1,0:T(8,128)(2,1)}), bf16[16,8,1024]{2,1,0:T(8,128)(2,1)S(1)}, u32[]{:S(2)}, u32[]{:S(2)}) async-start(bf16[16,8,1024]{2,1,0:T(8,128)(2,1)} %bitcast.60), calls=%async_computation.1 | async-start | bytes 524288 | tf_op jit(solution)/shard_map/all_to_all | solution.py:54
  17.5 0.8 fusion.80
  18.5 0.8 select_reduce_fusion.1
  20.0 22.2 %all-gather.1 = bf16[1,8192]{1,0:T(2,128)(2,1)S(1)} all-gather(bf16[1,512]{1,0:T(2,128)(2,1)} %param.11), channel_id=3, replica_groups=mesh['segment'=2,'slot'=16] {'slot'}, dimensions={1}, use_global_device_ids=true | all-gather | bytes 17408 | tf_op jit(solution)/shard_map/all_gather | solution.py:75
  42.3 0.7 slice_bitcast_fusion.8
  43.1 1.0 slice_bitcast_fusion.1
  44.2 6.5 %all-gather.7.cloned.1.call-done = bf16[1,4,16,8192]{3,2,1,0:T(8,128)(2,1)} async-done(((bf16[1,4,16,512]{3,2,1,0:T(8,128)(2,1)}), bf16[1,4,16,8192]{3,2,1,0:T(8,128)(2,1)}) %all-gather.7.cloned.1.call-update) | async-done | bytes 1048592 | tf_op jit(solution)/shard_map/all_gather | solution.py:74
  50.6 1.5 fusion.13
  52.2 4.5 %fusion.33 = bf16[4,16,320]{2,1,0:T(8,128)(2,1)S(1)} fusion(bf16[1,8192,320]{1,2,0:T(8,128)(2,1)} %param.12, bf16[1,4,16,8192]{3,2,1,0:T(8,128)(2,1)} %all-gather.7.cloned.1.call-done, f32[8192]{0:T(1024)S(1)} %bitcast.157, f32[4,16]{1,0:T(4,128)S(1)} %add_rsqrt_fusion.1), kind=kOutput, calls=%fused_computation.28 | convolution fusion | flops 337158144 | bytes 6365440 | tf_op jit(solution)/shard_map/bnk,kc->bnc/dot_general | solution.py:78
  56.7 0.6 copy.154
  57.3 4.4 %all-to-all-start = ((bf16[4,16,320]{2,0,1:T(4,128)(2,1)}), bf16[4,16,320]{2,0,1:T(4,128)(2,1)S(1)}, u32[]{:S(2)}, u32[]{:S(2)}) async-start(bf16[4,16,320]{2,0,1:T(4,128)(2,1)} %copy.154), calls=%async_computation | async-start | bytes 98304 | tf_op jit(solution)/shard_map/all_to_all | solution.py:83
  62.0 6.4 %all-to-all-done = bf16[4,16,320]{2,0,1:T(4,128)(2,1)S(1)} async-done(((bf16[4,16,320]{2,0,1:T(4,128)(2,1)}), bf16[4,16,320]{2,0,1:T(4,128)(2,1)S(1)}, u32[]{:S(2)}, u32[]{:S(2)}) %all-to-all-start) | async-done | bytes 40992 | tf_op jit(solution)/shard_map/all_to_all | solution.py:83
  69.1 3.9 %fusion.82 = (f32[4,4,8]{2,1,0:T(4,128)S(1)}, f32[4,4,8,145]{3,2,1,0:T(8,128)S(1)}) fusion(f32[4,4,8,1]{3,2,1,0:T(8,128)S(1)} %convolution_bitcast_fusion.4, f32[4,4,8,16]{3,2,1,0:T(8,128)S(1)} %fusion.60, pred[4,145]{1,0:T(4,128)(4,1)S(1)} %get-tuple-element.24, f32[4,4,8,128]{3,2,0,1:T(8,128)S(1)} %convolution_bitcast_fusion.5), kind=kOutput, calls=%fused_computation.115 | output fusion | flops 111504 | bytes 149572 | tf_op jit(solution)/shard_map/sub | solution.py:122
  73.8 19.0 %all_gather.18 = bf16[4,16,4096]{2,0,1:T(4,128)(2,1)S(1)} all-gather(bf16[4,1,4096]{2,0,1:T(4,128)(2,1)S(1)} %reshape.197), channel_id=1, replica_groups=mesh['segment'=2,'slot'=16] {'slot'}, dimensions={1}, use_global_device_ids=true | all-gather | bytes 557056 | tf_op jit(solution)/shard_map/all_gather | solution.py:143
  92.8 3.1 %fusion.21 = bf16[4,16,512]{2,1,0:T(8,128)(2,1)S(1)} fusion(bf16[1,4096,512]{2,1,0:T(8,128)(2,1)} %param.13, bf16[4,16,4096]{2,0,1:T(4,128)(2,1)S(1)} %all_gather.18, bf16[1,4,16,512]{3,2,1,0:T(8,128)(2,1)S(1)} %copy-done), kind=kOutput, calls=%fused_computation.24 | convolution fusion | flops 268533760 | bytes 4849664 | tf_op jit(solution)/shard_map/bnh,hc->bnc/dot_general | solution.py:141
  95.9 1.5 collective-permute-start
  97.4 2.9 %collective-permute-done = bf16[4,16,512]{2,1,0:T(8,128)(2,1)S(1)} collective-permute-done((bf16[4,16,512]{2,1,0:T(8,128)(2,1)S(1)}, bf16[4,16,512]{2,1,0:T(8,128)(2,1)S(1)}, u32[]{:S(2)}, u32[]{:S(2)}) %collective-permute-start) | collective-permute-done | bytes 65568 | tf_op jit(solution)/shard_map/ppermute | solution.py:18
  100.9 35.2 %all-gather.5.cloned.1.call-done = bf16[4,16,8192]{2,1,0:T(8,128)(2,1)} async-done(((bf16[4,16,512]{2,1,0:T(8,128)(2,1)}), bf16[4,16,8192]{2,1,0:T(8,128)(2,1)}) %all-gather.5.cloned.1.call-update) | async-done | bytes 1048592 | tf_op jit(solution)/shard_map/all_gather | solution.py:74
  136.2 1.5 fusion.11
  137.7 4.5 %fusion.30 = bf16[4,16,320]{2,1,0:T(8,128)(2,1)S(1)} fusion(bf16[1,8192,320]{1,2,0:T(8,128)(2,1)} %param.12, bf16[4,16,8192]{2,1,0:T(8,128)(2,1)} %all-gather.5.cloned.1.call-done, f32[8192]{0:T(1024)S(1)} %bitcast.158, f32[4,16]{1,0:T(4,128)S(1)} %add_rsqrt_fusion), kind=kOutput, calls=%fused_computation.27 | convolution fusion | flops 337158144 | bytes 6365440 | tf_op jit(solution)/shard_map/bnk,kc->bnc/dot_general | solution.py:78
  142.2 0.6 copy.174
  142.8 4.2 %all-to-all-start.2 = ((bf16[4,16,320]{2,0,1:T(4,128)(2,1)}), bf16[4,16,320]{2,0,1:T(4,128)(2,1)S(1)}, u32[]{:S(2)}, u32[]{:S(2)}) async-start(bf16[4,16,320]{2,0,1:T(4,128)(2,1)} %copy.174), calls=%async_computation.2 | async-start | bytes 98304 | tf_op jit(solution)/shard_map/all_to_all | solution.py:83
  147.1 6.7 %all-to-all-done.2 = bf16[4,16,320]{2,0,1:T(4,128)(2,1)S(1)} async-done(((bf16[4,16,320]{2,0,1:T(4,128)(2,1)}), bf16[4,16,320]{2,0,1:T(4,128)(2,1)S(1)}, u32[]{:S(2)}, u32[]{:S(2)}) %all-to-all-start.2) | async-done | bytes 40992 | tf_op jit(solution)/shard_map/all_to_all | solution.py:83
  154.4 3.9 %fusion.83 = (f32[4,4,8]{2,1,0:T(4,128)S(1)}, f32[4,4,8,145]{3,2,1,0:T(8,128)S(1)}) fusion(f32[4,4,8,1]{3,2,1,0:T(8,128)S(1)} %convolution_bitcast_fusion.1, f32[4,4,8,16]{3,2,1,0:T(8,128)S(1)} %fusion.54, pred[4,145]{1,0:T(4,128)(4,1)S(1)} %get-tuple-element.23, f32[4,4,8,128]{3,2,0,1:T(8,128)S(1)} %convolution_bitcast_fusion.2), kind=kOutput, calls=%fused_computation.116 | output fusion | flops 111504 | bytes 149572 | tf_op jit(solution)/shard_map/sub | solution.py:122
  159.1 19.0 %all_gather.20 = bf16[4,16,4096]{2,0,1:T(4,128)(2,1)S(1)} all-gather(bf16[4,1,4096]{2,0,1:T(4,128)(2,1)S(1)} %reshape.204), channel_id=1, replica_groups=mesh['segment'=2,'slot'=16] {'slot'}, dimensions={1}, use_global_device_ids=true | all-gather | bytes 557056 | tf_op jit(solution)/shard_map/all_gather | solution.py:143
  178.1 3.1 %add_convert_fusion = bf16[4,16,512]{2,1,0:T(8,128)(2,1)S(1)} fusion(bf16[4,16,512]{2,1,0:T(8,128)(2,1)S(1)} %copy-done.2, bf16[1,4096,512]{2,1,0:T(8,128)(2,1)} %param.13, bf16[4,16,4096]{2,0,1:T(4,128)(2,1)S(1)} %all_gather.20), kind=kOutput, calls=%fused_computation.50 | convolution fusion | flops 268533760 | bytes 4849664 | tf_op jit(solution)/shard_map/bnh,hc->bnc/dot_general | solution.py:141
  181.2 1.5 collective-permute-start.1
  182.8 2.9 %collective-permute-done.1 = bf16[4,16,512]{2,1,0:T(8,128)(2,1)S(1)} collective-permute-done((bf16[4,16,512]{2,1,0:T(8,128)(2,1)S(1)}, bf16[4,16,512]{2,1,0:T(8,128)(2,1)S(1)}, u32[]{:S(2)}, u32[]{:S(2)}) %collective-permute-start.1) | collective-permute-done | bytes 65568 | tf_op jit(solution)/shard_map/ppermute | solution.py:18
  (69 shorter events, 5.7 us)
Async XLA Ops:
  6.5 44.1 %all-gather.7.cloned.1.call-start = ((), (), s32[]{:S(2)}) async-start(), calls=%async_computation.4 | async-start | bytes 1114112 | tf_op jit(solution)/shard_map/all_gather | solution.py:74
  10.1 47.2 %all-to-all-start.1 = ((bf16[16,8,1024]{2,1,0:T(8,128)(2,1)}), bf16[16,8,1024]{2,1,0:T(8,128)(2,1)S(1)}, u32[]{:S(2)}, u32[]{:S(2)}) async-start(bf16[16,8,1024]{2,1,0:T(8,128)(2,1)} %bitcast.60), calls=%async_computation.1 | async-start | bytes 524288 | tf_op jit(solution)/shard_map/all_to_all | solution.py:54
  52.2 40.6 %copy-start = (bf16[1,4,16,512]{3,2,1,0:T(8,128)(2,1)S(1)}, bf16[1,4,16,512]{3,2,1,0:T(8,128)(2,1)}, u32[]{:S(2)}) copy-start(bf16[1,4,16,512]{3,2,1,0:T(8,128)(2,1)} %param.10) | copy-start | bytes 196612
  57.3 11.1 %all-to-all-start = ((bf16[4,16,320]{2,0,1:T(4,128)(2,1)}), bf16[4,16,320]{2,0,1:T(4,128)(2,1)S(1)}, u32[]{:S(2)}, u32[]{:S(2)}) async-start(bf16[4,16,320]{2,0,1:T(4,128)(2,1)} %copy.154), calls=%async_computation | async-start | bytes 98304 | tf_op jit(solution)/shard_map/all_to_all | solution.py:83
  61.7 74.5 %all-gather.5.cloned.1.call-start = ((), (), s32[]{:S(2)}) async-start(), calls=%async_computation.3 | async-start | bytes 1114112 | tf_op jit(solution)/shard_map/all_gather | solution.py:74
  95.9 4.4 %collective-permute-start = (bf16[4,16,512]{2,1,0:T(8,128)(2,1)S(1)}, bf16[4,16,512]{2,1,0:T(8,128)(2,1)S(1)}, u32[]{:S(2)}, u32[]{:S(2)}) collective-permute-start(bf16[4,16,512]{2,1,0:T(8,128)(2,1)S(1)} %fusion.21), channel_id=1, source_target_pairs={{16,0},{0,16},{17,1},{1,17},{18,2},{2,18},{19,3},{3,19},{20,4},{4,... | collective-permute-start | bytes 196616 | tf_op jit(solution)/shard_map/ppermute | solution.py:18
  100.3 0.6 copy-start.1
  137.7 40.4 %copy-start.2 = (bf16[4,16,512]{2,1,0:T(8,128)(2,1)S(1)}, bf16[4,16,512]{2,1,0:T(8,128)(2,1)}, u32[]{:S(2)}) copy-start(bf16[4,16,512]{2,1,0:T(8,128)(2,1)} %copy-done.1) | copy-start | bytes 196612
  142.8 11.0 %all-to-all-start.2 = ((bf16[4,16,320]{2,0,1:T(4,128)(2,1)}), bf16[4,16,320]{2,0,1:T(4,128)(2,1)S(1)}, u32[]{:S(2)}, u32[]{:S(2)}) async-start(bf16[4,16,320]{2,0,1:T(4,128)(2,1)} %copy.174), calls=%async_computation.2 | async-start | bytes 98304 | tf_op jit(solution)/shard_map/all_to_all | solution.py:83
  181.2 4.4 %collective-permute-start.1 = (bf16[4,16,512]{2,1,0:T(8,128)(2,1)S(1)}, bf16[4,16,512]{2,1,0:T(8,128)(2,1)S(1)}, u32[]{:S(2)}, u32[]{:S(2)}) collective-permute-start(bf16[4,16,512]{2,1,0:T(8,128)(2,1)S(1)} %add_convert_fusion), channel_id=1, source_target_pairs={{16,0},{0,16},{17,1},{1,17},{18,2},{2,18},{19,3},{3,19},{20,4},{4,... | collective-permute-start | bytes 196616 | tf_op jit(solution)/shard_map/ppermute | solution.py:18
Sparse Core Ops, SparseCore 0:
  9.5 41.0 all-gather.6
  101.1 35.0 all-gather.4
where the time goes:
time: 194 us; the launch traced here: 193 us
  waiting for transfers between devices  61.3 us (32%)
  blocking collectives  60.1 us (31%)
  starting transfers between devices  19 us (10%)
  matrix products  17 us (9%)
  between operations  13.7 us (7%)
  other arithmetic  13.1 us (7%)
  local copies, waits for them, and re-layouts  8.89 us (5%)
    all_gather x2, waiting for transfers between devices, shards(): feature_piece = lax.all_gather(current, 'slot', axis=2, tiled=True)  41.7 us
    all_gather x2, blocking collectives, shards(): lax.all_gather(context, 'slot', axis=1, tiled=True)  38 us
    all_gather x1, blocking collectives, shards(): gain_part = lax.all_gather(gain_piece, 'slot', axis=2, tiled=True)  22.2 us
    all_to_all x2, waiting for transfers between devices, shards(): lax.all_to_all(query_key_value_rows, 'slot', split_axis=1, concat_axis=2,...  13.2 us
    dot_general x2, matrix products, shards(): jnp.einsum('bnk,kc->bnc', scaled, weight_in, preferred_element_type=jnp.f...  8.99 us
    all_to_all x2, starting transfers between devices, shards(): lax.all_to_all(query_key_value_rows, 'slot', split_axis=1, concat_axis=2,...  8.55 us
    sub x2, other arithmetic, shards(): expd = jnp.exp(scores - row_max)  7.84 us
    all_to_all x1, starting transfers between devices, shards(): lax.all_to_all(outgoing, 'slot', split_axis=0, concat_axis=0, tiled=True)  7.36 us
  transfers between devices with their start and end apart: 7, of which 6 were waited for; matrix products, arithmetic and copies ran while one was open for 7% of the time, Pallas kernels for 0%

commit v1 on v0

v1 whole, which is shorter than its diff:
```python
import functools

import jax
import jax.numpy as jnp
import numpy as np
from jax import lax
from jax.experimental import pallas as pl
from jax.experimental.pallas import tpu as pltpu
from jax.sharding import PartitionSpec as P

QUERY_HEADS = 32
KEY_VALUE_HEADS = 4
HEAD_SIZE = 128
CYCLE_STEPS = 2
GROUP = QUERY_HEADS // KEY_VALUE_HEADS
KEY_WIDTH = KEY_VALUE_HEADS * HEAD_SIZE
LANES = 128

norm_eps = 1e-06
VMEM_LIMIT = 24 * 1024 * 1024


def params(**kw):
    return pltpu.CompilerParams(vmem_limit_bytes=VMEM_LIMIT, **kw)


def iota(shape, dim):
    return lax.broadcasted_iota(jnp.int32, shape, dim)


def exchange(block, mask):
    n = lax.axis_size("slot")
    return lax.ppermute(block, "slot", [(i, i ^ mask) for i in range(n)])


def next_segment(block):
    n = lax.axis_size("segment")
    return lax.ppermute(block, "segment", [(i, (i + 1) % n) for i in range(n)])


def row_order(slots, batch, inverse):
    rows = slots * batch
    out, src = iota((rows, rows), 0), iota((rows, rows), 1)
    if inverse:
        want = lax.rem(out, slots) * batch + out // slots
    else:
        want = lax.rem(out, batch) * slots + out // batch
    return (src == want).astype(jnp.bfloat16)


def prep_kernel(own_ref, dest_sm, x_ref, gain_ref, pages_ref, dest_ref, row_ref, count_ref,
                x_out, scaled_out, send_ref, code_ref, *, slots, batch):
    rows, width = x_ref.shape
    order = row_order(slots, batch, False)
    x = jnp.dot(order, x_ref[...], preferred_element_type=jnp.float32)
    x_out[...] = x.astype(jnp.bfloat16)
    gain = gain_ref[...].astype(jnp.float32)
    scaled_out[0] = (x * gain).astype(jnp.bfloat16)
    column = jnp.sum(x * x, axis=1, keepdims=True)
    extra = jnp.zeros((8, LANES), jnp.float32)
    at = iota((8, LANES), 0)
    gain_rows = width // LANES
    for r in range(gain_rows):
        extra = jnp.where(at == r, gain[:, r * LANES:(r + 1) * LANES], extra)
    spans = -(-rows // LANES)
    ident_row, ident_lane = iota((rows, LANES), 0), iota((rows, LANES), 1)
    for r in range(spans):
        line = jnp.sum(jnp.where(ident_row == ident_lane + r * LANES, column, 0.0), axis=0,
                       keepdims=True)
        for part in range(3):
            piece = line.astype(jnp.bfloat16).astype(jnp.float32)
            extra = jnp.where(at == gain_rows + 3 * r + part, piece, extra)
            line = line - piece
    extra = extra.astype(jnp.bfloat16)
    kv_width = pages_ref.shape[2]
    own = own_ref[0]
    for p in range(pages_ref.shape[0]):
        send_ref[dest_sm[own, p], :, :kv_width] = pages_ref[p]
    for j in range(slots):
        send_ref[j, :, kv_width:] = extra
    tokens = code_ref.shape[1]
    page_tok = tokens // slots
    mine = dest_ref[...] == own
    spread = (iota((slots, tokens), 1) // page_tok == iota((slots, tokens), 0)).astype(jnp.float32)

    def to_tokens(values):
        kept = jnp.where(mine, values, 0).astype(jnp.float32)
        wide = lax.dot_general(kept, spread, (((0,), (0,)), ((), ())),
                               preferred_element_type=jnp.float32)
        return jnp.sum(wide, axis=0, keepdims=True)

    place = lax.rem(iota((1, tokens), 1), page_tok).astype(jnp.float32)
    live = place < to_tokens(count_ref[...])
    code = jnp.where(live, to_tokens(row_ref[...]), -1.0)
    code_ref[...] = jnp.broadcast_to(code, code_ref.shape).astype(jnp.int32)


def prepare(own, x, gain, pages, dest, row, count):
    batch, slots, width = x.shape
    rows = batch * slots
    total, page_tok, kv_width = pages.shape
    whole = pl.BlockSpec(memory_space=pltpu.VMEM)
    scalar = pl.BlockSpec(memory_space=pltpu.SMEM)
    return pl.pallas_call(
        functools.partial(prep_kernel, slots=slots, batch=batch),
        out_shape=[
            jax.ShapeDtypeStruct((rows, width), jnp.bfloat16),
            jax.ShapeDtypeStruct((1, rows, width), jnp.bfloat16),
            jax.ShapeDtypeStruct((slots, page_tok, kv_width + LANES), jnp.bfloat16),
            jax.ShapeDtypeStruct((8, slots * page_tok), jnp.int32),
        ],
        in_specs=[scalar, scalar] + [whole] * 6,
        out_specs=[whole] * 4,
        compiler_params=params(),
        name="prepare",
    )(own, dest, x.reshape(rows, width), gain, pages, dest, row, count)


def project_kernel(*refs, first, last, scale, rows_sum, slots, batch, model_width):
    order_ref, x_ref, w_ref = refs[:3]
    refs = list(refs[3:])
    extra_ref = refs.pop(0) if (scale or (last and not scale)) else None
    acc_in = None if first else refs.pop(0)
    sum_in = None if first or not scale else refs.pop(0)
    if last:
        out_ref = refs.pop(0)
        acc = refs.pop(0)
        square = refs.pop(0) if scale else None
    else:
        acc = refs.pop(0)
        square = refs.pop(0) if scale else None
    step = pl.program_id(0)

    @pl.when(step == 0)
    def _():
        acc[...] = jnp.zeros_like(acc) if first else acc_in[...]
        if scale:
            square[...] = jnp.zeros_like(square) if first else sum_in[...]

    x = x_ref[0]
    rows, width = x.shape
    if scale:
        parts = []
        total = square[...]
        for r in range(width // LANES):
            part = x[:, r * LANES:(r + 1) * LANES].astype(jnp.float32)
            total = total + part * part
            parts.append((part * extra_ref[0, r:r + 1, :].astype(jnp.float32)).astype(jnp.bfloat16))
        square[...] = total
        x = parts[0] if len(parts) == 1 else jnp.concatenate(parts, axis=1)
    acc[...] += jnp.dot(x, w_ref[...], preferred_element_type=jnp.float32)

    if last:
        @pl.when(step == pl.num_programs(0) - 1)
        def _():
            if scale:
                sums = jnp.sum(square[...], axis=1, keepdims=True)
            else:
                gain_rows = width // LANES
                lines = jnp.sum(extra_ref[...].astype(jnp.float32), axis=0)
                sums = jnp.zeros((rows, 1), jnp.float32)
                ident_row, ident_lane = iota((rows, LANES), 0), iota((rows, LANES), 1)
                for r in range(-(-rows // LANES)):
                    at = gain_rows + 3 * r
                    line = lines[at:at + 1] + lines[at + 1:at + 2] + lines[at + 2:at + 3]
                    sums = sums + jnp.sum(
                        jnp.where(ident_row == ident_lane + r * LANES, line, 0.0), axis=1,
                        keepdims=True)
            out = acc[...] * lax.rsqrt(sums / model_width + norm_eps)
            for j in range(slots):
                out_ref[j] = out[j * batch:(j + 1) * batch].astype(jnp.bfloat16)


def project(order, start, x, weight, extra, state, *, scale, last, slots, batch, kv_width):
    blocks, rows, width = x.shape
    columns = weight.shape[1]
    first = state is None
    page_tok = extra.shape[1]
    in_specs = [
        pl.BlockSpec((1, rows, width), lambda s, order: (s, 0, 0)),
        pl.BlockSpec((width, columns), lambda s, order: (order[start + s], 0)),
    ]
    operands = [x, weight]
    if scale:
        in_specs.append(pl.BlockSpec((1, page_tok, LANES),
                                     lambda s, order: (order[start + s], 0, kv_width // LANES)))
        operands.append(extra)
    elif last:
        in_specs.append(pl.BlockSpec((slots, page_tok, LANES),
                                     lambda s, order: (0, 0, kv_width // LANES)))
        operands.append(extra)
    acc_shape = jax.ShapeDtypeStruct((rows, columns), jnp.float32)
    sum_shape = jax.ShapeDtypeStruct((rows, LANES), jnp.float32)
    fixed = lambda shape: pl.BlockSpec(shape, lambda s, order: (0,) * len(shape))
    if not first:
        for value in state:
            in_specs.append(fixed(value.shape))
            operands.append(value)
    scratch = []
    if last:
        out_shape = jax.ShapeDtypeStruct((slots, batch, columns), jnp.bfloat16)
        out_specs = fixed(out_shape.shape)
        scratch = [pltpu.VMEM((rows, columns), jnp.float32)]
        if scale:
            scratch.append(pltpu.VMEM((rows, LANES), jnp.float32))
    else:
        out_shape = [acc_shape] + ([sum_shape] if scale else [])
        out_specs = [fixed(s.shape) for s in out_shape]
    return pl.pallas_call(
        functools.partial(project_kernel, first=first, last=last, scale=scale, rows_sum=None,
                          slots=slots, batch=batch, model_width=weight.shape[0]),
        out_shape=out_shape,
        grid_spec=pltpu.PrefetchScalarGridSpec(
            num_scalar_prefetch=1, grid=(blocks,), in_specs=in_specs, out_specs=out_specs,
            scratch_shapes=scratch),
        compiler_params=params(),
        cost_estimate=pl.CostEstimate(flops=8 * rows * width * columns * blocks,
                                      bytes_accessed=2 * width * columns * blocks,
                                      transcendentals=0),
        name="project",
    )(order, *operands)


def attend_kernel(len_ref, qkv_ref, cache_ref, pages_ref, code_ref, out_ref, *, visit):
    slots, batch, columns = qkv_ref.shape
    positions = cache_ref.shape[2]
    tokens = pages_ref.shape[0]
    full = jnp.concatenate([qkv_ref[j].astype(jnp.float32) for j in range(slots)], axis=1)
    group_rows = GROUP * batch
    near = batch * positions
    near_pad = -(-(near + 16) // LANES) * LANES
    rows = KEY_VALUE_HEADS * group_rows
    nt = (((1,), (1,)), ((), ()))
    far_scores, near_scores, near_values = [], [], []
    key_at = QUERY_HEADS * HEAD_SIZE
    value_at = key_at + KEY_WIDTH
    for h in range(KEY_VALUE_HEADS):
        query = jnp.concatenate(
            [full[:, (h * GROUP + g) * HEAD_SIZE:(h * GROUP + g + 1) * HEAD_SIZE]
             for g in range(GROUP)], axis=0).astype(jnp.bfloat16)
        lo, hi = h * HEAD_SIZE, (h + 1) * HEAD_SIZE

        def nearby(cache_lo, fresh_lo):
            fresh = full[:, fresh_lo:fresh_lo + HEAD_SIZE]
            fresh = jnp.concatenate(
                [fresh, jnp.zeros((near_pad - near - batch, HEAD_SIZE), jnp.float32)], axis=0)
            old = [cache_ref[0, b, :, cache_lo:cache_lo + HEAD_SIZE] for b in range(batch)]
            return jnp.concatenate(old + [fresh.astype(jnp.bfloat16)], axis=0)

        keys = nearby(lo, key_at + lo)
        near_values.append(nearby(KEY_WIDTH + lo, value_at + lo))
        far_scores.append(lax.dot_general(query, pages_ref[:, lo:hi], nt,
                                          preferred_element_type=jnp.float32))
        near_scores.append(lax.dot_general(query, keys, nt, preferred_element_type=jnp.float32))
    scale = HEAD_SIZE ** (-0.5)
    far = jnp.concatenate(far_scores, axis=0) * scale
    close = jnp.concatenate(near_scores, axis=0) * scale
    far_row = lax.rem(iota((rows, tokens), 0), batch)
    far = jnp.where(code_ref[0:1, :] == far_row + visit * batch, far, -1e30)
    row = lax.rem(iota((rows, near_pad), 0), batch)
    lane = iota((rows, near_pad), 1)
    lengths = jnp.zeros((rows, near_pad), jnp.int32)
    for b in range(batch):
        lengths = jnp.where(row == b, len_ref[visit, b], lengths)
    position = lane - row * positions
    seen = (position >= 0) & (position < lengths) | (lane == near + row)
    close = jnp.where(seen, close, -1e30)
    top = jnp.maximum(jnp.max(far, axis=1, keepdims=True), jnp.max(close, axis=1, keepdims=True))
    far = jnp.exp(far - top)
    close = jnp.exp(close - top)
    denominator = jnp.sum(far, axis=1, keepdims=True) + jnp.sum(close, axis=1, keepdims=True)
    far = (far / denominator).astype(jnp.bfloat16)
    close = (close / denominator).astype(jnp.bfloat16)
    for h in range(KEY_VALUE_HEADS):
        mine = slice(h * group_rows, (h + 1) * group_rows)
        lo = KEY_WIDTH + h * HEAD_SIZE
        context = jnp.dot(far[mine], pages_ref[:, lo:lo + HEAD_SIZE],
                          preferred_element_type=jnp.float32)
        context = context + jnp.dot(close[mine], near_values[h],
                                    preferred_element_type=jnp.float32)
        for g in range(GROUP):
            at = (h * GROUP + g) * HEAD_SIZE
            out_ref[0, :, at:at + HEAD_SIZE] = context[g * batch:(g + 1) * batch].astype(
                jnp.bfloat16)


def attend(lengths, qkv, cache, pages, code, visit):
    slots, batch, columns = qkv.shape
    _, _, positions, kv_width = cache.shape
    tokens = pages.shape[0]
    return pl.pallas_call(
        functools.partial(attend_kernel, visit=visit),
        out_shape=jax.ShapeDtypeStruct((1, batch, QUERY_HEADS * HEAD_SIZE), jnp.bfloat16),
        grid=(1,),
        in_specs=[
            pl.BlockSpec(memory_space=pltpu.SMEM),
            pl.BlockSpec((slots, batch, columns), lambda s: (0, 0, 0)),
            pl.BlockSpec((1, batch, positions, kv_width), lambda s: (visit, 0, 0, 0)),
            pl.BlockSpec((tokens, kv_width), lambda s: (0, 0)),
            pl.BlockSpec(code.shape, lambda s: (0, 0)),
        ],
        out_specs=pl.BlockSpec((1, batch, QUERY_HEADS * HEAD_SIZE), lambda s: (0, 0, 0)),
        compiler_params=params(),
        name="attend",
    )(lengths, qkv, cache, pages, code)


def output_kernel(place_ref, near_ref, far_ref, w_ref, now_ref, out_ref, left, acc, *, slots,
                  batch, final):
    step = pl.program_id(0)
    depth = w_ref.shape[0]
    half = near_ref.shape[0]

    @pl.when(step == 0)
    def _():
        acc[...] = jnp.zeros_like(acc)
        for j in range(slots):
            place = place_ref[j]
            spot = lax.rem(place, half)
            held = jnp.where(place < half, near_ref[spot], far_ref[spot])
            held = held.astype(jnp.float32)
            for k in range(left.shape[0]):
                left[k, j * batch:(j + 1) * batch, :] = held[:, k * depth:(k + 1) * depth]

    acc[...] += jnp.dot(left[step].astype(jnp.bfloat16), w_ref[...],
                        preferred_element_type=jnp.float32)

    @pl.when(step == pl.num_programs(0) - 1)
    def _():
        updated = (now_ref[...].astype(jnp.float32) + acc[...]).astype(jnp.bfloat16)
        if final:
            back = row_order(slots, batch, True)
            updated = jnp.dot(back, updated, preferred_element_type=jnp.float32).astype(
                jnp.bfloat16)
        out_ref[...] = updated


def output(place, near, far, weight, now, final):
    half, batch, features = near.shape
    slots = 2 * half
    rows, columns = now.shape
    steps = 4
    depth = features // steps
    fixed = lambda *shape: pl.BlockSpec(shape, lambda s, place: (0,) * len(shape))
    return pl.pallas_call(
        functools.partial(output_kernel, slots=slots, batch=batch, final=final),
        out_shape=jax.ShapeDtypeStruct((rows, columns), jnp.bfloat16),
        grid_spec=pltpu.PrefetchScalarGridSpec(
            num_scalar_prefetch=1, grid=(steps,),
            in_specs=[
                fixed(*near.shape), fixed(*far.shape),
                pl.BlockSpec((depth, columns), lambda s, place: (s, 0)),
                fixed(rows, columns),
            ],
            out_specs=fixed(rows, columns),
            scratch_shapes=[
                pltpu.VMEM((steps, rows, depth), jnp.float32),
                pltpu.VMEM((rows, columns), jnp.float32),
            ]),
        compiler_params=params(),
        name="output",
    )(place, near, far, weight, now)


def shards(hidden_rows, norm_gain, qkv_weight, out_weight, cache_kv, cache_len, page_kv,
           page_dest, page_row, page_count):
    slots = lax.axis_size("slot")
    batch = hidden_rows.shape[1]
    rows = batch * slots
    width = hidden_rows.shape[3]
    kv_width = cache_kv.shape[5]
    own = lax.axis_index("slot").astype(jnp.int32)
    masks = [slots >> (k + 1) for k in range(slots.bit_length() - 1)]
    offsets = [0]
    for mask in masks:
        offsets = offsets + [mask ^ o for o in offsets]
    order = own ^ jnp.asarray(np.array(offsets, np.int32))
    places = np.argsort(np.array(offsets)).astype(np.int32)
    place = jnp.asarray(places)[own ^ jnp.arange(slots, dtype=jnp.int32)]
    cache = cache_kv[0, :, :, 0]
    lengths = cache_len[0, :, :, 0]
    current, scaled, outgoing, code = prepare(
        own.reshape(1), hidden_rows[0], norm_gain, page_kv[0, 0], page_dest[0], page_row[0],
        page_count[0])
    incoming = lax.all_to_all(outgoing, "slot", split_axis=0, concat_axis=0, tiled=True)
    pages = incoming.reshape(-1, kv_width + LANES)
    for visit in range(CYCLE_STEPS):
        later = visit > 0
        block = current[None] if later else scaled
        for mask in masks[:-2]:
            block = jnp.concatenate([block, exchange(block, mask)], axis=0)
        quarter = block.shape[0]
        side = exchange(block, masks[-2])
        pair = exchange(block, masks[-1])
        corner = exchange(side, masks[-1])
        run = functools.partial(project, order, weight=qkv_weight[0], extra=incoming,
                                scale=later, slots=slots, batch=batch, kv_width=kv_width)
        state = run(start=0, x=block, state=None, last=False)
        state = run(start=2 * quarter, x=pair, state=state, last=False)
        state = run(start=quarter, x=side, state=state, last=False)
        qkv = run(start=3 * quarter, x=corner, state=state, last=True)
        qkv = lax.all_to_all(qkv, "slot", split_axis=0, concat_axis=0, tiled=True)
        context = attend(lengths, qkv, cache, pages, code, visit)
        for mask in masks[:-1]:
            context = jnp.concatenate([context, exchange(context, mask)], axis=0)
        other = exchange(context, masks[-1])
        updated = output(place, context, other, out_weight[0], current,
                         visit == CYCLE_STEPS - 1)
        current = next_segment(updated)
    return current.reshape(hidden_rows.shape)


def solution(mesh):
    return jax.shard_map(
        shards,
        mesh=mesh,
        in_specs=(
            P("segment", None, None, "slot"),
            P("segment", "slot"),
            P("segment", None, "slot"),
            P("segment", None, "slot"),
            P("segment", None, None, "slot", None, None),
            P("segment", None, None, "slot"),
            P("segment", "slot", None, None, None),
            P("segment", None, None),
            P("segment", None, None),
            P("segment", None, None),
        ),
        out_specs=P("segment", None, None, "slot"),
        check_vma=False,
    )
```

time: 194 us -> 146 us (0.75)
  blocking collectives: 60.1 us -> 21.9 us
  Pallas kernels: 0 us -> 19.6 us
  local copies, waits for them, and re-layouts: 8.89 us -> 25.9 us
  matrix products: 17 us -> 0 us
  between operations: 13.7 us -> 0.29 us
  other arithmetic: 13.1 us -> 0.73 us
  waiting for transfers between devices: 61.3 us -> 57.8 us
    all_gather x3 -> x0, blocking collectives: 60.1 us -> none  [the longest x2 38 us: shards(): lax.all_gather(context, 'slot', axis=1, tiled=True)]
    ppermute x2 -> x20, waiting for transfers between devices: 5.75 us -> 57.8 us  [the longest x18 52.3 us: exchange(): return lax.ppermute(block, 'slot', [(i, i ^ mask) for i in range(n)])]
    all_gather x2 -> x0, waiting for transfers between devices: 41.7 us -> none  [shards(): feature_piece = lax.all_gather(current, 'slot', axis=2, tiled=True)]
    all_to_all x0 -> x2, blocking collectives: none -> 21.9 us  [shards(): qkv = lax.all_to_all(qkv, 'slot', split_axis=0, concat_axis=0, tiled=True)]
    unnamed x15 -> x34, local copies, waits for them, and re-layouts: 3.62 us -> 25.2 us
    pallas_call x0 -> x13, Pallas kernels: none -> 19.6 us  [the longest x8 11.6 us: project(): pl.pallas_call(functools.partial(project_kernel, first=first, last=last,...]
    dot_general x15 -> x0, matrix products: 17 us -> none  [the longest x2 8.99 us: shards(): jnp.einsum('bnk,kc->bnc', scaled, weight_in, preferred_element_type=jnp.f...]
    all_to_all x2 -> x0, waiting for transfers between devices: 13.2 us -> none  [shards(): lax.all_to_all(query_key_value_rows, 'slot', split_axis=1, concat_axis=2,...]
  transfers between devices with their start and end apart: 7 -> 21, of which waited for: 6 -> 15; matrix products, arithmetic and copies ran while one was open for 7% -> 6% of each run, Pallas kernels for 0% -> 6%
where the time goes in v1:
time: 146 us; the launch traced here: 145 us
  waiting for transfers between devices  57.8 us (40%)
  local copies, waits for them, and re-layouts  25.9 us (18%)
  blocking collectives  21.9 us (15%)
  Pallas kernels  19.6 us (13%)
  starting transfers between devices  18.6 us (13%)
    ppermute x18, waiting for transfers between devices, exchange(): return lax.ppermute(block, 'slot', [(i, i ^ mask) for i in range(n)])  52.3 us
    unnamed x34, local copies, waits for them, and re-layouts  25.2 us
    all_to_all x2, blocking collectives, shards(): qkv = lax.all_to_all(qkv, 'slot', split_axis=0, concat_axis=0, tiled=True)  21.9 us
    pallas_call x8, Pallas kernels, project(): pl.pallas_call(functools.partial(project_kernel, first=first, last=last,...  11.6 us
    ppermute x18, starting transfers between devices, exchange(): return lax.ppermute(block, 'slot', [(i, i ^ mask) for i in range(n)])  10.7 us
    ppermute x2, waiting for transfers between devices, next_segment(): return lax.ppermute(block, 'segment', [(i, (i + 1) % n) for i in range(n)])  5.49 us
    all_to_all x1, starting transfers between devices, shards(): lax.all_to_all(outgoing, 'slot', split_axis=0, concat_axis=0, tiled=True)  4.66 us
    pallas_call x2, Pallas kernels, output(): pl.pallas_call(functools.partial(output_kernel, slots=slots, batch=batch,...  4.05 us
  transfers between devices with their start and end apart: 21, of which 15 were waited for; matrix products, arithmetic and copies ran while one was open for 6% of the time, Pallas kernels for 6%

profile of v1, /device:TPU:0, one launch (start us, length us, event | category | flops | bytes accessed | tf_op | source)
XLA Modules:
  0.0 144.8 jit_solution(4811912788372760444)
XLA Ops:
  4.6 1.6 %prepare.1 = (bf16[64,512]{1,0:T(8,128)(2,1)S(1)}, bf16[1,64,512]{2,1,0:T(8,128)(2,1)S(1)}, bf16[16,8,1152]{2,1,0:T(8,128)(2,1)}, s32[8,128]{1,0:T(8,128)S(1)}) custom-call(s32[1]{0:T(128)} %bitcast.2.own_ref, s32[16,16]{1,0:T(8,128)S(1)} %bitcast.34, bf16[64,512]{1,0:T(8,128)(2,1)S(1)} %bitcast.33, bf16[1,512]{1,0:T(2,128)(2,1)S(1)} %copy-done.13, ...), custom_call_target="tpu_custom_call" | custom-call | tf_op jit(solution)/shard_map/prepare/pallas_call | solution.py:104
  6.2 4.0 %collective-permute-start = (bf16[1,64,512]{2,1,0:T(8,128)(2,1)S(1)}, bf16[1,64,512]{2,1,0:T(8,128)(2,1)S(1)}, u32[]{:S(2)}, u32[]{:S(2)}) collective-permute-start(bf16[1,64,512]{2,1,0:T(8,128)(2,1)S(1)} %get-tuple-element.15), channel_id=1, source_target_pairs={{0,8},{1,9},{2,10},{3,11},{4,12},{5,13},{6,14},{7,15},{8,0},{9,1},... | collective-permute-start | bytes 196616 | tf_op jit(solution)/shard_map/ppermute | solution.py:33
  10.2 3.6 %collective-permute-done = bf16[1,64,512]{2,1,0:T(8,128)(2,1)S(1)} collective-permute-done((bf16[1,64,512]{2,1,0:T(8,128)(2,1)S(1)}, bf16[1,64,512]{2,1,0:T(8,128)(2,1)S(1)}, u32[]{:S(2)}, u32[]{:S(2)}) %collective-permute-start) | collective-permute-done | bytes 65568 | tf_op jit(solution)/shard_map/ppermute | solution.py:33
  14.5 4.4 %collective-permute-done.1 = bf16[2,64,512]{2,1,0:T(8,128)(2,1)S(1)} collective-permute-done((bf16[2,64,512]{2,1,0:T(8,128)(2,1)S(1)}, bf16[2,64,512]{2,1,0:T(8,128)(2,1)S(1)}, u32[]{:S(2)}, u32[]{:S(2)}) %collective-permute-start.1) | collective-permute-done | bytes 131104 | tf_op jit(solution)/shard_map/ppermute | solution.py:33
  18.9 1.8 %collective-permute-start.2 = (bf16[4,64,512]{2,1,0:T(8,128)(2,1)S(1)}, bf16[4,64,512]{2,1,0:T(8,128)(2,1)S(1)}, u32[]{:S(2)}, u32[]{:S(2)}) collective-permute-start(bf16[4,64,512]{2,1,0:T(8,128)(2,1)S(1)} %constant_dynamic-update-slice_fusion.refs_1_), channel_id=1, source_target_pairs={{0,2},{1,3},{2,0},{3,1},{4,6},{5,7},{6,4},{7,5},{8,10},{9,11},{10,... | collective-permute-start | bytes 786440 | tf_op jit(solution)/shard_map/ppermute | solution.py:33
  20.7 4.7 %all-to-all-start = ((bf16[16,8,1152]{2,1,0:T(8,128)(2,1)}), bf16[16,8,1152]{2,1,0:T(8,128)(2,1)S(1)}, u32[]{:S(2)}, u32[]{:S(2)}) async-start(bf16[16,8,1152]{2,1,0:T(8,128)(2,1)} %get-tuple-element.16), calls=%async_computation | async-start | bytes 589824 | tf_op jit(solution)/shard_map/all_to_all | solution.py:385
  25.9 8.1 %copy.14 = bf16[1,8192,320]{2,1,0:T(8,128)(2,1)} copy(bf16[1,8192,320]{1,2,0:T(8,128)(2,1)} %param.14) | data formatting | bytes 10485760 | tf_op args[2]
  34.1 2.8 %copy-done = bf16[1,8192,320]{2,1,0:T(8,128)(2,1)S(1)} copy-done((bf16[1,8192,320]{2,1,0:T(8,128)(2,1)S(1)}, bf16[1,8192,320]{2,1,0:T(8,128)(2,1)}, u32[]{:S(2)}) %copy-start) | copy-done | bytes 5242904
  36.9 1.4 project.8.refs_3_
  42.6 2.8 %copy-done.2 = bf16[1,8192,320]{2,1,0:T(8,128)(2,1)S(1)} copy-done((bf16[1,8192,320]{2,1,0:T(8,128)(2,1)S(1)}, bf16[1,8192,320]{2,1,0:T(8,128)(2,1)}, u32[]{:S(2)}) %copy-start.2) | copy-done | bytes 5242904
  45.4 1.6 %project.11 = bf16[16,4,320]{2,1,0:T(4,128)(2,1)S(1)} custom-call(s32[16]{0:T(128)S(1)} %broadcast_xor_fusion.refs_0_, bf16[4,64,512]{2,1,0:T(8,128)(2,1)S(1)} %collective-permute-done.3.refs_1_, bf16[8192,320]{1,0:T(8,128)(2,1)S(1)} %bitcast.18, bf16[16,8,1152]{2,1,0:T(8,128)(2,1)S(1)} %all-to-all-done.refs_3_, f32[64,320]{1,0:T(8,128)S(1)} %project.10.refs_4_), custom_call_target="tpu_custom_call" | custom-call | flops 335544320 | bytes 1310720 | tf_op jit(solution)/shard_map/project/pallas_call | solution.py:209
  46.9 12.6 %all_to_all.15.qkv_ref = bf16[16,4,320]{2,1,0:T(4,128)(2,1)S(1)} all-to-all(bf16[16,4,320]{2,1,0:T(4,128)(2,1)S(1)} %project.11), channel_id=1, replica_groups=mesh['segment'=2,'slot'=16] {'slot'}, dimensions={0} | all-to-all | bytes 81920 | tf_op jit(solution)/shard_map/all_to_all | solution.py:402
  61.0 4.5 %collective-permute-done.5 = bf16[1,4,4096]{2,1,0:T(4,128)(2,1)S(1)} collective-permute-done((bf16[1,4,4096]{2,1,0:T(4,128)(2,1)S(1)}, bf16[1,4,4096]{2,1,0:T(4,128)(2,1)S(1)}, u32[]{:S(2)}, u32[]{:S(2)}) %collective-permute-start.5) | collective-permute-done | bytes 32800 | tf_op jit(solution)/shard_map/ppermute | solution.py:33
  65.9 4.1 %collective-permute-done.6 = bf16[2,4,4096]{2,1,0:T(4,128)(2,1)S(1)} collective-permute-done((bf16[2,4,4096]{2,1,0:T(4,128)(2,1)S(1)}, bf16[2,4,4096]{2,1,0:T(4,128)(2,1)S(1)}, u32[]{:S(2)}, u32[]{:S(2)}) %collective-permute-start.6) | collective-permute-done | bytes 65568 | tf_op jit(solution)/shard_map/ppermute | solution.py:33
  70.7 4.4 %collective-permute-done.7 = bf16[4,4,4096]{2,1,0:T(4,128)(2,1)S(1)} collective-permute-done((bf16[4,4,4096]{2,1,0:T(4,128)(2,1)S(1)}, bf16[4,4,4096]{2,1,0:T(4,128)(2,1)S(1)}, u32[]{:S(2)}, u32[]{:S(2)}) %collective-permute-start.7) | collective-permute-done | bytes 131104 | tf_op jit(solution)/shard_map/ppermute | solution.py:33
  76.9 2.2 %copy-done.4 = bf16[1,4096,512]{2,1,0:T(8,128)(2,1)S(1)} copy-done((bf16[1,4096,512]{2,1,0:T(8,128)(2,1)S(1)}, bf16[1,4096,512]{2,1,0:T(8,128)(2,1)}, u32[]{:S(2)}) %copy-start.4) | copy-done | bytes 4194328
  79.0 1.9 %output.2 = bf16[64,512]{1,0:T(8,128)(2,1)S(1)} custom-call(s32[16]{0:T(128)S(1)} %gather_fusion, bf16[8,4,4096]{2,1,0:T(4,128)(2,1)S(1)} %pad_maximum_fusion.near_ref, bf16[8,4,4096]{2,1,0:T(4,128)(2,1)S(1)} %collective-permute-done.8.far_ref, bf16[4096,512]{1,0:T(8,128)(2,1)S(1)} %bitcast.25, bf16[64,512]{1,0:T(8,128)(2,1)S(1)} %get-tuple-element.18.now_ref), custom_call_target="tpu_custom_call" | custom-call | tf_op jit(solution)/shard_map/output/pallas_call | solution.py:345
  81.0 1.6 %collective-permute-start.9 = (bf16[64,512]{1,0:T(8,128)(2,1)S(1)}, bf16[64,512]{1,0:T(8,128)(2,1)S(1)}, u32[]{:S(2)}, u32[]{:S(2)}) collective-permute-start(bf16[64,512]{1,0:T(8,128)(2,1)S(1)} %output.2), channel_id=1, source_target_pairs={{0,16},{16,0},{1,17},{17,1},{2,18},{18,2},{3,19},{19,3},{4,20},{20... | collective-permute-start | bytes 196616 | tf_op jit(solution)/shard_map/ppermute | solution.py:38
  82.6 2.7 %collective-permute-done.9.now_ref = bf16[64,512]{1,0:T(8,128)(2,1)S(1)} collective-permute-done((bf16[64,512]{1,0:T(8,128)(2,1)S(1)}, bf16[64,512]{1,0:T(8,128)(2,1)S(1)}, u32[]{:S(2)}, u32[]{:S(2)}) %collective-permute-start.9) | collective-permute-done | bytes 65568 | tf_op jit(solution)/shard_map/ppermute | solution.py:38
  85.6 5.2 %collective-permute-done.10 = bf16[1,64,512]{2,1,0:T(8,128)(2,1)S(1)} collective-permute-done((bf16[1,64,512]{2,1,0:T(8,128)(2,1)S(1)}, bf16[1,64,512]{2,1,0:T(8,128)(2,1)S(1)}, u32[]{:S(2)}, u32[]{:S(2)}) %collective-permute-start.10) | collective-permute-done | bytes 65568 | tf_op jit(solution)/shard_map/ppermute | solution.py:33
  90.9 5.0 %collective-permute-done.11 = bf16[2,64,512]{2,1,0:T(8,128)(2,1)S(1)} collective-permute-done((bf16[2,64,512]{2,1,0:T(8,128)(2,1)S(1)}, bf16[2,64,512]{2,1,0:T(8,128)(2,1)S(1)}, u32[]{:S(2)}, u32[]{:S(2)}) %collective-permute-start.11) | collective-permute-done | bytes 131104 | tf_op jit(solution)/shard_map/ppermute | solution.py:33
  96.6 5.7 %collective-permute-done.12.refs_1_ = bf16[4,64,512]{2,1,0:T(8,128)(2,1)S(1)} collective-permute-done((bf16[4,64,512]{2,1,0:T(8,128)(2,1)S(1)}, bf16[4,64,512]{2,1,0:T(8,128)(2,1)S(1)}, u32[]{:S(2)}, u32[]{:S(2)}) %collective-permute-start.12) | collective-permute-done | bytes 262176 | tf_op jit(solution)/shard_map/ppermute | solution.py:33
  102.4 2.8 %copy-done.3 = bf16[1,8192,320]{2,1,0:T(8,128)(2,1)S(1)} copy-done((bf16[1,8192,320]{2,1,0:T(8,128)(2,1)S(1)}, bf16[1,8192,320]{2,1,0:T(8,128)(2,1)}, u32[]{:S(2)}) %copy-start.3) | copy-done | bytes 5242904
  109.5 1.5 %project.15 = bf16[16,4,320]{2,1,0:T(4,128)(2,1)S(1)} custom-call(s32[16]{0:T(128)S(1)} %broadcast_xor_fusion.refs_0_, bf16[4,64,512]{2,1,0:T(8,128)(2,1)S(1)} %collective-permute-done.13.refs_1_, bf16[8192,320]{1,0:T(8,128)(2,1)S(1)} %bitcast.22, bf16[16,8,1152]{2,1,0:T(8,128)(2,1)S(1)} %all-to-all-done.refs_3_, f32[64,320]{1,0:T(8,128)S(1)} %get-tuple-element.23.refs_4_, ...), custom_call_target="tpu_custom_call" | custom-call | flops 335544320 | bytes 1310720 | tf_op jit(solution)/shard_map/project/pallas_call | solution.py:209
  111.0 9.3 %all_to_all.16.qkv_ref = bf16[16,4,320]{2,1,0:T(4,128)(2,1)S(1)} all-to-all(bf16[16,4,320]{2,1,0:T(4,128)(2,1)S(1)} %project.15), channel_id=1, replica_groups=mesh['segment'=2,'slot'=16] {'slot'}, dimensions={0} | all-to-all | bytes 81920 | tf_op jit(solution)/shard_map/all_to_all | solution.py:402
  121.8 4.5 %collective-permute-done.15 = bf16[1,4,4096]{2,1,0:T(4,128)(2,1)S(1)} collective-permute-done((bf16[1,4,4096]{2,1,0:T(4,128)(2,1)S(1)}, bf16[1,4,4096]{2,1,0:T(4,128)(2,1)S(1)}, u32[]{:S(2)}, u32[]{:S(2)}) %collective-permute-start.15) | collective-permute-done | bytes 32800 | tf_op jit(solution)/shard_map/ppermute | solution.py:33
  126.7 4.1 %collective-permute-done.16 = bf16[2,4,4096]{2,1,0:T(4,128)(2,1)S(1)} collective-permute-done((bf16[2,4,4096]{2,1,0:T(4,128)(2,1)S(1)}, bf16[2,4,4096]{2,1,0:T(4,128)(2,1)S(1)}, u32[]{:S(2)}, u32[]{:S(2)}) %collective-permute-start.16) | collective-permute-done | bytes 65568 | tf_op jit(solution)/shard_map/ppermute | solution.py:33
  131.5 4.4 %collective-permute-done.17 = bf16[4,4,4096]{2,1,0:T(4,128)(2,1)S(1)} collective-permute-done((bf16[4,4,4096]{2,1,0:T(4,128)(2,1)S(1)}, bf16[4,4,4096]{2,1,0:T(4,128)(2,1)S(1)}, u32[]{:S(2)}, u32[]{:S(2)}) %collective-permute-start.17) | collective-permute-done | bytes 131104 | tf_op jit(solution)/shard_map/ppermute | solution.py:33
  136.2 1.5 %collective-permute-done.18.far_ref = bf16[8,4,4096]{2,1,0:T(4,128)(2,1)S(1)} collective-permute-done((bf16[8,4,4096]{2,1,0:T(4,128)(2,1)S(1)}, bf16[8,4,4096]{2,1,0:T(4,128)(2,1)S(1)}, u32[]{:S(2)}, u32[]{:S(2)}) %collective-permute-start.18) | collective-permute-done | bytes 262176 | tf_op jit(solution)/shard_map/ppermute | solution.py:33
  137.7 2.1 %output.3 = bf16[64,512]{1,0:T(8,128)(2,1)S(1)} custom-call(s32[16]{0:T(128)S(1)} %gather_fusion, bf16[8,4,4096]{2,1,0:T(4,128)(2,1)S(1)} %pad_maximum_fusion.2.near_ref, bf16[8,4,4096]{2,1,0:T(4,128)(2,1)S(1)} %collective-permute-done.18.far_ref, bf16[4096,512]{1,0:T(8,128)(2,1)S(1)} %bitcast.26, bf16[64,512]{1,0:T(8,128)(2,1)S(1)} %collective-permute-done.9.now_ref), custom_call_target="tpu_custom_call" | custom-call | tf_op jit(solution)/shard_map/output/pallas_call | solution.py:345
  139.8 1.6 %collective-permute-start.19 = (bf16[64,512]{1,0:T(8,128)(2,1)S(1)}, bf16[64,512]{1,0:T(8,128)(2,1)S(1)}, u32[]{:S(2)}, u32[]{:S(2)}) collective-permute-start(bf16[64,512]{1,0:T(8,128)(2,1)S(1)} %output.3), channel_id=1, source_target_pairs={{0,16},{16,0},{1,17},{17,1},{2,18},{18,2},{3,19},{19,3},{4,20},{20... | collective-permute-start | bytes 196616 | tf_op jit(solution)/shard_map/ppermute | solution.py:38
  141.4 2.7 %collective-permute-done.19 = bf16[64,512]{1,0:T(8,128)(2,1)S(1)} collective-permute-done((bf16[64,512]{1,0:T(8,128)(2,1)S(1)}, bf16[64,512]{1,0:T(8,128)(2,1)S(1)}, u32[]{:S(2)}, u32[]{:S(2)}) %collective-permute-start.19) | collective-permute-done | bytes 65568 | tf_op jit(solution)/shard_map/ppermute | solution.py:38
  (73 shorter events, 23.1 us)
Async XLA Ops:
  0.0 0.9 copy-start.7
  1.0 0.8 copy-start.8
  6.2 7.7 %collective-permute-start = (bf16[1,64,512]{2,1,0:T(8,128)(2,1)S(1)}, bf16[1,64,512]{2,1,0:T(8,128)(2,1)S(1)}, u32[]{:S(2)}, u32[]{:S(2)}) collective-permute-start(bf16[1,64,512]{2,1,0:T(8,128)(2,1)S(1)} %get-tuple-element.15), channel_id=1, source_target_pairs={{0,8},{1,9},{2,10},{3,11},{4,12},{5,13},{6,14},{7,15},{8,0},{9,1},... | collective-permute-start | bytes 196616 | tf_op jit(solution)/shard_map/ppermute | solution.py:33
  13.9 5.0 %collective-permute-start.1 = (bf16[2,64,512]{2,1,0:T(8,128)(2,1)S(1)}, bf16[2,64,512]{2,1,0:T(8,128)(2,1)S(1)}, u32[]{:S(2)}, u32[]{:S(2)}) collective-permute-start(bf16[2,64,512]{2,1,0:T(8,128)(2,1)S(1)} %pad_maximum_fusion.3), channel_id=1, source_target_pairs={{0,4},{1,5},{2,6},{3,7},{4,0},{5,1},{6,2},{7,3},{8,12},{9,13},{10,... | collective-permute-start | bytes 393224 | tf_op jit(solution)/shard_map/ppermute | solution.py:33
  18.9 15.0 %collective-permute-start.2 = (bf16[4,64,512]{2,1,0:T(8,128)(2,1)S(1)}, bf16[4,64,512]{2,1,0:T(8,128)(2,1)S(1)}, u32[]{:S(2)}, u32[]{:S(2)}) collective-permute-start(bf16[4,64,512]{2,1,0:T(8,128)(2,1)S(1)} %constant_dynamic-update-slice_fusion.refs_1_), channel_id=1, source_target_pairs={{0,2},{1,3},{2,0},{3,1},{4,6},{5,7},{6,4},{7,5},{8,10},{9,11},{10,... | collective-permute-start | bytes 786440 | tf_op jit(solution)/shard_map/ppermute | solution.py:33
  20.7 21.9 %all-to-all-start = ((bf16[16,8,1152]{2,1,0:T(8,128)(2,1)}), bf16[16,8,1152]{2,1,0:T(8,128)(2,1)S(1)}, u32[]{:S(2)}, u32[]{:S(2)}) async-start(bf16[16,8,1152]{2,1,0:T(8,128)(2,1)} %get-tuple-element.16), calls=%async_computation | async-start | bytes 589824 | tf_op jit(solution)/shard_map/all_to_all | solution.py:385
  25.4 8.7 %copy-start.14 = (s32[16]{0:T(128)S(1)}, s32[16]{0:T(128)}, u32[]{:S(2)}) copy-start(s32[16]{0:T(128)} %constant.10.clone) | copy-start | bytes 196
  25.4 13.0 %collective-permute-start.4 = (bf16[4,64,512]{2,1,0:T(8,128)(2,1)S(1)}, bf16[4,64,512]{2,1,0:T(8,128)(2,1)S(1)}, u32[]{:S(2)}, u32[]{:S(2)}) collective-permute-start(bf16[4,64,512]{2,1,0:T(8,128)(2,1)S(1)} %constant_dynamic-update-slice_fusion.refs_1_), channel_id=1, source_target_pairs={{0,1},{1,0},{2,3},{3,2},{4,5},{5,4},{6,7},{7,6},{8,9},{9,8},{10,11... | collective-permute-start | bytes 786440 | tf_op jit(solution)/shard_map/ppermute | solution.py:33
  34.0 8.6 %collective-permute-start.3 = (bf16[4,64,512]{2,1,0:T(8,128)(2,1)S(1)}, bf16[4,64,512]{2,1,0:T(8,128)(2,1)S(1)}, u32[]{:S(2)}, u32[]{:S(2)}) collective-permute-start(bf16[4,64,512]{2,1,0:T(8,128)(2,1)S(1)} %collective-permute-done.2.refs_1_), channel_id=1, source_target_pairs={{0,1},{1,0},{2,3},{3,2},{4,5},{5,4},{6,7},{7,6},{8,9},{9,8},{10,11... | collective-permute-start | bytes 786440 | tf_op jit(solution)/shard_map/ppermute | solution.py:33
  34.1 2.8 %copy-start = (bf16[1,8192,320]{2,1,0:T(8,128)(2,1)S(1)}, bf16[1,8192,320]{2,1,0:T(8,128)(2,1)}, u32[]{:S(2)}) copy-start(bf16[1,8192,320]{2,1,0:T(8,128)(2,1)} %copy.14) | copy-start | bytes 15728644
  36.9 2.8 %copy-start.1 = (bf16[1,8192,320]{2,1,0:T(8,128)(2,1)S(1)}, bf16[1,8192,320]{2,1,0:T(8,128)(2,1)}, u32[]{:S(2)}) copy-start(bf16[1,8192,320]{2,1,0:T(8,128)(2,1)} %copy.14) | copy-start | bytes 15728644
  41.1 18.4 %copy-start.6 = (bf16[1,2,4,1,16,1024]{5,4,3,2,1,0:T(8,128)(2,1)S(1)}, bf16[1,2,4,1,16,1024]{5,4,3,2,1,0:T(8,128)(2,1)}, u32[]{:S(2)}) copy-start(bf16[1,2,4,1,16,1024]{5,4,3,2,1,0:T(8,128)(2,1)} %param.16) | copy-start | bytes 786436
  41.1 18.4 %copy-start.12 = (s32[1,2,4,1]{2,3,1,0:T(1,128)S(1)}, s32[1,2,4,1]{2,3,1,0:T(1,128)}, u32[]{:S(2)}) copy-start(s32[1,2,4,1]{2,3,1,0:T(1,128)} %param.17) | copy-start | bytes 100
  42.6 2.8 %copy-start.2 = (bf16[1,8192,320]{2,1,0:T(8,128)(2,1)S(1)}, bf16[1,8192,320]{2,1,0:T(8,128)(2,1)}, u32[]{:S(2)}) copy-start(bf16[1,8192,320]{2,1,0:T(8,128)(2,1)} %copy.14) | copy-start | bytes 15728644
  60.6 4.9 %collective-permute-start.5 = (bf16[1,4,4096]{2,1,0:T(4,128)(2,1)S(1)}, bf16[1,4,4096]{2,1,0:T(4,128)(2,1)S(1)}, u32[]{:S(2)}, u32[]{:S(2)}) collective-permute-start(bf16[1,4,4096]{2,1,0:T(4,128)(2,1)S(1)} %attend.2), channel_id=1, source_target_pairs={{0,8},{1,9},{2,10},{3,11},{4,12},{5,13},{6,14},{7,15},{8,0},{9,1},... | collective-permute-start | bytes 98312 | tf_op jit(solution)/shard_map/ppermute | solution.py:33
  65.6 4.3 %collective-permute-start.6 = (bf16[2,4,4096]{2,1,0:T(4,128)(2,1)S(1)}, bf16[2,4,4096]{2,1,0:T(4,128)(2,1)S(1)}, u32[]{:S(2)}, u32[]{:S(2)}) collective-permute-start(bf16[2,4,4096]{2,1,0:T(4,128)(2,1)S(1)} %pad_maximum_fusion.7), channel_id=1, source_target_pairs={{0,4},{1,5},{2,6},{3,7},{4,0},{5,1},{6,2},{7,3},{8,12},{9,13},{10,... | collective-permute-start | bytes 196616 | tf_op jit(solution)/shard_map/ppermute | solution.py:33
  70.0 5.0 %collective-permute-start.7 = (bf16[4,4,4096]{2,1,0:T(4,128)(2,1)S(1)}, bf16[4,4,4096]{2,1,0:T(4,128)(2,1)S(1)}, u32[]{:S(2)}, u32[]{:S(2)}) collective-permute-start(bf16[4,4,4096]{2,1,0:T(4,128)(2,1)S(1)} %pad_maximum_fusion.4), channel_id=1, source_target_pairs={{0,2},{1,3},{2,0},{3,1},{4,6},{5,7},{6,4},{7,5},{8,10},{9,11},{10,... | collective-permute-start | bytes 393224 | tf_op jit(solution)/shard_map/ppermute | solution.py:33
  75.3 1.6 %collective-permute-start.8 = (bf16[8,4,4096]{2,1,0:T(4,128)(2,1)S(1)}, bf16[8,4,4096]{2,1,0:T(4,128)(2,1)S(1)}, u32[]{:S(2)}, u32[]{:S(2)}) collective-permute-start(bf16[8,4,4096]{2,1,0:T(4,128)(2,1)S(1)} %pad_maximum_fusion.near_ref), channel_id=1, source_target_pairs={{0,1},{1,0},{2,3},{3,2},{4,5},{5,4},{6,7},{7,6},{8,9},{9,8},{10,11... | collective-permute-start | bytes 786440 | tf_op jit(solution)/shard_map/ppermute | solution.py:33
  76.9 2.2 %copy-start.4 = (bf16[1,4096,512]{2,1,0:T(8,128)(2,1)S(1)}, bf16[1,4096,512]{2,1,0:T(8,128)(2,1)}, u32[]{:S(2)}) copy-start(bf16[1,4096,512]{2,1,0:T(8,128)(2,1)} %param.15) | copy-start | bytes 12582916
  81.0 4.3 %collective-permute-start.9 = (bf16[64,512]{1,0:T(8,128)(2,1)S(1)}, bf16[64,512]{1,0:T(8,128)(2,1)S(1)}, u32[]{:S(2)}, u32[]{:S(2)}) collective-permute-start(bf16[64,512]{1,0:T(8,128)(2,1)S(1)} %output.2), channel_id=1, source_target_pairs={{0,16},{16,0},{1,17},{17,1},{2,18},{18,2},{3,19},{19,3},{4,20},{20... | collective-permute-start | bytes 196616 | tf_op jit(solution)/shard_map/ppermute | solution.py:38
  85.3 5.5 %collective-permute-start.10 = (bf16[1,64,512]{2,1,0:T(8,128)(2,1)S(1)}, bf16[1,64,512]{2,1,0:T(8,128)(2,1)S(1)}, u32[]{:S(2)}, u32[]{:S(2)}) collective-permute-start(bf16[1,64,512]{2,1,0:T(8,128)(2,1)S(1)} %bitcast.29), channel_id=1, source_target_pairs={{0,8},{1,9},{2,10},{3,11},{4,12},{5,13},{6,14},{7,15},{8,0},{9,1},... | collective-permute-start | bytes 196616 | tf_op jit(solution)/shard_map/ppermute | solution.py:33
  90.9 5.0 %collective-permute-start.11 = (bf16[2,64,512]{2,1,0:T(8,128)(2,1)S(1)}, bf16[2,64,512]{2,1,0:T(8,128)(2,1)S(1)}, u32[]{:S(2)}, u32[]{:S(2)}) collective-permute-start(bf16[2,64,512]{2,1,0:T(8,128)(2,1)S(1)} %pad_maximum_fusion.5), channel_id=1, source_target_pairs={{0,4},{1,5},{2,6},{3,7},{4,0},{5,1},{6,2},{7,3},{8,12},{9,13},{10,... | collective-permute-start | bytes 393224 | tf_op jit(solution)/shard_map/ppermute | solution.py:33
  95.9 6.4 %collective-permute-start.12 = (bf16[4,64,512]{2,1,0:T(8,128)(2,1)S(1)}, bf16[4,64,512]{2,1,0:T(8,128)(2,1)S(1)}, u32[]{:S(2)}, u32[]{:S(2)}) collective-permute-start(bf16[4,64,512]{2,1,0:T(8,128)(2,1)S(1)} %pad_maximum_fusion.1.refs_1_), channel_id=1, source_target_pairs={{0,2},{1,3},{2,0},{3,1},{4,6},{5,7},{6,4},{7,5},{8,10},{9,11},{10,... | collective-permute-start | bytes 786440 | tf_op jit(solution)/shard_map/ppermute | solution.py:33
  96.6 10.0 %collective-permute-start.14 = (bf16[4,64,512]{2,1,0:T(8,128)(2,1)S(1)}, bf16[4,64,512]{2,1,0:T(8,128)(2,1)S(1)}, u32[]{:S(2)}, u32[]{:S(2)}) collective-permute-start(bf16[4,64,512]{2,1,0:T(8,128)(2,1)S(1)} %pad_maximum_fusion.1.refs_1_), channel_id=1, source_target_pairs={{0,1},{1,0},{2,3},{3,2},{4,5},{5,4},{6,7},{7,6},{8,9},{9,8},{10,11... | collective-permute-start | bytes 786440 | tf_op jit(solution)/shard_map/ppermute | solution.py:33
  102.4 7.1 %collective-permute-start.13 = (bf16[4,64,512]{2,1,0:T(8,128)(2,1)S(1)}, bf16[4,64,512]{2,1,0:T(8,128)(2,1)S(1)}, u32[]{:S(2)}, u32[]{:S(2)}) collective-permute-start(bf16[4,64,512]{2,1,0:T(8,128)(2,1)S(1)} %collective-permute-done.12.refs_1_), channel_id=1, source_target_pairs={{0,1},{1,0},{2,3},{3,2},{4,5},{5,4},{6,7},{7,6},{8,9},{9,8},{10,11... | collective-permute-start | bytes 786440 | tf_op jit(solution)/shard_map/ppermute | solution.py:33
  102.4 2.8 %copy-start.3 = (bf16[1,8192,320]{2,1,0:T(8,128)(2,1)S(1)}, bf16[1,8192,320]{2,1,0:T(8,128)(2,1)}, u32[]{:S(2)}) copy-start(bf16[1,8192,320]{2,1,0:T(8,128)(2,1)} %copy.14) | copy-start | bytes 15728644
  109.5 28.2 %copy-start.5 = (bf16[1,4096,512]{2,1,0:T(8,128)(2,1)S(1)}, bf16[1,4096,512]{2,1,0:T(8,128)(2,1)}, u32[]{:S(2)}) copy-start(bf16[1,4096,512]{2,1,0:T(8,128)(2,1)} %param.15) | copy-start | bytes 12582916
  121.5 4.9 %collective-permute-start.15 = (bf16[1,4,4096]{2,1,0:T(4,128)(2,1)S(1)}, bf16[1,4,4096]{2,1,0:T(4,128)(2,1)S(1)}, u32[]{:S(2)}, u32[]{:S(2)}) collective-permute-start(bf16[1,4,4096]{2,1,0:T(4,128)(2,1)S(1)} %attend.3), channel_id=1, source_target_pairs={{0,8},{1,9},{2,10},{3,11},{4,12},{5,13},{6,14},{7,15},{8,0},{9,1},... | collective-permute-start | bytes 98312 | tf_op jit(solution)/shard_map/ppermute | solution.py:33
  126.4 4.3 %collective-permute-start.16 = (bf16[2,4,4096]{2,1,0:T(4,128)(2,1)S(1)}, bf16[2,4,4096]{2,1,0:T(4,128)(2,1)S(1)}, u32[]{:S(2)}, u32[]{:S(2)}) collective-permute-start(bf16[2,4,4096]{2,1,0:T(4,128)(2,1)S(1)} %pad_maximum_fusion.8), channel_id=1, source_target_pairs={{0,4},{1,5},{2,6},{3,7},{4,0},{5,1},{6,2},{7,3},{8,12},{9,13},{10,... | collective-permute-start | bytes 196616 | tf_op jit(solution)/shard_map/ppermute | solution.py:33
  130.9 5.0 %collective-permute-start.17 = (bf16[4,4,4096]{2,1,0:T(4,128)(2,1)S(1)}, bf16[4,4,4096]{2,1,0:T(4,128)(2,1)S(1)}, u32[]{:S(2)}, u32[]{:S(2)}) collective-permute-start(bf16[4,4,4096]{2,1,0:T(4,128)(2,1)S(1)} %pad_maximum_fusion.6), channel_id=1, source_target_pairs={{0,2},{1,3},{2,0},{3,1},{4,6},{5,7},{6,4},{7,5},{8,10},{9,11},{10,... | collective-permute-start | bytes 393224 | tf_op jit(solution)/shard_map/ppermute | solution.py:33
  136.1 1.6 %collective-permute-start.18 = (bf16[8,4,4096]{2,1,0:T(4,128)(2,1)S(1)}, bf16[8,4,4096]{2,1,0:T(4,128)(2,1)S(1)}, u32[]{:S(2)}, u32[]{:S(2)}) collective-permute-start(bf16[8,4,4096]{2,1,0:T(4,128)(2,1)S(1)} %pad_maximum_fusion.2.near_ref), channel_id=1, source_target_pairs={{0,1},{1,0},{2,3},{3,2},{4,5},{5,4},{6,7},{7,6},{8,9},{9,8},{10,11... | collective-permute-start | bytes 786440 | tf_op jit(solution)/shard_map/ppermute | solution.py:33
  139.8 4.3 %collective-permute-start.19 = (bf16[64,512]{1,0:T(8,128)(2,1)S(1)}, bf16[64,512]{1,0:T(8,128)(2,1)S(1)}, u32[]{:S(2)}, u32[]{:S(2)}) collective-permute-start(bf16[64,512]{1,0:T(8,128)(2,1)S(1)} %output.3), channel_id=1, source_target_pairs={{0,16},{16,0},{1,17},{17,1},{2,18},{18,2},{3,19},{19,3},{4,20},{20... | collective-permute-start | bytes 196616 | tf_op jit(solution)/shard_map/ppermute | solution.py:38
  (4 other events, 2.8 us)

commit v2 on v1

v2 whole, which is shorter than its diff:
```python
import functools

import jax
import jax.numpy as jnp
import numpy as np
from jax import lax
from jax.experimental import pallas as pl
from jax.experimental.pallas import tpu as pltpu
from jax.sharding import PartitionSpec as P

QUERY_HEADS = 32
KEY_VALUE_HEADS = 4
HEAD_SIZE = 128
CYCLE_STEPS = 2
GROUP = QUERY_HEADS // KEY_VALUE_HEADS
KEY_WIDTH = KEY_VALUE_HEADS * HEAD_SIZE
LANES = 128

norm_eps = 1e-06
VMEM_LIMIT = 12 * 1024 * 1024


def params(**kw):
    return pltpu.CompilerParams(vmem_limit_bytes=VMEM_LIMIT, **kw)


def iota(shape, dim):
    return lax.broadcasted_iota(jnp.int32, shape, dim)


def exchange(block, mask):
    n = lax.axis_size("slot")
    return lax.ppermute(block, "slot", [(i, i ^ mask) for i in range(n)])


def next_segment(block):
    n = lax.axis_size("segment")
    return lax.ppermute(block, "segment", [(i, (i + 1) % n) for i in range(n)])


def split_rows(index, slots, batch, slot_first):
    if slot_first:
        return index // batch, lax.rem(index, batch)
    return lax.rem(index, slots), index // slots


def slot_rows_first(slots, batch):
    rows = slots * batch
    to_slot, to_row = split_rows(iota((rows, rows), 0), slots, batch, True)
    from_slot, from_row = split_rows(iota((rows, rows), 1), slots, batch, False)
    return ((to_slot == from_slot) & (to_row == from_row)).astype(jnp.bfloat16)


def arrival_rows(own, slots, batch):
    rows = slots * batch
    to_slot, to_row = split_rows(iota((rows, rows), 0), slots, batch, False)
    arrival, from_row = split_rows(iota((rows, rows), 1), slots, batch, True)
    away = to_slot ^ own
    bits = slots.bit_length() - 1
    place = jnp.zeros_like(away)
    for k in range(bits):
        place = place | (((away >> k) & 1) << (bits - 1 - k))
    return ((place == arrival) & (to_row == from_row)).astype(jnp.bfloat16)


def pack_kernel(own_ref, dest_sm, *refs):
    sources, (send_ref, code_ref), held, sem = refs[:6], refs[6:8], refs[8:14], refs[14]
    copies = [pltpu.make_async_copy(src, dst, sem.at[k])
              for k, (src, dst) in enumerate(zip(sources, held))]
    for copy in copies:
        copy.start()
    for copy in copies:
        copy.wait()
    x_ref, gain_ref, pages_ref, dest_ref, row_ref, count_ref = held
    slots, page_tok, wide = send_ref.shape
    kv_width = pages_ref.shape[2]
    own = own_ref[0]
    gain = gain_ref[...].astype(jnp.float32)
    at = iota((page_tok, LANES), 0)
    extra = jnp.zeros((page_tok, LANES), jnp.float32)
    gain_rows = gain.shape[1] // LANES
    for r in range(gain_rows):
        extra = jnp.where(at == r, gain[:, r * LANES:(r + 1) * LANES], extra)
    x = x_ref[...].astype(jnp.float32)
    rows = x.shape[0]
    column = jnp.sum(x * x, axis=1, keepdims=True)
    for r in range(-(-rows // LANES)):
        same = iota((rows, LANES), 0) == iota((rows, LANES), 1) + r * LANES
        line = jnp.sum(jnp.where(same, column, 0.0), axis=0, keepdims=True)
        for k in range(3):
            piece = line.astype(jnp.bfloat16).astype(jnp.float32)
            extra = jnp.where(at == gain_rows + 3 * r + k, piece, extra)
            line = line - piece
    extra = extra.astype(jnp.bfloat16)
    for p in range(pages_ref.shape[0]):
        send_ref[dest_sm[own, p], :, :kv_width] = pages_ref[p]
    for j in range(slots):
        send_ref[j, :, kv_width:] = extra
    tokens = code_ref.shape[1]
    mine = dest_ref[...] == own
    spread = (iota((slots, tokens), 1) // page_tok == iota((slots, tokens), 0)).astype(jnp.float32)

    def to_tokens(values):
        kept = jnp.where(mine, values, 0).astype(jnp.float32)
        by_token = lax.dot_general(kept, spread, (((0,), (0,)), ((), ())),
                                   preferred_element_type=jnp.float32)
        return jnp.sum(by_token, axis=0, keepdims=True)

    place = lax.rem(iota((1, tokens), 1), page_tok).astype(jnp.float32)
    live = place < to_tokens(count_ref[...])
    code = jnp.where(live, to_tokens(row_ref[...]), -1.0)
    code_ref[...] = jnp.broadcast_to(code, code_ref.shape).astype(jnp.int32)


def pack(own, x, gain, pages, dest, row, count):
    slots, total = dest.shape
    _, page_tok, kv_width = pages.shape
    fixed = lambda shape: pl.BlockSpec(shape, lambda s, own, dest: (0,) * len(shape))
    out_shape = [
        jax.ShapeDtypeStruct((slots, page_tok, kv_width + LANES), jnp.bfloat16),
        jax.ShapeDtypeStruct((8, slots * page_tok), jnp.int32),
    ]
    operands = [x, gain, pages, dest, row, count]
    return pl.pallas_call(
        pack_kernel,
        out_shape=out_shape,
        grid_spec=pltpu.PrefetchScalarGridSpec(
            num_scalar_prefetch=2, grid=(1,),
            in_specs=[pl.BlockSpec(memory_space=pltpu.HBM) for v in operands],
            out_specs=[fixed(v.shape) for v in out_shape],
            scratch_shapes=[pltpu.VMEM(v.shape, v.dtype) for v in operands] + [
                pltpu.SemaphoreType.DMA((len(operands),))]),
        compiler_params=params(),
        name="pack",
    )(own, dest, *operands)


def project_kernel(order_ref, x_ref, w_ref, *refs, scaled, first, last, slots, batch,
                   model_width):
    refs = list(refs)
    extra_ref = refs.pop(0) if last or not scaled else None
    states = 1 if scaled else 2
    before = [] if first else [refs.pop(0) for _ in range(states)]
    out_ref = refs.pop(0) if last else None
    acc = refs[0]
    step = pl.program_id(0)

    @pl.when(step == 0)
    def _():
        for k, ref in enumerate(refs):
            ref[...] = jnp.zeros_like(ref) if first else before[k][...]

    x = x_ref[0]
    rows, width = x.shape
    gain_rows = width // LANES
    if not scaled:
        parts = []
        total = refs[1][...]
        for r in range(gain_rows):
            part = x[:, r * LANES:(r + 1) * LANES].astype(jnp.float32)
            total = total + part * part
            gain = extra_ref[0, r:r + 1, :].astype(jnp.float32)
            parts.append((part * gain).astype(jnp.bfloat16))
        refs[1][...] = total
        x = parts[0] if len(parts) == 1 else jnp.concatenate(parts, axis=1)
    acc[...] += lax.dot_general(x, w_ref[...], (((1,), (1,)), ((), ())),
                                preferred_element_type=jnp.float32)

    if last:
        @pl.when(step == pl.num_programs(0) - 1)
        def _():
            if scaled:
                lines = jnp.sum(extra_ref[...].astype(jnp.float32), axis=0)
                sums = jnp.zeros((rows, 1), jnp.float32)
                for r in range(-(-rows // LANES)):
                    at = gain_rows + 3 * r
                    line = lines[at:at + 1] + lines[at + 1:at + 2] + lines[at + 2:at + 3]
                    same = iota((rows, LANES), 0) == iota((rows, LANES), 1) + r * LANES
                    sums = sums + jnp.sum(jnp.where(same, line, 0.0), axis=1, keepdims=True)
            else:
                sums = jnp.sum(refs[1][...], axis=1, keepdims=True)
            out = (acc[...] * lax.rsqrt(sums / model_width + norm_eps)).astype(jnp.bfloat16)
            out = jnp.dot(slot_rows_first(slots, batch), out, preferred_element_type=jnp.float32)
            for j in range(slots):
                out_ref[j] = out[j * batch:(j + 1) * batch].astype(jnp.bfloat16)


def project(order, start, x, weight, extra, state, *, scaled, last, slots, batch, kv_width):
    blocks, rows, width = x.shape
    columns, model_width = weight.shape
    first = state is None
    page_tok = extra.shape[1]
    fixed = lambda shape: pl.BlockSpec(shape, lambda s, order: (0,) * len(shape))
    in_specs = [
        pl.BlockSpec((1, rows, width), lambda s, order: (s, 0, 0)),
        pl.BlockSpec((columns, width), lambda s, order: (0, order[start + s])),
    ]
    operands = [x, weight]
    if not scaled:
        in_specs.append(pl.BlockSpec(
            (1, page_tok, LANES), lambda s, order: (order[start + s], 0, kv_width // LANES)))
        operands.append(extra)
    elif last:
        in_specs.append(pl.BlockSpec(
            (slots, page_tok, LANES), lambda s, order: (0, 0, kv_width // LANES)))
        operands.append(extra)
    if not first:
        in_specs += [fixed(v.shape) for v in state]
        operands += list(state)
    state_shape = [(rows, columns)] + ([] if scaled else [(rows, LANES)])
    if last:
        out_shape = jax.ShapeDtypeStruct((slots, batch, columns), jnp.bfloat16)
        out_specs = fixed(out_shape.shape)
        scratch = [pltpu.VMEM(shape, jnp.float32) for shape in state_shape]
    else:
        out_shape = [jax.ShapeDtypeStruct(shape, jnp.float32) for shape in state_shape]
        out_specs = [fixed(shape) for shape in state_shape]
        scratch = []
    return pl.pallas_call(
        functools.partial(project_kernel, scaled=scaled, first=first, last=last, slots=slots,
                          batch=batch, model_width=model_width),
        out_shape=out_shape,
        grid_spec=pltpu.PrefetchScalarGridSpec(
            num_scalar_prefetch=1, grid=(blocks,), in_specs=in_specs, out_specs=out_specs,
            scratch_shapes=scratch),
        compiler_params=params(),
        cost_estimate=pl.CostEstimate(flops=8 * rows * width * columns * blocks,
                                      bytes_accessed=2 * width * columns * blocks,
                                      transcendentals=0),
        name="project",
    )(order, *operands)


def attend_kernel(len_ref, qkv_ref, cache_ref, pages_ref, code_ref, out_ref, *, visit):
    slots, batch, columns = qkv_ref.shape
    positions = cache_ref.shape[2]
    tokens = pages_ref.shape[0]
    full = jnp.concatenate([qkv_ref[j].astype(jnp.float32) for j in range(slots)], axis=1)
    group_rows = GROUP * batch
    near = batch * positions
    near_pad = -(-(near + 16) // LANES) * LANES
    rows = KEY_VALUE_HEADS * group_rows
    nt = (((1,), (1,)), ((), ()))
    far_scores, near_scores, near_values = [], [], []
    key_at = QUERY_HEADS * HEAD_SIZE
    value_at = key_at + KEY_WIDTH
    for h in range(KEY_VALUE_HEADS):
        query = jnp.concatenate(
            [full[:, (h * GROUP + g) * HEAD_SIZE:(h * GROUP + g + 1) * HEAD_SIZE]
             for g in range(GROUP)], axis=0).astype(jnp.bfloat16)
        lo, hi = h * HEAD_SIZE, (h + 1) * HEAD_SIZE

        def nearby(cache_lo, fresh_lo):
            fresh = full[:, fresh_lo:fresh_lo + HEAD_SIZE]
            fresh = jnp.concatenate(
                [fresh, jnp.zeros((near_pad - near - batch, HEAD_SIZE), jnp.float32)], axis=0)
            old = [cache_ref[0, b, :, cache_lo:cache_lo + HEAD_SIZE] for b in range(batch)]
            return jnp.concatenate(old + [fresh.astype(jnp.bfloat16)], axis=0)

        keys = nearby(lo, key_at + lo)
        near_values.append(nearby(KEY_WIDTH + lo, value_at + lo))
        far_scores.append(lax.dot_general(query, pages_ref[:, lo:hi], nt,
                                          preferred_element_type=jnp.float32))
        near_scores.append(lax.dot_general(query, keys, nt, preferred_element_type=jnp.float32))
    scale = HEAD_SIZE ** (-0.5)
    far = jnp.concatenate(far_scores, axis=0) * scale
    close = jnp.concatenate(near_scores, axis=0) * scale
    far_row = lax.rem(iota((rows, tokens), 0), batch)
    far = jnp.where(code_ref[0:1, :] == far_row + visit * batch, far, -1e30)
    row = lax.rem(iota((rows, near_pad), 0), batch)
    lane = iota((rows, near_pad), 1)
    lengths = jnp.zeros((rows, near_pad), jnp.int32)
    for b in range(batch):
        lengths = jnp.where(row == b, len_ref[visit, b], lengths)
    position = lane - row * positions
    seen = (position >= 0) & (position < lengths) | (lane == near + row)
    close = jnp.where(seen, close, -1e30)
    top = jnp.maximum(jnp.max(far, axis=1, keepdims=True), jnp.max(close, axis=1, keepdims=True))
    far = jnp.exp(far - top)
    close = jnp.exp(close - top)
    denominator = jnp.sum(far, axis=1, keepdims=True) + jnp.sum(close, axis=1, keepdims=True)
    far = (far / denominator).astype(jnp.bfloat16)
    close = (close / denominator).astype(jnp.bfloat16)
    for h in range(KEY_VALUE_HEADS):
        mine = slice(h * group_rows, (h + 1) * group_rows)
        lo = KEY_WIDTH + h * HEAD_SIZE
        context = jnp.dot(far[mine], pages_ref[:, lo:lo + HEAD_SIZE],
                          preferred_element_type=jnp.float32)
        context = context + jnp.dot(close[mine], near_values[h],
                                    preferred_element_type=jnp.float32)
        for g in range(GROUP):
            at = (h * GROUP + g) * HEAD_SIZE
            out_ref[0, :, at:at + HEAD_SIZE] = context[g * batch:(g + 1) * batch].astype(
                jnp.bfloat16)


def attend(lengths, qkv, cache, pages, code, visit):
    slots, batch, columns = qkv.shape
    _, _, positions, kv_width = cache.shape
    tokens = pages.shape[0]
    return pl.pallas_call(
        functools.partial(attend_kernel, visit=visit),
        out_shape=jax.ShapeDtypeStruct((1, batch, QUERY_HEADS * HEAD_SIZE), jnp.bfloat16),
        grid=(1,),
        in_specs=[
            pl.BlockSpec(memory_space=pltpu.SMEM),
            pl.BlockSpec((slots, batch, columns), lambda s: (0, 0, 0)),
            pl.BlockSpec((1, batch, positions, kv_width), lambda s: (visit, 0, 0, 0)),
            pl.BlockSpec((tokens, kv_width), lambda s: (0, 0)),
            pl.BlockSpec(code.shape, lambda s: (0, 0)),
        ],
        out_specs=pl.BlockSpec((1, batch, QUERY_HEADS * HEAD_SIZE), lambda s: (0, 0, 0)),
        compiler_params=params(),
        name="attend",
    )(lengths, qkv, cache, pages, code)


def output_kernel(own_ref, *refs, slots, batch):
    pieces, (w_ref, now_ref, out_ref, acc) = refs[:4], refs[4:]
    step = pl.program_id(0)
    depth = w_ref.shape[0]

    @pl.when(step == 0)
    def _():
        acc[...] = jnp.zeros_like(acc)

    left = jnp.concatenate(
        [piece[i].astype(jnp.float32) for piece in pieces for i in range(piece.shape[0])], axis=0)
    acc[...] += jnp.dot(left.astype(jnp.bfloat16), w_ref[...], preferred_element_type=jnp.float32)

    @pl.when(step == pl.num_programs(0) - 1)
    def _():
        rest = acc[...]
        move = arrival_rows(own_ref[0], slots, batch)
        total = now_ref[...].astype(jnp.float32)
        moved = None
        for _ in range(3):
            part = rest.astype(jnp.bfloat16)
            rest = rest - part.astype(jnp.float32)
            part = jnp.dot(move, part, preferred_element_type=jnp.float32)
            moved = part if moved is None else moved + part
        out_ref[...] = (total + moved).astype(jnp.bfloat16)


def output(own, pieces, weight, now, slots):
    quarter, batch, features = pieces[0].shape
    rows, columns = now.shape
    steps = 4
    depth = features // steps
    fixed = lambda *shape: pl.BlockSpec(shape, lambda s, own: (0,) * len(shape))
    return pl.pallas_call(
        functools.partial(output_kernel, slots=slots, batch=batch),
        out_shape=jax.ShapeDtypeStruct((rows, columns), jnp.bfloat16),
        grid_spec=pltpu.PrefetchScalarGridSpec(
            num_scalar_prefetch=1, grid=(steps,),
            in_specs=[pl.BlockSpec((quarter, batch, depth), lambda s, own: (0, 0, s))] * 4 + [
                pl.BlockSpec((depth, columns), lambda s, own: (s, 0)),
                fixed(rows, columns),
            ],
            out_specs=fixed(rows, columns),
            scratch_shapes=[pltpu.VMEM((rows, columns), jnp.float32)]),
        compiler_params=params(),
        name="output",
    )(own, *pieces, weight, now)


def shards(hidden_rows, norm_gain, qkv_weight, out_weight, cache_kv, cache_len, page_kv,
           page_dest, page_row, page_count):
    slots = lax.axis_size("slot")
    batch = hidden_rows.shape[1]
    rows = batch * slots
    width = hidden_rows.shape[3]
    kv_width = cache_kv.shape[5]
    own = lax.axis_index("slot").astype(jnp.int32)
    masks = [slots >> (k + 1) for k in range(slots.bit_length() - 1)]
    offsets = [0]
    for mask in masks:
        offsets = offsets + [mask ^ o for o in offsets]
    order = own ^ jnp.asarray(np.array(offsets, np.int32))
    own = own.reshape(1)
    cache = cache_kv[0, :, :, 0]
    lengths = cache_len[0, :, :, 0]
    weight_in = qkv_weight[0].T
    current = hidden_rows.reshape(rows, width)
    scaled = (current.astype(jnp.float32) * norm_gain.astype(jnp.float32)).astype(jnp.bfloat16)
    outgoing, code = pack(own, current, norm_gain, page_kv[0, 0], page_dest[0], page_row[0], page_count[0])
    for visit in range(CYCLE_STEPS):
        block = (current if visit else scaled)[None]
        for mask in masks[:-2]:
            block = jnp.concatenate([block, exchange(block, mask)], axis=0)
            if mask == masks[0] and visit == 0:
                block, outgoing = lax.optimization_barrier((block, outgoing))
                incoming = lax.all_to_all(outgoing, "slot", split_axis=0, concat_axis=0,
                                          tiled=True)
                pages = incoming.reshape(-1, kv_width + LANES)
        quarter = block.shape[0]
        run = functools.partial(project, order, weight=weight_in, extra=incoming,
                                scaled=visit == 0, slots=slots, batch=batch, kv_width=kv_width)
        side = exchange(block, masks[-2])
        pair = exchange(block, masks[-1])
        state = run(start=0, x=block, state=None, last=False)
        state = run(start=2 * quarter, x=pair, state=state, last=False)
        side, state = lax.optimization_barrier((side, state))
        corner = exchange(side, masks[-1])
        state = run(start=quarter, x=side, state=state, last=False)
        qkv = run(start=3 * quarter, x=corner, state=state, last=True)
        qkv = lax.all_to_all(qkv, "slot", split_axis=0, concat_axis=0, tiled=True)
        context = attend(lengths, qkv, cache, pages, code, visit)
        for mask in masks[:-2]:
            context = jnp.concatenate([context, exchange(context, mask)], axis=0)
        side = exchange(context, masks[-2])
        pair = exchange(context, masks[-1])
        corner = exchange(side, masks[-1])
        updated = output(own, (context, side, pair, corner), out_weight[0], current, slots)
        current = next_segment(updated)
    return current.reshape(hidden_rows.shape)


def solution(mesh):
    return jax.shard_map(
        shards,
        mesh=mesh,
        in_specs=(
            P("segment", None, None, "slot"),
            P("segment", "slot"),
            P("segment", None, "slot"),
            P("segment", None, "slot"),
            P("segment", None, None, "slot", None, None),
            P("segment", None, None, "slot"),
            P("segment", "slot", None, None, None),
            P("segment", None, None),
            P("segment", None, None),
            P("segment", None, None),
        ),
        out_specs=P("segment", None, None, "slot"),
        check_vma=False,
    )
```

time: 146 us -> 132 us (0.904)
  local copies, waits for them, and re-layouts: 25.9 us -> 13.2 us
  waiting for transfers between devices: 57.8 us -> 55.1 us
  other arithmetic: 0.73 us -> 2.54 us
    unnamed x34 -> x32, local copies, waits for them, and re-layouts: 25.2 us -> 13.2 us
    ppermute x18 -> x20, waiting for transfers between devices: 52.3 us -> 49.6 us  [exchange(): return lax.ppermute(block, 'slot', [(i, i ^ mask) for i in range(n)])]
    ppermute x18 -> x20, starting transfers between devices: 10.7 us -> 11.4 us  [exchange(): return lax.ppermute(block, 'slot', [(i, i ^ mask) for i in range(n)])]
  transfers between devices with their start and end apart: 21 -> 23, of which waited for: 15 -> 15; matrix products, arithmetic and copies ran while one was open for 6% -> 1% of each run, Pallas kernels for 6% -> 9%
where the time goes in v2:
time: 132 us; the launch traced here: 131 us
  waiting for transfers between devices  55.1 us (42%)
  Pallas kernels  20.7 us (16%)
  blocking collectives  20.7 us (16%)
  starting transfers between devices  18.6 us (14%)
  local copies, waits for them, and re-layouts  13.2 us (10%)
  other arithmetic  2.54 us (2%)
    ppermute x20, waiting for transfers between devices, exchange(): return lax.ppermute(block, 'slot', [(i, i ^ mask) for i in range(n)])  49.6 us
    all_to_all x2, blocking collectives, shards(): qkv = lax.all_to_all(qkv, 'slot', split_axis=0, concat_axis=0, tiled=True)  20.7 us
    pallas_call x8, Pallas kernels, project(): pl.pallas_call(functools.partial(project_kernel, scaled=scaled, first=fir...  13.6 us
    unnamed x32, local copies, waits for them, and re-layouts  13.2 us
    ppermute x20, starting transfers between devices, exchange(): return lax.ppermute(block, 'slot', [(i, i ^ mask) for i in range(n)])  11.4 us
    ppermute x2, waiting for transfers between devices, next_segment(): return lax.ppermute(block, 'segment', [(i, (i + 1) % n) for i in range(n)])  5.48 us
    all_to_all x1, starting transfers between devices, shards(): lax.all_to_all(outgoing, 'slot', split_axis=0, concat_axis=0, tiled=True)  3.99 us
    ppermute x2, starting transfers between devices, next_segment(): return lax.ppermute(block, 'segment', [(i, (i + 1) % n) for i in range(n)])  3.18 us
  transfers between devices with their start and end apart: 23, of which 15 were waited for; matrix products, arithmetic and copies ran while one was open for 1% of the time, Pallas kernels for 9%

profile of v2, /device:TPU:0, one launch (start us, length us, event | category | flops | bytes accessed | tf_op | source)
XLA Modules:
  0.0 131.1 jit_solution(862922014705587958)
XLA Ops:
  1.5 4.1 %collective-permute-start = (bf16[1,64,512]{2,1,0:T(8,128)(2,1)S(1)}, bf16[1,64,512]{2,1,0:T(8,128)(2,1)S(1)}, u32[]{:S(2)}, u32[]{:S(2)}) collective-permute-start(bf16[1,64,512]{2,1,0:T(8,128)(2,1)S(1)} %fusion), channel_id=1, source_target_pairs={{0,8},{1,9},{2,10},{3,11},{4,12},{5,13},{6,14},{7,15},{8,0},{9,1},... | collective-permute-start | bytes 196616 | tf_op jit(solution)/shard_map/ppermute | solution.py:33
  10.2 1.7 %pack.1 = (bf16[16,8,1152]{2,1,0:T(8,128)(2,1)}, s32[8,128]{1,0:T(8,128)S(1)}) custom-call(s32[1]{0:T(128)} %bitcast.own_ref, s32[16,16]{1,0:T(8,128)S(1)} %bitcast.39, bf16[64,512]{1,0:T(8,128)(2,1)S(1)} %bitcast.33, bf16[1,512]{1,0:T(2,128)(2,1)S(1)} %copy-done.11, bf16[16,8,1024]{2,1,0:T(8,128)(2,1)S(1)} %bitcast.38, s32[16,16]{1,0:T(8,128)S(1)} %bitcast.40, ...), custom_call_target="tpu_custom_call" | custom-call | tf_op jit(solution)/shard_map/pack/pallas_call | solution.py:124
  12.0 1.6 %collective-permute-start.1 = (bf16[2,64,512]{2,1,0:T(8,128)(2,1)S(1)}, bf16[2,64,512]{2,1,0:T(8,128)(2,1)S(1)}, u32[]{:S(2)}, u32[]{:S(2)}) collective-permute-start(bf16[2,64,512]{2,1,0:T(8,128)(2,1)S(1)} %pad_maximum_fusion.1), channel_id=1, source_target_pairs={{0,4},{1,5},{2,6},{3,7},{4,0},{5,1},{6,2},{7,3},{8,12},{9,13},{10,... | collective-permute-start | bytes 393224 | tf_op jit(solution)/shard_map/ppermute | solution.py:33
  13.6 3.4 %collective-permute-done.1 = bf16[2,64,512]{2,1,0:T(8,128)(2,1)S(1)} collective-permute-done((bf16[2,64,512]{2,1,0:T(8,128)(2,1)S(1)}, bf16[2,64,512]{2,1,0:T(8,128)(2,1)S(1)}, u32[]{:S(2)}, u32[]{:S(2)}) %collective-permute-start.1) | collective-permute-done | bytes 131104 | tf_op jit(solution)/shard_map/ppermute | solution.py:33
  17.1 4.0 %all-to-all-start = ((bf16[16,8,1152]{2,1,0:T(8,128)(2,1)}), bf16[16,8,1152]{2,1,0:T(8,128)(2,1)S(1)}, u32[]{:S(2)}, u32[]{:S(2)}) async-start(bf16[16,8,1152]{2,1,0:T(8,128)(2,1)} %get-tuple-element.23), calls=%async_computation | async-start | bytes 589824 | tf_op jit(solution)/shard_map/all_to_all | solution.py:393
  21.1 1.9 %collective-permute-start.2 = (bf16[4,64,512]{2,1,0:T(8,128)(2,1)S(1)}, bf16[4,64,512]{2,1,0:T(8,128)(2,1)S(1)}, u32[]{:S(2)}, u32[]{:S(2)}) collective-permute-start(bf16[4,64,512]{2,1,0:T(8,128)(2,1)S(1)} %constant_dynamic-update-slice_fusion.x_ref), channel_id=1, source_target_pairs={{0,2},{1,3},{2,0},{3,1},{4,6},{5,7},{6,4},{7,5},{8,10},{9,11},{10,... | collective-permute-start | bytes 786440 | tf_op jit(solution)/shard_map/ppermute | solution.py:33
  23.7 2.5 %copy-done = bf16[1,8192,320]{1,2,0:T(8,128)(2,1)S(1)} copy-done((bf16[1,8192,320]{1,2,0:T(8,128)(2,1)S(1)}, bf16[1,8192,320]{1,2,0:T(8,128)(2,1)}, u32[]{:S(2)}) %copy-start) | copy-done | bytes 5242904
  26.1 1.6 %project.8.refs_0_ = f32[64,320]{1,0:T(8,128)S(1)} custom-call(s32[16]{0:T(128)S(1)} %broadcast_xor_fusion.order_ref, bf16[4,64,512]{2,1,0:T(8,128)(2,1)S(1)} %constant_dynamic-update-slice_fusion.x_ref, bf16[320,8192]{1,0:T(8,128)(2,1)S(1)} %bitcast.19), custom_call_target="tpu_custom_call" | custom-call | flops 335544320 | bytes 1310720 | tf_op jit(solution)/shard_map/project/pallas_call | solution.py:219
  28.6 1.6 %project.9.refs_0_ = f32[64,320]{1,0:T(8,128)S(1)} custom-call(s32[16]{0:T(128)S(1)} %broadcast_xor_fusion.order_ref, bf16[4,64,512]{2,1,0:T(8,128)(2,1)S(1)} %collective-permute-done.3.x_ref, bf16[320,8192]{1,0:T(8,128)(2,1)S(1)} %bitcast.20, f32[64,320]{1,0:T(8,128)S(1)} %project.8.refs_0_), custom_call_target="tpu_custom_call" | custom-call | flops 335544320 | bytes 1310720 | tf_op jit(solution)/shard_map/project/pallas_call | solution.py:219
  30.3 2.7 %collective-permute-done.2.x_ref = bf16[4,64,512]{2,1,0:T(8,128)(2,1)S(1)} collective-permute-done((bf16[4,64,512]{2,1,0:T(8,128)(2,1)S(1)}, bf16[4,64,512]{2,1,0:T(8,128)(2,1)S(1)}, u32[]{:S(2)}, u32[]{:S(2)}) %collective-permute-start.2) | collective-permute-done | bytes 262176 | tf_op jit(solution)/shard_map/ppermute | solution.py:33
  33.0 1.6 %project.10.refs_1_ = f32[64,320]{1,0:T(8,128)S(1)} custom-call(s32[16]{0:T(128)S(1)} %broadcast_xor_fusion.order_ref, bf16[4,64,512]{2,1,0:T(8,128)(2,1)S(1)} %collective-permute-done.2.x_ref, bf16[320,8192]{1,0:T(8,128)(2,1)S(1)} %bitcast.21, f32[64,320]{1,0:T(8,128)S(1)} %project.9.refs_0_), custom_call_target="tpu_custom_call" | custom-call | flops 335544320 | bytes 1310720 | tf_op jit(solution)/shard_map/project/pallas_call | solution.py:219
  34.7 2.5 %copy-done.2 = bf16[1,8192,320]{1,2,0:T(8,128)(2,1)S(1)} copy-done((bf16[1,8192,320]{1,2,0:T(8,128)(2,1)S(1)}, bf16[1,8192,320]{1,2,0:T(8,128)(2,1)}, u32[]{:S(2)}) %copy-start.2) | copy-done | bytes 5242904
  37.1 1.9 %project.11 = bf16[16,4,320]{2,1,0:T(4,128)(2,1)S(1)} custom-call(s32[16]{0:T(128)S(1)} %broadcast_xor_fusion.order_ref, bf16[4,64,512]{2,1,0:T(8,128)(2,1)S(1)} %collective-permute-done.4.x_ref, bf16[320,8192]{1,0:T(8,128)(2,1)S(1)} %bitcast.22, bf16[16,8,1152]{2,1,0:T(8,128)(2,1)S(1)} %all-to-all-done.refs_0_, f32[64,320]{1,0:T(8,128)S(1)} %project.10.refs_1_), custom_call_target="tpu_custom_call" | custom-call | flops 335544320 | bytes 1310720 | tf_op jit(solution)/shard_map/project/pallas_call | solution.py:219
  39.1 11.3 %all_to_all.15.qkv_ref = bf16[16,4,320]{2,1,0:T(4,128)(2,1)S(1)} all-to-all(bf16[16,4,320]{2,1,0:T(4,128)(2,1)S(1)} %project.11), channel_id=1, replica_groups=mesh['segment'=2,'slot'=16] {'slot'}, dimensions={0} | all-to-all | bytes 81920 | tf_op jit(solution)/shard_map/all_to_all | solution.py:407
  51.9 4.5 %collective-permute-done.5 = bf16[1,4,4096]{2,1,0:T(4,128)(2,1)S(1)} collective-permute-done((bf16[1,4,4096]{2,1,0:T(4,128)(2,1)S(1)}, bf16[1,4,4096]{2,1,0:T(4,128)(2,1)S(1)}, u32[]{:S(2)}, u32[]{:S(2)}) %collective-permute-start.5) | collective-permute-done | bytes 32800 | tf_op jit(solution)/shard_map/ppermute | solution.py:33
  56.8 4.1 %collective-permute-done.6 = bf16[2,4,4096]{2,1,0:T(4,128)(2,1)S(1)} collective-permute-done((bf16[2,4,4096]{2,1,0:T(4,128)(2,1)S(1)}, bf16[2,4,4096]{2,1,0:T(4,128)(2,1)S(1)}, u32[]{:S(2)}, u32[]{:S(2)}) %collective-permute-start.6) | collective-permute-done | bytes 65568 | tf_op jit(solution)/shard_map/ppermute | solution.py:33
  61.5 4.4 %collective-permute-done.7.refs_1_ = bf16[4,4,4096]{2,1,0:T(4,128)(2,1)S(1)} collective-permute-done((bf16[4,4,4096]{2,1,0:T(4,128)(2,1)S(1)}, bf16[4,4,4096]{2,1,0:T(4,128)(2,1)S(1)}, u32[]{:S(2)}, u32[]{:S(2)}) %collective-permute-start.7) | collective-permute-done | bytes 131104 | tf_op jit(solution)/shard_map/ppermute | solution.py:33
  67.3 2.2 %copy-done.4 = bf16[1,4096,512]{2,1,0:T(8,128)(2,1)S(1)} copy-done((bf16[1,4096,512]{2,1,0:T(8,128)(2,1)S(1)}, bf16[1,4096,512]{2,1,0:T(8,128)(2,1)}, u32[]{:S(2)}) %copy-start.4) | copy-done | bytes 4194328
  71.1 1.6 %collective-permute-start.10 = (bf16[64,512]{1,0:T(8,128)(2,1)S(1)}, bf16[64,512]{1,0:T(8,128)(2,1)S(1)}, u32[]{:S(2)}, u32[]{:S(2)}) collective-permute-start(bf16[64,512]{1,0:T(8,128)(2,1)S(1)} %output.2), channel_id=1, source_target_pairs={{0,16},{16,0},{1,17},{17,1},{2,18},{18,2},{3,19},{19,3},{4,20},{20... | collective-permute-start | bytes 196616 | tf_op jit(solution)/shard_map/ppermute | solution.py:38
  72.6 2.7 %collective-permute-done.10.refs_5_ = bf16[64,512]{1,0:T(8,128)(2,1)S(1)} collective-permute-done((bf16[64,512]{1,0:T(8,128)(2,1)S(1)}, bf16[64,512]{1,0:T(8,128)(2,1)S(1)}, u32[]{:S(2)}, u32[]{:S(2)}) %collective-permute-start.10) | collective-permute-done | bytes 65568 | tf_op jit(solution)/shard_map/ppermute | solution.py:38
  75.7 5.2 %collective-permute-done.11 = bf16[1,64,512]{2,1,0:T(8,128)(2,1)S(1)} collective-permute-done((bf16[1,64,512]{2,1,0:T(8,128)(2,1)S(1)}, bf16[1,64,512]{2,1,0:T(8,128)(2,1)S(1)}, u32[]{:S(2)}, u32[]{:S(2)}) %collective-permute-start.11) | collective-permute-done | bytes 65568 | tf_op jit(solution)/shard_map/ppermute | solution.py:33
  81.0 5.0 %collective-permute-done.12 = bf16[2,64,512]{2,1,0:T(8,128)(2,1)S(1)} collective-permute-done((bf16[2,64,512]{2,1,0:T(8,128)(2,1)S(1)}, bf16[2,64,512]{2,1,0:T(8,128)(2,1)S(1)}, u32[]{:S(2)}, u32[]{:S(2)}) %collective-permute-start.12) | collective-permute-done | bytes 131104 | tf_op jit(solution)/shard_map/ppermute | solution.py:33
  86.8 1.6 %project.12 = (f32[64,320]{1,0:T(8,128)S(1)}, f32[64,128]{1,0:T(8,128)S(1)}) custom-call(s32[16]{0:T(128)S(1)} %broadcast_xor_fusion.order_ref, bf16[4,64,512]{2,1,0:T(8,128)(2,1)S(1)} %pad_maximum_fusion.x_ref, bf16[320,8192]{1,0:T(8,128)(2,1)S(1)} %bitcast.23, bf16[16,8,1152]{2,1,0:T(8,128)(2,1)S(1)} %all-to-all-done.refs_0_), custom_call_target="tpu_custom_call" | custom-call | flops 335544320 | bytes 1310720 | tf_op jit(solution)/shard_map/project/pallas_call | solution.py:219
  88.4 1.6 %project.13 = (f32[64,320]{1,0:T(8,128)S(1)}, f32[64,128]{1,0:T(8,128)S(1)}) custom-call(s32[16]{0:T(128)S(1)} %broadcast_xor_fusion.order_ref, bf16[4,64,512]{2,1,0:T(8,128)(2,1)S(1)} %collective-permute-done.14.x_ref, bf16[320,8192]{1,0:T(8,128)(2,1)S(1)} %bitcast.24, bf16[16,8,1152]{2,1,0:T(8,128)(2,1)S(1)} %all-to-all-done.refs_0_, ...), custom_call_target="tpu_custom_call" | custom-call | flops 335544320 | bytes 1310720 | tf_op jit(solution)/shard_map/project/pallas_call | solution.py:219
  90.1 4.7 %collective-permute-done.13.x_ref = bf16[4,64,512]{2,1,0:T(8,128)(2,1)S(1)} collective-permute-done((bf16[4,64,512]{2,1,0:T(8,128)(2,1)S(1)}, bf16[4,64,512]{2,1,0:T(8,128)(2,1)S(1)}, u32[]{:S(2)}, u32[]{:S(2)}) %collective-permute-start.13) | collective-permute-done | bytes 262176 | tf_op jit(solution)/shard_map/ppermute | solution.py:33
  94.8 1.6 %project.14 = (f32[64,320]{1,0:T(8,128)S(1)}, f32[64,128]{1,0:T(8,128)S(1)}) custom-call(s32[16]{0:T(128)S(1)} %broadcast_xor_fusion.order_ref, bf16[4,64,512]{2,1,0:T(8,128)(2,1)S(1)} %collective-permute-done.13.x_ref, bf16[320,8192]{1,0:T(8,128)(2,1)S(1)} %bitcast.25, bf16[16,8,1152]{2,1,0:T(8,128)(2,1)S(1)} %all-to-all-done.refs_0_, ...), custom_call_target="tpu_custom_call" | custom-call | flops 335544320 | bytes 1310720 | tf_op jit(solution)/shard_map/project/pallas_call | solution.py:219
  96.5 1.9 %project.15 = bf16[16,4,320]{2,1,0:T(4,128)(2,1)S(1)} custom-call(s32[16]{0:T(128)S(1)} %broadcast_xor_fusion.order_ref, bf16[4,64,512]{2,1,0:T(8,128)(2,1)S(1)} %collective-permute-done.15.x_ref, bf16[320,8192]{1,0:T(8,128)(2,1)S(1)} %bitcast.26, bf16[16,8,1152]{2,1,0:T(8,128)(2,1)S(1)} %all-to-all-done.refs_0_, f32[64,320]{1,0:T(8,128)S(1)} %get-tuple-element.33.refs_1_, ...), custom_call_target="tpu_custom_call" | custom-call | flops 335544320 | bytes 1310720 | tf_op jit(solution)/shard_map/project/pallas_call | solution.py:219
  98.3 9.3 %all_to_all.16.qkv_ref = bf16[16,4,320]{2,1,0:T(4,128)(2,1)S(1)} all-to-all(bf16[16,4,320]{2,1,0:T(4,128)(2,1)S(1)} %project.15), channel_id=1, replica_groups=mesh['segment'=2,'slot'=16] {'slot'}, dimensions={0} | all-to-all | bytes 81920 | tf_op jit(solution)/shard_map/all_to_all | solution.py:407
  109.2 4.5 %collective-permute-done.16 = bf16[1,4,4096]{2,1,0:T(4,128)(2,1)S(1)} collective-permute-done((bf16[1,4,4096]{2,1,0:T(4,128)(2,1)S(1)}, bf16[1,4,4096]{2,1,0:T(4,128)(2,1)S(1)}, u32[]{:S(2)}, u32[]{:S(2)}) %collective-permute-start.16) | collective-permute-done | bytes 32800 | tf_op jit(solution)/shard_map/ppermute | solution.py:33
  114.0 4.1 %collective-permute-done.17 = bf16[2,4,4096]{2,1,0:T(4,128)(2,1)S(1)} collective-permute-done((bf16[2,4,4096]{2,1,0:T(4,128)(2,1)S(1)}, bf16[2,4,4096]{2,1,0:T(4,128)(2,1)S(1)}, u32[]{:S(2)}, u32[]{:S(2)}) %collective-permute-start.17) | collective-permute-done | bytes 65568 | tf_op jit(solution)/shard_map/ppermute | solution.py:33
  118.8 4.4 %collective-permute-done.18.refs_1_ = bf16[4,4,4096]{2,1,0:T(4,128)(2,1)S(1)} collective-permute-done((bf16[4,4,4096]{2,1,0:T(4,128)(2,1)S(1)}, bf16[4,4,4096]{2,1,0:T(4,128)(2,1)S(1)}, u32[]{:S(2)}, u32[]{:S(2)}) %collective-permute-start.18) | collective-permute-done | bytes 131104 | tf_op jit(solution)/shard_map/ppermute | solution.py:33
  127.7 2.7 %collective-permute-done.21 = bf16[64,512]{1,0:T(8,128)(2,1)S(1)} collective-permute-done((bf16[64,512]{1,0:T(8,128)(2,1)S(1)}, bf16[64,512]{1,0:T(8,128)(2,1)S(1)}, u32[]{:S(2)}, u32[]{:S(2)}) %collective-permute-start.21) | collective-permute-done | bytes 65568 | tf_op jit(solution)/shard_map/ppermute | solution.py:38
  (72 shorter events, 22.0 us)
Async XLA Ops:
  1.5 10.4 %collective-permute-start = (bf16[1,64,512]{2,1,0:T(8,128)(2,1)S(1)}, bf16[1,64,512]{2,1,0:T(8,128)(2,1)S(1)}, u32[]{:S(2)}, u32[]{:S(2)}) collective-permute-start(bf16[1,64,512]{2,1,0:T(8,128)(2,1)S(1)} %fusion), channel_id=1, source_target_pairs={{0,8},{1,9},{2,10},{3,11},{4,12},{5,13},{6,14},{7,15},{8,0},{9,1},... | collective-permute-start | bytes 196616 | tf_op jit(solution)/shard_map/ppermute | solution.py:33
  12.0 5.0 %collective-permute-start.1 = (bf16[2,64,512]{2,1,0:T(8,128)(2,1)S(1)}, bf16[2,64,512]{2,1,0:T(8,128)(2,1)S(1)}, u32[]{:S(2)}, u32[]{:S(2)}) collective-permute-start(bf16[2,64,512]{2,1,0:T(8,128)(2,1)S(1)} %pad_maximum_fusion.1), channel_id=1, source_target_pairs={{0,4},{1,5},{2,6},{3,7},{4,0},{5,1},{6,2},{7,3},{8,12},{9,13},{10,... | collective-permute-start | bytes 393224 | tf_op jit(solution)/shard_map/ppermute | solution.py:33
  17.0 10.8 %collective-permute-start.3 = (bf16[4,64,512]{2,1,0:T(8,128)(2,1)S(1)}, bf16[4,64,512]{2,1,0:T(8,128)(2,1)S(1)}, u32[]{:S(2)}, u32[]{:S(2)}) collective-permute-start(bf16[4,64,512]{2,1,0:T(8,128)(2,1)S(1)} %constant_dynamic-update-slice_fusion.x_ref), channel_id=1, source_target_pairs={{0,1},{1,0},{2,3},{3,2},{4,5},{5,4},{6,7},{7,6},{8,9},{9,8},{10,11... | collective-permute-start | bytes 786440 | tf_op jit(solution)/shard_map/ppermute | solution.py:33
  17.1 17.6 %all-to-all-start = ((bf16[16,8,1152]{2,1,0:T(8,128)(2,1)}), bf16[16,8,1152]{2,1,0:T(8,128)(2,1)S(1)}, u32[]{:S(2)}, u32[]{:S(2)}) async-start(bf16[16,8,1152]{2,1,0:T(8,128)(2,1)} %get-tuple-element.23), calls=%async_computation | async-start | bytes 589824 | tf_op jit(solution)/shard_map/all_to_all | solution.py:393
  21.1 11.9 %collective-permute-start.2 = (bf16[4,64,512]{2,1,0:T(8,128)(2,1)S(1)}, bf16[4,64,512]{2,1,0:T(8,128)(2,1)S(1)}, u32[]{:S(2)}, u32[]{:S(2)}) collective-permute-start(bf16[4,64,512]{2,1,0:T(8,128)(2,1)S(1)} %constant_dynamic-update-slice_fusion.x_ref), channel_id=1, source_target_pairs={{0,2},{1,3},{2,0},{3,1},{4,6},{5,7},{6,4},{7,5},{8,10},{9,11},{10,... | collective-permute-start | bytes 786440 | tf_op jit(solution)/shard_map/ppermute | solution.py:33
  23.7 2.5 %copy-start = (bf16[1,8192,320]{1,2,0:T(8,128)(2,1)S(1)}, bf16[1,8192,320]{1,2,0:T(8,128)(2,1)}, u32[]{:S(2)}) copy-start(bf16[1,8192,320]{1,2,0:T(8,128)(2,1)} %param.13) | copy-start | bytes 15728644
  26.1 2.5 %copy-start.1 = (bf16[1,8192,320]{1,2,0:T(8,128)(2,1)S(1)}, bf16[1,8192,320]{1,2,0:T(8,128)(2,1)}, u32[]{:S(2)}) copy-start(bf16[1,8192,320]{1,2,0:T(8,128)(2,1)} %param.13) | copy-start | bytes 15728644
  30.3 20.1 %copy-start.6 = (bf16[1,2,4,1,16,1024]{5,4,3,2,1,0:T(8,128)(2,1)S(1)}, bf16[1,2,4,1,16,1024]{5,4,3,2,1,0:T(8,128)(2,1)}, u32[]{:S(2)}) copy-start(bf16[1,2,4,1,16,1024]{5,4,3,2,1,0:T(8,128)(2,1)} %param.15) | copy-start | bytes 786436
  30.3 20.1 %copy-start.14 = (s32[1,2,4,1]{2,3,1,0:T(1,128)S(1)}, s32[1,2,4,1]{2,3,1,0:T(1,128)}, u32[]{:S(2)}) copy-start(s32[1,2,4,1]{2,3,1,0:T(1,128)} %param.16) | copy-start | bytes 100
  30.3 37.0 %copy-start.8 = (bf16[1,4,16,512]{3,2,1,0:T(8,128)(2,1)S(1)}, bf16[1,4,16,512]{3,2,1,0:T(8,128)(2,1)}, u32[]{:S(2)}) copy-start(bf16[1,4,16,512]{3,2,1,0:T(8,128)(2,1)} %param.11) | copy-start | bytes 196612
  33.0 1.7 %collective-permute-start.4 = (bf16[4,64,512]{2,1,0:T(8,128)(2,1)S(1)}, bf16[4,64,512]{2,1,0:T(8,128)(2,1)S(1)}, u32[]{:S(2)}, u32[]{:S(2)}) collective-permute-start(bf16[4,64,512]{2,1,0:T(8,128)(2,1)S(1)} %collective-permute-done.2.x_ref), channel_id=1, source_target_pairs={{0,1},{1,0},{2,3},{3,2},{4,5},{5,4},{6,7},{7,6},{8,9},{9,8},{10,11... | collective-permute-start | bytes 786440 | tf_op jit(solution)/shard_map/ppermute | solution.py:33
  34.7 2.5 %copy-start.2 = (bf16[1,8192,320]{1,2,0:T(8,128)(2,1)S(1)}, bf16[1,8192,320]{1,2,0:T(8,128)(2,1)}, u32[]{:S(2)}) copy-start(bf16[1,8192,320]{1,2,0:T(8,128)(2,1)} %param.13) | copy-start | bytes 15728644
  37.1 49.6 %copy-start.3 = (bf16[1,8192,320]{1,2,0:T(8,128)(2,1)S(1)}, bf16[1,8192,320]{1,2,0:T(8,128)(2,1)}, u32[]{:S(2)}) copy-start(bf16[1,8192,320]{1,2,0:T(8,128)(2,1)} %param.13) | copy-start | bytes 15728644
  51.5 4.9 %collective-permute-start.5 = (bf16[1,4,4096]{2,1,0:T(4,128)(2,1)S(1)}, bf16[1,4,4096]{2,1,0:T(4,128)(2,1)S(1)}, u32[]{:S(2)}, u32[]{:S(2)}) collective-permute-start(bf16[1,4,4096]{2,1,0:T(4,128)(2,1)S(1)} %attend.2), channel_id=1, source_target_pairs={{0,8},{1,9},{2,10},{3,11},{4,12},{5,13},{6,14},{7,15},{8,0},{9,1},... | collective-permute-start | bytes 98312 | tf_op jit(solution)/shard_map/ppermute | solution.py:33
  56.5 4.3 %collective-permute-start.6 = (bf16[2,4,4096]{2,1,0:T(4,128)(2,1)S(1)}, bf16[2,4,4096]{2,1,0:T(4,128)(2,1)S(1)}, u32[]{:S(2)}, u32[]{:S(2)}) collective-permute-start(bf16[2,4,4096]{2,1,0:T(4,128)(2,1)S(1)} %pad_maximum_fusion.5), channel_id=1, source_target_pairs={{0,4},{1,5},{2,6},{3,7},{4,0},{5,1},{6,2},{7,3},{8,12},{9,13},{10,... | collective-permute-start | bytes 196616 | tf_op jit(solution)/shard_map/ppermute | solution.py:33
  60.9 5.0 %collective-permute-start.7 = (bf16[4,4,4096]{2,1,0:T(4,128)(2,1)S(1)}, bf16[4,4,4096]{2,1,0:T(4,128)(2,1)S(1)}, u32[]{:S(2)}, u32[]{:S(2)}) collective-permute-start(bf16[4,4,4096]{2,1,0:T(4,128)(2,1)S(1)} %pad_maximum_fusion.2.refs_0_), channel_id=1, source_target_pairs={{0,2},{1,3},{2,0},{3,1},{4,6},{5,7},{6,4},{7,5},{8,10},{9,11},{10,... | collective-permute-start | bytes 393224 | tf_op jit(solution)/shard_map/ppermute | solution.py:33
  61.5 4.4 %collective-permute-start.8 = (bf16[4,4,4096]{2,1,0:T(4,128)(2,1)S(1)}, bf16[4,4,4096]{2,1,0:T(4,128)(2,1)S(1)}, u32[]{:S(2)}, u32[]{:S(2)}) collective-permute-start(bf16[4,4,4096]{2,1,0:T(4,128)(2,1)S(1)} %pad_maximum_fusion.2.refs_0_), channel_id=1, source_target_pairs={{0,1},{1,0},{2,3},{3,2},{4,5},{5,4},{6,7},{7,6},{8,9},{9,8},{10,11... | collective-permute-start | bytes 393224 | tf_op jit(solution)/shard_map/ppermute | solution.py:33
  65.9 1.3 %collective-permute-start.9 = (bf16[4,4,4096]{2,1,0:T(4,128)(2,1)S(1)}, bf16[4,4,4096]{2,1,0:T(4,128)(2,1)S(1)}, u32[]{:S(2)}, u32[]{:S(2)}) collective-permute-start(bf16[4,4,4096]{2,1,0:T(4,128)(2,1)S(1)} %collective-permute-done.7.refs_1_), channel_id=1, source_target_pairs={{0,1},{1,0},{2,3},{3,2},{4,5},{5,4},{6,7},{7,6},{8,9},{9,8},{10,11... | collective-permute-start | bytes 393224 | tf_op jit(solution)/shard_map/ppermute | solution.py:33
  67.3 2.2 %copy-start.4 = (bf16[1,4096,512]{2,1,0:T(8,128)(2,1)S(1)}, bf16[1,4096,512]{2,1,0:T(8,128)(2,1)}, u32[]{:S(2)}) copy-start(bf16[1,4096,512]{2,1,0:T(8,128)(2,1)} %param.14) | copy-start | bytes 12582916
  71.1 4.3 %collective-permute-start.10 = (bf16[64,512]{1,0:T(8,128)(2,1)S(1)}, bf16[64,512]{1,0:T(8,128)(2,1)S(1)}, u32[]{:S(2)}, u32[]{:S(2)}) collective-permute-start(bf16[64,512]{1,0:T(8,128)(2,1)S(1)} %output.2), channel_id=1, source_target_pairs={{0,16},{16,0},{1,17},{17,1},{2,18},{18,2},{3,19},{19,3},{4,20},{20... | collective-permute-start | bytes 196616 | tf_op jit(solution)/shard_map/ppermute | solution.py:38
  75.4 5.5 %collective-permute-start.11 = (bf16[1,64,512]{2,1,0:T(8,128)(2,1)S(1)}, bf16[1,64,512]{2,1,0:T(8,128)(2,1)S(1)}, u32[]{:S(2)}, u32[]{:S(2)}) collective-permute-start(bf16[1,64,512]{2,1,0:T(8,128)(2,1)S(1)} %bitcast.35), channel_id=1, source_target_pairs={{0,8},{1,9},{2,10},{3,11},{4,12},{5,13},{6,14},{7,15},{8,0},{9,1},... | collective-permute-start | bytes 196616 | tf_op jit(solution)/shard_map/ppermute | solution.py:33
  80.9 5.0 %collective-permute-start.12 = (bf16[2,64,512]{2,1,0:T(8,128)(2,1)S(1)}, bf16[2,64,512]{2,1,0:T(8,128)(2,1)S(1)}, u32[]{:S(2)}, u32[]{:S(2)}) collective-permute-start(bf16[2,64,512]{2,1,0:T(8,128)(2,1)S(1)} %pad_maximum_fusion.3), channel_id=1, source_target_pairs={{0,4},{1,5},{2,6},{3,7},{4,0},{5,1},{6,2},{7,3},{8,12},{9,13},{10,... | collective-permute-start | bytes 393224 | tf_op jit(solution)/shard_map/ppermute | solution.py:33
  86.0 2.4 %collective-permute-start.14 = (bf16[4,64,512]{2,1,0:T(8,128)(2,1)S(1)}, bf16[4,64,512]{2,1,0:T(8,128)(2,1)S(1)}, u32[]{:S(2)}, u32[]{:S(2)}) collective-permute-start(bf16[4,64,512]{2,1,0:T(8,128)(2,1)S(1)} %pad_maximum_fusion.x_ref), channel_id=1, source_target_pairs={{0,1},{1,0},{2,3},{3,2},{4,5},{5,4},{6,7},{7,6},{8,9},{9,8},{10,11... | collective-permute-start | bytes 786440 | tf_op jit(solution)/shard_map/ppermute | solution.py:33
  86.1 8.7 %collective-permute-start.13 = (bf16[4,64,512]{2,1,0:T(8,128)(2,1)S(1)}, bf16[4,64,512]{2,1,0:T(8,128)(2,1)S(1)}, u32[]{:S(2)}, u32[]{:S(2)}) collective-permute-start(bf16[4,64,512]{2,1,0:T(8,128)(2,1)S(1)} %pad_maximum_fusion.x_ref), channel_id=1, source_target_pairs={{0,2},{1,3},{2,0},{3,1},{4,6},{5,7},{6,4},{7,5},{8,10},{9,11},{10,... | collective-permute-start | bytes 786440 | tf_op jit(solution)/shard_map/ppermute | solution.py:33
  94.8 29.8 %copy-start.5 = (bf16[1,4096,512]{2,1,0:T(8,128)(2,1)S(1)}, bf16[1,4096,512]{2,1,0:T(8,128)(2,1)}, u32[]{:S(2)}) copy-start(bf16[1,4096,512]{2,1,0:T(8,128)(2,1)} %param.14) | copy-start | bytes 12582916
  94.8 1.7 %collective-permute-start.15 = (bf16[4,64,512]{2,1,0:T(8,128)(2,1)S(1)}, bf16[4,64,512]{2,1,0:T(8,128)(2,1)S(1)}, u32[]{:S(2)}, u32[]{:S(2)}) collective-permute-start(bf16[4,64,512]{2,1,0:T(8,128)(2,1)S(1)} %collective-permute-done.13.x_ref), channel_id=1, source_target_pairs={{0,1},{1,0},{2,3},{3,2},{4,5},{5,4},{6,7},{7,6},{8,9},{9,8},{10,11... | collective-permute-start | bytes 786440 | tf_op jit(solution)/shard_map/ppermute | solution.py:33
  108.8 4.9 %collective-permute-start.16 = (bf16[1,4,4096]{2,1,0:T(4,128)(2,1)S(1)}, bf16[1,4,4096]{2,1,0:T(4,128)(2,1)S(1)}, u32[]{:S(2)}, u32[]{:S(2)}) collective-permute-start(bf16[1,4,4096]{2,1,0:T(4,128)(2,1)S(1)} %attend.3), channel_id=1, source_target_pairs={{0,8},{1,9},{2,10},{3,11},{4,12},{5,13},{6,14},{7,15},{8,0},{9,1},... | collective-permute-start | bytes 98312 | tf_op jit(solution)/shard_map/ppermute | solution.py:33
  113.8 4.3 %collective-permute-start.17 = (bf16[2,4,4096]{2,1,0:T(4,128)(2,1)S(1)}, bf16[2,4,4096]{2,1,0:T(4,128)(2,1)S(1)}, u32[]{:S(2)}, u32[]{:S(2)}) collective-permute-start(bf16[2,4,4096]{2,1,0:T(4,128)(2,1)S(1)} %pad_maximum_fusion.6), channel_id=1, source_target_pairs={{0,4},{1,5},{2,6},{3,7},{4,0},{5,1},{6,2},{7,3},{8,12},{9,13},{10,... | collective-permute-start | bytes 196616 | tf_op jit(solution)/shard_map/ppermute | solution.py:33
  118.2 5.0 %collective-permute-start.18 = (bf16[4,4,4096]{2,1,0:T(4,128)(2,1)S(1)}, bf16[4,4,4096]{2,1,0:T(4,128)(2,1)S(1)}, u32[]{:S(2)}, u32[]{:S(2)}) collective-permute-start(bf16[4,4,4096]{2,1,0:T(4,128)(2,1)S(1)} %pad_maximum_fusion.4.refs_0_), channel_id=1, source_target_pairs={{0,2},{1,3},{2,0},{3,1},{4,6},{5,7},{6,4},{7,5},{8,10},{9,11},{10,... | collective-permute-start | bytes 393224 | tf_op jit(solution)/shard_map/ppermute | solution.py:33
  118.8 4.4 %collective-permute-start.19 = (bf16[4,4,4096]{2,1,0:T(4,128)(2,1)S(1)}, bf16[4,4,4096]{2,1,0:T(4,128)(2,1)S(1)}, u32[]{:S(2)}, u32[]{:S(2)}) collective-permute-start(bf16[4,4,4096]{2,1,0:T(4,128)(2,1)S(1)} %pad_maximum_fusion.4.refs_0_), channel_id=1, source_target_pairs={{0,1},{1,0},{2,3},{3,2},{4,5},{5,4},{6,7},{7,6},{8,9},{9,8},{10,11... | collective-permute-start | bytes 393224 | tf_op jit(solution)/shard_map/ppermute | solution.py:33
  123.2 1.3 %collective-permute-start.20 = (bf16[4,4,4096]{2,1,0:T(4,128)(2,1)S(1)}, bf16[4,4,4096]{2,1,0:T(4,128)(2,1)S(1)}, u32[]{:S(2)}, u32[]{:S(2)}) collective-permute-start(bf16[4,4,4096]{2,1,0:T(4,128)(2,1)S(1)} %collective-permute-done.18.refs_1_), channel_id=1, source_target_pairs={{0,1},{1,0},{2,3},{3,2},{4,5},{5,4},{6,7},{7,6},{8,9},{9,8},{10,11... | collective-permute-start | bytes 393224 | tf_op jit(solution)/shard_map/ppermute | solution.py:33
  126.2 4.3 %collective-permute-start.21 = (bf16[64,512]{1,0:T(8,128)(2,1)S(1)}, bf16[64,512]{1,0:T(8,128)(2,1)S(1)}, u32[]{:S(2)}, u32[]{:S(2)}) collective-permute-start(bf16[64,512]{1,0:T(8,128)(2,1)S(1)} %output.3), channel_id=1, source_target_pairs={{0,16},{16,0},{1,17},{17,1},{2,18},{18,2},{3,19},{19,3},{4,20},{20... | collective-permute-start | bytes 196616 | tf_op jit(solution)/shard_map/ppermute | solution.py:38
  (6 other events, 4.6 us)

commit v3 on v2

v3 whole, which is shorter than its diff:
```python
import functools

import jax
import jax.numpy as jnp
import numpy as np
from jax import lax
from jax.experimental import pallas as pl
from jax.experimental.pallas import tpu as pltpu
from jax.sharding import PartitionSpec as P

QUERY_HEADS = 32
KEY_VALUE_HEADS = 4
HEAD_SIZE = 128
CYCLE_STEPS = 2
GROUP = QUERY_HEADS // KEY_VALUE_HEADS
KEY_WIDTH = KEY_VALUE_HEADS * HEAD_SIZE
LANES = 128

norm_eps = 1e-06
FIRST_LIMIT = 63 * 1024 * 1024
VMEM_LIMIT = 12 * 1024 * 1024


def params(**kw):
    return pltpu.CompilerParams(vmem_limit_bytes=VMEM_LIMIT, **kw)


def iota(shape, dim):
    return lax.broadcasted_iota(jnp.int32, shape, dim)


def exchange(block, mask):
    n = lax.axis_size("slot")
    return lax.ppermute(block, "slot", [(i, i ^ mask) for i in range(n)])


def next_segment(block):
    n = lax.axis_size("segment")
    return lax.ppermute(block, "segment", [(i, (i + 1) % n) for i in range(n)])


def split_rows(index, slots, batch, slot_first):
    if slot_first:
        return index // batch, lax.rem(index, batch)
    return lax.rem(index, slots), index // slots


def slot_rows_first(slots, batch):
    rows = slots * batch
    to_slot, to_row = split_rows(iota((rows, rows), 0), slots, batch, True)
    from_slot, from_row = split_rows(iota((rows, rows), 1), slots, batch, False)
    return ((to_slot == from_slot) & (to_row == from_row)).astype(jnp.bfloat16)


def arrival_rows(own, slots, batch):
    rows = slots * batch
    to_slot, to_row = split_rows(iota((rows, rows), 0), slots, batch, False)
    arrival, from_row = split_rows(iota((rows, rows), 1), slots, batch, True)
    away = to_slot ^ own
    bits = slots.bit_length() - 1
    place = jnp.zeros_like(away)
    for k in range(bits):
        place = place | (((away >> k) & 1) << (bits - 1 - k))
    return ((place == arrival) & (to_row == from_row)).astype(jnp.bfloat16)


def pack_kernel(own_ref, dest_ref, gain_hbm, pages_hbm, send_ref, gain_ref, pages_ref, sem):
    copies = [pltpu.make_async_copy(gain_hbm, gain_ref, sem.at[0]),
              pltpu.make_async_copy(pages_hbm, pages_ref, sem.at[1])]
    for copy in copies:
        copy.start()
    for copy in copies:
        copy.wait()
    slots, page_tok, wide = send_ref.shape
    kv_width = pages_ref.shape[2]
    gain = gain_ref[...].astype(jnp.float32)
    at = iota((page_tok, LANES), 0)
    extra = jnp.zeros((page_tok, LANES), jnp.float32)
    for r in range(gain.shape[1] // LANES):
        extra = jnp.where(at == r, gain[:, r * LANES:(r + 1) * LANES], extra)
    extra = extra.astype(jnp.bfloat16)
    for p in range(pages_ref.shape[0]):
        send_ref[dest_ref[own_ref[0], p], :, :kv_width] = pages_ref[p]
    for j in range(slots):
        send_ref[j, :, kv_width:] = extra


def pack(own, gain, pages, dest):
    _, page_tok, kv_width = pages.shape
    shape = (dest.shape[0], page_tok, kv_width + LANES)
    there = pl.BlockSpec(memory_space=pl.ANY)
    return pl.pallas_call(
        pack_kernel,
        out_shape=jax.ShapeDtypeStruct(shape, pages.dtype),
        grid_spec=pltpu.PrefetchScalarGridSpec(
            num_scalar_prefetch=2, grid=(1,), in_specs=[there, there],
            out_specs=pl.BlockSpec(shape, lambda s, own, dest: (0, 0, 0)),
            scratch_shapes=[pltpu.VMEM(gain.shape, gain.dtype), pltpu.VMEM(pages.shape, pages.dtype),
                            pltpu.SemaphoreType.DMA((2,))]),
        compiler_params=pltpu.CompilerParams(vmem_limit_bytes=FIRST_LIMIT),
        name="pack",
    )(own, dest, gain, pages)


def project_kernel(order_ref, x_ref, w_ref, extra_ref, *refs, start, first, last, batch, kv_width):
    acc_in, square_in = (None, None) if first else refs[:2]
    outs = refs if first else refs[2:]
    blocks, rows, width = x_ref.shape
    columns, model_width = w_ref.shape
    acc = jnp.zeros((rows, columns), jnp.float32) if first else acc_in[...]
    square = jnp.zeros((rows, LANES), jnp.float32) if first else square_in[...]
    for i in range(blocks):
        source = order_ref[start + i]
        x = x_ref[i]
        gain = extra_ref[source, :, kv_width:].astype(jnp.float32)
        parts = []
        for r in range(width // LANES):
            part = x[:, r * LANES:(r + 1) * LANES].astype(jnp.float32)
            square = square + part * part
            parts.append((part * gain[r:r + 1]).astype(jnp.bfloat16))
        x = parts[0] if len(parts) == 1 else jnp.concatenate(parts, axis=1)
        here = pl.ds(pl.multiple_of(source * width, width), width)
        acc = acc + lax.dot_general(x, w_ref[:, here], (((1,), (1,)), ((), ())),
                                    preferred_element_type=jnp.float32)
    if not last:
        outs[0][...] = acc
        outs[1][...] = square
        return
    sums = jnp.sum(square, axis=1, keepdims=True)
    out = (acc * lax.rsqrt(sums / model_width + norm_eps)).astype(jnp.bfloat16)
    slots = rows // batch
    out = jnp.dot(slot_rows_first(slots, batch), out, preferred_element_type=jnp.float32)
    for j in range(slots):
        outs[0][j] = out[j * batch:(j + 1) * batch].astype(jnp.bfloat16)


def project(order, start, x, weight, extra, state, *, last, batch, kv_width):
    blocks, rows, width = x.shape
    columns = weight.shape[0]
    first = state is None
    operands = [x, weight, extra] + ([] if first else list(state))
    if last:
        out_shape = jax.ShapeDtypeStruct((rows // batch, batch, columns), jnp.bfloat16)
    else:
        out_shape = [jax.ShapeDtypeStruct((rows, columns), jnp.float32),
                     jax.ShapeDtypeStruct((rows, LANES), jnp.float32)]
    whole = pl.BlockSpec(memory_space=pltpu.VMEM)
    return pl.pallas_call(
        functools.partial(project_kernel, start=start, first=first, last=last, batch=batch,
                          kv_width=kv_width),
        out_shape=out_shape,
        in_specs=[pl.BlockSpec(memory_space=pltpu.SMEM)] + [whole] * len(operands),
        out_specs=whole if last else [whole] * len(out_shape),
        compiler_params=params(),
        cost_estimate=pl.CostEstimate(flops=8 * rows * width * columns * blocks,
                                      bytes_accessed=2 * width * columns * blocks,
                                      transcendentals=0),
        name="project",
    )(order, *operands)


def token_rows(own, dest_ref, row_ref, count_ref, page_tok):
    slots = dest_ref.shape[0]
    tokens = slots * page_tok
    mine = dest_ref[...] == own
    spread = (iota((slots, tokens), 1) // page_tok == iota((slots, tokens), 0)).astype(jnp.float32)

    def to_tokens(values):
        kept = jnp.where(mine, values, 0).astype(jnp.float32)
        by_token = lax.dot_general(kept, spread, (((0,), (0,)), ((), ())),
                                   preferred_element_type=jnp.float32)
        return jnp.sum(by_token, axis=0, keepdims=True)

    place = lax.rem(iota((1, tokens), 1), page_tok).astype(jnp.float32)
    live = place < to_tokens(count_ref[...])
    return jnp.where(live, to_tokens(row_ref[...]), -1.0).astype(jnp.int32)


def attend_kernel(own_ref, len_ref, qkv_ref, cache_ref, pages_ref, dest_ref, page_row_ref, count_ref,
                  out_ref, *, visit):
    slots, batch, columns = qkv_ref.shape
    positions = cache_ref.shape[2]
    tokens = pages_ref.shape[0]
    full = jnp.concatenate([qkv_ref[j].astype(jnp.float32) for j in range(slots)], axis=1)
    group_rows = GROUP * batch
    near = batch * positions
    near_pad = -(-(near + 16) // LANES) * LANES
    rows = KEY_VALUE_HEADS * group_rows
    nt = (((1,), (1,)), ((), ()))
    far_scores, near_scores, near_values = [], [], []
    key_at = QUERY_HEADS * HEAD_SIZE
    value_at = key_at + KEY_WIDTH
    for h in range(KEY_VALUE_HEADS):
        query = jnp.concatenate(
            [full[:, (h * GROUP + g) * HEAD_SIZE:(h * GROUP + g + 1) * HEAD_SIZE]
             for g in range(GROUP)], axis=0).astype(jnp.bfloat16)
        lo, hi = h * HEAD_SIZE, (h + 1) * HEAD_SIZE

        def nearby(cache_lo, fresh_lo):
            fresh = full[:, fresh_lo:fresh_lo + HEAD_SIZE]
            fresh = jnp.concatenate(
                [fresh, jnp.zeros((near_pad - near - batch, HEAD_SIZE), jnp.float32)], axis=0)
            old = [cache_ref[0, b, :, cache_lo:cache_lo + HEAD_SIZE] for b in range(batch)]
            return jnp.concatenate(old + [fresh.astype(jnp.bfloat16)], axis=0)

        keys = nearby(lo, key_at + lo)
        near_values.append(nearby(KEY_WIDTH + lo, value_at + lo))
        far_scores.append(lax.dot_general(query, pages_ref[:, lo:hi], nt,
                                          preferred_element_type=jnp.float32))
        near_scores.append(lax.dot_general(query, keys, nt, preferred_element_type=jnp.float32))
    scale = HEAD_SIZE ** (-0.5)
    far = jnp.concatenate(far_scores, axis=0) * scale
    close = jnp.concatenate(near_scores, axis=0) * scale
    far_row = lax.rem(iota((rows, tokens), 0), batch)
    code = token_rows(own_ref[0], dest_ref, page_row_ref, count_ref, tokens // slots)
    far = jnp.where(code == far_row + visit * batch, far, -1e30)
    row = lax.rem(iota((rows, near_pad), 0), batch)
    lane = iota((rows, near_pad), 1)
    lengths = jnp.zeros((rows, near_pad), jnp.int32)
    for b in range(batch):
        lengths = jnp.where(row == b, len_ref[visit, b], lengths)
    position = lane - row * positions
    seen = (position >= 0) & (position < lengths) | (lane == near + row)
    close = jnp.where(seen, close, -1e30)
    top = jnp.maximum(jnp.max(far, axis=1, keepdims=True), jnp.max(close, axis=1, keepdims=True))
    far = jnp.exp(far - top)
    close = jnp.exp(close - top)
    denominator = jnp.sum(far, axis=1, keepdims=True) + jnp.sum(close, axis=1, keepdims=True)
    far = (far / denominator).astype(jnp.bfloat16)
    close = (close / denominator).astype(jnp.bfloat16)
    for h in range(KEY_VALUE_HEADS):
        mine = slice(h * group_rows, (h + 1) * group_rows)
        lo = KEY_WIDTH + h * HEAD_SIZE
        context = jnp.dot(far[mine], pages_ref[:, lo:lo + HEAD_SIZE],
                          preferred_element_type=jnp.float32)
        context = context + jnp.dot(close[mine], near_values[h],
                                    preferred_element_type=jnp.float32)
        for g in range(GROUP):
            at = (h * GROUP + g) * HEAD_SIZE
            out_ref[0, :, at:at + HEAD_SIZE] = context[g * batch:(g + 1) * batch].astype(
                jnp.bfloat16)


def attend(own, lengths, qkv, cache, pages, arrivals, visit):
    slots, batch, columns = qkv.shape
    _, _, positions, kv_width = cache.shape
    tokens = pages.shape[0]
    scalars = pl.BlockSpec(memory_space=pltpu.SMEM)
    fixed = lambda *shape: pl.BlockSpec(shape, lambda s: (0,) * len(shape))
    return pl.pallas_call(
        functools.partial(attend_kernel, visit=visit),
        out_shape=jax.ShapeDtypeStruct((1, batch, QUERY_HEADS * HEAD_SIZE), jnp.bfloat16),
        grid=(1,),
        in_specs=[
            scalars, scalars, fixed(slots, batch, columns),
            pl.BlockSpec((1, batch, positions, kv_width), lambda s: (visit, 0, 0, 0)),
            fixed(tokens, kv_width)] + [fixed(*v.shape) for v in arrivals],
        out_specs=fixed(1, batch, QUERY_HEADS * HEAD_SIZE),
        compiler_params=params(),
        name="attend",
    )(own, lengths, qkv, cache, pages, *arrivals)


def output_kernel(own_ref, *refs, slots, batch):
    pieces, (w_ref, now_ref, out_ref) = refs[:4], refs[4:]
    features = w_ref.shape[0]
    depth = features // 4
    acc = jnp.zeros(out_ref.shape, jnp.float32)
    for k in range(0, features, depth):
        left = jnp.concatenate(
            [piece[i, :, k:k + depth].astype(jnp.float32)
             for piece in pieces for i in range(piece.shape[0])], axis=0)
        acc = acc + jnp.dot(left.astype(jnp.bfloat16), w_ref[k:k + depth],
                            preferred_element_type=jnp.float32)
    move = arrival_rows(own_ref[0], slots, batch)
    moved = None
    for _ in range(3):
        part = acc.astype(jnp.bfloat16)
        acc = acc - part.astype(jnp.float32)
        part = jnp.dot(move, part, preferred_element_type=jnp.float32)
        moved = part if moved is None else moved + part
    out_ref[...] = (now_ref[...].astype(jnp.float32) + moved).astype(jnp.bfloat16)


def output(own, pieces, weight, now, slots):
    batch = pieces[0].shape[1]
    whole = pl.BlockSpec(memory_space=pltpu.VMEM)
    return pl.pallas_call(
        functools.partial(output_kernel, slots=slots, batch=batch),
        out_shape=jax.ShapeDtypeStruct(now.shape, jnp.bfloat16),
        in_specs=[pl.BlockSpec(memory_space=pltpu.SMEM)] + [whole] * 6,
        out_specs=whole,
        compiler_params=params(),
        name="output",
    )(own, *pieces, weight, now)


def shards(hidden_rows, norm_gain, qkv_weight, out_weight, cache_kv, cache_len, page_kv,
           page_dest, page_row, page_count):
    slots = lax.axis_size("slot")
    batch = hidden_rows.shape[1]
    rows = batch * slots
    width = hidden_rows.shape[3]
    kv_width = cache_kv.shape[5]
    own = lax.axis_index("slot").astype(jnp.int32)
    masks = [slots >> (k + 1) for k in range(slots.bit_length() - 1)]
    offsets = [0]
    for mask in masks:
        offsets = offsets + [mask ^ o for o in offsets]
    order = own ^ jnp.asarray(np.array(offsets, np.int32))
    cache = cache_kv[0, :, :, 0]
    lengths = cache_len[0, :, :, 0]
    weight_in = qkv_weight[0].T
    weight_out = out_weight[0]
    own = own.reshape(1)
    current = hidden_rows.reshape(rows, width)
    outgoing = pack(own, norm_gain, page_kv[0, 0], page_dest[0])
    current, outgoing = lax.optimization_barrier((current, outgoing))
    incoming = lax.all_to_all(outgoing, "slot", split_axis=0, concat_axis=0, tiled=True)
    arrivals = (page_dest[0], page_row[0], page_count[0])
    for visit in range(CYCLE_STEPS):
        block = current[None]
        for mask in masks[:-2]:
            block = jnp.concatenate([block, exchange(block, mask)], axis=0)
        quarter = block.shape[0]
        run = functools.partial(project, order, weight=weight_in,
                                batch=batch, kv_width=kv_width)
        side = exchange(block, masks[-2])
        pair = exchange(block, masks[-1])
        held, incoming = lax.optimization_barrier((block, incoming))
        state = run(start=0, x=held, extra=incoming, state=None, last=False)
        state = run(start=2 * quarter, x=pair, extra=incoming, state=state, last=False)
        side, state = lax.optimization_barrier((side, state))
        corner = exchange(side, masks[-1])
        state = run(start=quarter, x=side, extra=incoming, state=state, last=False)
        qkv = run(start=3 * quarter, x=corner, extra=incoming, state=state, last=True)
        qkv = lax.all_to_all(qkv, "slot", split_axis=0, concat_axis=0, tiled=True)
        pages = incoming.reshape(-1, kv_width + LANES)
        context = attend(own, lengths, qkv, cache, pages, arrivals, visit)
        for mask in masks[:-2]:
            context = jnp.concatenate([context, exchange(context, mask)], axis=0)
        side = exchange(context, masks[-2])
        pair = exchange(context, masks[-1])
        corner = exchange(side, masks[-1])
        updated = output(own, (context, side, pair, corner), weight_out, current, slots)
        current = next_segment(updated)
    return current.reshape(hidden_rows.shape)


def solution(mesh):
    return jax.shard_map(
        shards,
        mesh=mesh,
        in_specs=(
            P("segment", None, None, "slot"),
            P("segment", "slot"),
            P("segment", None, "slot"),
            P("segment", None, "slot"),
            P("segment", None, None, "slot", None, None),
            P("segment", None, None, "slot"),
            P("segment", "slot", None, None, None),
            P("segment", None, None),
            P("segment", None, None),
            P("segment", None, None),
        ),
        out_specs=P("segment", None, None, "slot"),
        check_vma=False,
    )
```

time: 132 us -> 122 us (0.924)
  local copies, waits for them, and re-layouts: 13.2 us -> 4.57 us
  Pallas kernels: 20.7 us -> 15.6 us
  waiting for transfers between devices: 55.1 us -> 59.5 us
    unnamed x32 -> x19, local copies, waits for them, and re-layouts: 13.2 us -> 4.57 us
    ppermute x20, waiting for transfers between devices: 49.6 us -> 54.1 us  [exchange(): return lax.ppermute(block, 'slot', [(i, i ^ mask) for i in range(n)])]
    pallas_call x9, Pallas kernels: 15.3 us -> 11.2 us  [the longest x8 8.69 us: project(): pl.pallas_call(functools.partial(project_kernel, start=start, first=first...]
    concatenate x3 -> x4, other arithmetic: 0.06 us -> 1.77 us  [shards(): block = jnp.concatenate([block, exchange(block, mask)], axis=0)]
  transfers between devices with their start and end apart: 23 -> 23, of which waited for: 15 -> 17; matrix products, arithmetic and copies ran while one was open for 1% -> 2% of each run, Pallas kernels for 9% -> 5%
where the time goes in v3:
time: 122 us
  waiting for transfers between devices  59.5 us (49%)
  blocking collectives  20.5 us (17%)
  starting transfers between devices  18.5 us (15%)
  Pallas kernels  15.6 us (13%)
  local copies, waits for them, and re-layouts  4.57 us (4%)
  other arithmetic  2.71 us (2%)
    ppermute x20, waiting for transfers between devices, exchange(): return lax.ppermute(block, 'slot', [(i, i ^ mask) for i in range(n)])  54.1 us
    all_to_all x2, blocking collectives, shards(): qkv = lax.all_to_all(qkv, 'slot', split_axis=0, concat_axis=0, tiled=True)  20.5 us
    ppermute x20, starting transfers between devices, exchange(): return lax.ppermute(block, 'slot', [(i, i ^ mask) for i in range(n)])  11.4 us
    pallas_call x8, Pallas kernels, project(): pl.pallas_call(functools.partial(project_kernel, start=start, first=first...  8.69 us
    ppermute x2, waiting for transfers between devices, next_segment(): return lax.ppermute(block, 'segment', [(i, (i + 1) % n) for i in range(n)])  5.49 us
    unnamed x19, local copies, waits for them, and re-layouts  4.57 us
    all_to_all x1, starting transfers between devices, shards(): lax.all_to_all(outgoing, 'slot', split_axis=0, concat_axis=0, tiled=True)  3.88 us
    ppermute x2, starting transfers between devices, next_segment(): return lax.ppermute(block, 'segment', [(i, (i + 1) % n) for i in range(n)])  3.17 us
  transfers between devices with their start and end apart: 23, of which 17 were waited for; matrix products, arithmetic and copies ran while one was open for 2% of the time, Pallas kernels for 5%

profile of v3, /device:TPU:0, one launch (start us, length us, event | category | flops | bytes accessed | tf_op | source)
XLA Modules:
  0.0 121.7 jit_solution(16608224986289900746)
XLA Ops:
  0.0 2.5 %pack.1 = bf16[16,8,1152]{2,1,0:T(8,128)(2,1)} custom-call(s32[1]{0:T(128)} %bitcast.own_ref, s32[16,16]{1,0:T(8,128)} %bitcast.38, bf16[1,512]{1,0:T(2,128)(2,1)} %gain_hbm.1, bf16[16,8,1024]{2,1,0:T(8,128)(2,1)} %bitcast.47), custom_call_target="tpu_custom_call" | custom-call | tf_op jit(solution)/shard_map/pack/pallas_call | solution.py:92
  2.5 4.1 %collective-permute-start = (bf16[1,64,512]{2,1,0:T(8,128)(2,1)}, bf16[1,64,512]{2,1,0:T(8,128)(2,1)S(1)}, u32[]{:S(2)}, u32[]{:S(2)}) collective-permute-start(bf16[1,64,512]{2,1,0:T(8,128)(2,1)} %bitcast.31), channel_id=1, source_target_pairs={{0,8},{1,9},{2,10},{3,11},{4,12},{5,13},{6,14},{7,15},{8,0},{9,1},... | collective-permute-start | bytes 196616 | tf_op jit(solution)/shard_map/ppermute | solution.py:34
  6.6 3.9 %all-to-all-start = ((bf16[16,8,1152]{2,1,0:T(8,128)(2,1)}), bf16[16,8,1152]{2,1,0:T(8,128)(2,1)S(1)}, u32[]{:S(2)}, u32[]{:S(2)}) async-start(bf16[16,8,1152]{2,1,0:T(8,128)(2,1)} %pack.1), calls=%async_computation | async-start | bytes 589824 | tf_op jit(solution)/shard_map/all_to_all | solution.py:319
  11.4 2.0 %collective-permute-start.1 = (bf16[2,64,512]{2,1,0:T(8,128)(2,1)S(1)}, bf16[2,64,512]{2,1,0:T(8,128)(2,1)S(1)}, u32[]{:S(2)}, u32[]{:S(2)}) collective-permute-start(bf16[2,64,512]{2,1,0:T(8,128)(2,1)S(1)} %pad_maximum_fusion.2), channel_id=1, source_target_pairs={{0,4},{1,5},{2,6},{3,7},{4,0},{5,1},{6,2},{7,3},{8,12},{9,13},{10,... | collective-permute-start | bytes 393224 | tf_op jit(solution)/shard_map/ppermute | solution.py:34
  13.4 7.8 %collective-permute-done.1 = bf16[2,64,512]{2,1,0:T(8,128)(2,1)S(1)} collective-permute-done((bf16[2,64,512]{2,1,0:T(8,128)(2,1)S(1)}, bf16[2,64,512]{2,1,0:T(8,128)(2,1)S(1)}, u32[]{:S(2)}, u32[]{:S(2)}) %collective-permute-start.1) | collective-permute-done | bytes 131104 | tf_op jit(solution)/shard_map/ppermute | solution.py:34
  22.1 1.5 %collective-permute-start.2 = (bf16[4,64,512]{2,1,0:T(8,128)(2,1)S(1)}, bf16[4,64,512]{2,1,0:T(8,128)(2,1)S(1)}, u32[]{:S(2)}, u32[]{:S(2)}) collective-permute-start(bf16[4,64,512]{2,1,0:T(8,128)(2,1)S(1)} %pad_maximum_fusion.x_ref), channel_id=1, source_target_pairs={{0,2},{1,3},{2,0},{3,1},{4,6},{5,7},{6,4},{7,5},{8,10},{9,11},{10,... | collective-permute-start | bytes 786440 | tf_op jit(solution)/shard_map/ppermute | solution.py:34
  24.3 2.5 %copy-done = bf16[1,8192,320]{1,2,0:T(8,128)(2,1)S(1)} copy-done((bf16[1,8192,320]{1,2,0:T(8,128)(2,1)S(1)}, bf16[1,8192,320]{1,2,0:T(8,128)(2,1)}, u32[]{:S(2)}) %copy-start) | copy-done | bytes 5242904
  26.8 1.0 project.8
  27.9 1.4 %copy-done.1 = bf16[1,8192,320]{1,2,0:T(8,128)(2,1)S(1)} copy-done((bf16[1,8192,320]{1,2,0:T(8,128)(2,1)S(1)}, bf16[1,8192,320]{1,2,0:T(8,128)(2,1)}, u32[]{:S(2)}) %copy-start.1) | copy-done | bytes 5242904
  31.0 1.0 project.10
  32.5 1.2 project.11
  33.7 11.2 %all_to_all.15.qkv_ref = bf16[16,4,320]{2,1,0:T(4,128)(2,1)S(1)} all-to-all(bf16[16,4,320]{2,1,0:T(4,128)(2,1)S(1)} %project.11), channel_id=1, replica_groups=mesh['segment'=2,'slot'=16] {'slot'}, dimensions={0} | all-to-all | bytes 81920 | tf_op jit(solution)/shard_map/all_to_all | solution.py:337
  45.0 1.2 attend.2
  46.5 4.5 %collective-permute-done.5 = bf16[1,4,4096]{2,1,0:T(4,128)(2,1)S(1)} collective-permute-done((bf16[1,4,4096]{2,1,0:T(4,128)(2,1)S(1)}, bf16[1,4,4096]{2,1,0:T(4,128)(2,1)S(1)}, u32[]{:S(2)}, u32[]{:S(2)}) %collective-permute-start.5) | collective-permute-done | bytes 32800 | tf_op jit(solution)/shard_map/ppermute | solution.py:34
  51.4 4.1 %collective-permute-done.6 = bf16[2,4,4096]{2,1,0:T(4,128)(2,1)S(1)} collective-permute-done((bf16[2,4,4096]{2,1,0:T(4,128)(2,1)S(1)}, bf16[2,4,4096]{2,1,0:T(4,128)(2,1)S(1)}, u32[]{:S(2)}, u32[]{:S(2)}) %collective-permute-start.6) | collective-permute-done | bytes 65568 | tf_op jit(solution)/shard_map/ppermute | solution.py:34
  56.2 4.4 %collective-permute-done.7.refs_1_ = bf16[4,4,4096]{2,1,0:T(4,128)(2,1)S(1)} collective-permute-done((bf16[4,4,4096]{2,1,0:T(4,128)(2,1)S(1)}, bf16[4,4,4096]{2,1,0:T(4,128)(2,1)S(1)}, u32[]{:S(2)}, u32[]{:S(2)}) %collective-permute-start.7) | collective-permute-done | bytes 131104 | tf_op jit(solution)/shard_map/ppermute | solution.py:34
  60.6 1.3 %collective-permute-done.9.refs_3_ = bf16[4,4,4096]{2,1,0:T(4,128)(2,1)S(1)} collective-permute-done((bf16[4,4,4096]{2,1,0:T(4,128)(2,1)S(1)}, bf16[4,4,4096]{2,1,0:T(4,128)(2,1)S(1)}, u32[]{:S(2)}, u32[]{:S(2)}) %collective-permute-start.9) | collective-permute-done | bytes 131104 | tf_op jit(solution)/shard_map/ppermute | solution.py:34
  63.0 1.6 %collective-permute-start.10 = (bf16[64,512]{1,0:T(8,128)(2,1)S(1)}, bf16[64,512]{1,0:T(8,128)(2,1)S(1)}, u32[]{:S(2)}, u32[]{:S(2)}) collective-permute-start(bf16[64,512]{1,0:T(8,128)(2,1)S(1)} %output.2), channel_id=1, source_target_pairs={{0,16},{16,0},{1,17},{17,1},{2,18},{18,2},{3,19},{19,3},{4,20},{20... | collective-permute-start | bytes 196616 | tf_op jit(solution)/shard_map/ppermute | solution.py:39
  64.5 2.7 %collective-permute-done.10.refs_5_ = bf16[64,512]{1,0:T(8,128)(2,1)S(1)} collective-permute-done((bf16[64,512]{1,0:T(8,128)(2,1)S(1)}, bf16[64,512]{1,0:T(8,128)(2,1)S(1)}, u32[]{:S(2)}, u32[]{:S(2)}) %collective-permute-start.10) | collective-permute-done | bytes 65568 | tf_op jit(solution)/shard_map/ppermute | solution.py:39
  67.6 5.2 %collective-permute-done.11 = bf16[1,64,512]{2,1,0:T(8,128)(2,1)S(1)} collective-permute-done((bf16[1,64,512]{2,1,0:T(8,128)(2,1)S(1)}, bf16[1,64,512]{2,1,0:T(8,128)(2,1)S(1)}, u32[]{:S(2)}, u32[]{:S(2)}) %collective-permute-start.11) | collective-permute-done | bytes 65568 | tf_op jit(solution)/shard_map/ppermute | solution.py:34
  72.9 5.0 %collective-permute-done.12 = bf16[2,64,512]{2,1,0:T(8,128)(2,1)S(1)} collective-permute-done((bf16[2,64,512]{2,1,0:T(8,128)(2,1)S(1)}, bf16[2,64,512]{2,1,0:T(8,128)(2,1)S(1)}, u32[]{:S(2)}, u32[]{:S(2)}) %collective-permute-start.12) | collective-permute-done | bytes 131104 | tf_op jit(solution)/shard_map/ppermute | solution.py:34
  79.7 1.0 project.13
  80.8 5.9 %collective-permute-done.13.x_ref = bf16[4,64,512]{2,1,0:T(8,128)(2,1)S(1)} collective-permute-done((bf16[4,64,512]{2,1,0:T(8,128)(2,1)S(1)}, bf16[4,64,512]{2,1,0:T(8,128)(2,1)S(1)}, u32[]{:S(2)}, u32[]{:S(2)}) %collective-permute-start.13) | collective-permute-done | bytes 262176 | tf_op jit(solution)/shard_map/ppermute | solution.py:34
  88.2 1.2 project.15
  89.4 9.3 %all_to_all.16.qkv_ref = bf16[16,4,320]{2,1,0:T(4,128)(2,1)S(1)} all-to-all(bf16[16,4,320]{2,1,0:T(4,128)(2,1)S(1)} %project.15), channel_id=1, replica_groups=mesh['segment'=2,'slot'=16] {'slot'}, dimensions={0} | all-to-all | bytes 81920 | tf_op jit(solution)/shard_map/all_to_all | solution.py:337
  98.8 1.2 attend.3
  100.3 4.5 %collective-permute-done.16 = bf16[1,4,4096]{2,1,0:T(4,128)(2,1)S(1)} collective-permute-done((bf16[1,4,4096]{2,1,0:T(4,128)(2,1)S(1)}, bf16[1,4,4096]{2,1,0:T(4,128)(2,1)S(1)}, u32[]{:S(2)}, u32[]{:S(2)}) %collective-permute-start.16) | collective-permute-done | bytes 32800 | tf_op jit(solution)/shard_map/ppermute | solution.py:34
  105.2 4.1 %collective-permute-done.17 = bf16[2,4,4096]{2,1,0:T(4,128)(2,1)S(1)} collective-permute-done((bf16[2,4,4096]{2,1,0:T(4,128)(2,1)S(1)}, bf16[2,4,4096]{2,1,0:T(4,128)(2,1)S(1)}, u32[]{:S(2)}, u32[]{:S(2)}) %collective-permute-start.17) | collective-permute-done | bytes 65568 | tf_op jit(solution)/shard_map/ppermute | solution.py:34
  109.9 4.4 %collective-permute-done.18.refs_1_ = bf16[4,4,4096]{2,1,0:T(4,128)(2,1)S(1)} collective-permute-done((bf16[4,4,4096]{2,1,0:T(4,128)(2,1)S(1)}, bf16[4,4,4096]{2,1,0:T(4,128)(2,1)S(1)}, u32[]{:S(2)}, u32[]{:S(2)}) %collective-permute-start.18) | collective-permute-done | bytes 131104 | tf_op jit(solution)/shard_map/ppermute | solution.py:34
  114.4 1.3 %collective-permute-done.20.refs_3_ = bf16[4,4,4096]{2,1,0:T(4,128)(2,1)S(1)} collective-permute-done((bf16[4,4,4096]{2,1,0:T(4,128)(2,1)S(1)}, bf16[4,4,4096]{2,1,0:T(4,128)(2,1)S(1)}, u32[]{:S(2)}, u32[]{:S(2)}) %collective-permute-start.20) | collective-permute-done | bytes 131104 | tf_op jit(solution)/shard_map/ppermute | solution.py:34
  116.7 1.6 %collective-permute-start.21 = (bf16[64,512]{1,0:T(8,128)(2,1)S(1)}, bf16[64,512]{1,0:T(8,128)(2,1)S(1)}, u32[]{:S(2)}, u32[]{:S(2)}) collective-permute-start(bf16[64,512]{1,0:T(8,128)(2,1)S(1)} %output.3), channel_id=1, source_target_pairs={{0,16},{16,0},{1,17},{17,1},{2,18},{18,2},{3,19},{19,3},{4,20},{20... | collective-permute-start | bytes 196616 | tf_op jit(solution)/shard_map/ppermute | solution.py:39
  118.3 2.7 %collective-permute-done.21 = bf16[64,512]{1,0:T(8,128)(2,1)S(1)} collective-permute-done((bf16[64,512]{1,0:T(8,128)(2,1)S(1)}, bf16[64,512]{1,0:T(8,128)(2,1)S(1)}, u32[]{:S(2)}, u32[]{:S(2)}) %collective-permute-start.21) | collective-permute-done | bytes 65568 | tf_op jit(solution)/shard_map/ppermute | solution.py:39
  (57 shorter events, 13.8 us)
Async XLA Ops:
  2.5 8.0 %collective-permute-start = (bf16[1,64,512]{2,1,0:T(8,128)(2,1)}, bf16[1,64,512]{2,1,0:T(8,128)(2,1)S(1)}, u32[]{:S(2)}, u32[]{:S(2)}) collective-permute-start(bf16[1,64,512]{2,1,0:T(8,128)(2,1)} %bitcast.31), channel_id=1, source_target_pairs={{0,8},{1,9},{2,10},{3,11},{4,12},{5,13},{6,14},{7,15},{8,0},{9,1},... | collective-permute-start | bytes 196616 | tf_op jit(solution)/shard_map/ppermute | solution.py:34
  6.6 17.7 %all-to-all-start = ((bf16[16,8,1152]{2,1,0:T(8,128)(2,1)}), bf16[16,8,1152]{2,1,0:T(8,128)(2,1)S(1)}, u32[]{:S(2)}, u32[]{:S(2)}) async-start(bf16[16,8,1152]{2,1,0:T(8,128)(2,1)} %pack.1), calls=%async_computation | async-start | bytes 589824 | tf_op jit(solution)/shard_map/all_to_all | solution.py:319
  11.4 9.8 %collective-permute-start.1 = (bf16[2,64,512]{2,1,0:T(8,128)(2,1)S(1)}, bf16[2,64,512]{2,1,0:T(8,128)(2,1)S(1)}, u32[]{:S(2)}, u32[]{:S(2)}) collective-permute-start(bf16[2,64,512]{2,1,0:T(8,128)(2,1)S(1)} %pad_maximum_fusion.2), channel_id=1, source_target_pairs={{0,4},{1,5},{2,6},{3,7},{4,0},{5,1},{6,2},{7,3},{8,12},{9,13},{10,... | collective-permute-start | bytes 393224 | tf_op jit(solution)/shard_map/ppermute | solution.py:34
  22.1 5.8 %collective-permute-start.3 = (bf16[4,64,512]{2,1,0:T(8,128)(2,1)S(1)}, bf16[4,64,512]{2,1,0:T(8,128)(2,1)S(1)}, u32[]{:S(2)}, u32[]{:S(2)}) collective-permute-start(bf16[4,64,512]{2,1,0:T(8,128)(2,1)S(1)} %pad_maximum_fusion.x_ref), channel_id=1, source_target_pairs={{0,1},{1,0},{2,3},{3,2},{4,5},{5,4},{6,7},{7,6},{8,9},{9,8},{10,11... | collective-permute-start | bytes 786440 | tf_op jit(solution)/shard_map/ppermute | solution.py:34
  22.1 8.7 %collective-permute-start.2 = (bf16[4,64,512]{2,1,0:T(8,128)(2,1)S(1)}, bf16[4,64,512]{2,1,0:T(8,128)(2,1)S(1)}, u32[]{:S(2)}, u32[]{:S(2)}) collective-permute-start(bf16[4,64,512]{2,1,0:T(8,128)(2,1)S(1)} %pad_maximum_fusion.x_ref), channel_id=1, source_target_pairs={{0,2},{1,3},{2,0},{3,1},{4,6},{5,7},{6,4},{7,5},{8,10},{9,11},{10,... | collective-permute-start | bytes 786440 | tf_op jit(solution)/shard_map/ppermute | solution.py:34
  24.3 2.5 %copy-start = (bf16[1,8192,320]{1,2,0:T(8,128)(2,1)S(1)}, bf16[1,8192,320]{1,2,0:T(8,128)(2,1)}, u32[]{:S(2)}) copy-start(bf16[1,8192,320]{1,2,0:T(8,128)(2,1)} %param.13) | copy-start | bytes 15728644
  26.8 2.5 %copy-start.1 = (bf16[1,8192,320]{1,2,0:T(8,128)(2,1)S(1)}, bf16[1,8192,320]{1,2,0:T(8,128)(2,1)}, u32[]{:S(2)}) copy-start(bf16[1,8192,320]{1,2,0:T(8,128)(2,1)} %param.13) | copy-start | bytes 15728644
  30.9 14.1 %copy-start.3 = (bf16[1,2,4,1,16,1024]{5,4,3,2,1,0:T(8,128)(2,1)S(1)}, bf16[1,2,4,1,16,1024]{5,4,3,2,1,0:T(8,128)(2,1)}, u32[]{:S(2)}) copy-start(bf16[1,2,4,1,16,1024]{5,4,3,2,1,0:T(8,128)(2,1)} %param.15) | copy-start | bytes 786436
  30.9 14.1 %copy-start.5 = (s32[1,16,16]{2,1,0:T(8,128)S(1)}, s32[1,16,16]{2,1,0:T(8,128)}, u32[]{:S(2)}) copy-start(s32[1,16,16]{2,1,0:T(8,128)} %param.18) | copy-start | bytes 3076
  30.9 14.1 %copy-start.6 = (s32[1,16,16]{2,1,0:T(8,128)S(1)}, s32[1,16,16]{2,1,0:T(8,128)}, u32[]{:S(2)}) copy-start(s32[1,16,16]{2,1,0:T(8,128)} %param.19) | copy-start | bytes 3076
  30.9 14.1 %copy-start.7 = (s32[1,16,16]{2,1,0:T(8,128)S(1)}, s32[1,16,16]{2,1,0:T(8,128)}, u32[]{:S(2)}) copy-start(s32[1,16,16]{2,1,0:T(8,128)} %param.20) | copy-start | bytes 3076
  30.9 14.1 %copy-start.8 = (s32[1,2,4,1]{2,3,1,0:T(1,128)S(1)}, s32[1,2,4,1]{2,3,1,0:T(1,128)}, u32[]{:S(2)}) copy-start(s32[1,2,4,1]{2,3,1,0:T(1,128)} %param.16) | copy-start | bytes 100
  30.9 31.0 %copy-start.2 = (bf16[1,4096,512]{2,1,0:T(8,128)(2,1)S(1)}, bf16[1,4096,512]{2,1,0:T(8,128)(2,1)}, u32[]{:S(2)}) copy-start(bf16[1,4096,512]{2,1,0:T(8,128)(2,1)} %param.14) | copy-start | bytes 12582916
  30.9 31.0 %copy-start.4 = (bf16[1,4,16,512]{3,2,1,0:T(8,128)(2,1)S(1)}, bf16[1,4,16,512]{3,2,1,0:T(8,128)(2,1)}, u32[]{:S(2)}) copy-start(bf16[1,4,16,512]{3,2,1,0:T(8,128)(2,1)} %param.11) | copy-start | bytes 196612
  30.9 1.6 %collective-permute-start.4 = (bf16[4,64,512]{2,1,0:T(8,128)(2,1)S(1)}, bf16[4,64,512]{2,1,0:T(8,128)(2,1)S(1)}, u32[]{:S(2)}, u32[]{:S(2)}) collective-permute-start(bf16[4,64,512]{2,1,0:T(8,128)(2,1)S(1)} %collective-permute-done.2.x_ref), channel_id=1, source_target_pairs={{0,1},{1,0},{2,3},{3,2},{4,5},{5,4},{6,7},{7,6},{8,9},{9,8},{10,11... | collective-permute-start | bytes 786440 | tf_op jit(solution)/shard_map/ppermute | solution.py:34
  46.2 4.9 %collective-permute-start.5 = (bf16[1,4,4096]{2,1,0:T(4,128)(2,1)S(1)}, bf16[1,4,4096]{2,1,0:T(4,128)(2,1)S(1)}, u32[]{:S(2)}, u32[]{:S(2)}) collective-permute-start(bf16[1,4,4096]{2,1,0:T(4,128)(2,1)S(1)} %attend.2), channel_id=1, source_target_pairs={{0,8},{1,9},{2,10},{3,11},{4,12},{5,13},{6,14},{7,15},{8,0},{9,1},... | collective-permute-start | bytes 98312 | tf_op jit(solution)/shard_map/ppermute | solution.py:34
  51.1 4.3 %collective-permute-start.6 = (bf16[2,4,4096]{2,1,0:T(4,128)(2,1)S(1)}, bf16[2,4,4096]{2,1,0:T(4,128)(2,1)S(1)}, u32[]{:S(2)}, u32[]{:S(2)}) collective-permute-start(bf16[2,4,4096]{2,1,0:T(4,128)(2,1)S(1)} %pad_maximum_fusion.6), channel_id=1, source_target_pairs={{0,4},{1,5},{2,6},{3,7},{4,0},{5,1},{6,2},{7,3},{8,12},{9,13},{10,... | collective-permute-start | bytes 196616 | tf_op jit(solution)/shard_map/ppermute | solution.py:34
  55.5 5.0 %collective-permute-start.7 = (bf16[4,4,4096]{2,1,0:T(4,128)(2,1)S(1)}, bf16[4,4,4096]{2,1,0:T(4,128)(2,1)S(1)}, u32[]{:S(2)}, u32[]{:S(2)}) collective-permute-start(bf16[4,4,4096]{2,1,0:T(4,128)(2,1)S(1)} %pad_maximum_fusion.3.refs_0_), channel_id=1, source_target_pairs={{0,2},{1,3},{2,0},{3,1},{4,6},{5,7},{6,4},{7,5},{8,10},{9,11},{10,... | collective-permute-start | bytes 393224 | tf_op jit(solution)/shard_map/ppermute | solution.py:34
  56.2 4.4 %collective-permute-start.8 = (bf16[4,4,4096]{2,1,0:T(4,128)(2,1)S(1)}, bf16[4,4,4096]{2,1,0:T(4,128)(2,1)S(1)}, u32[]{:S(2)}, u32[]{:S(2)}) collective-permute-start(bf16[4,4,4096]{2,1,0:T(4,128)(2,1)S(1)} %pad_maximum_fusion.3.refs_0_), channel_id=1, source_target_pairs={{0,1},{1,0},{2,3},{3,2},{4,5},{5,4},{6,7},{7,6},{8,9},{9,8},{10,11... | collective-permute-start | bytes 393224 | tf_op jit(solution)/shard_map/ppermute | solution.py:34
  60.6 1.3 %collective-permute-start.9 = (bf16[4,4,4096]{2,1,0:T(4,128)(2,1)S(1)}, bf16[4,4,4096]{2,1,0:T(4,128)(2,1)S(1)}, u32[]{:S(2)}, u32[]{:S(2)}) collective-permute-start(bf16[4,4,4096]{2,1,0:T(4,128)(2,1)S(1)} %collective-permute-done.7.refs_1_), channel_id=1, source_target_pairs={{0,1},{1,0},{2,3},{3,2},{4,5},{5,4},{6,7},{7,6},{8,9},{9,8},{10,11... | collective-permute-start | bytes 393224 | tf_op jit(solution)/shard_map/ppermute | solution.py:34
  63.0 4.3 %collective-permute-start.10 = (bf16[64,512]{1,0:T(8,128)(2,1)S(1)}, bf16[64,512]{1,0:T(8,128)(2,1)S(1)}, u32[]{:S(2)}, u32[]{:S(2)}) collective-permute-start(bf16[64,512]{1,0:T(8,128)(2,1)S(1)} %output.2), channel_id=1, source_target_pairs={{0,16},{16,0},{1,17},{17,1},{2,18},{18,2},{3,19},{19,3},{4,20},{20... | collective-permute-start | bytes 196616 | tf_op jit(solution)/shard_map/ppermute | solution.py:39
  67.3 5.5 %collective-permute-start.11 = (bf16[1,64,512]{2,1,0:T(8,128)(2,1)S(1)}, bf16[1,64,512]{2,1,0:T(8,128)(2,1)S(1)}, u32[]{:S(2)}, u32[]{:S(2)}) collective-permute-start(bf16[1,64,512]{2,1,0:T(8,128)(2,1)S(1)} %bitcast.35), channel_id=1, source_target_pairs={{0,8},{1,9},{2,10},{3,11},{4,12},{5,13},{6,14},{7,15},{8,0},{9,1},... | collective-permute-start | bytes 196616 | tf_op jit(solution)/shard_map/ppermute | solution.py:34
  72.8 5.0 %collective-permute-start.12 = (bf16[2,64,512]{2,1,0:T(8,128)(2,1)S(1)}, bf16[2,64,512]{2,1,0:T(8,128)(2,1)S(1)}, u32[]{:S(2)}, u32[]{:S(2)}) collective-permute-start(bf16[2,64,512]{2,1,0:T(8,128)(2,1)S(1)} %pad_maximum_fusion.4), channel_id=1, source_target_pairs={{0,4},{1,5},{2,6},{3,7},{4,0},{5,1},{6,2},{7,3},{8,12},{9,13},{10,... | collective-permute-start | bytes 393224 | tf_op jit(solution)/shard_map/ppermute | solution.py:34
  77.9 1.8 %collective-permute-start.14 = (bf16[4,64,512]{2,1,0:T(8,128)(2,1)S(1)}, bf16[4,64,512]{2,1,0:T(8,128)(2,1)S(1)}, u32[]{:S(2)}, u32[]{:S(2)}) collective-permute-start(bf16[4,64,512]{2,1,0:T(8,128)(2,1)S(1)} %pad_maximum_fusion.1.x_ref), channel_id=1, source_target_pairs={{0,1},{1,0},{2,3},{3,2},{4,5},{5,4},{6,7},{7,6},{8,9},{9,8},{10,11... | collective-permute-start | bytes 786440 | tf_op jit(solution)/shard_map/ppermute | solution.py:34
  78.0 8.7 %collective-permute-start.13 = (bf16[4,64,512]{2,1,0:T(8,128)(2,1)S(1)}, bf16[4,64,512]{2,1,0:T(8,128)(2,1)S(1)}, u32[]{:S(2)}, u32[]{:S(2)}) collective-permute-start(bf16[4,64,512]{2,1,0:T(8,128)(2,1)S(1)} %pad_maximum_fusion.1.x_ref), channel_id=1, source_target_pairs={{0,2},{1,3},{2,0},{3,1},{4,6},{5,7},{6,4},{7,5},{8,10},{9,11},{10,... | collective-permute-start | bytes 786440 | tf_op jit(solution)/shard_map/ppermute | solution.py:34
  86.7 1.5 %collective-permute-start.15 = (bf16[4,64,512]{2,1,0:T(8,128)(2,1)S(1)}, bf16[4,64,512]{2,1,0:T(8,128)(2,1)S(1)}, u32[]{:S(2)}, u32[]{:S(2)}) collective-permute-start(bf16[4,64,512]{2,1,0:T(8,128)(2,1)S(1)} %collective-permute-done.13.x_ref), channel_id=1, source_target_pairs={{0,1},{1,0},{2,3},{3,2},{4,5},{5,4},{6,7},{7,6},{8,9},{9,8},{10,11... | collective-permute-start | bytes 786440 | tf_op jit(solution)/shard_map/ppermute | solution.py:34
  100.0 4.9 %collective-permute-start.16 = (bf16[1,4,4096]{2,1,0:T(4,128)(2,1)S(1)}, bf16[1,4,4096]{2,1,0:T(4,128)(2,1)S(1)}, u32[]{:S(2)}, u32[]{:S(2)}) collective-permute-start(bf16[1,4,4096]{2,1,0:T(4,128)(2,1)S(1)} %attend.3), channel_id=1, source_target_pairs={{0,8},{1,9},{2,10},{3,11},{4,12},{5,13},{6,14},{7,15},{8,0},{9,1},... | collective-permute-start | bytes 98312 | tf_op jit(solution)/shard_map/ppermute | solution.py:34
  104.9 4.3 %collective-permute-start.17 = (bf16[2,4,4096]{2,1,0:T(4,128)(2,1)S(1)}, bf16[2,4,4096]{2,1,0:T(4,128)(2,1)S(1)}, u32[]{:S(2)}, u32[]{:S(2)}) collective-permute-start(bf16[2,4,4096]{2,1,0:T(4,128)(2,1)S(1)} %pad_maximum_fusion.7), channel_id=1, source_target_pairs={{0,4},{1,5},{2,6},{3,7},{4,0},{5,1},{6,2},{7,3},{8,12},{9,13},{10,... | collective-permute-start | bytes 196616 | tf_op jit(solution)/shard_map/ppermute | solution.py:34
  109.3 5.0 %collective-permute-start.18 = (bf16[4,4,4096]{2,1,0:T(4,128)(2,1)S(1)}, bf16[4,4,4096]{2,1,0:T(4,128)(2,1)S(1)}, u32[]{:S(2)}, u32[]{:S(2)}) collective-permute-start(bf16[4,4,4096]{2,1,0:T(4,128)(2,1)S(1)} %pad_maximum_fusion.5.refs_0_), channel_id=1, source_target_pairs={{0,2},{1,3},{2,0},{3,1},{4,6},{5,7},{6,4},{7,5},{8,10},{9,11},{10,... | collective-permute-start | bytes 393224 | tf_op jit(solution)/shard_map/ppermute | solution.py:34
  109.9 4.4 %collective-permute-start.19 = (bf16[4,4,4096]{2,1,0:T(4,128)(2,1)S(1)}, bf16[4,4,4096]{2,1,0:T(4,128)(2,1)S(1)}, u32[]{:S(2)}, u32[]{:S(2)}) collective-permute-start(bf16[4,4,4096]{2,1,0:T(4,128)(2,1)S(1)} %pad_maximum_fusion.5.refs_0_), channel_id=1, source_target_pairs={{0,1},{1,0},{2,3},{3,2},{4,5},{5,4},{6,7},{7,6},{8,9},{9,8},{10,11... | collective-permute-start | bytes 393224 | tf_op jit(solution)/shard_map/ppermute | solution.py:34
  114.4 1.3 %collective-permute-start.20 = (bf16[4,4,4096]{2,1,0:T(4,128)(2,1)S(1)}, bf16[4,4,4096]{2,1,0:T(4,128)(2,1)S(1)}, u32[]{:S(2)}, u32[]{:S(2)}) collective-permute-start(bf16[4,4,4096]{2,1,0:T(4,128)(2,1)S(1)} %collective-permute-done.18.refs_1_), channel_id=1, source_target_pairs={{0,1},{1,0},{2,3},{3,2},{4,5},{5,4},{6,7},{7,6},{8,9},{9,8},{10,11... | collective-permute-start | bytes 393224 | tf_op jit(solution)/shard_map/ppermute | solution.py:34
  116.7 4.3 %collective-permute-start.21 = (bf16[64,512]{1,0:T(8,128)(2,1)S(1)}, bf16[64,512]{1,0:T(8,128)(2,1)S(1)}, u32[]{:S(2)}, u32[]{:S(2)}) collective-permute-start(bf16[64,512]{1,0:T(8,128)(2,1)S(1)} %output.3), channel_id=1, source_target_pairs={{0,16},{16,0},{1,17},{17,1},{2,18},{18,2},{3,19},{19,3},{4,20},{20... | collective-permute-start | bytes 196616 | tf_op jit(solution)/shard_map/ppermute | solution.py:39

commit v4 on v3

--- a/solution.py
+++ b/solution.py
@@ -17,7 +17,6 @@
 LANES = 128
 
 norm_eps = 1e-06
-FIRST_LIMIT = 63 * 1024 * 1024
 VMEM_LIMIT = 12 * 1024 * 1024
 
 
@@ -34,9 +33,20 @@
     return lax.ppermute(block, "slot", [(i, i ^ mask) for i in range(n)])
 
 
-def next_segment(block):
-    n = lax.axis_size("segment")
-    return lax.ppermute(block, "segment", [(i, (i + 1) % n) for i in range(n)])
+def spread(block, masks):
+    across, over, core = masks
+    second = exchange(block, across)
+    third = exchange(block, over)
+    fourth = exchange(second, over)
+    groups = [block, second, third, fourth]
+    return groups + [exchange(group, core) for group in groups]
+
+
+def next_segment(block, mask=0):
+    n, slots = lax.axis_size("segment"), lax.axis_size("slot")
+    route = [(s * slots + i, (s + 1) % n * slots + (i ^ mask)) for s in range(n)
+             for i in range(slots)]
+    return lax.ppermute(block, ("segment", "slot"), route)
 
 
 def split_rows(index, slots, batch, slot_first):
@@ -64,99 +74,117 @@
     return ((place == arrival) & (to_row == from_row)).astype(jnp.bfloat16)
 
 
-def pack_kernel(own_ref, dest_ref, gain_hbm, pages_hbm, send_ref, gain_ref, pages_ref, sem):
-    copies = [pltpu.make_async_copy(gain_hbm, gain_ref, sem.at[0]),
-              pltpu.make_async_copy(pages_hbm, pages_ref, sem.at[1])]
-    for copy in copies:
-        copy.start()
-    for copy in copies:
-        copy.wait()
+def room_for(columns):
+    return -(-(columns // 2) // LANES) * LANES
+
+
+def pack_kernel(own_ref, dest_ref, pages_ref, send_ref):
     slots, page_tok, wide = send_ref.shape
     kv_width = pages_ref.shape[2]
-    gain = gain_ref[...].astype(jnp.float32)
-    at = iota((page_tok, LANES), 0)
-    extra = jnp.zeros((page_tok, LANES), jnp.float32)
-    for r in range(gain.shape[1] // LANES):
-        extra = jnp.where(at == r, gain[:, r * LANES:(r + 1) * LANES], extra)
-    extra = extra.astype(jnp.bfloat16)
     for p in range(pages_ref.shape[0]):
         send_ref[dest_ref[own_ref[0], p], :, :kv_width] = pages_ref[p]
     for j in range(slots):
-        send_ref[j, :, kv_width:] = extra
-
-
-def pack(own, gain, pages, dest):
+        send_ref[j, :, kv_width:] = jnp.zeros((page_tok, wide - kv_width), send_ref.dtype)
+
+
+def pack(own, pages, dest, room):
     _, page_tok, kv_width = pages.shape
-    shape = (dest.shape[0], page_tok, kv_width + LANES)
-    there = pl.BlockSpec(memory_space=pl.ANY)
+    whole = pl.BlockSpec(memory_space=pltpu.VMEM)
+    scalars = pl.BlockSpec(memory_space=pltpu.SMEM)
     return pl.pallas_call(
         pack_kernel,
-        out_shape=jax.ShapeDtypeStruct(shape, pages.dtype),
-        grid_spec=pltpu.PrefetchScalarGridSpec(
-            num_scalar_prefetch=2, grid=(1,), in_specs=[there, there],
-            out_specs=pl.BlockSpec(shape, lambda s, own, dest: (0, 0, 0)),
-            scratch_shapes=[pltpu.VMEM(gain.shape, gain.dtype), pltpu.VMEM(pages.shape, pages.dtype),
-                            pltpu.SemaphoreType.DMA((2,))]),
-        compiler_params=pltpu.CompilerParams(vmem_limit_bytes=FIRST_LIMIT),
+        out_shape=jax.ShapeDtypeStruct((dest.shape[0], page_tok, kv_width + room), pages.dtype),
+        in_specs=[scalars, scalars, whole],
+        out_specs=whole,
+        compiler_params=params(),
         name="pack",
-    )(own, dest, gain, pages)
-
-
-def project_kernel(order_ref, x_ref, w_ref, extra_ref, *refs, start, first, last, batch, kv_width):
-    acc_in, square_in = (None, None) if first else refs[:2]
-    outs = refs if first else refs[2:]
-    blocks, rows, width = x_ref.shape
+    )(own, dest, pages)
+
+
+def project_kernel(order_ref, w_ref, *refs, starts, rows, carried, first, last, packed, batch):
+    refs = list(refs)
+    x_refs = [refs.pop(0) for _ in starts]
+    kept = None if carried else refs.pop(0)
+    acc_in, square_in = (None, None) if first else (refs.pop(0), refs.pop(0))
+    if packed:
+        refs.pop(0)
+    if carried:
+        kept = refs.pop(0)
+    blocks, _, width = x_refs[0].shape
     columns, model_width = w_ref.shape
     acc = jnp.zeros((rows, columns), jnp.float32) if first else acc_in[...]
     square = jnp.zeros((rows, LANES), jnp.float32) if first else square_in[...]
-    for i in range(blocks):
-        source = order_ref[start + i]
-        x = x_ref[i]
-        gain = extra_ref[source, :, kv_width:].astype(jnp.float32)
-        parts = []
-        for r in range(width // LANES):
-            part = x[:, r * LANES:(r + 1) * LANES].astype(jnp.float32)
-            square = square + part * part
-            parts.append((part * gain[r:r + 1]).astype(jnp.bfloat16))
-        x = parts[0] if len(parts) == 1 else jnp.concatenate(parts, axis=1)
-        here = pl.ds(pl.multiple_of(source * width, width), width)
-        acc = acc + lax.dot_general(x, w_ref[:, here], (((1,), (1,)), ((), ())),
-                                    preferred_element_type=jnp.float32)
+    for g, start in enumerate(starts):
+        for i in range(blocks):
+            if carried:
+                kept[g * blocks + i] = x_refs[g][i, rows:]
+            x = x_refs[g][i, :rows]
+            gain = kept[g * blocks + i].astype(jnp.float32)[:1]
+            parts = []
+            for r in range(0, width, LANES):
+                part = x[:, r:r + LANES].astype(jnp.float32)
+                square = square + part * part
+                parts.append((part * gain[:, r:r + LANES]).astype(jnp.bfloat16))
+            x = parts[0] if len(parts) == 1 else jnp.concatenate(parts, axis=1)
+            here = pl.ds(pl.multiple_of(order_ref[start + i] * width, width), width)
+            acc = acc + lax.dot_general(x, w_ref[:, here], (((1,), (1,)), ((), ())),
+                                        preferred_element_type=jnp.float32)
     if not last:
-        outs[0][...] = acc
-        outs[1][...] = square
+        refs[0][...] = acc
+        refs[1][...] = square
         return
     sums = jnp.sum(square, axis=1, keepdims=True)
     out = (acc * lax.rsqrt(sums / model_width + norm_eps)).astype(jnp.bfloat16)
     slots = rows // batch
     out = jnp.dot(slot_rows_first(slots, batch), out, preferred_element_type=jnp.float32)
+    half = columns // 2
     for j in range(slots):
-        outs[0][j] = out[j * batch:(j + 1) * batch].astype(jnp.bfloat16)
-
-
-def project(order, start, x, weight, extra, state, *, last, batch, kv_width):
-    blocks, rows, width = x.shape
+        mine = out[j * batch:(j + 1) * batch]
+        if packed:
+            at = refs[0].shape[2] - room_for(columns)
+            mine = jnp.concatenate([mine[:, :half], mine[:, half:]], axis=0)
+            refs[0][j, :, at:at + half] = mine.astype(jnp.bfloat16)
+        else:
+            refs[0][j] = mine.astype(jnp.bfloat16)
+
+
+def project(order, rows, batch, weight, groups, gains, state, last=False, outgoing=None):
+    blocks, held, width = groups[0][1].shape
     columns = weight.shape[0]
-    first = state is None
-    operands = [x, weight, extra] + ([] if first else list(state))
-    if last:
-        out_shape = jax.ShapeDtypeStruct((rows // batch, batch, columns), jnp.bfloat16)
+    carried, first, packed = gains is None, state is None, outgoing is not None
+    operands = [weight] + [x for _, x in groups] + ([] if carried else [gains])
+    operands += [] if first else list(state)
+    aliases = {}
+    out_shape = []
+    if carried:
+        out_shape.append(jax.ShapeDtypeStruct((len(groups) * blocks, held - rows, width),
+                                              jnp.bfloat16))
+    if packed:
+        aliases = {len(operands) + 1: len(out_shape)}
+        operands.append(outgoing)
+        out_shape.append(jax.ShapeDtypeStruct(outgoing.shape, outgoing.dtype))
+    elif last:
+        out_shape.append(jax.ShapeDtypeStruct((rows // batch, batch, columns), jnp.bfloat16))
     else:
-        out_shape = [jax.ShapeDtypeStruct((rows, columns), jnp.float32),
-                     jax.ShapeDtypeStruct((rows, LANES), jnp.float32)]
+        out_shape += [jax.ShapeDtypeStruct((rows, columns), jnp.float32),
+                      jax.ShapeDtypeStruct((rows, LANES), jnp.float32)]
     whole = pl.BlockSpec(memory_space=pltpu.VMEM)
-    return pl.pallas_call(
-        functools.partial(project_kernel, start=start, first=first, last=last, batch=batch,
-                          kv_width=kv_width),
+    work = rows * width * columns * blocks * len(groups)
+    out = pl.pallas_call(
+        functools.partial(project_kernel, starts=[g * blocks for g, _ in groups], rows=rows,
+                          carried=carried, first=first, last=last, packed=packed, batch=batch),
         out_shape=out_shape,
         in_specs=[pl.BlockSpec(memory_space=pltpu.SMEM)] + [whole] * len(operands),
-        out_specs=whole if last else [whole] * len(out_shape),
+        out_specs=[whole] * len(out_shape),
+        input_output_aliases=aliases,
         compiler_params=params(),
-        cost_estimate=pl.CostEstimate(flops=8 * rows * width * columns * blocks,
-                                      bytes_accessed=2 * width * columns * blocks,
+        cost_estimate=pl.CostEstimate(flops=8 * work, bytes_accessed=2 * work // rows,
                                       transcendentals=0),
         name="project",
     )(order, *operands)
+    if carried:
+        gains, *out = out
+    return gains, (out[0] if last else out)
 
 
 def token_rows(own, dest_ref, row_ref, count_ref, page_tok):
@@ -177,11 +205,19 @@
 
 
 def attend_kernel(own_ref, len_ref, qkv_ref, cache_ref, pages_ref, dest_ref, page_row_ref, count_ref,
-                  out_ref, *, visit):
-    slots, batch, columns = qkv_ref.shape
-    positions = cache_ref.shape[2]
+                  out_ref, *, visit, columns, packed):
+    slots = qkv_ref.shape[0]
+    batch, positions = cache_ref.shape[1:3]
     tokens = pages_ref.shape[0]
-    full = jnp.concatenate([qkv_ref[j].astype(jnp.float32) for j in range(slots)], axis=1)
+    pieces = []
+    for j in range(slots):
+        piece = qkv_ref[j].astype(jnp.float32)
+        if packed:
+            half = columns // 2
+            pieces += [piece[:batch, :half], piece[batch:2 * batch, :half]]
+        else:
+            pieces.append(piece)
+    full = jnp.concatenate(pieces, axis=1)
     group_rows = GROUP * batch
     near = batch * positions
     near_pad = -(-(near + 16) // LANES) * LANES
@@ -241,18 +277,22 @@
                 jnp.bfloat16)
 
 
-def attend(own, lengths, qkv, cache, pages, arrivals, visit):
-    slots, batch, columns = qkv.shape
-    _, _, positions, kv_width = cache.shape
+def attend(own, lengths, qkv, columns, cache, pages, arrivals, visit):
+    packed = qkv.ndim == 3 and qkv.shape[2] != columns
+    slots = qkv.shape[0]
+    _, batch, positions, kv_width = cache.shape
     tokens = pages.shape[0]
     scalars = pl.BlockSpec(memory_space=pltpu.SMEM)
     fixed = lambda *shape: pl.BlockSpec(shape, lambda s: (0,) * len(shape))
     return pl.pallas_call(
-        functools.partial(attend_kernel, visit=visit),
+        functools.partial(attend_kernel, visit=visit, columns=columns, packed=packed),
         out_shape=jax.ShapeDtypeStruct((1, batch, QUERY_HEADS * HEAD_SIZE), jnp.bfloat16),
         grid=(1,),
         in_specs=[
-            scalars, scalars, fixed(slots, batch, columns),
+            scalars, scalars,
+            pl.BlockSpec((slots, qkv.shape[1], room_for(columns)),
+                         lambda s: (0, 0, kv_width // room_for(columns))) if packed
+            else fixed(*qkv.shape),
             pl.BlockSpec((1, batch, positions, kv_width), lambda s: (visit, 0, 0, 0)),
             fixed(tokens, kv_width)] + [fixed(*v.shape) for v in arrivals],
         out_specs=fixed(1, batch, QUERY_HEADS * HEAD_SIZE),
@@ -262,7 +302,7 @@
 
 
 def output_kernel(own_ref, *refs, slots, batch):
-    pieces, (w_ref, now_ref, out_ref) = refs[:4], refs[4:]
+    pieces, (w_ref, now_ref, out_ref) = refs[:-3], refs[-3:]
     features = w_ref.shape[0]
     depth = features // 4
     acc = jnp.zeros(out_ref.shape, jnp.float32)
@@ -288,7 +328,7 @@
     return pl.pallas_call(
         functools.partial(output_kernel, slots=slots, batch=batch),
         out_shape=jax.ShapeDtypeStruct(now.shape, jnp.bfloat16),
-        in_specs=[pl.BlockSpec(memory_space=pltpu.SMEM)] + [whole] * 6,
+        in_specs=[pl.BlockSpec(memory_space=pltpu.SMEM)] + [whole] * (len(pieces) + 2),
         out_specs=whole,
         compiler_params=params(),
         name="output",
@@ -314,36 +354,41 @@
     weight_out = out_weight[0]
     own = own.reshape(1)
     current = hidden_rows.reshape(rows, width)
-    outgoing = pack(own, norm_gain, page_kv[0, 0], page_dest[0])
-    current, outgoing = lax.optimization_barrier((current, outgoing))
-    incoming = lax.all_to_all(outgoing, "slot", split_axis=0, concat_axis=0, tiled=True)
+    columns = weight_in.shape[0]
     arrivals = (page_dest[0], page_row[0], page_count[0])
+    gains = [None] * 5
     for visit in range(CYCLE_STEPS):
-        block = current[None]
-        for mask in masks[:-2]:
+        if visit == 0:
+            spare = jnp.zeros((15, width), norm_gain.dtype)
+            block = jnp.concatenate([current, norm_gain, spare], axis=0)[None]
+            block = jnp.concatenate([block, exchange(block, masks[0])], axis=0)
+            outgoing = pack(own, page_kv[0, 0], page_dest[0], room_for(columns))
+            block, outgoing = lax.optimization_barrier((block, outgoing))
+        else:
+            block = jnp.stack([current, beyond])
+        for mask in masks[1:-3]:
             block = jnp.concatenate([block, exchange(block, mask)], axis=0)
-        quarter = block.shape[0]
-        run = functools.partial(project, order, weight=weight_in,
-                                batch=batch, kv_width=kv_width)
-        side = exchange(block, masks[-2])
-        pair = exchange(block, masks[-1])
-        held, incoming = lax.optimization_barrier((block, incoming))
-        state = run(start=0, x=held, extra=incoming, state=None, last=False)
-        state = run(start=2 * quarter, x=pair, extra=incoming, state=state, last=False)
-        side, state = lax.optimization_barrier((side, state))
-        corner = exchange(side, masks[-1])
-        state = run(start=quarter, x=side, extra=incoming, state=state, last=False)
-        qkv = run(start=3 * quarter, x=corner, extra=incoming, state=state, last=True)
+        run = functools.partial(project, order, rows, batch, weight_in)
+        state = None
+        groups = spread(block, masks[-3:])
+        for k, names in enumerate([(0, 4), (1, 5), (2, 6)]):
+            gains[k], state = run([(g, groups[g]) for g in names], gains[k], state)
+        groups[3], state = lax.optimization_barrier((groups[3], state))
+        groups[7] = exchange(groups[3], masks[-1])
+        gains[3], state = run([(3, groups[3])], gains[3], state)
+        gains[4], qkv = run([(7, groups[7])], gains[4], state, last=True,
+                             outgoing=None if visit else outgoing)
         qkv = lax.all_to_all(qkv, "slot", split_axis=0, concat_axis=0, tiled=True)
-        pages = incoming.reshape(-1, kv_width + LANES)
-        context = attend(own, lengths, qkv, cache, pages, arrivals, visit)
-        for mask in masks[:-2]:
+        if visit == 0:
+            pages = qkv.reshape(-1, qkv.shape[2])
+        context = attend(own, lengths, qkv, columns, cache, pages, arrivals, visit)
+        for mask in masks[:-3]:
             context = jnp.concatenate([context, exchange(context, mask)], axis=0)
-        side = exchange(context, masks[-2])
-        pair = exchange(context, masks[-1])
-        corner = exchange(side, masks[-1])
-        updated = output(own, (context, side, pair, corner), weight_out, current, slots)
+        groups = spread(context, masks[-3:])
+        updated = output(own, groups, weight_out, current, slots)
         current = next_segment(updated)
+        if visit < CYCLE_STEPS - 1:
+            beyond = next_segment(updated, masks[0])
     return current.reshape(hidden_rows.shape)
 
 

time: 122 us -> 114 us (0.934)
  waiting for transfers between devices: 59.5 us -> 44.7 us
  blocking collectives: 20.5 us -> 26.6 us
  starting transfers between devices: 18.5 us -> 19.8 us
    ppermute x20 -> x31, waiting for transfers between devices: 54.1 us -> 35.4 us  [exchange(): return lax.ppermute(block, 'slot', [(i, i ^ mask) for i in range(n)])]
    all_to_all x2, blocking collectives: 20.5 us -> 26.6 us  [shards(): qkv = lax.all_to_all(qkv, 'slot', split_axis=0, concat_axis=0, tiled=True)]
    ppermute x20 -> x31, starting transfers between devices: 11.4 us -> 16.5 us  [exchange(): return lax.ppermute(block, 'slot', [(i, i ^ mask) for i in range(n)])]
    all_to_all x1 -> x0, starting transfers between devices: 3.88 us -> none  [shards(): lax.all_to_all(outgoing, 'slot', split_axis=0, concat_axis=0, tiled=True)]
    ppermute x2 -> x3, waiting for transfers between devices: 5.49 us -> 9.34 us  [next_segment(): return lax.ppermute(block, ('segment', 'slot'), route)]
    concatenate x4 -> x1, other arithmetic: 1.77 us -> 0.02 us  [shards(): block = jnp.concatenate([block, exchange(block, masks[0])], axis=0)]
    pallas_call x11 -> x13, Pallas kernels: 13.6 us -> 13.3 us  [the longest x10 10.2 us: project(): pl.pallas_call(functools.partial(project_kernel, starts=[g * blocks for g...]
    unnamed x19 -> x25, local copies, waits for them, and re-layouts: 4.57 us -> 4.81 us
  transfers between devices with their start and end apart: 23 -> 34, of which waited for: 17 -> 18; matrix products, arithmetic and copies ran while one was open for 2% -> 1% of each run, Pallas kernels for 5% -> 8%
where the time goes in v4:
time: 114 us; the launch traced here: 113 us
  waiting for transfers between devices  44.7 us (39%)
  blocking collectives  26.6 us (23%)
  starting transfers between devices  19.8 us (17%)
  Pallas kernels  15.4 us (14%)
  local copies, waits for them, and re-layouts  4.89 us (4%)
  other arithmetic  1.72 us (2%)
    ppermute x31, waiting for transfers between devices, exchange(): return lax.ppermute(block, 'slot', [(i, i ^ mask) for i in range(n)])  35.4 us
    all_to_all x2, blocking collectives, shards(): qkv = lax.all_to_all(qkv, 'slot', split_axis=0, concat_axis=0, tiled=True)  26.6 us
    ppermute x31, starting transfers between devices, exchange(): return lax.ppermute(block, 'slot', [(i, i ^ mask) for i in range(n)])  16.5 us
    pallas_call x10, Pallas kernels, project(): pl.pallas_call(functools.partial(project_kernel, starts=[g * blocks for g...  10.2 us
    ppermute x3, waiting for transfers between devices, next_segment(): return lax.ppermute(block, ('segment', 'slot'), route)  9.34 us
    unnamed x25, local copies, waits for them, and re-layouts  4.81 us
    ppermute x3, starting transfers between devices, next_segment(): return lax.ppermute(block, ('segment', 'slot'), route)  3.32 us
    pallas_call x2, Pallas kernels, attend(): pl.pallas_call(functools.partial(attend_kernel, visit=visit, columns=colu...  2.39 us
  transfers between devices with their start and end apart: 34, of which 18 were waited for; matrix products, arithmetic and copies ran while one was open for 1% of the time, Pallas kernels for 8%

profile of v4, /device:TPU:0, one launch (start us, length us, event | category | flops | bytes accessed | tf_op | source)
XLA Modules:
  0.0 113.4 jit_solution(6157241828438027214)
XLA Ops:
  1.0 4.1 %collective-permute-start = (bf16[1,80,512]{2,1,0:T(8,128)(2,1)S(1)}, bf16[1,80,512]{2,1,0:T(8,128)(2,1)S(1)}, u32[]{:S(2)}, u32[]{:S(2)}) collective-permute-start(bf16[1,80,512]{2,1,0:T(8,128)(2,1)S(1)} %maximum_bitcast_fusion), channel_id=1, source_target_pairs={{0,8},{1,9},{2,10},{3,11},{4,12},{5,13},{6,14},{7,15},{8,0},{9,1},... | collective-permute-start | bytes 245768 | tf_op jit(solution)/shard_map/ppermute | solution.py:33
  7.5 1.8 %collective-permute-done = bf16[1,80,512]{2,1,0:T(8,128)(2,1)S(1)} collective-permute-done((bf16[1,80,512]{2,1,0:T(8,128)(2,1)S(1)}, bf16[1,80,512]{2,1,0:T(8,128)(2,1)S(1)}, u32[]{:S(2)}, u32[]{:S(2)}) %collective-permute-start) | collective-permute-done | bytes 81952 | tf_op jit(solution)/shard_map/ppermute | solution.py:33
  10.1 1.5 %collective-permute-start.3 = (bf16[2,80,512]{2,1,0:T(8,128)(2,1)S(1)}, bf16[2,80,512]{2,1,0:T(8,128)(2,1)S(1)}, u32[]{:S(2)}, u32[]{:S(2)}) collective-permute-start(bf16[2,80,512]{2,1,0:T(8,128)(2,1)S(1)} %pad_maximum_fusion.refs_0_), channel_id=1, source_target_pairs={{0,2},{1,3},{2,0},{3,1},{4,6},{5,7},{6,4},{7,5},{8,10},{9,11},{10,... | collective-permute-start | bytes 491528 | tf_op jit(solution)/shard_map/ppermute | solution.py:33
  11.6 3.1 %collective-permute-done.1.refs_0_ = bf16[2,80,512]{2,1,0:T(8,128)(2,1)S(1)} collective-permute-done((bf16[2,80,512]{2,1,0:T(8,128)(2,1)S(1)}, bf16[2,80,512]{2,1,0:T(8,128)(2,1)S(1)}, u32[]{:S(2)}, u32[]{:S(2)}) %collective-permute-start.1) | collective-permute-done | bytes 163872 | tf_op jit(solution)/shard_map/ppermute | solution.py:33
  14.7 1.7 %collective-permute-start.2 = (bf16[2,80,512]{2,1,0:T(8,128)(2,1)S(1)}, bf16[2,80,512]{2,1,0:T(8,128)(2,1)S(1)}, u32[]{:S(2)}, u32[]{:S(2)}) collective-permute-start(bf16[2,80,512]{2,1,0:T(8,128)(2,1)S(1)} %collective-permute-done.1.refs_0_), channel_id=1, source_target_pairs={{0,2},{1,3},{2,0},{3,1},{4,6},{5,7},{6,4},{7,5},{8,10},{9,11},{10,... | collective-permute-start | bytes 491528 | tf_op jit(solution)/shard_map/ppermute | solution.py:33
  17.3 2.5 %copy-done = bf16[1,8192,320]{1,2,0:T(8,128)(2,1)S(1)} copy-done((bf16[1,8192,320]{1,2,0:T(8,128)(2,1)S(1)}, bf16[1,8192,320]{1,2,0:T(8,128)(2,1)}, u32[]{:S(2)}) %copy-start) | copy-done | bytes 5242904
  20.9 1.1 project.11
  21.9 1.1 project.12
  24.5 1.1 project.14
  25.7 16.4 %all_to_all.10.qkv_ref = bf16[16,8,1280]{2,1,0:T(8,128)(2,1)S(1)} all-to-all(bf16[16,8,1280]{2,1,0:T(8,128)(2,1)S(1)} %get-tuple-element.48), channel_id=1, replica_groups=mesh['segment'=2,'slot'=16] {'slot'}, dimensions={0} | all-to-all | bytes 655360 | tf_op jit(solution)/shard_map/all_to_all | solution.py:381
  42.1 1.2 %attend.2 = bf16[1,4,4096]{2,1,0:T(4,128)(2,1)S(1)} custom-call(s32[1]{0:T(128)} %bitcast.own_ref, s32[2,4]{1,0:T(2,128)S(1)} %bitcast.47, bf16[16,8,1280]{2,1,0:T(8,128)(2,1)S(1)} %all_to_all.10.qkv_ref, bf16[2,4,16,1024]{3,2,1,0:T(8,128)(2,1)S(1)} %bitcast.34, bf16[128,1280]{1,0:T(8,128)(2,1)S(1)} %bitcast.32, s32[16,16]{1,0:T(8,128)S(1)} %bitcast.41, ...), custom_call_target="tpu_custom_call" | custom-call | tf_op jit(solution)/shard_map/attend/pallas_call | solution.py:287
  43.3 1.5 %collective-permute-start.8 = (bf16[1,4,4096]{2,1,0:T(4,128)(2,1)S(1)}, bf16[1,4,4096]{2,1,0:T(4,128)(2,1)S(1)}, u32[]{:S(2)}, u32[]{:S(2)}) collective-permute-start(bf16[1,4,4096]{2,1,0:T(4,128)(2,1)S(1)} %attend.2), channel_id=1, source_target_pairs={{0,8},{1,9},{2,10},{3,11},{4,12},{5,13},{6,14},{7,15},{8,0},{9,1},... | collective-permute-start | bytes 98312 | tf_op jit(solution)/shard_map/ppermute | solution.py:33
  44.8 3.6 %collective-permute-done.8 = bf16[1,4,4096]{2,1,0:T(4,128)(2,1)S(1)} collective-permute-done((bf16[1,4,4096]{2,1,0:T(4,128)(2,1)S(1)}, bf16[1,4,4096]{2,1,0:T(4,128)(2,1)S(1)}, u32[]{:S(2)}, u32[]{:S(2)}) %collective-permute-start.8) | collective-permute-done | bytes 32800 | tf_op jit(solution)/shard_map/ppermute | solution.py:33
  48.7 1.1 collective-permute-start.10
  49.8 3.0 %collective-permute-done.9.refs_1_ = bf16[2,4,4096]{2,1,0:T(4,128)(2,1)S(1)} collective-permute-done((bf16[2,4,4096]{2,1,0:T(4,128)(2,1)S(1)}, bf16[2,4,4096]{2,1,0:T(4,128)(2,1)S(1)}, u32[]{:S(2)}, u32[]{:S(2)}) %collective-permute-start.9) | collective-permute-done | bytes 65568 | tf_op jit(solution)/shard_map/ppermute | solution.py:33
  53.6 3.4 %collective-permute-done.11.refs_3_ = bf16[2,4,4096]{2,1,0:T(4,128)(2,1)S(1)} collective-permute-done((bf16[2,4,4096]{2,1,0:T(4,128)(2,1)S(1)}, bf16[2,4,4096]{2,1,0:T(4,128)(2,1)S(1)}, u32[]{:S(2)}, u32[]{:S(2)}) %collective-permute-start.11) | collective-permute-done | bytes 65568 | tf_op jit(solution)/shard_map/ppermute | solution.py:33
  57.1 1.2 %collective-permute-done.15.refs_7_ = bf16[2,4,4096]{2,1,0:T(4,128)(2,1)S(1)} collective-permute-done((bf16[2,4,4096]{2,1,0:T(4,128)(2,1)S(1)}, bf16[2,4,4096]{2,1,0:T(4,128)(2,1)S(1)}, u32[]{:S(2)}, u32[]{:S(2)}) %collective-permute-start.15) | collective-permute-done | bytes 65568 | tf_op jit(solution)/shard_map/ppermute | solution.py:33
  59.3 1.6 %collective-permute-start.16 = (bf16[64,512]{1,0:T(8,128)(2,1)S(1)}, bf16[64,512]{1,0:T(8,128)(2,1)S(1)}, u32[]{:S(2)}, u32[]{:S(2)}) collective-permute-start(bf16[64,512]{1,0:T(8,128)(2,1)S(1)} %output.2), channel_id=1, source_target_pairs={{0,16},{1,17},{2,18},{3,19},{4,20},{5,21},{6,22},{7,23},{8,24},{9,... | collective-permute-start | bytes 196616 | tf_op jit(solution)/shard_map/ppermute | solution.py:49
  60.9 1.2 %collective-permute-start.17 = (bf16[64,512]{1,0:T(8,128)(2,1)S(1)}, bf16[64,512]{1,0:T(8,128)(2,1)S(1)}, u32[]{:S(2)}, u32[]{:S(2)}) collective-permute-start(bf16[64,512]{1,0:T(8,128)(2,1)S(1)} %output.2), channel_id=1, source_target_pairs={{0,24},{1,25},{2,26},{3,27},{4,28},{5,29},{6,30},{7,31},{8,16},{9,... | collective-permute-start | bytes 196616 | tf_op jit(solution)/shard_map/ppermute | solution.py:49
  62.1 1.6 %collective-permute-done.16.refs_9_ = bf16[64,512]{1,0:T(8,128)(2,1)S(1)} collective-permute-done((bf16[64,512]{1,0:T(8,128)(2,1)S(1)}, bf16[64,512]{1,0:T(8,128)(2,1)S(1)}, u32[]{:S(2)}, u32[]{:S(2)}) %collective-permute-start.16) | collective-permute-done | bytes 65568 | tf_op jit(solution)/shard_map/ppermute | solution.py:49
  63.7 4.0 %collective-permute-done.17 = bf16[64,512]{1,0:T(8,128)(2,1)S(1)} collective-permute-done((bf16[64,512]{1,0:T(8,128)(2,1)S(1)}, bf16[64,512]{1,0:T(8,128)(2,1)S(1)}, u32[]{:S(2)}, u32[]{:S(2)}) %collective-permute-start.17) | collective-permute-done | bytes 65568 | tf_op jit(solution)/shard_map/ppermute | solution.py:49
  68.5 4.4 %collective-permute-done.18.refs_0_ = bf16[2,64,512]{2,1,0:T(8,128)(2,1)S(1)} collective-permute-done((bf16[2,64,512]{2,1,0:T(8,128)(2,1)S(1)}, bf16[2,64,512]{2,1,0:T(8,128)(2,1)S(1)}, u32[]{:S(2)}, u32[]{:S(2)}) %collective-permute-start.18) | collective-permute-done | bytes 131104 | tf_op jit(solution)/shard_map/ppermute | solution.py:33
  75.0 1.1 project.16
  76.1 1.1 project.17
  77.1 1.7 %collective-permute-done.19.refs_0_ = bf16[2,64,512]{2,1,0:T(8,128)(2,1)S(1)} collective-permute-done((bf16[2,64,512]{2,1,0:T(8,128)(2,1)S(1)}, bf16[2,64,512]{2,1,0:T(8,128)(2,1)S(1)}, u32[]{:S(2)}, u32[]{:S(2)}) %collective-permute-start.19) | collective-permute-done | bytes 131104 | tf_op jit(solution)/shard_map/ppermute | solution.py:33
  81.2 10.2 %all_to_all.11.qkv_ref = bf16[16,4,320]{2,1,0:T(4,128)(2,1)S(1)} all-to-all(bf16[16,4,320]{2,1,0:T(4,128)(2,1)S(1)} %project.19), channel_id=1, replica_groups=mesh['segment'=2,'slot'=16] {'slot'}, dimensions={0} | all-to-all | bytes 81920 | tf_op jit(solution)/shard_map/all_to_all | solution.py:381
  91.4 1.2 %attend.3 = bf16[1,4,4096]{2,1,0:T(4,128)(2,1)S(1)} custom-call(s32[1]{0:T(128)} %bitcast.own_ref, s32[2,4]{1,0:T(2,128)S(1)} %bitcast.48, bf16[16,4,320]{2,1,0:T(4,128)(2,1)S(1)} %all_to_all.11.qkv_ref, bf16[2,4,16,1024]{3,2,1,0:T(8,128)(2,1)S(1)} %bitcast.35, bf16[128,1280]{1,0:T(8,128)(2,1)S(1)} %bitcast.33, s32[16,16]{1,0:T(8,128)S(1)} %bitcast.42, ...), custom_call_target="tpu_custom_call" | custom-call | tf_op jit(solution)/shard_map/attend/pallas_call | solution.py:287
  93.0 4.5 %collective-permute-done.25 = bf16[1,4,4096]{2,1,0:T(4,128)(2,1)S(1)} collective-permute-done((bf16[1,4,4096]{2,1,0:T(4,128)(2,1)S(1)}, bf16[1,4,4096]{2,1,0:T(4,128)(2,1)S(1)}, u32[]{:S(2)}, u32[]{:S(2)}) %collective-permute-start.25) | collective-permute-done | bytes 32800 | tf_op jit(solution)/shard_map/ppermute | solution.py:33
  98.5 3.4 %collective-permute-done.26.refs_1_ = bf16[2,4,4096]{2,1,0:T(4,128)(2,1)S(1)} collective-permute-done((bf16[2,4,4096]{2,1,0:T(4,128)(2,1)S(1)}, bf16[2,4,4096]{2,1,0:T(4,128)(2,1)S(1)}, u32[]{:S(2)}, u32[]{:S(2)}) %collective-permute-start.26) | collective-permute-done | bytes 65568 | tf_op jit(solution)/shard_map/ppermute | solution.py:33
  103.0 3.2 %collective-permute-done.28.refs_3_ = bf16[2,4,4096]{2,1,0:T(4,128)(2,1)S(1)} collective-permute-done((bf16[2,4,4096]{2,1,0:T(4,128)(2,1)S(1)}, bf16[2,4,4096]{2,1,0:T(4,128)(2,1)S(1)}, u32[]{:S(2)}, u32[]{:S(2)}) %collective-permute-start.28) | collective-permute-done | bytes 65568 | tf_op jit(solution)/shard_map/ppermute | solution.py:33
  106.2 1.2 %collective-permute-done.32.refs_7_ = bf16[2,4,4096]{2,1,0:T(4,128)(2,1)S(1)} collective-permute-done((bf16[2,4,4096]{2,1,0:T(4,128)(2,1)S(1)}, bf16[2,4,4096]{2,1,0:T(4,128)(2,1)S(1)}, u32[]{:S(2)}, u32[]{:S(2)}) %collective-permute-start.32) | collective-permute-done | bytes 65568 | tf_op jit(solution)/shard_map/ppermute | solution.py:33
  109.0 3.8 %collective-permute-done.33 = bf16[64,512]{1,0:T(8,128)(2,1)S(1)} collective-permute-done((bf16[64,512]{1,0:T(8,128)(2,1)S(1)}, bf16[64,512]{1,0:T(8,128)(2,1)S(1)}, u32[]{:S(2)}, u32[]{:S(2)}) %collective-permute-start.33) | collective-permute-done | bytes 65568 | tf_op jit(solution)/shard_map/ppermute | solution.py:49
  (87 shorter events, 19.8 us)
Async XLA Ops:
  1.0 8.3 %collective-permute-start = (bf16[1,80,512]{2,1,0:T(8,128)(2,1)S(1)}, bf16[1,80,512]{2,1,0:T(8,128)(2,1)S(1)}, u32[]{:S(2)}, u32[]{:S(2)}) collective-permute-start(bf16[1,80,512]{2,1,0:T(8,128)(2,1)S(1)} %maximum_bitcast_fusion), channel_id=1, source_target_pairs={{0,8},{1,9},{2,10},{3,11},{4,12},{5,13},{6,14},{7,15},{8,0},{9,1},... | collective-permute-start | bytes 245768 | tf_op jit(solution)/shard_map/ppermute | solution.py:33
  9.3 5.4 %collective-permute-start.1 = (bf16[2,80,512]{2,1,0:T(8,128)(2,1)S(1)}, bf16[2,80,512]{2,1,0:T(8,128)(2,1)S(1)}, u32[]{:S(2)}, u32[]{:S(2)}) collective-permute-start(bf16[2,80,512]{2,1,0:T(8,128)(2,1)S(1)} %pad_maximum_fusion.refs_0_), channel_id=1, source_target_pairs={{0,4},{1,5},{2,6},{3,7},{4,0},{5,1},{6,2},{7,3},{8,12},{9,13},{10,... | collective-permute-start | bytes 491528 | tf_op jit(solution)/shard_map/ppermute | solution.py:33
  10.1 6.3 %collective-permute-start.3 = (bf16[2,80,512]{2,1,0:T(8,128)(2,1)S(1)}, bf16[2,80,512]{2,1,0:T(8,128)(2,1)S(1)}, u32[]{:S(2)}, u32[]{:S(2)}) collective-permute-start(bf16[2,80,512]{2,1,0:T(8,128)(2,1)S(1)} %pad_maximum_fusion.refs_0_), channel_id=1, source_target_pairs={{0,2},{1,3},{2,0},{3,1},{4,6},{5,7},{6,4},{7,5},{8,10},{9,11},{10,... | collective-permute-start | bytes 491528 | tf_op jit(solution)/shard_map/ppermute | solution.py:33
  11.6 5.7 %collective-permute-start.6 = (bf16[2,80,512]{2,1,0:T(8,128)(2,1)S(1)}, bf16[2,80,512]{2,1,0:T(8,128)(2,1)S(1)}, u32[]{:S(2)}, u32[]{:S(2)}) collective-permute-start(bf16[2,80,512]{2,1,0:T(8,128)(2,1)S(1)} %pad_maximum_fusion.refs_0_), channel_id=1, source_target_pairs={{0,1},{1,0},{2,3},{3,2},{4,5},{5,4},{6,7},{7,6},{8,9},{9,8},{10,11... | collective-permute-start | bytes 491528 | tf_op jit(solution)/shard_map/ppermute | solution.py:33
  14.7 6.1 %collective-permute-start.5 = (bf16[2,80,512]{2,1,0:T(8,128)(2,1)S(1)}, bf16[2,80,512]{2,1,0:T(8,128)(2,1)S(1)}, u32[]{:S(2)}, u32[]{:S(2)}) collective-permute-start(bf16[2,80,512]{2,1,0:T(8,128)(2,1)S(1)} %collective-permute-done.1.refs_0_), channel_id=1, source_target_pairs={{0,1},{1,0},{2,3},{3,2},{4,5},{5,4},{6,7},{7,6},{8,9},{9,8},{10,11... | collective-permute-start | bytes 491528 | tf_op jit(solution)/shard_map/ppermute | solution.py:33
  14.7 8.3 %collective-permute-start.2 = (bf16[2,80,512]{2,1,0:T(8,128)(2,1)S(1)}, bf16[2,80,512]{2,1,0:T(8,128)(2,1)S(1)}, u32[]{:S(2)}, u32[]{:S(2)}) collective-permute-start(bf16[2,80,512]{2,1,0:T(8,128)(2,1)S(1)} %collective-permute-done.1.refs_0_), channel_id=1, source_target_pairs={{0,2},{1,3},{2,0},{3,1},{4,6},{5,7},{6,4},{7,5},{8,10},{9,11},{10,... | collective-permute-start | bytes 491528 | tf_op jit(solution)/shard_map/ppermute | solution.py:33
  16.4 5.5 %collective-permute-start.4 = (bf16[2,80,512]{2,1,0:T(8,128)(2,1)S(1)}, bf16[2,80,512]{2,1,0:T(8,128)(2,1)S(1)}, u32[]{:S(2)}, u32[]{:S(2)}) collective-permute-start(bf16[2,80,512]{2,1,0:T(8,128)(2,1)S(1)} %collective-permute-done.3.refs_0_), channel_id=1, source_target_pairs={{0,1},{1,0},{2,3},{3,2},{4,5},{5,4},{6,7},{7,6},{8,9},{9,8},{10,11... | collective-permute-start | bytes 491528 | tf_op jit(solution)/shard_map/ppermute | solution.py:33
  23.1 1.5 %collective-permute-start.7 = (bf16[2,80,512]{2,1,0:T(8,128)(2,1)S(1)}, bf16[2,80,512]{2,1,0:T(8,128)(2,1)S(1)}, u32[]{:S(2)}, u32[]{:S(2)}) collective-permute-start(bf16[2,80,512]{2,1,0:T(8,128)(2,1)S(1)} %collective-permute-done.2.refs_0_), channel_id=1, source_target_pairs={{0,1},{1,0},{2,3},{3,2},{4,5},{5,4},{6,7},{7,6},{8,9},{9,8},{10,11... | collective-permute-start | bytes 491528 | tf_op jit(solution)/shard_map/ppermute | solution.py:33
  43.3 5.1 %collective-permute-start.8 = (bf16[1,4,4096]{2,1,0:T(4,128)(2,1)S(1)}, bf16[1,4,4096]{2,1,0:T(4,128)(2,1)S(1)}, u32[]{:S(2)}, u32[]{:S(2)}) collective-permute-start(bf16[1,4,4096]{2,1,0:T(4,128)(2,1)S(1)} %attend.2), channel_id=1, source_target_pairs={{0,8},{1,9},{2,10},{3,11},{4,12},{5,13},{6,14},{7,15},{8,0},{9,1},... | collective-permute-start | bytes 98312 | tf_op jit(solution)/shard_map/ppermute | solution.py:33
  48.4 4.3 %collective-permute-start.9 = (bf16[2,4,4096]{2,1,0:T(4,128)(2,1)S(1)}, bf16[2,4,4096]{2,1,0:T(4,128)(2,1)S(1)}, u32[]{:S(2)}, u32[]{:S(2)}) collective-permute-start(bf16[2,4,4096]{2,1,0:T(4,128)(2,1)S(1)} %pad_maximum_fusion.2.refs_0_), channel_id=1, source_target_pairs={{0,4},{1,5},{2,6},{3,7},{4,0},{5,1},{6,2},{7,3},{8,12},{9,13},{10,... | collective-permute-start | bytes 196616 | tf_op jit(solution)/shard_map/ppermute | solution.py:33
  48.7 4.9 %collective-permute-start.10 = (bf16[2,4,4096]{2,1,0:T(4,128)(2,1)S(1)}, bf16[2,4,4096]{2,1,0:T(4,128)(2,1)S(1)}, u32[]{:S(2)}, u32[]{:S(2)}) collective-permute-start(bf16[2,4,4096]{2,1,0:T(4,128)(2,1)S(1)} %pad_maximum_fusion.2.refs_0_), channel_id=1, source_target_pairs={{0,2},{1,3},{2,0},{3,1},{4,6},{5,7},{6,4},{7,5},{8,10},{9,11},{10,... | collective-permute-start | bytes 196616 | tf_op jit(solution)/shard_map/ppermute | solution.py:33
  52.8 4.3 %collective-permute-start.11 = (bf16[2,4,4096]{2,1,0:T(4,128)(2,1)S(1)}, bf16[2,4,4096]{2,1,0:T(4,128)(2,1)S(1)}, u32[]{:S(2)}, u32[]{:S(2)}) collective-permute-start(bf16[2,4,4096]{2,1,0:T(4,128)(2,1)S(1)} %collective-permute-done.9.refs_1_), channel_id=1, source_target_pairs={{0,2},{1,3},{2,0},{3,1},{4,6},{5,7},{6,4},{7,5},{8,10},{9,11},{10,... | collective-permute-start | bytes 196616 | tf_op jit(solution)/shard_map/ppermute | solution.py:33
  53.1 3.9 %collective-permute-start.12 = (bf16[2,4,4096]{2,1,0:T(4,128)(2,1)S(1)}, bf16[2,4,4096]{2,1,0:T(4,128)(2,1)S(1)}, u32[]{:S(2)}, u32[]{:S(2)}) collective-permute-start(bf16[2,4,4096]{2,1,0:T(4,128)(2,1)S(1)} %pad_maximum_fusion.2.refs_0_), channel_id=1, source_target_pairs={{0,1},{1,0},{2,3},{3,2},{4,5},{5,4},{6,7},{7,6},{8,9},{9,8},{10,11... | collective-permute-start | bytes 196616 | tf_op jit(solution)/shard_map/ppermute | solution.py:33
  53.1 3.9 %collective-permute-start.13 = (bf16[2,4,4096]{2,1,0:T(4,128)(2,1)S(1)}, bf16[2,4,4096]{2,1,0:T(4,128)(2,1)S(1)}, u32[]{:S(2)}, u32[]{:S(2)}) collective-permute-start(bf16[2,4,4096]{2,1,0:T(4,128)(2,1)S(1)} %collective-permute-done.9.refs_1_), channel_id=1, source_target_pairs={{0,1},{1,0},{2,3},{3,2},{4,5},{5,4},{6,7},{7,6},{8,9},{9,8},{10,11... | collective-permute-start | bytes 196616 | tf_op jit(solution)/shard_map/ppermute | solution.py:33
  53.6 3.4 %collective-permute-start.14 = (bf16[2,4,4096]{2,1,0:T(4,128)(2,1)S(1)}, bf16[2,4,4096]{2,1,0:T(4,128)(2,1)S(1)}, u32[]{:S(2)}, u32[]{:S(2)}) collective-permute-start(bf16[2,4,4096]{2,1,0:T(4,128)(2,1)S(1)} %collective-permute-done.10.refs_2_), channel_id=1, source_target_pairs={{0,1},{1,0},{2,3},{3,2},{4,5},{5,4},{6,7},{7,6},{8,9},{9,8},{10,11... | collective-permute-start | bytes 196616 | tf_op jit(solution)/shard_map/ppermute | solution.py:33
  59.3 4.3 %collective-permute-start.16 = (bf16[64,512]{1,0:T(8,128)(2,1)S(1)}, bf16[64,512]{1,0:T(8,128)(2,1)S(1)}, u32[]{:S(2)}, u32[]{:S(2)}) collective-permute-start(bf16[64,512]{1,0:T(8,128)(2,1)S(1)} %output.2), channel_id=1, source_target_pairs={{0,16},{1,17},{2,18},{3,19},{4,20},{5,21},{6,22},{7,23},{8,24},{9,... | collective-permute-start | bytes 196616 | tf_op jit(solution)/shard_map/ppermute | solution.py:49
  60.9 6.7 %collective-permute-start.17 = (bf16[64,512]{1,0:T(8,128)(2,1)S(1)}, bf16[64,512]{1,0:T(8,128)(2,1)S(1)}, u32[]{:S(2)}, u32[]{:S(2)}) collective-permute-start(bf16[64,512]{1,0:T(8,128)(2,1)S(1)} %output.2), channel_id=1, source_target_pairs={{0,24},{1,25},{2,26},{3,27},{4,28},{5,29},{6,30},{7,31},{8,16},{9,... | collective-permute-start | bytes 196616 | tf_op jit(solution)/shard_map/ppermute | solution.py:49
  67.7 5.2 %collective-permute-start.18 = (bf16[2,64,512]{2,1,0:T(8,128)(2,1)S(1)}, bf16[2,64,512]{2,1,0:T(8,128)(2,1)S(1)}, u32[]{:S(2)}, u32[]{:S(2)}) collective-permute-start(bf16[2,64,512]{2,1,0:T(8,128)(2,1)S(1)} %pad_maximum_fusion.1.refs_0_), channel_id=1, source_target_pairs={{0,4},{1,5},{2,6},{3,7},{4,0},{5,1},{6,2},{7,3},{8,12},{9,13},{10,... | collective-permute-start | bytes 393224 | tf_op jit(solution)/shard_map/ppermute | solution.py:33
  67.8 5.2 %collective-permute-start.20 = (bf16[2,64,512]{2,1,0:T(8,128)(2,1)S(1)}, bf16[2,64,512]{2,1,0:T(8,128)(2,1)S(1)}, u32[]{:S(2)}, u32[]{:S(2)}) collective-permute-start(bf16[2,64,512]{2,1,0:T(8,128)(2,1)S(1)} %pad_maximum_fusion.1.refs_0_), channel_id=1, source_target_pairs={{0,2},{1,3},{2,0},{3,1},{4,6},{5,7},{6,4},{7,5},{8,10},{9,11},{10,... | collective-permute-start | bytes 393224 | tf_op jit(solution)/shard_map/ppermute | solution.py:33
  68.5 5.4 %collective-permute-start.23 = (bf16[2,64,512]{2,1,0:T(8,128)(2,1)S(1)}, bf16[2,64,512]{2,1,0:T(8,128)(2,1)S(1)}, u32[]{:S(2)}, u32[]{:S(2)}) collective-permute-start(bf16[2,64,512]{2,1,0:T(8,128)(2,1)S(1)} %pad_maximum_fusion.1.refs_0_), channel_id=1, source_target_pairs={{0,1},{1,0},{2,3},{3,2},{4,5},{5,4},{6,7},{7,6},{8,9},{9,8},{10,11... | collective-permute-start | bytes 393224 | tf_op jit(solution)/shard_map/ppermute | solution.py:33
  72.9 2.1 %collective-permute-start.22 = (bf16[2,64,512]{2,1,0:T(8,128)(2,1)S(1)}, bf16[2,64,512]{2,1,0:T(8,128)(2,1)S(1)}, u32[]{:S(2)}, u32[]{:S(2)}) collective-permute-start(bf16[2,64,512]{2,1,0:T(8,128)(2,1)S(1)} %collective-permute-done.18.refs_0_), channel_id=1, source_target_pairs={{0,1},{1,0},{2,3},{3,2},{4,5},{5,4},{6,7},{7,6},{8,9},{9,8},{10,11... | collective-permute-start | bytes 393224 | tf_op jit(solution)/shard_map/ppermute | solution.py:33
  72.9 3.1 %collective-permute-start.21 = (bf16[2,64,512]{2,1,0:T(8,128)(2,1)S(1)}, bf16[2,64,512]{2,1,0:T(8,128)(2,1)S(1)}, u32[]{:S(2)}, u32[]{:S(2)}) collective-permute-start(bf16[2,64,512]{2,1,0:T(8,128)(2,1)S(1)} %collective-permute-done.20.refs_0_), channel_id=1, source_target_pairs={{0,1},{1,0},{2,3},{3,2},{4,5},{5,4},{6,7},{7,6},{8,9},{9,8},{10,11... | collective-permute-start | bytes 393224 | tf_op jit(solution)/shard_map/ppermute | solution.py:33
  73.4 5.5 %collective-permute-start.19 = (bf16[2,64,512]{2,1,0:T(8,128)(2,1)S(1)}, bf16[2,64,512]{2,1,0:T(8,128)(2,1)S(1)}, u32[]{:S(2)}, u32[]{:S(2)}) collective-permute-start(bf16[2,64,512]{2,1,0:T(8,128)(2,1)S(1)} %collective-permute-done.18.refs_0_), channel_id=1, source_target_pairs={{0,2},{1,3},{2,0},{3,1},{4,6},{5,7},{6,4},{7,5},{8,10},{9,11},{10,... | collective-permute-start | bytes 393224 | tf_op jit(solution)/shard_map/ppermute | solution.py:33
  78.8 1.3 %collective-permute-start.24 = (bf16[2,64,512]{2,1,0:T(8,128)(2,1)S(1)}, bf16[2,64,512]{2,1,0:T(8,128)(2,1)S(1)}, u32[]{:S(2)}, u32[]{:S(2)}) collective-permute-start(bf16[2,64,512]{2,1,0:T(8,128)(2,1)S(1)} %collective-permute-done.19.refs_0_), channel_id=1, source_target_pairs={{0,1},{1,0},{2,3},{3,2},{4,5},{5,4},{6,7},{7,6},{8,9},{9,8},{10,11... | collective-permute-start | bytes 393224 | tf_op jit(solution)/shard_map/ppermute | solution.py:33
  92.6 4.9 %collective-permute-start.25 = (bf16[1,4,4096]{2,1,0:T(4,128)(2,1)S(1)}, bf16[1,4,4096]{2,1,0:T(4,128)(2,1)S(1)}, u32[]{:S(2)}, u32[]{:S(2)}) collective-permute-start(bf16[1,4,4096]{2,1,0:T(4,128)(2,1)S(1)} %attend.3), channel_id=1, source_target_pairs={{0,8},{1,9},{2,10},{3,11},{4,12},{5,13},{6,14},{7,15},{8,0},{9,1},... | collective-permute-start | bytes 98312 | tf_op jit(solution)/shard_map/ppermute | solution.py:33
  97.5 4.3 %collective-permute-start.26 = (bf16[2,4,4096]{2,1,0:T(4,128)(2,1)S(1)}, bf16[2,4,4096]{2,1,0:T(4,128)(2,1)S(1)}, u32[]{:S(2)}, u32[]{:S(2)}) collective-permute-start(bf16[2,4,4096]{2,1,0:T(4,128)(2,1)S(1)} %pad_maximum_fusion.3.refs_0_), channel_id=1, source_target_pairs={{0,4},{1,5},{2,6},{3,7},{4,0},{5,1},{6,2},{7,3},{8,12},{9,13},{10,... | collective-permute-start | bytes 196616 | tf_op jit(solution)/shard_map/ppermute | solution.py:33
  97.8 5.1 %collective-permute-start.27 = (bf16[2,4,4096]{2,1,0:T(4,128)(2,1)S(1)}, bf16[2,4,4096]{2,1,0:T(4,128)(2,1)S(1)}, u32[]{:S(2)}, u32[]{:S(2)}) collective-permute-start(bf16[2,4,4096]{2,1,0:T(4,128)(2,1)S(1)} %pad_maximum_fusion.3.refs_0_), channel_id=1, source_target_pairs={{0,2},{1,3},{2,0},{3,1},{4,6},{5,7},{6,4},{7,5},{8,10},{9,11},{10,... | collective-permute-start | bytes 196616 | tf_op jit(solution)/shard_map/ppermute | solution.py:33
  101.9 4.3 %collective-permute-start.28 = (bf16[2,4,4096]{2,1,0:T(4,128)(2,1)S(1)}, bf16[2,4,4096]{2,1,0:T(4,128)(2,1)S(1)}, u32[]{:S(2)}, u32[]{:S(2)}) collective-permute-start(bf16[2,4,4096]{2,1,0:T(4,128)(2,1)S(1)} %collective-permute-done.26.refs_1_), channel_id=1, source_target_pairs={{0,2},{1,3},{2,0},{3,1},{4,6},{5,7},{6,4},{7,5},{8,10},{9,11},{10,... | collective-permute-start | bytes 196616 | tf_op jit(solution)/shard_map/ppermute | solution.py:33
  102.4 3.7 %collective-permute-start.29 = (bf16[2,4,4096]{2,1,0:T(4,128)(2,1)S(1)}, bf16[2,4,4096]{2,1,0:T(4,128)(2,1)S(1)}, u32[]{:S(2)}, u32[]{:S(2)}) collective-permute-start(bf16[2,4,4096]{2,1,0:T(4,128)(2,1)S(1)} %pad_maximum_fusion.3.refs_0_), channel_id=1, source_target_pairs={{0,1},{1,0},{2,3},{3,2},{4,5},{5,4},{6,7},{7,6},{8,9},{9,8},{10,11... | collective-permute-start | bytes 196616 | tf_op jit(solution)/shard_map/ppermute | solution.py:33
  102.4 3.7 %collective-permute-start.30 = (bf16[2,4,4096]{2,1,0:T(4,128)(2,1)S(1)}, bf16[2,4,4096]{2,1,0:T(4,128)(2,1)S(1)}, u32[]{:S(2)}, u32[]{:S(2)}) collective-permute-start(bf16[2,4,4096]{2,1,0:T(4,128)(2,1)S(1)} %collective-permute-done.26.refs_1_), channel_id=1, source_target_pairs={{0,1},{1,0},{2,3},{3,2},{4,5},{5,4},{6,7},{7,6},{8,9},{9,8},{10,11... | collective-permute-start | bytes 196616 | tf_op jit(solution)/shard_map/ppermute | solution.py:33
  103.0 3.2 %collective-permute-start.31 = (bf16[2,4,4096]{2,1,0:T(4,128)(2,1)S(1)}, bf16[2,4,4096]{2,1,0:T(4,128)(2,1)S(1)}, u32[]{:S(2)}, u32[]{:S(2)}) collective-permute-start(bf16[2,4,4096]{2,1,0:T(4,128)(2,1)S(1)} %collective-permute-done.27.refs_2_), channel_id=1, source_target_pairs={{0,1},{1,0},{2,3},{3,2},{4,5},{5,4},{6,7},{7,6},{8,9},{9,8},{10,11... | collective-permute-start | bytes 196616 | tf_op jit(solution)/shard_map/ppermute | solution.py:33
  108.4 4.3 %collective-permute-start.33 = (bf16[64,512]{1,0:T(8,128)(2,1)S(1)}, bf16[64,512]{1,0:T(8,128)(2,1)S(1)}, u32[]{:S(2)}, u32[]{:S(2)}) collective-permute-start(bf16[64,512]{1,0:T(8,128)(2,1)S(1)} %output.3), channel_id=1, source_target_pairs={{0,16},{1,17},{2,18},{3,19},{4,20},{5,21},{6,22},{7,23},{8,24},{9,... | collective-permute-start | bytes 196616 | tf_op jit(solution)/shard_map/ppermute | solution.py:49
  (14 other events, 272.3 us)

commit v5 on v4

--- a/solution.py
+++ b/solution.py
@@ -2,7 +2,6 @@
 
 import jax
 import jax.numpy as jnp
-import numpy as np
 from jax import lax
 from jax.experimental import pallas as pl
 from jax.experimental.pallas import tpu as pltpu
@@ -42,6 +41,18 @@
     return groups + [exchange(group, core) for group in groups]
 
 
+def gather(block, phases):
+    held = [([0], block)]
+    for phase in phases:
+        merged = block if len(held) == 1 else jnp.concatenate([b for _, b in held], axis=0)
+        names = [m for n, _ in held for m in n]
+        if phase == phases[-1] and len(phase) == 1:
+            return held + [([phase[0] ^ m for m in n], exchange(b, phase[0])) for n, b in held]
+        if len(held) > 1:
+            held = [(names, merged)]
+        held = held + [([m ^ n for n in names], exchange(merged, m)) for m in phase]
+
+
 def next_segment(block, mask=0):
     n, slots = lax.axis_size("segment"), lax.axis_size("slot")
     route = [(s * slots + i, (s + 1) % n * slots + (i ^ mask)) for s in range(n)
@@ -62,48 +73,48 @@
     return ((to_slot == from_slot) & (to_row == from_row)).astype(jnp.bfloat16)
 
 
-def arrival_rows(own, slots, batch):
+def arrival_rows(own, slots, batch, arrivals):
     rows = slots * batch
     to_slot, to_row = split_rows(iota((rows, rows), 0), slots, batch, False)
     arrival, from_row = split_rows(iota((rows, rows), 1), slots, batch, True)
-    away = to_slot ^ own
-    bits = slots.bit_length() - 1
-    place = jnp.zeros_like(away)
-    for k in range(bits):
-        place = place | (((away >> k) & 1) << (bits - 1 - k))
-    return ((place == arrival) & (to_row == from_row)).astype(jnp.bfloat16)
+    from_slot = jnp.zeros_like(arrival)
+    for place, mask in enumerate(arrivals):
+        from_slot = jnp.where(arrival == place, mask, from_slot)
+    return ((to_slot == (from_slot ^ own)) & (to_row == from_row)).astype(jnp.bfloat16)
 
 
 def room_for(columns):
     return -(-(columns // 2) // LANES) * LANES
 
 
-def pack_kernel(own_ref, dest_ref, pages_ref, send_ref):
+def pack_kernel(dest_ref, pages_ref, send_ref):
+    own = lax.axis_index("slot")
     slots, page_tok, wide = send_ref.shape
     kv_width = pages_ref.shape[2]
     for p in range(pages_ref.shape[0]):
-        send_ref[dest_ref[own_ref[0], p], :, :kv_width] = pages_ref[p]
+        send_ref[dest_ref[own, p], :, :kv_width] = pages_ref[p]
     for j in range(slots):
         send_ref[j, :, kv_width:] = jnp.zeros((page_tok, wide - kv_width), send_ref.dtype)
 
 
-def pack(own, pages, dest, room):
+def pack(pages, dest, room):
     _, page_tok, kv_width = pages.shape
     whole = pl.BlockSpec(memory_space=pltpu.VMEM)
     scalars = pl.BlockSpec(memory_space=pltpu.SMEM)
     return pl.pallas_call(
         pack_kernel,
         out_shape=jax.ShapeDtypeStruct((dest.shape[0], page_tok, kv_width + room), pages.dtype),
-        in_specs=[scalars, scalars, whole],
+        in_specs=[scalars, whole],
         out_specs=whole,
         compiler_params=params(),
         name="pack",
-    )(own, dest, pages)
-
-
-def project_kernel(order_ref, w_ref, *refs, starts, rows, carried, first, last, packed, batch):
+    )(dest, pages)
+
+
+def project_kernel(w_ref, *refs, away, rows, carried, first, last, packed, batch):
     refs = list(refs)
-    x_refs = [refs.pop(0) for _ in starts]
+    own = lax.axis_index("slot")
+    x_refs = [refs.pop(0) for _ in away]
     kept = None if carried else refs.pop(0)
     acc_in, square_in = (None, None) if first else (refs.pop(0), refs.pop(0))
     if packed:
@@ -114,7 +125,7 @@
     columns, model_width = w_ref.shape
     acc = jnp.zeros((rows, columns), jnp.float32) if first else acc_in[...]
     square = jnp.zeros((rows, LANES), jnp.float32) if first else square_in[...]
-    for g, start in enumerate(starts):
+    for g, masks in enumerate(away):
         for i in range(blocks):
             if carried:
                 kept[g * blocks + i] = x_refs[g][i, rows:]
@@ -126,7 +137,7 @@
                 square = square + part * part
                 parts.append((part * gain[:, r:r + LANES]).astype(jnp.bfloat16))
             x = parts[0] if len(parts) == 1 else jnp.concatenate(parts, axis=1)
-            here = pl.ds(pl.multiple_of(order_ref[start + i] * width, width), width)
+            here = pl.ds(pl.multiple_of((own ^ masks[i]) * width, width), width)
             acc = acc + lax.dot_general(x, w_ref[:, here], (((1,), (1,)), ((), ())),
                                         preferred_element_type=jnp.float32)
     if not last:
@@ -148,7 +159,7 @@
             refs[0][j] = mine.astype(jnp.bfloat16)
 
 
-def project(order, rows, batch, weight, groups, gains, state, last=False, outgoing=None):
+def project(rows, batch, weight, groups, gains, state, last=False, outgoing=None):
     blocks, held, width = groups[0][1].shape
     columns = weight.shape[0]
     carried, first, packed = gains is None, state is None, outgoing is not None
@@ -160,7 +171,7 @@
         out_shape.append(jax.ShapeDtypeStruct((len(groups) * blocks, held - rows, width),
                                               jnp.bfloat16))
     if packed:
-        aliases = {len(operands) + 1: len(out_shape)}
+        aliases = {len(operands): len(out_shape)}
         operands.append(outgoing)
         out_shape.append(jax.ShapeDtypeStruct(outgoing.shape, outgoing.dtype))
     elif last:
@@ -171,17 +182,17 @@
     whole = pl.BlockSpec(memory_space=pltpu.VMEM)
     work = rows * width * columns * blocks * len(groups)
     out = pl.pallas_call(
-        functools.partial(project_kernel, starts=[g * blocks for g, _ in groups], rows=rows,
+        functools.partial(project_kernel, away=[masks for masks, _ in groups], rows=rows,
                           carried=carried, first=first, last=last, packed=packed, batch=batch),
         out_shape=out_shape,
-        in_specs=[pl.BlockSpec(memory_space=pltpu.SMEM)] + [whole] * len(operands),
+        in_specs=[whole] * len(operands),
         out_specs=[whole] * len(out_shape),
         input_output_aliases=aliases,
         compiler_params=params(),
         cost_estimate=pl.CostEstimate(flops=8 * work, bytes_accessed=2 * work // rows,
                                       transcendentals=0),
         name="project",
-    )(order, *operands)
+    )(*operands)
     if carried:
         gains, *out = out
     return gains, (out[0] if last else out)
@@ -204,19 +215,19 @@
     return jnp.where(live, to_tokens(row_ref[...]), -1.0).astype(jnp.int32)
 
 
-def attend_kernel(own_ref, len_ref, qkv_ref, cache_ref, pages_ref, dest_ref, page_row_ref, count_ref,
+def attend_kernel(len_ref, qkv_ref, cache_ref, pages_ref, dest_ref, page_row_ref, count_ref,
                   out_ref, *, visit, columns, packed):
     slots = qkv_ref.shape[0]
     batch, positions = cache_ref.shape[1:3]
     tokens = pages_ref.shape[0]
     pieces = []
     for j in range(slots):
-        piece = qkv_ref[j].astype(jnp.float32)
         if packed:
             half = columns // 2
+            piece = qkv_ref[j, :, qkv_ref.shape[2] - room_for(columns):].astype(jnp.float32)
             pieces += [piece[:batch, :half], piece[batch:2 * batch, :half]]
         else:
-            pieces.append(piece)
+            pieces.append(qkv_ref[j].astype(jnp.float32))
     full = jnp.concatenate(pieces, axis=1)
     group_rows = GROUP * batch
     near = batch * positions
@@ -236,7 +247,7 @@
             fresh = full[:, fresh_lo:fresh_lo + HEAD_SIZE]
             fresh = jnp.concatenate(
                 [fresh, jnp.zeros((near_pad - near - batch, HEAD_SIZE), jnp.float32)], axis=0)
-            old = [cache_ref[0, b, :, cache_lo:cache_lo + HEAD_SIZE] for b in range(batch)]
+            old = [cache_ref[visit, b, :, cache_lo:cache_lo + HEAD_SIZE] for b in range(batch)]
             return jnp.concatenate(old + [fresh.astype(jnp.bfloat16)], axis=0)
 
         keys = nearby(lo, key_at + lo)
@@ -248,13 +259,13 @@
     far = jnp.concatenate(far_scores, axis=0) * scale
     close = jnp.concatenate(near_scores, axis=0) * scale
     far_row = lax.rem(iota((rows, tokens), 0), batch)
-    code = token_rows(own_ref[0], dest_ref, page_row_ref, count_ref, tokens // slots)
+    code = token_rows(lax.axis_index("slot"), dest_ref, page_row_ref, count_ref, tokens // slots)
     far = jnp.where(code == far_row + visit * batch, far, -1e30)
     row = lax.rem(iota((rows, near_pad), 0), batch)
     lane = iota((rows, near_pad), 1)
     lengths = jnp.zeros((rows, near_pad), jnp.int32)
     for b in range(batch):
-        lengths = jnp.where(row == b, len_ref[visit, b], lengths)
+        lengths = jnp.where(row == b, len_ref[visit:visit + 1, b:b + 1], lengths)
     position = lane - row * positions
     seen = (position >= 0) & (position < lengths) | (lane == near + row)
     close = jnp.where(seen, close, -1e30)
@@ -277,31 +288,22 @@
                 jnp.bfloat16)
 
 
-def attend(own, lengths, qkv, columns, cache, pages, arrivals, visit):
-    packed = qkv.ndim == 3 and qkv.shape[2] != columns
-    slots = qkv.shape[0]
-    _, batch, positions, kv_width = cache.shape
-    tokens = pages.shape[0]
-    scalars = pl.BlockSpec(memory_space=pltpu.SMEM)
-    fixed = lambda *shape: pl.BlockSpec(shape, lambda s: (0,) * len(shape))
+def attend(lengths, qkv, columns, cache, pages, arrivals, visit):
+    batch = cache.shape[1]
+    whole = pl.BlockSpec(memory_space=pltpu.VMEM)
+    operands = [lengths, qkv, cache, pages, *arrivals]
     return pl.pallas_call(
-        functools.partial(attend_kernel, visit=visit, columns=columns, packed=packed),
+        functools.partial(attend_kernel, visit=visit, columns=columns,
+                          packed=qkv.shape[2] != columns),
         out_shape=jax.ShapeDtypeStruct((1, batch, QUERY_HEADS * HEAD_SIZE), jnp.bfloat16),
-        grid=(1,),
-        in_specs=[
-            scalars, scalars,
-            pl.BlockSpec((slots, qkv.shape[1], room_for(columns)),
-                         lambda s: (0, 0, kv_width // room_for(columns))) if packed
-            else fixed(*qkv.shape),
-            pl.BlockSpec((1, batch, positions, kv_width), lambda s: (visit, 0, 0, 0)),
-            fixed(tokens, kv_width)] + [fixed(*v.shape) for v in arrivals],
-        out_specs=fixed(1, batch, QUERY_HEADS * HEAD_SIZE),
+        in_specs=[whole] * len(operands),
+        out_specs=whole,
         compiler_params=params(),
         name="attend",
-    )(own, lengths, qkv, cache, pages, *arrivals)
-
-
-def output_kernel(own_ref, *refs, slots, batch):
+    )(*operands)
+
+
+def output_kernel(*refs, slots, batch, arrivals):
     pieces, (w_ref, now_ref, out_ref) = refs[:-3], refs[-3:]
     features = w_ref.shape[0]
     depth = features // 4
@@ -312,7 +314,7 @@
              for piece in pieces for i in range(piece.shape[0])], axis=0)
         acc = acc + jnp.dot(left.astype(jnp.bfloat16), w_ref[k:k + depth],
                             preferred_element_type=jnp.float32)
-    move = arrival_rows(own_ref[0], slots, batch)
+    move = arrival_rows(lax.axis_index("slot"), slots, batch, arrivals)
     moved = None
     for _ in range(3):
         part = acc.astype(jnp.bfloat16)
@@ -322,17 +324,19 @@
     out_ref[...] = (now_ref[...].astype(jnp.float32) + moved).astype(jnp.bfloat16)
 
 
-def output(own, pieces, weight, now, slots):
+def output(groups, weight, now, slots):
+    arrivals = [m for n, _ in groups for m in n]
+    pieces = [b for _, b in groups]
     batch = pieces[0].shape[1]
     whole = pl.BlockSpec(memory_space=pltpu.VMEM)
     return pl.pallas_call(
-        functools.partial(output_kernel, slots=slots, batch=batch),
+        functools.partial(output_kernel, slots=slots, batch=batch, arrivals=arrivals),
         out_shape=jax.ShapeDtypeStruct(now.shape, jnp.bfloat16),
-        in_specs=[pl.BlockSpec(memory_space=pltpu.SMEM)] + [whole] * (len(pieces) + 2),
+        in_specs=[whole] * (len(pieces) + 2),
         out_specs=whole,
         compiler_params=params(),
         name="output",
-    )(own, *pieces, weight, now)
+    )(*pieces, weight, now)
 
 
 def shards(hidden_rows, norm_gain, qkv_weight, out_weight, cache_kv, cache_len, page_kv,
@@ -342,17 +346,16 @@
     rows = batch * slots
     width = hidden_rows.shape[3]
     kv_width = cache_kv.shape[5]
-    own = lax.axis_index("slot").astype(jnp.int32)
     masks = [slots >> (k + 1) for k in range(slots.bit_length() - 1)]
-    offsets = [0]
-    for mask in masks:
+    across, over, core = masks[-3:]
+    phases = [[mask] for mask in masks[:-3]] + [[across ^ over, over, across], [core]]
+    offsets = [masks[0], 0]
+    for mask in masks[1:]:
         offsets = offsets + [mask ^ o for o in offsets]
-    order = own ^ jnp.asarray(np.array(offsets, np.int32))
     cache = cache_kv[0, :, :, 0]
     lengths = cache_len[0, :, :, 0]
     weight_in = qkv_weight[0].T
     weight_out = out_weight[0]
-    own = own.reshape(1)
     current = hidden_rows.reshape(rows, width)
     columns = weight_in.shape[0]
     arrivals = (page_dest[0], page_row[0], page_count[0])
@@ -361,31 +364,31 @@
         if visit == 0:
             spare = jnp.zeros((15, width), norm_gain.dtype)
             block = jnp.concatenate([current, norm_gain, spare], axis=0)[None]
-            block = jnp.concatenate([block, exchange(block, masks[0])], axis=0)
-            outgoing = pack(own, page_kv[0, 0], page_dest[0], room_for(columns))
+            block = jnp.concatenate([exchange(block, masks[0]), block], axis=0)
+            outgoing = pack(page_kv[0, 0], page_dest[0], room_for(columns))
             block, outgoing = lax.optimization_barrier((block, outgoing))
         else:
-            block = jnp.stack([current, beyond])
+            block = jnp.stack([beyond, current])
         for mask in masks[1:-3]:
             block = jnp.concatenate([block, exchange(block, mask)], axis=0)
-        run = functools.partial(project, order, rows, batch, weight_in)
+        size = slots // 8
+        away = [offsets[g * size:(g + 1) * size] for g in range(8)]
+        run = functools.partial(project, rows, batch, weight_in)
         state = None
         groups = spread(block, masks[-3:])
         for k, names in enumerate([(0, 4), (1, 5), (2, 6)]):
-            gains[k], state = run([(g, groups[g]) for g in names], gains[k], state)
+            gains[k], state = run([(away[g], groups[g]) for g in names], gains[k], state)
         groups[3], state = lax.optimization_barrier((groups[3], state))
         groups[7] = exchange(groups[3], masks[-1])
-        gains[3], state = run([(3, groups[3])], gains[3], state)
-        gains[4], qkv = run([(7, groups[7])], gains[4], state, last=True,
+        gains[3], state = run([(away[3], groups[3])], gains[3], state)
+        gains[4], qkv = run([(away[7], groups[7])], gains[4], state, last=True,
                              outgoing=None if visit else outgoing)
         qkv = lax.all_to_all(qkv, "slot", split_axis=0, concat_axis=0, tiled=True)
         if visit == 0:
             pages = qkv.reshape(-1, qkv.shape[2])
-        context = attend(own, lengths, qkv, columns, cache, pages, arrivals, visit)
-        for mask in masks[:-3]:
-            context = jnp.concatenate([context, exchange(context, mask)], axis=0)
-        groups = spread(context, masks[-3:])
-        updated = output(own, groups, weight_out, current, slots)
+        context = attend(lengths, qkv, columns, cache, pages, arrivals, visit)
+        groups = gather(context, phases)
+        updated = output(groups, weight_out, current, slots)
         current = next_segment(updated)
         if visit < CYCLE_STEPS - 1:
             beyond = next_segment(updated, masks[0])

time: 114 us -> 107 us (0.939)
  Pallas kernels: 15.4 us -> 8.9 us
  starting transfers between devices: 19.8 us -> 24.2 us
  waiting for transfers between devices: 44.7 us -> 40.4 us
    pallas_call x12, Pallas kernels: 12.3 us -> 6.88 us  [the longest x10 4.84 us: project(): pl.pallas_call(functools.partial(project_kernel, away=[masks for masks, _...]
    ppermute x31, starting transfers between devices: 16.5 us -> 20.2 us  [exchange(): return lax.ppermute(block, 'slot', [(i, i ^ mask) for i in range(n)])]
    ppermute x31, waiting for transfers between devices: 35.4 us -> 32.5 us  [exchange(): return lax.ppermute(block, 'slot', [(i, i ^ mask) for i in range(n)])]
    ppermute x3, waiting for transfers between devices: 9.34 us -> 7.9 us  [next_segment(): return lax.ppermute(block, ('segment', 'slot'), route)]
  transfers between devices with their start and end apart: 34 -> 34, of which waited for: 18 -> 24; matrix products, arithmetic and copies ran while one was open for 1% -> 0% of each run, Pallas kernels for 8% -> 4%
where the time goes in v5:
time: 107 us; the launch traced here: 106 us
  waiting for transfers between devices  40.4 us (38%)
  blocking collectives  26.5 us (25%)
  starting transfers between devices  24.2 us (23%)
  Pallas kernels  8.9 us (8%)
  local copies, waits for them, and re-layouts  4.89 us (5%)
    ppermute x31, waiting for transfers between devices, exchange(): return lax.ppermute(block, 'slot', [(i, i ^ mask) for i in range(n)])  32.5 us
    all_to_all x2, blocking collectives, shards(): qkv = lax.all_to_all(qkv, 'slot', split_axis=0, concat_axis=0, tiled=True)  26.5 us
    ppermute x31, starting transfers between devices, exchange(): return lax.ppermute(block, 'slot', [(i, i ^ mask) for i in range(n)])  20.2 us
    ppermute x3, waiting for transfers between devices, next_segment(): return lax.ppermute(block, ('segment', 'slot'), route)  7.9 us
    pallas_call x10, Pallas kernels, project(): pl.pallas_call(functools.partial(project_kernel, away=[masks for masks, _...  4.84 us
    unnamed x25, local copies, waits for them, and re-layouts  4.81 us
    ppermute x3, starting transfers between devices, next_segment(): return lax.ppermute(block, ('segment', 'slot'), route)  3.97 us
  transfers between devices with their start and end apart: 34, of which 24 were waited for; matrix products, arithmetic and copies ran while one was open for 0% of the time, Pallas kernels for 4%

profile of v5, /device:TPU:0, one launch (start us, length us, event | category | flops | bytes accessed | tf_op | source)
XLA Modules:
  0.0 106.3 jit_solution(4937697970616709979)
XLA Ops:
  1.0 4.1 %collective-permute-start = (bf16[1,80,512]{2,1,0:T(8,128)(2,1)S(1)}, bf16[1,80,512]{2,1,0:T(8,128)(2,1)S(1)}, u32[]{:S(2)}, u32[]{:S(2)}) collective-permute-start(bf16[1,80,512]{2,1,0:T(8,128)(2,1)S(1)} %maximum_bitcast_fusion), channel_id=1, source_target_pairs={{0,8},{1,9},{2,10},{3,11},{4,12},{5,13},{6,14},{7,15},{8,0},{9,1},... | collective-permute-start | bytes 245768 | tf_op jit(solution)/shard_map/ppermute | solution.py:32
  5.1 0.9 copy-done.4
  7.5 1.8 %collective-permute-done = bf16[1,80,512]{2,1,0:T(8,128)(2,1)S(1)} collective-permute-done((bf16[1,80,512]{2,1,0:T(8,128)(2,1)S(1)}, bf16[1,80,512]{2,1,0:T(8,128)(2,1)S(1)}, u32[]{:S(2)}, u32[]{:S(2)}) %collective-permute-start) | collective-permute-done | bytes 81952 | tf_op jit(solution)/shard_map/ppermute | solution.py:32
  10.1 1.5 %collective-permute-start.3 = (bf16[2,80,512]{2,1,0:T(8,128)(2,1)S(1)}, bf16[2,80,512]{2,1,0:T(8,128)(2,1)S(1)}, u32[]{:S(2)}, u32[]{:S(2)}) collective-permute-start(bf16[2,80,512]{2,1,0:T(8,128)(2,1)S(1)} %pad_maximum_fusion.refs_0_), channel_id=1, source_target_pairs={{0,2},{1,3},{2,0},{3,1},{4,6},{5,7},{6,4},{7,5},{8,10},{9,11},{10,... | collective-permute-start | bytes 491528 | tf_op jit(solution)/shard_map/ppermute | solution.py:32
  11.6 3.1 %collective-permute-done.1.refs_0_ = bf16[2,80,512]{2,1,0:T(8,128)(2,1)S(1)} collective-permute-done((bf16[2,80,512]{2,1,0:T(8,128)(2,1)S(1)}, bf16[2,80,512]{2,1,0:T(8,128)(2,1)S(1)}, u32[]{:S(2)}, u32[]{:S(2)}) %collective-permute-start.1) | collective-permute-done | bytes 163872 | tf_op jit(solution)/shard_map/ppermute | solution.py:32
  14.7 1.1 %collective-permute-done.3.refs_0_ = bf16[2,80,512]{2,1,0:T(8,128)(2,1)S(1)} collective-permute-done((bf16[2,80,512]{2,1,0:T(8,128)(2,1)S(1)}, bf16[2,80,512]{2,1,0:T(8,128)(2,1)S(1)}, u32[]{:S(2)}, u32[]{:S(2)}) %collective-permute-start.3) | collective-permute-done | bytes 163872 | tf_op jit(solution)/shard_map/ppermute | solution.py:32
  15.8 1.5 %collective-permute-start.2 = (bf16[2,80,512]{2,1,0:T(8,128)(2,1)S(1)}, bf16[2,80,512]{2,1,0:T(8,128)(2,1)S(1)}, u32[]{:S(2)}, u32[]{:S(2)}) collective-permute-start(bf16[2,80,512]{2,1,0:T(8,128)(2,1)S(1)} %collective-permute-done.1.refs_0_), channel_id=1, source_target_pairs={{0,2},{1,3},{2,0},{3,1},{4,6},{5,7},{6,4},{7,5},{8,10},{9,11},{10,... | collective-permute-start | bytes 491528 | tf_op jit(solution)/shard_map/ppermute | solution.py:32
  17.3 2.5 %copy-done = bf16[1,8192,320]{1,2,0:T(8,128)(2,1)S(1)} copy-done((bf16[1,8192,320]{1,2,0:T(8,128)(2,1)S(1)}, bf16[1,8192,320]{1,2,0:T(8,128)(2,1)}, u32[]{:S(2)}) %copy-start) | copy-done | bytes 5242904
  21.4 1.1 collective-permute-done.2.refs_0_
  22.9 1.0 collective-permute-done.7.refs_0_
  24.5 16.9 %all_to_all.10.qkv_ref = bf16[16,8,1280]{2,1,0:T(8,128)(2,1)S(1)} all-to-all(bf16[16,8,1280]{2,1,0:T(8,128)(2,1)S(1)} %get-tuple-element.48), channel_id=1, replica_groups=mesh['segment'=2,'slot'=16] {'slot'}, dimensions={0} | all-to-all | bytes 655360 | tf_op jit(solution)/shard_map/all_to_all | solution.py:386
  42.1 1.4 %collective-permute-start.8 = (bf16[1,4,4096]{2,1,0:T(4,128)(2,1)S(1)}, bf16[1,4,4096]{2,1,0:T(4,128)(2,1)S(1)}, u32[]{:S(2)}, u32[]{:S(2)}) collective-permute-start(bf16[1,4,4096]{2,1,0:T(4,128)(2,1)S(1)} %attend.2), channel_id=1, source_target_pairs={{0,8},{1,9},{2,10},{3,11},{4,12},{5,13},{6,14},{7,15},{8,0},{9,1},... | collective-permute-start | bytes 98312 | tf_op jit(solution)/shard_map/ppermute | solution.py:32
  43.5 3.6 %collective-permute-done.8 = bf16[1,4,4096]{2,1,0:T(4,128)(2,1)S(1)} collective-permute-done((bf16[1,4,4096]{2,1,0:T(4,128)(2,1)S(1)}, bf16[1,4,4096]{2,1,0:T(4,128)(2,1)S(1)}, u32[]{:S(2)}, u32[]{:S(2)}) %collective-permute-start.8) | collective-permute-done | bytes 32800 | tf_op jit(solution)/shard_map/ppermute | solution.py:32
  48.0 0.9 collective-permute-start.10
  48.9 1.8 %collective-permute-start.11 = (bf16[2,4,4096]{2,1,0:T(4,128)(2,1)S(1)}, bf16[2,4,4096]{2,1,0:T(4,128)(2,1)S(1)}, u32[]{:S(2)}, u32[]{:S(2)}) collective-permute-start(bf16[2,4,4096]{2,1,0:T(4,128)(2,1)S(1)} %pad_maximum_fusion.2.refs_0_), channel_id=1, source_target_pairs={{0,4},{1,5},{2,6},{3,7},{4,0},{5,1},{6,2},{7,3},{8,12},{9,13},{10,... | collective-permute-start | bytes 196616 | tf_op jit(solution)/shard_map/ppermute | solution.py:32
  50.7 1.8 %collective-permute-done.9.refs_1_ = bf16[2,4,4096]{2,1,0:T(4,128)(2,1)S(1)} collective-permute-done((bf16[2,4,4096]{2,1,0:T(4,128)(2,1)S(1)}, bf16[2,4,4096]{2,1,0:T(4,128)(2,1)S(1)}, u32[]{:S(2)}, u32[]{:S(2)}) %collective-permute-start.9) | collective-permute-done | bytes 65568 | tf_op jit(solution)/shard_map/ppermute | solution.py:32
  54.5 1.0 output.2
  55.5 2.5 %collective-permute-start.16 = (bf16[64,512]{1,0:T(8,128)(2,1)S(1)}, bf16[64,512]{1,0:T(8,128)(2,1)S(1)}, u32[]{:S(2)}, u32[]{:S(2)}) collective-permute-start(bf16[64,512]{1,0:T(8,128)(2,1)S(1)} %output.2), channel_id=1, source_target_pairs={{0,24},{1,25},{2,26},{3,27},{4,28},{5,29},{6,30},{7,31},{8,16},{9,... | collective-permute-start | bytes 196616 | tf_op jit(solution)/shard_map/ppermute | solution.py:60
  58.5 4.6 %collective-permute-done.16 = bf16[64,512]{1,0:T(8,128)(2,1)S(1)} collective-permute-done((bf16[64,512]{1,0:T(8,128)(2,1)S(1)}, bf16[64,512]{1,0:T(8,128)(2,1)S(1)}, u32[]{:S(2)}, u32[]{:S(2)}) %collective-permute-start.16) | collective-permute-done | bytes 65568 | tf_op jit(solution)/shard_map/ppermute | solution.py:60
  63.0 1.8 %collective-permute-start.18 = (bf16[2,64,512]{2,1,0:T(8,128)(2,1)S(1)}, bf16[2,64,512]{2,1,0:T(8,128)(2,1)S(1)}, u32[]{:S(2)}, u32[]{:S(2)}) collective-permute-start(bf16[2,64,512]{2,1,0:T(8,128)(2,1)S(1)} %pad_maximum_fusion.1.refs_0_), channel_id=1, source_target_pairs={{0,4},{1,5},{2,6},{3,7},{4,0},{5,1},{6,2},{7,3},{8,12},{9,13},{10,... | collective-permute-start | bytes 393224 | tf_op jit(solution)/shard_map/ppermute | solution.py:32
  65.2 3.3 %collective-permute-done.18.refs_0_ = bf16[2,64,512]{2,1,0:T(8,128)(2,1)S(1)} collective-permute-done((bf16[2,64,512]{2,1,0:T(8,128)(2,1)S(1)}, bf16[2,64,512]{2,1,0:T(8,128)(2,1)S(1)}, u32[]{:S(2)}, u32[]{:S(2)}) %collective-permute-start.18) | collective-permute-done | bytes 131104 | tf_op jit(solution)/shard_map/ppermute | solution.py:32
  68.5 1.5 %collective-permute-done.20.refs_0_ = bf16[2,64,512]{2,1,0:T(8,128)(2,1)S(1)} collective-permute-done((bf16[2,64,512]{2,1,0:T(8,128)(2,1)S(1)}, bf16[2,64,512]{2,1,0:T(8,128)(2,1)S(1)}, u32[]{:S(2)}, u32[]{:S(2)}) %collective-permute-start.20) | collective-permute-done | bytes 131104 | tf_op jit(solution)/shard_map/ppermute | solution.py:32
  71.9 4.0 %collective-permute-done.19.refs_0_ = bf16[2,64,512]{2,1,0:T(8,128)(2,1)S(1)} collective-permute-done((bf16[2,64,512]{2,1,0:T(8,128)(2,1)S(1)}, bf16[2,64,512]{2,1,0:T(8,128)(2,1)S(1)}, u32[]{:S(2)}, u32[]{:S(2)}) %collective-permute-start.19) | collective-permute-done | bytes 131104 | tf_op jit(solution)/shard_map/ppermute | solution.py:32
  76.3 1.0 collective-permute-done.24.refs_0_
  77.8 9.7 %all_to_all.11.qkv_ref = bf16[16,4,320]{2,1,0:T(4,128)(2,1)S(1)} all-to-all(bf16[16,4,320]{2,1,0:T(4,128)(2,1)S(1)} %project.19), channel_id=1, replica_groups=mesh['segment'=2,'slot'=16] {'slot'}, dimensions={0} | all-to-all | bytes 81920 | tf_op jit(solution)/shard_map/all_to_all | solution.py:386
  88.4 4.5 %collective-permute-done.25 = bf16[1,4,4096]{2,1,0:T(4,128)(2,1)S(1)} collective-permute-done((bf16[1,4,4096]{2,1,0:T(4,128)(2,1)S(1)}, bf16[1,4,4096]{2,1,0:T(4,128)(2,1)S(1)}, u32[]{:S(2)}, u32[]{:S(2)}) %collective-permute-start.25) | collective-permute-done | bytes 32800 | tf_op jit(solution)/shard_map/ppermute | solution.py:32
  93.3 1.4 %collective-permute-start.27 = (bf16[2,4,4096]{2,1,0:T(4,128)(2,1)S(1)}, bf16[2,4,4096]{2,1,0:T(4,128)(2,1)S(1)}, u32[]{:S(2)}, u32[]{:S(2)}) collective-permute-start(bf16[2,4,4096]{2,1,0:T(4,128)(2,1)S(1)} %pad_maximum_fusion.3.refs_0_), channel_id=1, source_target_pairs={{0,2},{1,3},{2,0},{3,1},{4,6},{5,7},{6,4},{7,5},{8,10},{9,11},{10,... | collective-permute-start | bytes 196616 | tf_op jit(solution)/shard_map/ppermute | solution.py:32
  94.7 1.8 %collective-permute-start.28 = (bf16[2,4,4096]{2,1,0:T(4,128)(2,1)S(1)}, bf16[2,4,4096]{2,1,0:T(4,128)(2,1)S(1)}, u32[]{:S(2)}, u32[]{:S(2)}) collective-permute-start(bf16[2,4,4096]{2,1,0:T(4,128)(2,1)S(1)} %pad_maximum_fusion.3.refs_0_), channel_id=1, source_target_pairs={{0,4},{1,5},{2,6},{3,7},{4,0},{5,1},{6,2},{7,3},{8,12},{9,13},{10,... | collective-permute-start | bytes 196616 | tf_op jit(solution)/shard_map/ppermute | solution.py:32
  96.6 1.8 %collective-permute-done.26.refs_1_ = bf16[2,4,4096]{2,1,0:T(4,128)(2,1)S(1)} collective-permute-done((bf16[2,4,4096]{2,1,0:T(4,128)(2,1)S(1)}, bf16[2,4,4096]{2,1,0:T(4,128)(2,1)S(1)}, u32[]{:S(2)}, u32[]{:S(2)}) %collective-permute-start.26) | collective-permute-done | bytes 65568 | tf_op jit(solution)/shard_map/ppermute | solution.py:32
  100.3 1.0 output.3
  101.3 1.0 collective-permute-start.33
  102.3 3.3 %collective-permute-done.33 = bf16[64,512]{1,0:T(8,128)(2,1)S(1)} collective-permute-done((bf16[64,512]{1,0:T(8,128)(2,1)S(1)}, bf16[64,512]{1,0:T(8,128)(2,1)S(1)}, u32[]{:S(2)}, u32[]{:S(2)}) %collective-permute-start.33) | collective-permute-done | bytes 65568 | tf_op jit(solution)/shard_map/ppermute | solution.py:60
  (86 shorter events, 16.8 us)
Async XLA Ops:
  1.0 8.3 %collective-permute-start = (bf16[1,80,512]{2,1,0:T(8,128)(2,1)S(1)}, bf16[1,80,512]{2,1,0:T(8,128)(2,1)S(1)}, u32[]{:S(2)}, u32[]{:S(2)}) collective-permute-start(bf16[1,80,512]{2,1,0:T(8,128)(2,1)S(1)} %maximum_bitcast_fusion), channel_id=1, source_target_pairs={{0,8},{1,9},{2,10},{3,11},{4,12},{5,13},{6,14},{7,15},{8,0},{9,1},... | collective-permute-start | bytes 245768 | tf_op jit(solution)/shard_map/ppermute | solution.py:32
  9.3 5.4 %collective-permute-start.1 = (bf16[2,80,512]{2,1,0:T(8,128)(2,1)S(1)}, bf16[2,80,512]{2,1,0:T(8,128)(2,1)S(1)}, u32[]{:S(2)}, u32[]{:S(2)}) collective-permute-start(bf16[2,80,512]{2,1,0:T(8,128)(2,1)S(1)} %pad_maximum_fusion.refs_0_), channel_id=1, source_target_pairs={{0,4},{1,5},{2,6},{3,7},{4,0},{5,1},{6,2},{7,3},{8,12},{9,13},{10,... | collective-permute-start | bytes 491528 | tf_op jit(solution)/shard_map/ppermute | solution.py:32
  10.1 5.7 %collective-permute-start.3 = (bf16[2,80,512]{2,1,0:T(8,128)(2,1)S(1)}, bf16[2,80,512]{2,1,0:T(8,128)(2,1)S(1)}, u32[]{:S(2)}, u32[]{:S(2)}) collective-permute-start(bf16[2,80,512]{2,1,0:T(8,128)(2,1)S(1)} %pad_maximum_fusion.refs_0_), channel_id=1, source_target_pairs={{0,2},{1,3},{2,0},{3,1},{4,6},{5,7},{6,4},{7,5},{8,10},{9,11},{10,... | collective-permute-start | bytes 491528 | tf_op jit(solution)/shard_map/ppermute | solution.py:32
  11.6 5.7 %collective-permute-start.6 = (bf16[2,80,512]{2,1,0:T(8,128)(2,1)S(1)}, bf16[2,80,512]{2,1,0:T(8,128)(2,1)S(1)}, u32[]{:S(2)}, u32[]{:S(2)}) collective-permute-start(bf16[2,80,512]{2,1,0:T(8,128)(2,1)S(1)} %pad_maximum_fusion.refs_0_), channel_id=1, source_target_pairs={{0,1},{1,0},{2,3},{3,2},{4,5},{5,4},{6,7},{7,6},{8,9},{9,8},{10,11... | collective-permute-start | bytes 491528 | tf_op jit(solution)/shard_map/ppermute | solution.py:32
  14.7 5.6 %collective-permute-start.5 = (bf16[2,80,512]{2,1,0:T(8,128)(2,1)S(1)}, bf16[2,80,512]{2,1,0:T(8,128)(2,1)S(1)}, u32[]{:S(2)}, u32[]{:S(2)}) collective-permute-start(bf16[2,80,512]{2,1,0:T(8,128)(2,1)S(1)} %collective-permute-done.1.refs_0_), channel_id=1, source_target_pairs={{0,1},{1,0},{2,3},{3,2},{4,5},{5,4},{6,7},{7,6},{8,9},{9,8},{10,11... | collective-permute-start | bytes 491528 | tf_op jit(solution)/shard_map/ppermute | solution.py:32
  15.8 5.0 %collective-permute-start.4 = (bf16[2,80,512]{2,1,0:T(8,128)(2,1)S(1)}, bf16[2,80,512]{2,1,0:T(8,128)(2,1)S(1)}, u32[]{:S(2)}, u32[]{:S(2)}) collective-permute-start(bf16[2,80,512]{2,1,0:T(8,128)(2,1)S(1)} %collective-permute-done.3.refs_0_), channel_id=1, source_target_pairs={{0,1},{1,0},{2,3},{3,2},{4,5},{5,4},{6,7},{7,6},{8,9},{9,8},{10,11... | collective-permute-start | bytes 491528 | tf_op jit(solution)/shard_map/ppermute | solution.py:32
  15.8 6.6 %collective-permute-start.2 = (bf16[2,80,512]{2,1,0:T(8,128)(2,1)S(1)}, bf16[2,80,512]{2,1,0:T(8,128)(2,1)S(1)}, u32[]{:S(2)}, u32[]{:S(2)}) collective-permute-start(bf16[2,80,512]{2,1,0:T(8,128)(2,1)S(1)} %collective-permute-done.1.refs_0_), channel_id=1, source_target_pairs={{0,2},{1,3},{2,0},{3,1},{4,6},{5,7},{6,4},{7,5},{8,10},{9,11},{10,... | collective-permute-start | bytes 491528 | tf_op jit(solution)/shard_map/ppermute | solution.py:32
  22.5 1.5 %collective-permute-start.7 = (bf16[2,80,512]{2,1,0:T(8,128)(2,1)S(1)}, bf16[2,80,512]{2,1,0:T(8,128)(2,1)S(1)}, u32[]{:S(2)}, u32[]{:S(2)}) collective-permute-start(bf16[2,80,512]{2,1,0:T(8,128)(2,1)S(1)} %collective-permute-done.2.refs_0_), channel_id=1, source_target_pairs={{0,1},{1,0},{2,3},{3,2},{4,5},{5,4},{6,7},{7,6},{8,9},{9,8},{10,11... | collective-permute-start | bytes 491528 | tf_op jit(solution)/shard_map/ppermute | solution.py:32
  42.1 5.0 %collective-permute-start.8 = (bf16[1,4,4096]{2,1,0:T(4,128)(2,1)S(1)}, bf16[1,4,4096]{2,1,0:T(4,128)(2,1)S(1)}, u32[]{:S(2)}, u32[]{:S(2)}) collective-permute-start(bf16[1,4,4096]{2,1,0:T(4,128)(2,1)S(1)} %attend.2), channel_id=1, source_target_pairs={{0,8},{1,9},{2,10},{3,11},{4,12},{5,13},{6,14},{7,15},{8,0},{9,1},... | collective-permute-start | bytes 98312 | tf_op jit(solution)/shard_map/ppermute | solution.py:32
  47.2 5.3 %collective-permute-start.9 = (bf16[2,4,4096]{2,1,0:T(4,128)(2,1)S(1)}, bf16[2,4,4096]{2,1,0:T(4,128)(2,1)S(1)}, u32[]{:S(2)}, u32[]{:S(2)}) collective-permute-start(bf16[2,4,4096]{2,1,0:T(4,128)(2,1)S(1)} %pad_maximum_fusion.2.refs_0_), channel_id=1, source_target_pairs={{0,6},{1,7},{2,4},{3,5},{4,2},{5,3},{6,0},{7,1},{8,14},{9,15},{10,... | collective-permute-start | bytes 196616 | tf_op jit(solution)/shard_map/ppermute | solution.py:32
  48.0 5.0 %collective-permute-start.10 = (bf16[2,4,4096]{2,1,0:T(4,128)(2,1)S(1)}, bf16[2,4,4096]{2,1,0:T(4,128)(2,1)S(1)}, u32[]{:S(2)}, u32[]{:S(2)}) collective-permute-start(bf16[2,4,4096]{2,1,0:T(4,128)(2,1)S(1)} %pad_maximum_fusion.2.refs_0_), channel_id=1, source_target_pairs={{0,2},{1,3},{2,0},{3,1},{4,6},{5,7},{6,4},{7,5},{8,10},{9,11},{10,... | collective-permute-start | bytes 196616 | tf_op jit(solution)/shard_map/ppermute | solution.py:32
  48.9 4.3 %collective-permute-start.11 = (bf16[2,4,4096]{2,1,0:T(4,128)(2,1)S(1)}, bf16[2,4,4096]{2,1,0:T(4,128)(2,1)S(1)}, u32[]{:S(2)}, u32[]{:S(2)}) collective-permute-start(bf16[2,4,4096]{2,1,0:T(4,128)(2,1)S(1)} %pad_maximum_fusion.2.refs_0_), channel_id=1, source_target_pairs={{0,4},{1,5},{2,6},{3,7},{4,0},{5,1},{6,2},{7,3},{8,12},{9,13},{10,... | collective-permute-start | bytes 196616 | tf_op jit(solution)/shard_map/ppermute | solution.py:32
  50.7 2.7 %collective-permute-start.12 = (bf16[2,4,4096]{2,1,0:T(4,128)(2,1)S(1)}, bf16[2,4,4096]{2,1,0:T(4,128)(2,1)S(1)}, u32[]{:S(2)}, u32[]{:S(2)}) collective-permute-start(bf16[2,4,4096]{2,1,0:T(4,128)(2,1)S(1)} %pad_maximum_fusion.2.refs_0_), channel_id=1, source_target_pairs={{0,1},{1,0},{2,3},{3,2},{4,5},{5,4},{6,7},{7,6},{8,9},{9,8},{10,11... | collective-permute-start | bytes 196616 | tf_op jit(solution)/shard_map/ppermute | solution.py:32
  52.5 1.3 %collective-permute-start.13 = (bf16[2,4,4096]{2,1,0:T(4,128)(2,1)S(1)}, bf16[2,4,4096]{2,1,0:T(4,128)(2,1)S(1)}, u32[]{:S(2)}, u32[]{:S(2)}) collective-permute-start(bf16[2,4,4096]{2,1,0:T(4,128)(2,1)S(1)} %collective-permute-done.9.refs_1_), channel_id=1, source_target_pairs={{0,1},{1,0},{2,3},{3,2},{4,5},{5,4},{6,7},{7,6},{8,9},{9,8},{10,11... | collective-permute-start | bytes 196616 | tf_op jit(solution)/shard_map/ppermute | solution.py:32
  52.9 1.3 %collective-permute-start.14 = (bf16[2,4,4096]{2,1,0:T(4,128)(2,1)S(1)}, bf16[2,4,4096]{2,1,0:T(4,128)(2,1)S(1)}, u32[]{:S(2)}, u32[]{:S(2)}) collective-permute-start(bf16[2,4,4096]{2,1,0:T(4,128)(2,1)S(1)} %collective-permute-done.10.refs_2_), channel_id=1, source_target_pairs={{0,1},{1,0},{2,3},{3,2},{4,5},{5,4},{6,7},{7,6},{8,9},{9,8},{10,11... | collective-permute-start | bytes 196616 | tf_op jit(solution)/shard_map/ppermute | solution.py:32
  53.2 1.3 %collective-permute-start.15 = (bf16[2,4,4096]{2,1,0:T(4,128)(2,1)S(1)}, bf16[2,4,4096]{2,1,0:T(4,128)(2,1)S(1)}, u32[]{:S(2)}, u32[]{:S(2)}) collective-permute-start(bf16[2,4,4096]{2,1,0:T(4,128)(2,1)S(1)} %collective-permute-done.11.refs_3_), channel_id=1, source_target_pairs={{0,1},{1,0},{2,3},{3,2},{4,5},{5,4},{6,7},{7,6},{8,9},{9,8},{10,11... | collective-permute-start | bytes 196616 | tf_op jit(solution)/shard_map/ppermute | solution.py:32
  55.5 7.5 %collective-permute-start.16 = (bf16[64,512]{1,0:T(8,128)(2,1)S(1)}, bf16[64,512]{1,0:T(8,128)(2,1)S(1)}, u32[]{:S(2)}, u32[]{:S(2)}) collective-permute-start(bf16[64,512]{1,0:T(8,128)(2,1)S(1)} %output.2), channel_id=1, source_target_pairs={{0,24},{1,25},{2,26},{3,27},{4,28},{5,29},{6,30},{7,31},{8,16},{9,... | collective-permute-start | bytes 196616 | tf_op jit(solution)/shard_map/ppermute | solution.py:60
  57.9 5.1 %collective-permute-start.17 = (bf16[64,512]{1,0:T(8,128)(2,1)S(1)}, bf16[64,512]{1,0:T(8,128)(2,1)S(1)}, u32[]{:S(2)}, u32[]{:S(2)}) collective-permute-start(bf16[64,512]{1,0:T(8,128)(2,1)S(1)} %output.2), channel_id=1, source_target_pairs={{0,16},{1,17},{2,18},{3,19},{4,20},{5,21},{6,22},{7,23},{8,24},{9,... | collective-permute-start | bytes 196616 | tf_op jit(solution)/shard_map/ppermute | solution.py:60
  63.0 5.5 %collective-permute-start.18 = (bf16[2,64,512]{2,1,0:T(8,128)(2,1)S(1)}, bf16[2,64,512]{2,1,0:T(8,128)(2,1)S(1)}, u32[]{:S(2)}, u32[]{:S(2)}) collective-permute-start(bf16[2,64,512]{2,1,0:T(8,128)(2,1)S(1)} %pad_maximum_fusion.1.refs_0_), channel_id=1, source_target_pairs={{0,4},{1,5},{2,6},{3,7},{4,0},{5,1},{6,2},{7,3},{8,12},{9,13},{10,... | collective-permute-start | bytes 393224 | tf_op jit(solution)/shard_map/ppermute | solution.py:32
  64.9 5.1 %collective-permute-start.20 = (bf16[2,64,512]{2,1,0:T(8,128)(2,1)S(1)}, bf16[2,64,512]{2,1,0:T(8,128)(2,1)S(1)}, u32[]{:S(2)}, u32[]{:S(2)}) collective-permute-start(bf16[2,64,512]{2,1,0:T(8,128)(2,1)S(1)} %pad_maximum_fusion.1.refs_0_), channel_id=1, source_target_pairs={{0,2},{1,3},{2,0},{3,1},{4,6},{5,7},{6,4},{7,5},{8,10},{9,11},{10,... | collective-permute-start | bytes 393224 | tf_op jit(solution)/shard_map/ppermute | solution.py:32
  65.2 5.1 %collective-permute-start.23 = (bf16[2,64,512]{2,1,0:T(8,128)(2,1)S(1)}, bf16[2,64,512]{2,1,0:T(8,128)(2,1)S(1)}, u32[]{:S(2)}, u32[]{:S(2)}) collective-permute-start(bf16[2,64,512]{2,1,0:T(8,128)(2,1)S(1)} %pad_maximum_fusion.1.refs_0_), channel_id=1, source_target_pairs={{0,1},{1,0},{2,3},{3,2},{4,5},{5,4},{6,7},{7,6},{8,9},{9,8},{10,11... | collective-permute-start | bytes 393224 | tf_op jit(solution)/shard_map/ppermute | solution.py:32
  68.5 2.3 %collective-permute-start.22 = (bf16[2,64,512]{2,1,0:T(8,128)(2,1)S(1)}, bf16[2,64,512]{2,1,0:T(8,128)(2,1)S(1)}, u32[]{:S(2)}, u32[]{:S(2)}) collective-permute-start(bf16[2,64,512]{2,1,0:T(8,128)(2,1)S(1)} %collective-permute-done.18.refs_0_), channel_id=1, source_target_pairs={{0,1},{1,0},{2,3},{3,2},{4,5},{5,4},{6,7},{7,6},{8,9},{9,8},{10,11... | collective-permute-start | bytes 393224 | tf_op jit(solution)/shard_map/ppermute | solution.py:32
  70.0 1.4 %collective-permute-start.21 = (bf16[2,64,512]{2,1,0:T(8,128)(2,1)S(1)}, bf16[2,64,512]{2,1,0:T(8,128)(2,1)S(1)}, u32[]{:S(2)}, u32[]{:S(2)}) collective-permute-start(bf16[2,64,512]{2,1,0:T(8,128)(2,1)S(1)} %collective-permute-done.20.refs_0_), channel_id=1, source_target_pairs={{0,1},{1,0},{2,3},{3,2},{4,5},{5,4},{6,7},{7,6},{8,9},{9,8},{10,11... | collective-permute-start | bytes 393224 | tf_op jit(solution)/shard_map/ppermute | solution.py:32
  70.0 5.9 %collective-permute-start.19 = (bf16[2,64,512]{2,1,0:T(8,128)(2,1)S(1)}, bf16[2,64,512]{2,1,0:T(8,128)(2,1)S(1)}, u32[]{:S(2)}, u32[]{:S(2)}) collective-permute-start(bf16[2,64,512]{2,1,0:T(8,128)(2,1)S(1)} %collective-permute-done.18.refs_0_), channel_id=1, source_target_pairs={{0,2},{1,3},{2,0},{3,1},{4,6},{5,7},{6,4},{7,5},{8,10},{9,11},{10,... | collective-permute-start | bytes 393224 | tf_op jit(solution)/shard_map/ppermute | solution.py:32
  75.9 1.3 %collective-permute-start.24 = (bf16[2,64,512]{2,1,0:T(8,128)(2,1)S(1)}, bf16[2,64,512]{2,1,0:T(8,128)(2,1)S(1)}, u32[]{:S(2)}, u32[]{:S(2)}) collective-permute-start(bf16[2,64,512]{2,1,0:T(8,128)(2,1)S(1)} %collective-permute-done.19.refs_0_), channel_id=1, source_target_pairs={{0,1},{1,0},{2,3},{3,2},{4,5},{5,4},{6,7},{7,6},{8,9},{9,8},{10,11... | collective-permute-start | bytes 393224 | tf_op jit(solution)/shard_map/ppermute | solution.py:32
  88.1 4.9 %collective-permute-start.25 = (bf16[1,4,4096]{2,1,0:T(4,128)(2,1)S(1)}, bf16[1,4,4096]{2,1,0:T(4,128)(2,1)S(1)}, u32[]{:S(2)}, u32[]{:S(2)}) collective-permute-start(bf16[1,4,4096]{2,1,0:T(4,128)(2,1)S(1)} %attend.3), channel_id=1, source_target_pairs={{0,8},{1,9},{2,10},{3,11},{4,12},{5,13},{6,14},{7,15},{8,0},{9,1},... | collective-permute-start | bytes 98312 | tf_op jit(solution)/shard_map/ppermute | solution.py:32
  93.0 5.3 %collective-permute-start.26 = (bf16[2,4,4096]{2,1,0:T(4,128)(2,1)S(1)}, bf16[2,4,4096]{2,1,0:T(4,128)(2,1)S(1)}, u32[]{:S(2)}, u32[]{:S(2)}) collective-permute-start(bf16[2,4,4096]{2,1,0:T(4,128)(2,1)S(1)} %pad_maximum_fusion.3.refs_0_), channel_id=1, source_target_pairs={{0,6},{1,7},{2,4},{3,5},{4,2},{5,3},{6,0},{7,1},{8,14},{9,15},{10,... | collective-permute-start | bytes 196616 | tf_op jit(solution)/shard_map/ppermute | solution.py:32
  93.3 5.0 %collective-permute-start.27 = (bf16[2,4,4096]{2,1,0:T(4,128)(2,1)S(1)}, bf16[2,4,4096]{2,1,0:T(4,128)(2,1)S(1)}, u32[]{:S(2)}, u32[]{:S(2)}) collective-permute-start(bf16[2,4,4096]{2,1,0:T(4,128)(2,1)S(1)} %pad_maximum_fusion.3.refs_0_), channel_id=1, source_target_pairs={{0,2},{1,3},{2,0},{3,1},{4,6},{5,7},{6,4},{7,5},{8,10},{9,11},{10,... | collective-permute-start | bytes 196616 | tf_op jit(solution)/shard_map/ppermute | solution.py:32
  94.7 4.3 %collective-permute-start.28 = (bf16[2,4,4096]{2,1,0:T(4,128)(2,1)S(1)}, bf16[2,4,4096]{2,1,0:T(4,128)(2,1)S(1)}, u32[]{:S(2)}, u32[]{:S(2)}) collective-permute-start(bf16[2,4,4096]{2,1,0:T(4,128)(2,1)S(1)} %pad_maximum_fusion.3.refs_0_), channel_id=1, source_target_pairs={{0,4},{1,5},{2,6},{3,7},{4,0},{5,1},{6,2},{7,3},{8,12},{9,13},{10,... | collective-permute-start | bytes 196616 | tf_op jit(solution)/shard_map/ppermute | solution.py:32
  96.6 2.5 %collective-permute-start.29 = (bf16[2,4,4096]{2,1,0:T(4,128)(2,1)S(1)}, bf16[2,4,4096]{2,1,0:T(4,128)(2,1)S(1)}, u32[]{:S(2)}, u32[]{:S(2)}) collective-permute-start(bf16[2,4,4096]{2,1,0:T(4,128)(2,1)S(1)} %pad_maximum_fusion.3.refs_0_), channel_id=1, source_target_pairs={{0,1},{1,0},{2,3},{3,2},{4,5},{5,4},{6,7},{7,6},{8,9},{9,8},{10,11... | collective-permute-start | bytes 196616 | tf_op jit(solution)/shard_map/ppermute | solution.py:32
  98.3 1.4 %collective-permute-start.31 = (bf16[2,4,4096]{2,1,0:T(4,128)(2,1)S(1)}, bf16[2,4,4096]{2,1,0:T(4,128)(2,1)S(1)}, u32[]{:S(2)}, u32[]{:S(2)}) collective-permute-start(bf16[2,4,4096]{2,1,0:T(4,128)(2,1)S(1)} %collective-permute-done.27.refs_2_), channel_id=1, source_target_pairs={{0,1},{1,0},{2,3},{3,2},{4,5},{5,4},{6,7},{7,6},{8,9},{9,8},{10,11... | collective-permute-start | bytes 196616 | tf_op jit(solution)/shard_map/ppermute | solution.py:32
  101.3 4.3 %collective-permute-start.33 = (bf16[64,512]{1,0:T(8,128)(2,1)S(1)}, bf16[64,512]{1,0:T(8,128)(2,1)S(1)}, u32[]{:S(2)}, u32[]{:S(2)}) collective-permute-start(bf16[64,512]{1,0:T(8,128)(2,1)S(1)} %output.3), channel_id=1, source_target_pairs={{0,16},{1,17},{2,18},{3,19},{4,20},{5,21},{6,22},{7,23},{8,24},{9,... | collective-permute-start | bytes 196616 | tf_op jit(solution)/shard_map/ppermute | solution.py:60
  (14 other events, 259.5 us)

commit v6 on v5

--- a/solution.py
+++ b/solution.py
@@ -30,15 +30,6 @@
 def exchange(block, mask):
     n = lax.axis_size("slot")
     return lax.ppermute(block, "slot", [(i, i ^ mask) for i in range(n)])
-
-
-def spread(block, masks):
-    across, over, core = masks
-    second = exchange(block, across)
-    third = exchange(block, over)
-    fourth = exchange(second, over)
-    groups = [block, second, third, fourth]
-    return groups + [exchange(group, core) for group in groups]
 
 
 def gather(block, phases):
@@ -374,14 +365,18 @@
         size = slots // 8
         away = [offsets[g * size:(g + 1) * size] for g in range(8)]
         run = functools.partial(project, rows, batch, weight_in)
-        state = None
-        groups = spread(block, masks[-3:])
-        for k, names in enumerate([(0, 4), (1, 5), (2, 6)]):
-            gains[k], state = run([(away[g], groups[g]) for g in names], gains[k], state)
-        groups[3], state = lax.optimization_barrier((groups[3], state))
-        groups[7] = exchange(groups[3], masks[-1])
-        gains[3], state = run([(away[3], groups[3])], gains[3], state)
-        gains[4], qkv = run([(away[7], groups[7])], gains[4], state, last=True,
+        second = exchange(block, across)
+        third = exchange(block, over)
+        pair = exchange(block, core)
+        fourth = exchange(second, over)
+        gains[0], state = run([(away[0], block), (away[4], pair)], gains[0], None)
+        gains[1], state = run([(away[1], second), (away[2], third)], gains[1], state)
+        second, third, state = lax.optimization_barrier((second, third, state))
+        others = [exchange(x, core) for x in (second, third)]
+        fourth, state = lax.optimization_barrier((fourth, state))
+        corner = exchange(fourth, core)
+        gains[3], state = run([(away[3], fourth), *zip(away[5:7], others)], gains[3], state)
+        gains[4], qkv = run([(away[7], corner)], gains[4], state, last=True,
                              outgoing=None if visit else outgoing)
         qkv = lax.all_to_all(qkv, "slot", split_axis=0, concat_axis=0, tiled=True)
         if visit == 0:

time: 107 us -> 105 us (0.981)
  waiting for transfers between devices: 40.4 us -> 36.7 us
  starting transfers between devices: 24.2 us -> 25.6 us
    ppermute x31, waiting for transfers between devices: 32.5 us -> 27.3 us  [exchange(): return lax.ppermute(block, 'slot', [(i, i ^ mask) for i in range(n)])]
    ppermute x31, starting transfers between devices: 20.2 us -> 22 us  [exchange(): return lax.ppermute(block, 'slot', [(i, i ^ mask) for i in range(n)])]
    ppermute x3, waiting for transfers between devices: 7.9 us -> 9.4 us  [next_segment(): return lax.ppermute(block, ('segment', 'slot'), route)]
    pallas_call x10 -> x8, Pallas kernels: 4.84 us -> 4.56 us  [project(): pl.pallas_call(functools.partial(project_kernel, away=[masks for masks, _...]
  transfers between devices with their start and end apart: 34 -> 34, of which waited for: 24 -> 20; matrix products, arithmetic and copies ran while one was open for 0% -> 0% of each run, Pallas kernels for 4% -> 4%
where the time goes in v6:
time: 105 us
  waiting for transfers between devices  36.7 us (35%)
  blocking collectives  27.4 us (26%)
  starting transfers between devices  25.6 us (24%)
  Pallas kernels  8.62 us (8%)
  local copies, waits for them, and re-layouts  4.9 us (5%)
  other arithmetic  1.06 us (1%)
    all_to_all x2, blocking collectives, shards(): qkv = lax.all_to_all(qkv, 'slot', split_axis=0, concat_axis=0, tiled=True)  27.4 us
    ppermute x31, waiting for transfers between devices, exchange(): return lax.ppermute(block, 'slot', [(i, i ^ mask) for i in range(n)])  27.3 us
    ppermute x31, starting transfers between devices, exchange(): return lax.ppermute(block, 'slot', [(i, i ^ mask) for i in range(n)])  22 us
    ppermute x3, waiting for transfers between devices, next_segment(): return lax.ppermute(block, ('segment', 'slot'), route)  9.4 us
    unnamed x25, local copies, waits for them, and re-layouts  4.82 us
    pallas_call x8, Pallas kernels, project(): pl.pallas_call(functools.partial(project_kernel, away=[masks for masks, _...  4.56 us
    ppermute x3, starting transfers between devices, next_segment(): return lax.ppermute(block, ('segment', 'slot'), route)  3.59 us
  transfers between devices with their start and end apart: 34, of which 20 were waited for; matrix products, arithmetic and copies ran while one was open for 0% of the time, Pallas kernels for 4%

profile of v6, /device:TPU:0, one launch (start us, length us, event | category | flops | bytes accessed | tf_op | source)
XLA Modules:
  0.0 104.6 jit_solution(17870555280097510102)
XLA Ops:
  0.1 0.9 maximum_bitcast_fusion
  1.0 4.1 %collective-permute-start = (bf16[1,80,512]{2,1,0:T(8,128)(2,1)S(1)}, bf16[1,80,512]{2,1,0:T(8,128)(2,1)S(1)}, u32[]{:S(2)}, u32[]{:S(2)}) collective-permute-start(bf16[1,80,512]{2,1,0:T(8,128)(2,1)S(1)} %maximum_bitcast_fusion), channel_id=1, source_target_pairs={{0,8},{1,9},{2,10},{3,11},{4,12},{5,13},{6,14},{7,15},{8,0},{9,1},... | collective-permute-start | bytes 245768 | tf_op jit(solution)/shard_map/ppermute | solution.py:32
  5.1 0.9 copy-done.4
  7.5 1.8 %collective-permute-done = bf16[1,80,512]{2,1,0:T(8,128)(2,1)S(1)} collective-permute-done((bf16[1,80,512]{2,1,0:T(8,128)(2,1)S(1)}, bf16[1,80,512]{2,1,0:T(8,128)(2,1)S(1)}, u32[]{:S(2)}, u32[]{:S(2)}) %collective-permute-start) | collective-permute-done | bytes 81952 | tf_op jit(solution)/shard_map/ppermute | solution.py:32
  10.1 1.5 %collective-permute-start.3 = (bf16[2,80,512]{2,1,0:T(8,128)(2,1)S(1)}, bf16[2,80,512]{2,1,0:T(8,128)(2,1)S(1)}, u32[]{:S(2)}, u32[]{:S(2)}) collective-permute-start(bf16[2,80,512]{2,1,0:T(8,128)(2,1)S(1)} %pad_maximum_fusion.refs_0_), channel_id=1, source_target_pairs={{0,2},{1,3},{2,0},{3,1},{4,6},{5,7},{6,4},{7,5},{8,10},{9,11},{10,... | collective-permute-start | bytes 491528 | tf_op jit(solution)/shard_map/ppermute | solution.py:32
  11.6 3.1 %collective-permute-done.1.refs_0_ = bf16[2,80,512]{2,1,0:T(8,128)(2,1)S(1)} collective-permute-done((bf16[2,80,512]{2,1,0:T(8,128)(2,1)S(1)}, bf16[2,80,512]{2,1,0:T(8,128)(2,1)S(1)}, u32[]{:S(2)}, u32[]{:S(2)}) %collective-permute-start.1) | collective-permute-done | bytes 163872 | tf_op jit(solution)/shard_map/ppermute | solution.py:32
  14.7 1.7 %collective-permute-start.2 = (bf16[2,80,512]{2,1,0:T(8,128)(2,1)S(1)}, bf16[2,80,512]{2,1,0:T(8,128)(2,1)S(1)}, u32[]{:S(2)}, u32[]{:S(2)}) collective-permute-start(bf16[2,80,512]{2,1,0:T(8,128)(2,1)S(1)} %collective-permute-done.1.refs_0_), channel_id=1, source_target_pairs={{0,2},{1,3},{2,0},{3,1},{4,6},{5,7},{6,4},{7,5},{8,10},{9,11},{10,... | collective-permute-start | bytes 491528 | tf_op jit(solution)/shard_map/ppermute | solution.py:32
  16.4 2.5 %copy-done = bf16[1,8192,320]{1,2,0:T(8,128)(2,1)S(1)} copy-done((bf16[1,8192,320]{1,2,0:T(8,128)(2,1)S(1)}, bf16[1,8192,320]{1,2,0:T(8,128)(2,1)}, u32[]{:S(2)}) %copy-start) | copy-done | bytes 5242904
  23.1 16.6 %all_to_all.10.qkv_ref = bf16[16,8,1280]{2,1,0:T(8,128)(2,1)S(1)} all-to-all(bf16[16,8,1280]{2,1,0:T(8,128)(2,1)S(1)} %get-tuple-element.53), channel_id=1, replica_groups=mesh['segment'=2,'slot'=16] {'slot'}, dimensions={0} | all-to-all | bytes 655360 | tf_op jit(solution)/shard_map/all_to_all | solution.py:381
  40.4 1.4 %collective-permute-start.8 = (bf16[1,4,4096]{2,1,0:T(4,128)(2,1)S(1)}, bf16[1,4,4096]{2,1,0:T(4,128)(2,1)S(1)}, u32[]{:S(2)}, u32[]{:S(2)}) collective-permute-start(bf16[1,4,4096]{2,1,0:T(4,128)(2,1)S(1)} %attend.2), channel_id=1, source_target_pairs={{0,8},{1,9},{2,10},{3,11},{4,12},{5,13},{6,14},{7,15},{8,0},{9,1},... | collective-permute-start | bytes 98312 | tf_op jit(solution)/shard_map/ppermute | solution.py:32
  41.8 3.6 %collective-permute-done.8 = bf16[1,4,4096]{2,1,0:T(4,128)(2,1)S(1)} collective-permute-done((bf16[1,4,4096]{2,1,0:T(4,128)(2,1)S(1)}, bf16[1,4,4096]{2,1,0:T(4,128)(2,1)S(1)}, u32[]{:S(2)}, u32[]{:S(2)}) %collective-permute-start.8) | collective-permute-done | bytes 32800 | tf_op jit(solution)/shard_map/ppermute | solution.py:32
  45.8 1.1 %collective-permute-start.10 = (bf16[2,4,4096]{2,1,0:T(4,128)(2,1)S(1)}, bf16[2,4,4096]{2,1,0:T(4,128)(2,1)S(1)}, u32[]{:S(2)}, u32[]{:S(2)}) collective-permute-start(bf16[2,4,4096]{2,1,0:T(4,128)(2,1)S(1)} %pad_maximum_fusion.2.refs_0_), channel_id=1, source_target_pairs={{0,2},{1,3},{2,0},{3,1},{4,6},{5,7},{6,4},{7,5},{8,10},{9,11},{10,... | collective-permute-start | bytes 196616 | tf_op jit(solution)/shard_map/ppermute | solution.py:32
  46.8 2.2 %collective-permute-start.9 = (bf16[2,4,4096]{2,1,0:T(4,128)(2,1)S(1)}, bf16[2,4,4096]{2,1,0:T(4,128)(2,1)S(1)}, u32[]{:S(2)}, u32[]{:S(2)}) collective-permute-start(bf16[2,4,4096]{2,1,0:T(4,128)(2,1)S(1)} %pad_maximum_fusion.2.refs_0_), channel_id=1, source_target_pairs={{0,6},{1,7},{2,4},{3,5},{4,2},{5,3},{6,0},{7,1},{8,14},{9,15},{10,... | collective-permute-start | bytes 196616 | tf_op jit(solution)/shard_map/ppermute | solution.py:32
  49.0 1.5 %collective-permute-done.11.refs_3_ = bf16[2,4,4096]{2,1,0:T(4,128)(2,1)S(1)} collective-permute-done((bf16[2,4,4096]{2,1,0:T(4,128)(2,1)S(1)}, bf16[2,4,4096]{2,1,0:T(4,128)(2,1)S(1)}, u32[]{:S(2)}, u32[]{:S(2)}) %collective-permute-start.11) | collective-permute-done | bytes 65568 | tf_op jit(solution)/shard_map/ppermute | solution.py:32
  51.0 1.0 collective-permute-done.9.refs_1_
  52.0 1.2 %collective-permute-done.13.refs_5_ = bf16[2,4,4096]{2,1,0:T(4,128)(2,1)S(1)} collective-permute-done((bf16[2,4,4096]{2,1,0:T(4,128)(2,1)S(1)}, bf16[2,4,4096]{2,1,0:T(4,128)(2,1)S(1)}, u32[]{:S(2)}, u32[]{:S(2)}) %collective-permute-start.13) | collective-permute-done | bytes 65568 | tf_op jit(solution)/shard_map/ppermute | solution.py:32
  53.3 1.0 output.2
  54.3 1.6 %collective-permute-start.17 = (bf16[64,512]{1,0:T(8,128)(2,1)S(1)}, bf16[64,512]{1,0:T(8,128)(2,1)S(1)}, u32[]{:S(2)}, u32[]{:S(2)}) collective-permute-start(bf16[64,512]{1,0:T(8,128)(2,1)S(1)} %output.2), channel_id=1, source_target_pairs={{0,16},{1,17},{2,18},{3,19},{4,20},{5,21},{6,22},{7,23},{8,24},{9,... | collective-permute-start | bytes 196616 | tf_op jit(solution)/shard_map/ppermute | solution.py:51
  55.9 1.4 %collective-permute-start.16 = (bf16[64,512]{1,0:T(8,128)(2,1)S(1)}, bf16[64,512]{1,0:T(8,128)(2,1)S(1)}, u32[]{:S(2)}, u32[]{:S(2)}) collective-permute-start(bf16[64,512]{1,0:T(8,128)(2,1)S(1)} %output.2), channel_id=1, source_target_pairs={{0,24},{1,25},{2,26},{3,27},{4,28},{5,29},{6,30},{7,31},{8,16},{9,... | collective-permute-start | bytes 196616 | tf_op jit(solution)/shard_map/ppermute | solution.py:51
  57.3 1.3 %collective-permute-done.17.refs_9_ = bf16[64,512]{1,0:T(8,128)(2,1)S(1)} collective-permute-done((bf16[64,512]{1,0:T(8,128)(2,1)S(1)}, bf16[64,512]{1,0:T(8,128)(2,1)S(1)}, u32[]{:S(2)}, u32[]{:S(2)}) %collective-permute-start.17) | collective-permute-done | bytes 65568 | tf_op jit(solution)/shard_map/ppermute | solution.py:51
  58.6 4.3 %collective-permute-done.16 = bf16[64,512]{1,0:T(8,128)(2,1)S(1)} collective-permute-done((bf16[64,512]{1,0:T(8,128)(2,1)S(1)}, bf16[64,512]{1,0:T(8,128)(2,1)S(1)}, u32[]{:S(2)}, u32[]{:S(2)}) %collective-permute-start.16) | collective-permute-done | bytes 65568 | tf_op jit(solution)/shard_map/ppermute | solution.py:51
  63.1 1.6 %collective-permute-start.20 = (bf16[2,64,512]{2,1,0:T(8,128)(2,1)S(1)}, bf16[2,64,512]{2,1,0:T(8,128)(2,1)S(1)}, u32[]{:S(2)}, u32[]{:S(2)}) collective-permute-start(bf16[2,64,512]{2,1,0:T(8,128)(2,1)S(1)} %pad_maximum_fusion.1.refs_0_), channel_id=1, source_target_pairs={{0,2},{1,3},{2,0},{3,1},{4,6},{5,7},{6,4},{7,5},{8,10},{9,11},{10,... | collective-permute-start | bytes 393224 | tf_op jit(solution)/shard_map/ppermute | solution.py:32
  64.8 3.2 %collective-permute-done.18.refs_0_ = bf16[2,64,512]{2,1,0:T(8,128)(2,1)S(1)} collective-permute-done((bf16[2,64,512]{2,1,0:T(8,128)(2,1)S(1)}, bf16[2,64,512]{2,1,0:T(8,128)(2,1)S(1)}, u32[]{:S(2)}, u32[]{:S(2)}) %collective-permute-start.18) | collective-permute-done | bytes 131104 | tf_op jit(solution)/shard_map/ppermute | solution.py:32
  68.0 1.3 %collective-permute-start.19 = (bf16[2,64,512]{2,1,0:T(8,128)(2,1)S(1)}, bf16[2,64,512]{2,1,0:T(8,128)(2,1)S(1)}, u32[]{:S(2)}, u32[]{:S(2)}) collective-permute-start(bf16[2,64,512]{2,1,0:T(8,128)(2,1)S(1)} %collective-permute-done.18.refs_0_), channel_id=1, source_target_pairs={{0,2},{1,3},{2,0},{3,1},{4,6},{5,7},{6,4},{7,5},{8,10},{9,11},{10,... | collective-permute-start | bytes 393224 | tf_op jit(solution)/shard_map/ppermute | solution.py:32
  71.0 2.0 %collective-permute-done.19.refs_0_ = bf16[2,64,512]{2,1,0:T(8,128)(2,1)S(1)} collective-permute-done((bf16[2,64,512]{2,1,0:T(8,128)(2,1)S(1)}, bf16[2,64,512]{2,1,0:T(8,128)(2,1)S(1)}, u32[]{:S(2)}, u32[]{:S(2)}) %collective-permute-start.19) | collective-permute-done | bytes 131104 | tf_op jit(solution)/shard_map/ppermute | solution.py:32
  74.8 10.8 %all_to_all.11.qkv_ref = bf16[16,4,320]{2,1,0:T(4,128)(2,1)S(1)} all-to-all(bf16[16,4,320]{2,1,0:T(4,128)(2,1)S(1)} %project.15), channel_id=1, replica_groups=mesh['segment'=2,'slot'=16] {'slot'}, dimensions={0} | all-to-all | bytes 81920 | tf_op jit(solution)/shard_map/all_to_all | solution.py:381
  86.7 4.5 %collective-permute-done.25 = bf16[1,4,4096]{2,1,0:T(4,128)(2,1)S(1)} collective-permute-done((bf16[1,4,4096]{2,1,0:T(4,128)(2,1)S(1)}, bf16[1,4,4096]{2,1,0:T(4,128)(2,1)S(1)}, u32[]{:S(2)}, u32[]{:S(2)}) %collective-permute-start.25) | collective-permute-done | bytes 32800 | tf_op jit(solution)/shard_map/ppermute | solution.py:32
  92.2 2.6 %collective-permute-start.26 = (bf16[2,4,4096]{2,1,0:T(4,128)(2,1)S(1)}, bf16[2,4,4096]{2,1,0:T(4,128)(2,1)S(1)}, u32[]{:S(2)}, u32[]{:S(2)}) collective-permute-start(bf16[2,4,4096]{2,1,0:T(4,128)(2,1)S(1)} %pad_maximum_fusion.3.refs_0_), channel_id=1, source_target_pairs={{0,6},{1,7},{2,4},{3,5},{4,2},{5,3},{6,0},{7,1},{8,14},{9,15},{10,... | collective-permute-start | bytes 196616 | tf_op jit(solution)/shard_map/ppermute | solution.py:32
  96.1 1.2 %collective-permute-done.26.refs_1_ = bf16[2,4,4096]{2,1,0:T(4,128)(2,1)S(1)} collective-permute-done((bf16[2,4,4096]{2,1,0:T(4,128)(2,1)S(1)}, bf16[2,4,4096]{2,1,0:T(4,128)(2,1)S(1)}, u32[]{:S(2)}, u32[]{:S(2)}) %collective-permute-start.26) | collective-permute-done | bytes 65568 | tf_op jit(solution)/shard_map/ppermute | solution.py:32
  97.3 1.2 %collective-permute-done.30.refs_5_ = bf16[2,4,4096]{2,1,0:T(4,128)(2,1)S(1)} collective-permute-done((bf16[2,4,4096]{2,1,0:T(4,128)(2,1)S(1)}, bf16[2,4,4096]{2,1,0:T(4,128)(2,1)S(1)}, u32[]{:S(2)}, u32[]{:S(2)}) %collective-permute-start.30) | collective-permute-done | bytes 65568 | tf_op jit(solution)/shard_map/ppermute | solution.py:32
  98.6 1.0 output.3
  100.2 3.8 %collective-permute-done.33 = bf16[64,512]{1,0:T(8,128)(2,1)S(1)} collective-permute-done((bf16[64,512]{1,0:T(8,128)(2,1)S(1)}, bf16[64,512]{1,0:T(8,128)(2,1)S(1)}, u32[]{:S(2)}, u32[]{:S(2)}) %collective-permute-start.33) | collective-permute-done | bytes 65568 | tf_op jit(solution)/shard_map/ppermute | solution.py:51
  (84 shorter events, 15.9 us)
Async XLA Ops:
  1.0 8.3 %collective-permute-start = (bf16[1,80,512]{2,1,0:T(8,128)(2,1)S(1)}, bf16[1,80,512]{2,1,0:T(8,128)(2,1)S(1)}, u32[]{:S(2)}, u32[]{:S(2)}) collective-permute-start(bf16[1,80,512]{2,1,0:T(8,128)(2,1)S(1)} %maximum_bitcast_fusion), channel_id=1, source_target_pairs={{0,8},{1,9},{2,10},{3,11},{4,12},{5,13},{6,14},{7,15},{8,0},{9,1},... | collective-permute-start | bytes 245768 | tf_op jit(solution)/shard_map/ppermute | solution.py:32
  9.3 5.4 %collective-permute-start.1 = (bf16[2,80,512]{2,1,0:T(8,128)(2,1)S(1)}, bf16[2,80,512]{2,1,0:T(8,128)(2,1)S(1)}, u32[]{:S(2)}, u32[]{:S(2)}) collective-permute-start(bf16[2,80,512]{2,1,0:T(8,128)(2,1)S(1)} %pad_maximum_fusion.refs_0_), channel_id=1, source_target_pairs={{0,4},{1,5},{2,6},{3,7},{4,0},{5,1},{6,2},{7,3},{8,12},{9,13},{10,... | collective-permute-start | bytes 491528 | tf_op jit(solution)/shard_map/ppermute | solution.py:32
  10.1 6.3 %collective-permute-start.4 = (bf16[2,80,512]{2,1,0:T(8,128)(2,1)S(1)}, bf16[2,80,512]{2,1,0:T(8,128)(2,1)S(1)}, u32[]{:S(2)}, u32[]{:S(2)}) collective-permute-start(bf16[2,80,512]{2,1,0:T(8,128)(2,1)S(1)} %pad_maximum_fusion.refs_0_), channel_id=1, source_target_pairs={{0,1},{1,0},{2,3},{3,2},{4,5},{5,4},{6,7},{7,6},{8,9},{9,8},{10,11... | collective-permute-start | bytes 491528 | tf_op jit(solution)/shard_map/ppermute | solution.py:32
  10.1 9.3 %collective-permute-start.3 = (bf16[2,80,512]{2,1,0:T(8,128)(2,1)S(1)}, bf16[2,80,512]{2,1,0:T(8,128)(2,1)S(1)}, u32[]{:S(2)}, u32[]{:S(2)}) collective-permute-start(bf16[2,80,512]{2,1,0:T(8,128)(2,1)S(1)} %pad_maximum_fusion.refs_0_), channel_id=1, source_target_pairs={{0,2},{1,3},{2,0},{3,1},{4,6},{5,7},{6,4},{7,5},{8,10},{9,11},{10,... | collective-permute-start | bytes 491528 | tf_op jit(solution)/shard_map/ppermute | solution.py:32
  14.7 5.8 %collective-permute-start.2 = (bf16[2,80,512]{2,1,0:T(8,128)(2,1)S(1)}, bf16[2,80,512]{2,1,0:T(8,128)(2,1)S(1)}, u32[]{:S(2)}, u32[]{:S(2)}) collective-permute-start(bf16[2,80,512]{2,1,0:T(8,128)(2,1)S(1)} %collective-permute-done.1.refs_0_), channel_id=1, source_target_pairs={{0,2},{1,3},{2,0},{3,1},{4,6},{5,7},{6,4},{7,5},{8,10},{9,11},{10,... | collective-permute-start | bytes 491528 | tf_op jit(solution)/shard_map/ppermute | solution.py:32
  20.0 1.5 %collective-permute-start.6 = (bf16[2,80,512]{2,1,0:T(8,128)(2,1)S(1)}, bf16[2,80,512]{2,1,0:T(8,128)(2,1)S(1)}, u32[]{:S(2)}, u32[]{:S(2)}) collective-permute-start(bf16[2,80,512]{2,1,0:T(8,128)(2,1)S(1)} %collective-permute-done.1.refs_0_), channel_id=1, source_target_pairs={{0,1},{1,0},{2,3},{3,2},{4,5},{5,4},{6,7},{7,6},{8,9},{9,8},{10,11... | collective-permute-start | bytes 491528 | tf_op jit(solution)/shard_map/ppermute | solution.py:32
  20.1 1.6 %collective-permute-start.7 = (bf16[2,80,512]{2,1,0:T(8,128)(2,1)S(1)}, bf16[2,80,512]{2,1,0:T(8,128)(2,1)S(1)}, u32[]{:S(2)}, u32[]{:S(2)}) collective-permute-start(bf16[2,80,512]{2,1,0:T(8,128)(2,1)S(1)} %collective-permute-done.3.refs_1_), channel_id=1, source_target_pairs={{0,1},{1,0},{2,3},{3,2},{4,5},{5,4},{6,7},{7,6},{8,9},{9,8},{10,11... | collective-permute-start | bytes 491528 | tf_op jit(solution)/shard_map/ppermute | solution.py:32
  20.6 1.9 %collective-permute-start.5 = (bf16[2,80,512]{2,1,0:T(8,128)(2,1)S(1)}, bf16[2,80,512]{2,1,0:T(8,128)(2,1)S(1)}, u32[]{:S(2)}, u32[]{:S(2)}) collective-permute-start(bf16[2,80,512]{2,1,0:T(8,128)(2,1)S(1)} %collective-permute-done.2.refs_0_), channel_id=1, source_target_pairs={{0,1},{1,0},{2,3},{3,2},{4,5},{5,4},{6,7},{7,6},{8,9},{9,8},{10,11... | collective-permute-start | bytes 491528 | tf_op jit(solution)/shard_map/ppermute | solution.py:32
  40.4 5.0 %collective-permute-start.8 = (bf16[1,4,4096]{2,1,0:T(4,128)(2,1)S(1)}, bf16[1,4,4096]{2,1,0:T(4,128)(2,1)S(1)}, u32[]{:S(2)}, u32[]{:S(2)}) collective-permute-start(bf16[1,4,4096]{2,1,0:T(4,128)(2,1)S(1)} %attend.2), channel_id=1, source_target_pairs={{0,8},{1,9},{2,10},{3,11},{4,12},{5,13},{6,14},{7,15},{8,0},{9,1},... | collective-permute-start | bytes 98312 | tf_op jit(solution)/shard_map/ppermute | solution.py:32
  45.5 5.0 %collective-permute-start.11 = (bf16[2,4,4096]{2,1,0:T(4,128)(2,1)S(1)}, bf16[2,4,4096]{2,1,0:T(4,128)(2,1)S(1)}, u32[]{:S(2)}, u32[]{:S(2)}) collective-permute-start(bf16[2,4,4096]{2,1,0:T(4,128)(2,1)S(1)} %pad_maximum_fusion.2.refs_0_), channel_id=1, source_target_pairs={{0,4},{1,5},{2,6},{3,7},{4,0},{5,1},{6,2},{7,3},{8,12},{9,13},{10,... | collective-permute-start | bytes 196616 | tf_op jit(solution)/shard_map/ppermute | solution.py:32
  45.8 4.9 %collective-permute-start.10 = (bf16[2,4,4096]{2,1,0:T(4,128)(2,1)S(1)}, bf16[2,4,4096]{2,1,0:T(4,128)(2,1)S(1)}, u32[]{:S(2)}, u32[]{:S(2)}) collective-permute-start(bf16[2,4,4096]{2,1,0:T(4,128)(2,1)S(1)} %pad_maximum_fusion.2.refs_0_), channel_id=1, source_target_pairs={{0,2},{1,3},{2,0},{3,1},{4,6},{5,7},{6,4},{7,5},{8,10},{9,11},{10,... | collective-permute-start | bytes 196616 | tf_op jit(solution)/shard_map/ppermute | solution.py:32
  46.8 5.2 %collective-permute-start.9 = (bf16[2,4,4096]{2,1,0:T(4,128)(2,1)S(1)}, bf16[2,4,4096]{2,1,0:T(4,128)(2,1)S(1)}, u32[]{:S(2)}, u32[]{:S(2)}) collective-permute-start(bf16[2,4,4096]{2,1,0:T(4,128)(2,1)S(1)} %pad_maximum_fusion.2.refs_0_), channel_id=1, source_target_pairs={{0,6},{1,7},{2,4},{3,5},{4,2},{5,3},{6,0},{7,1},{8,14},{9,15},{10,... | collective-permute-start | bytes 196616 | tf_op jit(solution)/shard_map/ppermute | solution.py:32
  49.0 3.0 %collective-permute-start.12 = (bf16[2,4,4096]{2,1,0:T(4,128)(2,1)S(1)}, bf16[2,4,4096]{2,1,0:T(4,128)(2,1)S(1)}, u32[]{:S(2)}, u32[]{:S(2)}) collective-permute-start(bf16[2,4,4096]{2,1,0:T(4,128)(2,1)S(1)} %pad_maximum_fusion.2.refs_0_), channel_id=1, source_target_pairs={{0,1},{1,0},{2,3},{3,2},{4,5},{5,4},{6,7},{7,6},{8,9},{9,8},{10,11... | collective-permute-start | bytes 196616 | tf_op jit(solution)/shard_map/ppermute | solution.py:32
  50.5 1.5 %collective-permute-start.15 = (bf16[2,4,4096]{2,1,0:T(4,128)(2,1)S(1)}, bf16[2,4,4096]{2,1,0:T(4,128)(2,1)S(1)}, u32[]{:S(2)}, u32[]{:S(2)}) collective-permute-start(bf16[2,4,4096]{2,1,0:T(4,128)(2,1)S(1)} %collective-permute-done.11.refs_3_), channel_id=1, source_target_pairs={{0,1},{1,0},{2,3},{3,2},{4,5},{5,4},{6,7},{7,6},{8,9},{9,8},{10,11... | collective-permute-start | bytes 196616 | tf_op jit(solution)/shard_map/ppermute | solution.py:32
  50.7 1.4 %collective-permute-start.14 = (bf16[2,4,4096]{2,1,0:T(4,128)(2,1)S(1)}, bf16[2,4,4096]{2,1,0:T(4,128)(2,1)S(1)}, u32[]{:S(2)}, u32[]{:S(2)}) collective-permute-start(bf16[2,4,4096]{2,1,0:T(4,128)(2,1)S(1)} %collective-permute-done.10.refs_2_), channel_id=1, source_target_pairs={{0,1},{1,0},{2,3},{3,2},{4,5},{5,4},{6,7},{7,6},{8,9},{9,8},{10,11... | collective-permute-start | bytes 196616 | tf_op jit(solution)/shard_map/ppermute | solution.py:32
  54.3 4.3 %collective-permute-start.17 = (bf16[64,512]{1,0:T(8,128)(2,1)S(1)}, bf16[64,512]{1,0:T(8,128)(2,1)S(1)}, u32[]{:S(2)}, u32[]{:S(2)}) collective-permute-start(bf16[64,512]{1,0:T(8,128)(2,1)S(1)} %output.2), channel_id=1, source_target_pairs={{0,16},{1,17},{2,18},{3,19},{4,20},{5,21},{6,22},{7,23},{8,24},{9,... | collective-permute-start | bytes 196616 | tf_op jit(solution)/shard_map/ppermute | solution.py:51
  55.9 7.1 %collective-permute-start.16 = (bf16[64,512]{1,0:T(8,128)(2,1)S(1)}, bf16[64,512]{1,0:T(8,128)(2,1)S(1)}, u32[]{:S(2)}, u32[]{:S(2)}) collective-permute-start(bf16[64,512]{1,0:T(8,128)(2,1)S(1)} %output.2), channel_id=1, source_target_pairs={{0,24},{1,25},{2,26},{3,27},{4,28},{5,29},{6,30},{7,31},{8,16},{9,... | collective-permute-start | bytes 196616 | tf_op jit(solution)/shard_map/ppermute | solution.py:51
  63.0 5.0 %collective-permute-start.18 = (bf16[2,64,512]{2,1,0:T(8,128)(2,1)S(1)}, bf16[2,64,512]{2,1,0:T(8,128)(2,1)S(1)}, u32[]{:S(2)}, u32[]{:S(2)}) collective-permute-start(bf16[2,64,512]{2,1,0:T(8,128)(2,1)S(1)} %pad_maximum_fusion.1.refs_0_), channel_id=1, source_target_pairs={{0,4},{1,5},{2,6},{3,7},{4,0},{5,1},{6,2},{7,3},{8,12},{9,13},{10,... | collective-permute-start | bytes 393224 | tf_op jit(solution)/shard_map/ppermute | solution.py:32
  63.1 6.3 %collective-permute-start.21 = (bf16[2,64,512]{2,1,0:T(8,128)(2,1)S(1)}, bf16[2,64,512]{2,1,0:T(8,128)(2,1)S(1)}, u32[]{:S(2)}, u32[]{:S(2)}) collective-permute-start(bf16[2,64,512]{2,1,0:T(8,128)(2,1)S(1)} %pad_maximum_fusion.1.refs_0_), channel_id=1, source_target_pairs={{0,1},{1,0},{2,3},{3,2},{4,5},{5,4},{6,7},{7,6},{8,9},{9,8},{10,11... | collective-permute-start | bytes 393224 | tf_op jit(solution)/shard_map/ppermute | solution.py:32
  63.1 6.8 %collective-permute-start.20 = (bf16[2,64,512]{2,1,0:T(8,128)(2,1)S(1)}, bf16[2,64,512]{2,1,0:T(8,128)(2,1)S(1)}, u32[]{:S(2)}, u32[]{:S(2)}) collective-permute-start(bf16[2,64,512]{2,1,0:T(8,128)(2,1)S(1)} %pad_maximum_fusion.1.refs_0_), channel_id=1, source_target_pairs={{0,2},{1,3},{2,0},{3,1},{4,6},{5,7},{6,4},{7,5},{8,10},{9,11},{10,... | collective-permute-start | bytes 393224 | tf_op jit(solution)/shard_map/ppermute | solution.py:32
  68.0 5.0 %collective-permute-start.19 = (bf16[2,64,512]{2,1,0:T(8,128)(2,1)S(1)}, bf16[2,64,512]{2,1,0:T(8,128)(2,1)S(1)}, u32[]{:S(2)}, u32[]{:S(2)}) collective-permute-start(bf16[2,64,512]{2,1,0:T(8,128)(2,1)S(1)} %collective-permute-done.18.refs_0_), channel_id=1, source_target_pairs={{0,2},{1,3},{2,0},{3,1},{4,6},{5,7},{6,4},{7,5},{8,10},{9,11},{10,... | collective-permute-start | bytes 393224 | tf_op jit(solution)/shard_map/ppermute | solution.py:32
  70.4 2.6 %collective-permute-start.23 = (bf16[2,64,512]{2,1,0:T(8,128)(2,1)S(1)}, bf16[2,64,512]{2,1,0:T(8,128)(2,1)S(1)}, u32[]{:S(2)}, u32[]{:S(2)}) collective-permute-start(bf16[2,64,512]{2,1,0:T(8,128)(2,1)S(1)} %collective-permute-done.18.refs_0_), channel_id=1, source_target_pairs={{0,1},{1,0},{2,3},{3,2},{4,5},{5,4},{6,7},{7,6},{8,9},{9,8},{10,11... | collective-permute-start | bytes 393224 | tf_op jit(solution)/shard_map/ppermute | solution.py:32
  70.5 2.5 %collective-permute-start.24 = (bf16[2,64,512]{2,1,0:T(8,128)(2,1)S(1)}, bf16[2,64,512]{2,1,0:T(8,128)(2,1)S(1)}, u32[]{:S(2)}, u32[]{:S(2)}) collective-permute-start(bf16[2,64,512]{2,1,0:T(8,128)(2,1)S(1)} %collective-permute-done.20.refs_1_), channel_id=1, source_target_pairs={{0,1},{1,0},{2,3},{3,2},{4,5},{5,4},{6,7},{7,6},{8,9},{9,8},{10,11... | collective-permute-start | bytes 393224 | tf_op jit(solution)/shard_map/ppermute | solution.py:32
  73.0 1.3 %collective-permute-start.22 = (bf16[2,64,512]{2,1,0:T(8,128)(2,1)S(1)}, bf16[2,64,512]{2,1,0:T(8,128)(2,1)S(1)}, u32[]{:S(2)}, u32[]{:S(2)}) collective-permute-start(bf16[2,64,512]{2,1,0:T(8,128)(2,1)S(1)} %collective-permute-done.19.refs_0_), channel_id=1, source_target_pairs={{0,1},{1,0},{2,3},{3,2},{4,5},{5,4},{6,7},{7,6},{8,9},{9,8},{10,11... | collective-permute-start | bytes 393224 | tf_op jit(solution)/shard_map/ppermute | solution.py:32
  86.3 4.9 %collective-permute-start.25 = (bf16[1,4,4096]{2,1,0:T(4,128)(2,1)S(1)}, bf16[1,4,4096]{2,1,0:T(4,128)(2,1)S(1)}, u32[]{:S(2)}, u32[]{:S(2)}) collective-permute-start(bf16[1,4,4096]{2,1,0:T(4,128)(2,1)S(1)} %attend.3), channel_id=1, source_target_pairs={{0,8},{1,9},{2,10},{3,11},{4,12},{5,13},{6,14},{7,15},{8,0},{9,1},... | collective-permute-start | bytes 98312 | tf_op jit(solution)/shard_map/ppermute | solution.py:32
  91.2 4.3 %collective-permute-start.28 = (bf16[2,4,4096]{2,1,0:T(4,128)(2,1)S(1)}, bf16[2,4,4096]{2,1,0:T(4,128)(2,1)S(1)}, u32[]{:S(2)}, u32[]{:S(2)}) collective-permute-start(bf16[2,4,4096]{2,1,0:T(4,128)(2,1)S(1)} %pad_maximum_fusion.3.refs_0_), channel_id=1, source_target_pairs={{0,4},{1,5},{2,6},{3,7},{4,0},{5,1},{6,2},{7,3},{8,12},{9,13},{10,... | collective-permute-start | bytes 196616 | tf_op jit(solution)/shard_map/ppermute | solution.py:32
  91.5 4.3 %collective-permute-start.27 = (bf16[2,4,4096]{2,1,0:T(4,128)(2,1)S(1)}, bf16[2,4,4096]{2,1,0:T(4,128)(2,1)S(1)}, u32[]{:S(2)}, u32[]{:S(2)}) collective-permute-start(bf16[2,4,4096]{2,1,0:T(4,128)(2,1)S(1)} %pad_maximum_fusion.3.refs_0_), channel_id=1, source_target_pairs={{0,2},{1,3},{2,0},{3,1},{4,6},{5,7},{6,4},{7,5},{8,10},{9,11},{10,... | collective-permute-start | bytes 196616 | tf_op jit(solution)/shard_map/ppermute | solution.py:32
  92.2 5.2 %collective-permute-start.26 = (bf16[2,4,4096]{2,1,0:T(4,128)(2,1)S(1)}, bf16[2,4,4096]{2,1,0:T(4,128)(2,1)S(1)}, u32[]{:S(2)}, u32[]{:S(2)}) collective-permute-start(bf16[2,4,4096]{2,1,0:T(4,128)(2,1)S(1)} %pad_maximum_fusion.3.refs_0_), channel_id=1, source_target_pairs={{0,6},{1,7},{2,4},{3,5},{4,2},{5,3},{6,0},{7,1},{8,14},{9,15},{10,... | collective-permute-start | bytes 196616 | tf_op jit(solution)/shard_map/ppermute | solution.py:32
  94.8 2.5 %collective-permute-start.29 = (bf16[2,4,4096]{2,1,0:T(4,128)(2,1)S(1)}, bf16[2,4,4096]{2,1,0:T(4,128)(2,1)S(1)}, u32[]{:S(2)}, u32[]{:S(2)}) collective-permute-start(bf16[2,4,4096]{2,1,0:T(4,128)(2,1)S(1)} %pad_maximum_fusion.3.refs_0_), channel_id=1, source_target_pairs={{0,1},{1,0},{2,3},{3,2},{4,5},{5,4},{6,7},{7,6},{8,9},{9,8},{10,11... | collective-permute-start | bytes 196616 | tf_op jit(solution)/shard_map/ppermute | solution.py:32
  95.6 1.8 %collective-permute-start.32 = (bf16[2,4,4096]{2,1,0:T(4,128)(2,1)S(1)}, bf16[2,4,4096]{2,1,0:T(4,128)(2,1)S(1)}, u32[]{:S(2)}, u32[]{:S(2)}) collective-permute-start(bf16[2,4,4096]{2,1,0:T(4,128)(2,1)S(1)} %collective-permute-done.28.refs_3_), channel_id=1, source_target_pairs={{0,1},{1,0},{2,3},{3,2},{4,5},{5,4},{6,7},{7,6},{8,9},{9,8},{10,11... | collective-permute-start | bytes 196616 | tf_op jit(solution)/shard_map/ppermute | solution.py:32
  95.8 1.5 %collective-permute-start.31 = (bf16[2,4,4096]{2,1,0:T(4,128)(2,1)S(1)}, bf16[2,4,4096]{2,1,0:T(4,128)(2,1)S(1)}, u32[]{:S(2)}, u32[]{:S(2)}) collective-permute-start(bf16[2,4,4096]{2,1,0:T(4,128)(2,1)S(1)} %collective-permute-done.27.refs_2_), channel_id=1, source_target_pairs={{0,1},{1,0},{2,3},{3,2},{4,5},{5,4},{6,7},{7,6},{8,9},{9,8},{10,11... | collective-permute-start | bytes 196616 | tf_op jit(solution)/shard_map/ppermute | solution.py:32
  99.6 4.3 %collective-permute-start.33 = (bf16[64,512]{1,0:T(8,128)(2,1)S(1)}, bf16[64,512]{1,0:T(8,128)(2,1)S(1)}, u32[]{:S(2)}, u32[]{:S(2)}) collective-permute-start(bf16[64,512]{1,0:T(8,128)(2,1)S(1)} %output.3), channel_id=1, source_target_pairs={{0,16},{1,17},{2,18},{3,19},{4,20},{5,21},{6,22},{7,23},{8,24},{9,... | collective-permute-start | bytes 196616 | tf_op jit(solution)/shard_map/ppermute | solution.py:51
  (14 other events, 261.6 us)

commit v7 on v6

--- a/solution.py
+++ b/solution.py
@@ -37,8 +37,15 @@
     for phase in phases:
         merged = block if len(held) == 1 else jnp.concatenate([b for _, b in held], axis=0)
         names = [m for n, _ in held for m in n]
-        if phase == phases[-1] and len(phase) == 1:
-            return held + [([phase[0] ^ m for m in n], exchange(b, phase[0])) for n, b in held]
+        if phase == phases[-1]:
+            core = phase[0]
+            for some in [[0, 3], [2], [1]]:
+                both = [held[k] for k in some]
+                away = [core ^ m for n, _ in both for m in n]
+                both = [b for _, b in both]
+                both = both[0] if len(both) == 1 else jnp.concatenate(both, axis=0)
+                held = held + [(away, exchange(both, core))]
+            return held
         if len(held) > 1:
             held = [(names, merged)]
         held = held + [([m ^ n for n in names], exchange(merged, m)) for m in phase]
@@ -78,7 +85,9 @@
     return -(-(columns // 2) // LANES) * LANES
 
 
-def pack_kernel(dest_ref, pages_ref, send_ref):
+def pack_kernel(dest_ref, pages_ref, x_ref, gain_ref, send_ref, x_out, gain_out):
+    x_out[...] = x_ref[...]
+    gain_out[...] = gain_ref[...]
     own = lax.axis_index("slot")
     slots, page_tok, wide = send_ref.shape
     kv_width = pages_ref.shape[2]
@@ -88,18 +97,22 @@
         send_ref[j, :, kv_width:] = jnp.zeros((page_tok, wide - kv_width), send_ref.dtype)
 
 
-def pack(pages, dest, room):
+def pack(pages, dest, x, gain, room):
     _, page_tok, kv_width = pages.shape
     whole = pl.BlockSpec(memory_space=pltpu.VMEM)
     scalars = pl.BlockSpec(memory_space=pltpu.SMEM)
     return pl.pallas_call(
         pack_kernel,
-        out_shape=jax.ShapeDtypeStruct((dest.shape[0], page_tok, kv_width + room), pages.dtype),
-        in_specs=[scalars, whole],
-        out_specs=whole,
+        out_shape=[
+            jax.ShapeDtypeStruct((dest.shape[0], page_tok, kv_width + room), pages.dtype),
+            jax.ShapeDtypeStruct(x.shape, x.dtype),
+            jax.ShapeDtypeStruct(gain.shape, gain.dtype),
+        ],
+        in_specs=[scalars] + [whole] * 3,
+        out_specs=[whole] * 3,
         compiler_params=params(),
         name="pack",
-    )(dest, pages)
+    )(dest, pages, x, gain)
 
 
 def project_kernel(w_ref, *refs, away, rows, carried, first, last, packed, batch):
@@ -112,16 +125,17 @@
         refs.pop(0)
     if carried:
         kept = refs.pop(0)
-    blocks, _, width = x_refs[0].shape
+    blocks, width = len(away[0]), x_refs[0].shape[1]
     columns, model_width = w_ref.shape
     acc = jnp.zeros((rows, columns), jnp.float32) if first else acc_in[...]
     square = jnp.zeros((rows, LANES), jnp.float32) if first else square_in[...]
     for g, masks in enumerate(away):
+        if carried:
+            kept[g] = x_refs[g][blocks * rows:]
+        gains = kept[g].astype(jnp.float32)
         for i in range(blocks):
-            if carried:
-                kept[g * blocks + i] = x_refs[g][i, rows:]
-            x = x_refs[g][i, :rows]
-            gain = kept[g * blocks + i].astype(jnp.float32)[:1]
+            x = x_refs[g][i * rows:(i + 1) * rows]
+            gain = gains[i:i + 1]
             parts = []
             for r in range(0, width, LANES):
                 part = x[:, r:r + LANES].astype(jnp.float32)
@@ -151,7 +165,7 @@
 
 
 def project(rows, batch, weight, groups, gains, state, last=False, outgoing=None):
-    blocks, held, width = groups[0][1].shape
+    blocks, (held, width) = len(groups[0][0]), groups[0][1].shape
     columns = weight.shape[0]
     carried, first, packed = gains is None, state is None, outgoing is not None
     operands = [weight] + [x for _, x in groups] + ([] if carried else [gains])
@@ -159,7 +173,7 @@
     aliases = {}
     out_shape = []
     if carried:
-        out_shape.append(jax.ShapeDtypeStruct((len(groups) * blocks, held - rows, width),
+        out_shape.append(jax.ShapeDtypeStruct((len(groups), held - blocks * rows, width),
                                               jnp.bfloat16))
     if packed:
         aliases = {len(operands): len(out_shape)}
@@ -339,7 +353,7 @@
     kv_width = cache_kv.shape[5]
     masks = [slots >> (k + 1) for k in range(slots.bit_length() - 1)]
     across, over, core = masks[-3:]
-    phases = [[mask] for mask in masks[:-3]] + [[across ^ over, over, across], [core]]
+    phases = [[mask] for mask in masks[:-3]] + [[across, over, across ^ over], [core]]
     offsets = [masks[0], 0]
     for mask in masks[1:]:
         offsets = offsets + [mask ^ o for o in offsets]
@@ -353,15 +367,19 @@
     gains = [None] * 5
     for visit in range(CYCLE_STEPS):
         if visit == 0:
-            spare = jnp.zeros((15, width), norm_gain.dtype)
-            block = jnp.concatenate([current, norm_gain, spare], axis=0)[None]
-            block = jnp.concatenate([exchange(block, masks[0]), block], axis=0)
-            outgoing = pack(page_kv[0, 0], page_dest[0], room_for(columns))
-            block, outgoing = lax.optimization_barrier((block, outgoing))
+            block, gain = exchange(current, masks[0]), exchange(norm_gain, masks[0])
+            outgoing, current, mine = pack(page_kv[0, 0], page_dest[0], current, norm_gain,
+                                           room_for(columns))
+            block, gain = jnp.concatenate([block, current]), jnp.concatenate([gain, mine])
         else:
-            block = jnp.stack([beyond, current])
+            block = jnp.concatenate([beyond, current])
         for mask in masks[1:-3]:
-            block = jnp.concatenate([block, exchange(block, mask)], axis=0)
+            block = jnp.concatenate([block, exchange(block, mask)])
+            if visit == 0:
+                gain = jnp.concatenate([gain, exchange(gain, mask)])
+        if visit == 0:
+            spare = jnp.zeros((-gain.shape[0] % 16, width), gain.dtype)
+            block = jnp.concatenate([block, gain, spare])
         size = slots // 8
         away = [offsets[g * size:(g + 1) * size] for g in range(8)]
         run = functools.partial(project, rows, batch, weight_in)

time: 105 us -> 101 us (0.962)
  waiting for transfers between devices: 36.7 us -> 32.2 us
  local copies, waits for them, and re-layouts: 4.9 us -> 6.52 us
  blocking collectives: 27.4 us -> 25.9 us
  starting transfers between devices: 25.6 us -> 27.1 us
    ppermute x31 -> x30, waiting for transfers between devices: 27.3 us -> 24.8 us  [exchange(): return lax.ppermute(block, 'slot', [(i, i ^ mask) for i in range(n)])]
    ppermute x3, waiting for transfers between devices: 9.4 us -> 7.46 us  [next_segment(): return lax.ppermute(block, ('segment', 'slot'), route)]
    unnamed x25 -> x28, local copies, waits for them, and re-layouts: 4.82 us -> 6.34 us
    all_to_all x2, blocking collectives: 27.4 us -> 25.9 us  [shards(): qkv = lax.all_to_all(qkv, 'slot', split_axis=0, concat_axis=0, tiled=True)]
    ppermute x31 -> x30, starting transfers between devices: 22 us -> 22.7 us  [exchange(): return lax.ppermute(block, 'slot', [(i, i ^ mask) for i in range(n)])]
  transfers between devices with their start and end apart: 34 -> 33, of which waited for: 20 -> 20; matrix products, arithmetic and copies ran while one was open for 0% -> 0% of each run, Pallas kernels for 4% -> 4%
where the time goes in v7:
time: 101 us
  waiting for transfers between devices  32.2 us (32%)
  starting transfers between devices  27.1 us (27%)
  blocking collectives  25.9 us (26%)
  Pallas kernels  8.62 us (9%)
  local copies, waits for them, and re-layouts  6.52 us (6%)
    all_to_all x2, blocking collectives, shards(): qkv = lax.all_to_all(qkv, 'slot', split_axis=0, concat_axis=0, tiled=True)  25.9 us
    ppermute x30, waiting for transfers between devices, exchange(): return lax.ppermute(block, 'slot', [(i, i ^ mask) for i in range(n)])  24.8 us
    ppermute x30, starting transfers between devices, exchange(): return lax.ppermute(block, 'slot', [(i, i ^ mask) for i in range(n)])  22.7 us
    ppermute x3, waiting for transfers between devices, next_segment(): return lax.ppermute(block, ('segment', 'slot'), route)  7.46 us
    unnamed x28, local copies, waits for them, and re-layouts  6.34 us
    pallas_call x8, Pallas kernels, project(): pl.pallas_call(functools.partial(project_kernel, away=[masks for masks, _...  4.56 us
    ppermute x3, starting transfers between devices, next_segment(): return lax.ppermute(block, ('segment', 'slot'), route)  4.41 us
    pallas_call x2, Pallas kernels, output(): pl.pallas_call(functools.partial(output_kernel, slots=slots, batch=batch,...  2.05 us
  transfers between devices with their start and end apart: 33, of which 20 were waited for; matrix products, arithmetic and copies ran while one was open for 0% of the time, Pallas kernels for 4%

profile of v7, /device:TPU:0, one launch (start us, length us, event | category | flops | bytes accessed | tf_op | source)
XLA Modules:
  0.0 101.0 jit_solution(7785964415581659220)
XLA Ops:
  0.0 4.0 %collective-permute-start = (bf16[64,512]{1,0:T(8,128)(2,1)}, bf16[64,512]{1,0:T(8,128)(2,1)S(1)}, u32[]{:S(2)}, u32[]{:S(2)}) collective-permute-start(bf16[64,512]{1,0:T(8,128)(2,1)} %bitcast.33), channel_id=1, source_target_pairs={{0,8},{1,9},{2,10},{3,11},{4,12},{5,13},{6,14},{7,15},{8,0},{9,1},... | collective-permute-start | bytes 196616 | tf_op jit(solution)/shard_map/ppermute | solution.py:32
  4.1 0.9 copy-done.3
  5.7 0.8 copy-done.6
  8.0 0.8 collective-permute-done.1
  8.9 1.6 %collective-permute-start.2 = (bf16[144,512]{1,0:T(8,128)(2,1)S(1)}, bf16[144,512]{1,0:T(8,128)(2,1)S(1)}, u32[]{:S(2)}, u32[]{:S(2)}) collective-permute-start(bf16[144,512]{1,0:T(8,128)(2,1)S(1)} %concatenate.20.refs_0_), channel_id=1, source_target_pairs={{0,4},{1,5},{2,6},{3,7},{4,0},{5,1},{6,2},{7,3},{8,12},{9,13},{10,... | collective-permute-start | bytes 442376 | tf_op jit(solution)/shard_map/ppermute | solution.py:32
  10.6 1.5 %collective-permute-start.4 = (bf16[144,512]{1,0:T(8,128)(2,1)S(1)}, bf16[144,512]{1,0:T(8,128)(2,1)S(1)}, u32[]{:S(2)}, u32[]{:S(2)}) collective-permute-start(bf16[144,512]{1,0:T(8,128)(2,1)S(1)} %concatenate.20.refs_0_), channel_id=1, source_target_pairs={{0,2},{1,3},{2,0},{3,1},{4,6},{5,7},{6,4},{7,5},{8,10},{9,11},{10,... | collective-permute-start | bytes 442376 | tf_op jit(solution)/shard_map/ppermute | solution.py:32
  12.1 2.1 %collective-permute-done.2.refs_0_ = bf16[144,512]{1,0:T(8,128)(2,1)S(1)} collective-permute-done((bf16[144,512]{1,0:T(8,128)(2,1)S(1)}, bf16[144,512]{1,0:T(8,128)(2,1)S(1)}, u32[]{:S(2)}, u32[]{:S(2)}) %collective-permute-start.2) | collective-permute-done | bytes 147488 | tf_op jit(solution)/shard_map/ppermute | solution.py:32
  14.1 1.5 %collective-permute-start.3 = (bf16[144,512]{1,0:T(8,128)(2,1)S(1)}, bf16[144,512]{1,0:T(8,128)(2,1)S(1)}, u32[]{:S(2)}, u32[]{:S(2)}) collective-permute-start(bf16[144,512]{1,0:T(8,128)(2,1)S(1)} %collective-permute-done.2.refs_0_), channel_id=1, source_target_pairs={{0,2},{1,3},{2,0},{3,1},{4,6},{5,7},{6,4},{7,5},{8,10},{9,11},{10,... | collective-permute-start | bytes 442376 | tf_op jit(solution)/shard_map/ppermute | solution.py:32
  15.6 2.5 %copy-done = bf16[1,8192,320]{1,2,0:T(8,128)(2,1)S(1)} copy-done((bf16[1,8192,320]{1,2,0:T(8,128)(2,1)S(1)}, bf16[1,8192,320]{1,2,0:T(8,128)(2,1)}, u32[]{:S(2)}) %copy-start) | copy-done | bytes 5242904
  22.2 15.6 %all_to_all.10.qkv_ref = bf16[16,8,1280]{2,1,0:T(8,128)(2,1)S(1)} all-to-all(bf16[16,8,1280]{2,1,0:T(8,128)(2,1)S(1)} %get-tuple-element.55), channel_id=1, replica_groups=mesh['segment'=2,'slot'=16] {'slot'}, dimensions={0} | all-to-all | bytes 655360 | tf_op jit(solution)/shard_map/all_to_all | solution.py:399
  38.5 1.4 %collective-permute-start.9 = (bf16[1,4,4096]{2,1,0:T(4,128)(2,1)S(1)}, bf16[1,4,4096]{2,1,0:T(4,128)(2,1)S(1)}, u32[]{:S(2)}, u32[]{:S(2)}) collective-permute-start(bf16[1,4,4096]{2,1,0:T(4,128)(2,1)S(1)} %attend.2), channel_id=1, source_target_pairs={{0,8},{1,9},{2,10},{3,11},{4,12},{5,13},{6,14},{7,15},{8,0},{9,1},... | collective-permute-start | bytes 98312 | tf_op jit(solution)/shard_map/ppermute | solution.py:32
  40.0 3.6 %collective-permute-done.9 = bf16[1,4,4096]{2,1,0:T(4,128)(2,1)S(1)} collective-permute-done((bf16[1,4,4096]{2,1,0:T(4,128)(2,1)S(1)}, bf16[1,4,4096]{2,1,0:T(4,128)(2,1)S(1)}, u32[]{:S(2)}, u32[]{:S(2)}) %collective-permute-start.9) | collective-permute-done | bytes 32800 | tf_op jit(solution)/shard_map/ppermute | solution.py:32
  43.6 0.8 collective-permute-start.12
  44.4 0.9 collective-permute-start.11
  45.4 1.8 %collective-permute-start.10 = (bf16[2,4,4096]{2,1,0:T(4,128)(2,1)S(1)}, bf16[2,4,4096]{2,1,0:T(4,128)(2,1)S(1)}, u32[]{:S(2)}, u32[]{:S(2)}) collective-permute-start(bf16[2,4,4096]{2,1,0:T(4,128)(2,1)S(1)} %pad_maximum_fusion.2.refs_0_), channel_id=1, source_target_pairs={{0,4},{1,5},{2,6},{3,7},{4,0},{5,1},{6,2},{7,3},{8,12},{9,13},{10,... | collective-permute-start | bytes 196616 | tf_op jit(solution)/shard_map/ppermute | solution.py:32
  47.2 1.8 %collective-permute-done.12.refs_3_ = bf16[2,4,4096]{2,1,0:T(4,128)(2,1)S(1)} collective-permute-done((bf16[2,4,4096]{2,1,0:T(4,128)(2,1)S(1)}, bf16[2,4,4096]{2,1,0:T(4,128)(2,1)S(1)}, u32[]{:S(2)}, u32[]{:S(2)}) %collective-permute-start.12) | collective-permute-done | bytes 65568 | tf_op jit(solution)/shard_map/ppermute | solution.py:32
  50.9 1.0 %output.2 = bf16[64,512]{1,0:T(8,128)(2,1)S(1)} custom-call(bf16[2,4,4096]{2,1,0:T(4,128)(2,1)S(1)} %pad_maximum_fusion.2.refs_0_, bf16[2,4,4096]{2,1,0:T(4,128)(2,1)S(1)} %collective-permute-done.10.refs_1_, bf16[2,4,4096]{2,1,0:T(4,128)(2,1)S(1)} %collective-permute-done.11.refs_2_, bf16[2,4,4096]{2,1,0:T(4,128)(2,1)S(1)} %collective-permute-done.12.refs_3_, ...), custom_call_target="tpu_custom_call" | custom-call | tf_op jit(solution)/shard_map/output/pallas_call | solution.py:337
  51.9 2.5 %collective-permute-start.16 = (bf16[64,512]{1,0:T(8,128)(2,1)S(1)}, bf16[64,512]{1,0:T(8,128)(2,1)S(1)}, u32[]{:S(2)}, u32[]{:S(2)}) collective-permute-start(bf16[64,512]{1,0:T(8,128)(2,1)S(1)} %output.2), channel_id=1, source_target_pairs={{0,24},{1,25},{2,26},{3,27},{4,28},{5,29},{6,30},{7,31},{8,16},{9,... | collective-permute-start | bytes 196616 | tf_op jit(solution)/shard_map/ppermute | solution.py:58
  54.9 4.6 %collective-permute-done.16 = bf16[64,512]{1,0:T(8,128)(2,1)S(1)} collective-permute-done((bf16[64,512]{1,0:T(8,128)(2,1)S(1)}, bf16[64,512]{1,0:T(8,128)(2,1)S(1)}, u32[]{:S(2)}, u32[]{:S(2)}) %collective-permute-start.16) | collective-permute-done | bytes 65568 | tf_op jit(solution)/shard_map/ppermute | solution.py:58
  59.5 1.7 %collective-permute-start.18 = (bf16[128,512]{1,0:T(8,128)(2,1)S(1)}, bf16[128,512]{1,0:T(8,128)(2,1)S(1)}, u32[]{:S(2)}, u32[]{:S(2)}) collective-permute-start(bf16[128,512]{1,0:T(8,128)(2,1)S(1)} %constant_dynamic-update-slice_fusion.refs_0_), channel_id=1, source_target_pairs={{0,4},{1,5},{2,6},{3,7},{4,0},{5,1},{6,2},{7,3},{8,12},{9,13},{10,... | collective-permute-start | bytes 393224 | tf_op jit(solution)/shard_map/ppermute | solution.py:32
  61.6 3.3 %collective-permute-done.18.refs_0_ = bf16[128,512]{1,0:T(8,128)(2,1)S(1)} collective-permute-done((bf16[128,512]{1,0:T(8,128)(2,1)S(1)}, bf16[128,512]{1,0:T(8,128)(2,1)S(1)}, u32[]{:S(2)}, u32[]{:S(2)}) %collective-permute-start.18) | collective-permute-done | bytes 131104 | tf_op jit(solution)/shard_map/ppermute | solution.py:32
  66.1 1.5 %collective-permute-done.20.refs_1_ = bf16[128,512]{1,0:T(8,128)(2,1)S(1)} collective-permute-done((bf16[128,512]{1,0:T(8,128)(2,1)S(1)}, bf16[128,512]{1,0:T(8,128)(2,1)S(1)}, u32[]{:S(2)}, u32[]{:S(2)}) %collective-permute-start.20) | collective-permute-done | bytes 131104 | tf_op jit(solution)/shard_map/ppermute | solution.py:32
  68.6 1.3 %collective-permute-done.19.refs_0_ = bf16[128,512]{1,0:T(8,128)(2,1)S(1)} collective-permute-done((bf16[128,512]{1,0:T(8,128)(2,1)S(1)}, bf16[128,512]{1,0:T(8,128)(2,1)S(1)}, u32[]{:S(2)}, u32[]{:S(2)}) %collective-permute-start.19) | collective-permute-done | bytes 131104 | tf_op jit(solution)/shard_map/ppermute | solution.py:32
  71.8 10.4 %all_to_all.11.qkv_ref = bf16[16,4,320]{2,1,0:T(4,128)(2,1)S(1)} all-to-all(bf16[16,4,320]{2,1,0:T(4,128)(2,1)S(1)} %project.15), channel_id=1, replica_groups=mesh['segment'=2,'slot'=16] {'slot'}, dimensions={0} | all-to-all | bytes 81920 | tf_op jit(solution)/shard_map/all_to_all | solution.py:399
  83.2 4.5 %collective-permute-done.25 = bf16[1,4,4096]{2,1,0:T(4,128)(2,1)S(1)} collective-permute-done((bf16[1,4,4096]{2,1,0:T(4,128)(2,1)S(1)}, bf16[1,4,4096]{2,1,0:T(4,128)(2,1)S(1)}, u32[]{:S(2)}, u32[]{:S(2)}) %collective-permute-start.25) | collective-permute-done | bytes 32800 | tf_op jit(solution)/shard_map/ppermute | solution.py:32
  88.1 1.4 %collective-permute-start.27 = (bf16[2,4,4096]{2,1,0:T(4,128)(2,1)S(1)}, bf16[2,4,4096]{2,1,0:T(4,128)(2,1)S(1)}, u32[]{:S(2)}, u32[]{:S(2)}) collective-permute-start(bf16[2,4,4096]{2,1,0:T(4,128)(2,1)S(1)} %pad_maximum_fusion.3.refs_0_), channel_id=1, source_target_pairs={{0,2},{1,3},{2,0},{3,1},{4,6},{5,7},{6,4},{7,5},{8,10},{9,11},{10,... | collective-permute-start | bytes 196616 | tf_op jit(solution)/shard_map/ppermute | solution.py:32
  89.5 1.8 %collective-permute-start.26 = (bf16[2,4,4096]{2,1,0:T(4,128)(2,1)S(1)}, bf16[2,4,4096]{2,1,0:T(4,128)(2,1)S(1)}, u32[]{:S(2)}, u32[]{:S(2)}) collective-permute-start(bf16[2,4,4096]{2,1,0:T(4,128)(2,1)S(1)} %pad_maximum_fusion.3.refs_0_), channel_id=1, source_target_pairs={{0,4},{1,5},{2,6},{3,7},{4,0},{5,1},{6,2},{7,3},{8,12},{9,13},{10,... | collective-permute-start | bytes 196616 | tf_op jit(solution)/shard_map/ppermute | solution.py:32
  91.3 1.8 %collective-permute-done.28.refs_3_ = bf16[2,4,4096]{2,1,0:T(4,128)(2,1)S(1)} collective-permute-done((bf16[2,4,4096]{2,1,0:T(4,128)(2,1)S(1)}, bf16[2,4,4096]{2,1,0:T(4,128)(2,1)S(1)}, u32[]{:S(2)}, u32[]{:S(2)}) %collective-permute-start.28) | collective-permute-done | bytes 65568 | tf_op jit(solution)/shard_map/ppermute | solution.py:32
  93.9 0.8 collective-permute-done.30.refs_5_
  95.0 1.0 %output.3 = bf16[64,512]{1,0:T(8,128)(2,1)S(1)} custom-call(bf16[2,4,4096]{2,1,0:T(4,128)(2,1)S(1)} %pad_maximum_fusion.3.refs_0_, bf16[2,4,4096]{2,1,0:T(4,128)(2,1)S(1)} %collective-permute-done.26.refs_1_, bf16[2,4,4096]{2,1,0:T(4,128)(2,1)S(1)} %collective-permute-done.27.refs_2_, bf16[2,4,4096]{2,1,0:T(4,128)(2,1)S(1)} %collective-permute-done.28.refs_3_, ...), custom_call_target="tpu_custom_call" | custom-call | tf_op jit(solution)/shard_map/output/pallas_call | solution.py:337
  96.1 1.4 %collective-permute-start.32 = (bf16[64,512]{1,0:T(8,128)(2,1)S(1)}, bf16[64,512]{1,0:T(8,128)(2,1)S(1)}, u32[]{:S(2)}, u32[]{:S(2)}) collective-permute-start(bf16[64,512]{1,0:T(8,128)(2,1)S(1)} %output.3), channel_id=1, source_target_pairs={{0,16},{1,17},{2,18},{3,19},{4,20},{5,21},{6,22},{7,23},{8,24},{9,... | collective-permute-start | bytes 196616 | tf_op jit(solution)/shard_map/ppermute | solution.py:58
  97.5 2.9 %collective-permute-done.32 = bf16[64,512]{1,0:T(8,128)(2,1)S(1)} collective-permute-done((bf16[64,512]{1,0:T(8,128)(2,1)S(1)}, bf16[64,512]{1,0:T(8,128)(2,1)S(1)}, u32[]{:S(2)}, u32[]{:S(2)}) %collective-permute-start.32) | collective-permute-done | bytes 65568 | tf_op jit(solution)/shard_map/ppermute | solution.py:58
  (85 shorter events, 17.0 us)
Async XLA Ops:
  0.0 8.7 %collective-permute-start = (bf16[64,512]{1,0:T(8,128)(2,1)}, bf16[64,512]{1,0:T(8,128)(2,1)S(1)}, u32[]{:S(2)}, u32[]{:S(2)}) collective-permute-start(bf16[64,512]{1,0:T(8,128)(2,1)} %bitcast.33), channel_id=1, source_target_pairs={{0,8},{1,9},{2,10},{3,11},{4,12},{5,13},{6,14},{7,15},{8,0},{9,1},... | collective-permute-start | bytes 196616 | tf_op jit(solution)/shard_map/ppermute | solution.py:32
  4.0 4.7 %collective-permute-start.1 = (bf16[1,512]{1,0:T(2,128)(2,1)}, bf16[1,512]{1,0:T(2,128)(2,1)S(1)}, u32[]{:S(2)}, u32[]{:S(2)}) collective-permute-start(bf16[1,512]{1,0:T(2,128)(2,1)} %gain_ref.1), channel_id=1, source_target_pairs={{0,8},{1,9},{2,10},{3,11},{4,12},{5,13},{6,14},{7,15},{8,0},{9,1},... | collective-permute-start | bytes 3080 | tf_op jit(solution)/shard_map/ppermute | solution.py:32
  8.9 5.2 %collective-permute-start.2 = (bf16[144,512]{1,0:T(8,128)(2,1)S(1)}, bf16[144,512]{1,0:T(8,128)(2,1)S(1)}, u32[]{:S(2)}, u32[]{:S(2)}) collective-permute-start(bf16[144,512]{1,0:T(8,128)(2,1)S(1)} %concatenate.20.refs_0_), channel_id=1, source_target_pairs={{0,4},{1,5},{2,6},{3,7},{4,0},{5,1},{6,2},{7,3},{8,12},{9,13},{10,... | collective-permute-start | bytes 442376 | tf_op jit(solution)/shard_map/ppermute | solution.py:32
  10.6 5.1 %collective-permute-start.5 = (bf16[144,512]{1,0:T(8,128)(2,1)S(1)}, bf16[144,512]{1,0:T(8,128)(2,1)S(1)}, u32[]{:S(2)}, u32[]{:S(2)}) collective-permute-start(bf16[144,512]{1,0:T(8,128)(2,1)S(1)} %concatenate.20.refs_0_), channel_id=1, source_target_pairs={{0,1},{1,0},{2,3},{3,2},{4,5},{5,4},{6,7},{7,6},{8,9},{9,8},{10,11... | collective-permute-start | bytes 442376 | tf_op jit(solution)/shard_map/ppermute | solution.py:32
  10.6 8.1 %collective-permute-start.4 = (bf16[144,512]{1,0:T(8,128)(2,1)S(1)}, bf16[144,512]{1,0:T(8,128)(2,1)S(1)}, u32[]{:S(2)}, u32[]{:S(2)}) collective-permute-start(bf16[144,512]{1,0:T(8,128)(2,1)S(1)} %concatenate.20.refs_0_), channel_id=1, source_target_pairs={{0,2},{1,3},{2,0},{3,1},{4,6},{5,7},{6,4},{7,5},{8,10},{9,11},{10,... | collective-permute-start | bytes 442376 | tf_op jit(solution)/shard_map/ppermute | solution.py:32
  14.1 5.9 %collective-permute-start.3 = (bf16[144,512]{1,0:T(8,128)(2,1)S(1)}, bf16[144,512]{1,0:T(8,128)(2,1)S(1)}, u32[]{:S(2)}, u32[]{:S(2)}) collective-permute-start(bf16[144,512]{1,0:T(8,128)(2,1)S(1)} %collective-permute-done.2.refs_0_), channel_id=1, source_target_pairs={{0,2},{1,3},{2,0},{3,1},{4,6},{5,7},{6,4},{7,5},{8,10},{9,11},{10,... | collective-permute-start | bytes 442376 | tf_op jit(solution)/shard_map/ppermute | solution.py:32
  19.2 1.4 %collective-permute-start.7 = (bf16[144,512]{1,0:T(8,128)(2,1)S(1)}, bf16[144,512]{1,0:T(8,128)(2,1)S(1)}, u32[]{:S(2)}, u32[]{:S(2)}) collective-permute-start(bf16[144,512]{1,0:T(8,128)(2,1)S(1)} %collective-permute-done.2.refs_0_), channel_id=1, source_target_pairs={{0,1},{1,0},{2,3},{3,2},{4,5},{5,4},{6,7},{7,6},{8,9},{9,8},{10,11... | collective-permute-start | bytes 442376 | tf_op jit(solution)/shard_map/ppermute | solution.py:32
  19.3 1.6 %collective-permute-start.8 = (bf16[144,512]{1,0:T(8,128)(2,1)S(1)}, bf16[144,512]{1,0:T(8,128)(2,1)S(1)}, u32[]{:S(2)}, u32[]{:S(2)}) collective-permute-start(bf16[144,512]{1,0:T(8,128)(2,1)S(1)} %collective-permute-done.4.refs_1_), channel_id=1, source_target_pairs={{0,1},{1,0},{2,3},{3,2},{4,5},{5,4},{6,7},{7,6},{8,9},{9,8},{10,11... | collective-permute-start | bytes 442376 | tf_op jit(solution)/shard_map/ppermute | solution.py:32
  20.0 1.6 %collective-permute-start.6 = (bf16[144,512]{1,0:T(8,128)(2,1)S(1)}, bf16[144,512]{1,0:T(8,128)(2,1)S(1)}, u32[]{:S(2)}, u32[]{:S(2)}) collective-permute-start(bf16[144,512]{1,0:T(8,128)(2,1)S(1)} %collective-permute-done.3.refs_0_), channel_id=1, source_target_pairs={{0,1},{1,0},{2,3},{3,2},{4,5},{5,4},{6,7},{7,6},{8,9},{9,8},{10,11... | collective-permute-start | bytes 442376 | tf_op jit(solution)/shard_map/ppermute | solution.py:32
  38.5 5.0 %collective-permute-start.9 = (bf16[1,4,4096]{2,1,0:T(4,128)(2,1)S(1)}, bf16[1,4,4096]{2,1,0:T(4,128)(2,1)S(1)}, u32[]{:S(2)}, u32[]{:S(2)}) collective-permute-start(bf16[1,4,4096]{2,1,0:T(4,128)(2,1)S(1)} %attend.2), channel_id=1, source_target_pairs={{0,8},{1,9},{2,10},{3,11},{4,12},{5,13},{6,14},{7,15},{8,0},{9,1},... | collective-permute-start | bytes 98312 | tf_op jit(solution)/shard_map/ppermute | solution.py:32
  43.6 5.3 %collective-permute-start.12 = (bf16[2,4,4096]{2,1,0:T(4,128)(2,1)S(1)}, bf16[2,4,4096]{2,1,0:T(4,128)(2,1)S(1)}, u32[]{:S(2)}, u32[]{:S(2)}) collective-permute-start(bf16[2,4,4096]{2,1,0:T(4,128)(2,1)S(1)} %pad_maximum_fusion.2.refs_0_), channel_id=1, source_target_pairs={{0,6},{1,7},{2,4},{3,5},{4,2},{5,3},{6,0},{7,1},{8,14},{9,15},{10,... | collective-permute-start | bytes 196616 | tf_op jit(solution)/shard_map/ppermute | solution.py:32
  44.4 5.0 %collective-permute-start.11 = (bf16[2,4,4096]{2,1,0:T(4,128)(2,1)S(1)}, bf16[2,4,4096]{2,1,0:T(4,128)(2,1)S(1)}, u32[]{:S(2)}, u32[]{:S(2)}) collective-permute-start(bf16[2,4,4096]{2,1,0:T(4,128)(2,1)S(1)} %pad_maximum_fusion.2.refs_0_), channel_id=1, source_target_pairs={{0,2},{1,3},{2,0},{3,1},{4,6},{5,7},{6,4},{7,5},{8,10},{9,11},{10,... | collective-permute-start | bytes 196616 | tf_op jit(solution)/shard_map/ppermute | solution.py:32
  45.4 4.3 %collective-permute-start.10 = (bf16[2,4,4096]{2,1,0:T(4,128)(2,1)S(1)}, bf16[2,4,4096]{2,1,0:T(4,128)(2,1)S(1)}, u32[]{:S(2)}, u32[]{:S(2)}) collective-permute-start(bf16[2,4,4096]{2,1,0:T(4,128)(2,1)S(1)} %pad_maximum_fusion.2.refs_0_), channel_id=1, source_target_pairs={{0,4},{1,5},{2,6},{3,7},{4,0},{5,1},{6,2},{7,3},{8,12},{9,13},{10,... | collective-permute-start | bytes 196616 | tf_op jit(solution)/shard_map/ppermute | solution.py:32
  49.0 1.8 %collective-permute-start.13 = (bf16[4,4,4096]{2,1,0:T(4,128)(2,1)S(1)}, bf16[4,4,4096]{2,1,0:T(4,128)(2,1)S(1)}, u32[]{:S(2)}, u32[]{:S(2)}) collective-permute-start(bf16[4,4,4096]{2,1,0:T(4,128)(2,1)S(1)} %pad_maximum_fusion), channel_id=1, source_target_pairs={{0,1},{1,0},{2,3},{3,2},{4,5},{5,4},{6,7},{7,6},{8,9},{9,8},{10,11... | collective-permute-start | bytes 393224 | tf_op jit(solution)/shard_map/ppermute | solution.py:32
  49.4 1.3 %collective-permute-start.14 = (bf16[2,4,4096]{2,1,0:T(4,128)(2,1)S(1)}, bf16[2,4,4096]{2,1,0:T(4,128)(2,1)S(1)}, u32[]{:S(2)}, u32[]{:S(2)}) collective-permute-start(bf16[2,4,4096]{2,1,0:T(4,128)(2,1)S(1)} %collective-permute-done.11.refs_2_), channel_id=1, source_target_pairs={{0,1},{1,0},{2,3},{3,2},{4,5},{5,4},{6,7},{7,6},{8,9},{9,8},{10,11... | collective-permute-start | bytes 196616 | tf_op jit(solution)/shard_map/ppermute | solution.py:32
  49.6 1.3 %collective-permute-start.15 = (bf16[2,4,4096]{2,1,0:T(4,128)(2,1)S(1)}, bf16[2,4,4096]{2,1,0:T(4,128)(2,1)S(1)}, u32[]{:S(2)}, u32[]{:S(2)}) collective-permute-start(bf16[2,4,4096]{2,1,0:T(4,128)(2,1)S(1)} %collective-permute-done.10.refs_1_), channel_id=1, source_target_pairs={{0,1},{1,0},{2,3},{3,2},{4,5},{5,4},{6,7},{7,6},{8,9},{9,8},{10,11... | collective-permute-start | bytes 196616 | tf_op jit(solution)/shard_map/ppermute | solution.py:32
  51.9 7.5 %collective-permute-start.16 = (bf16[64,512]{1,0:T(8,128)(2,1)S(1)}, bf16[64,512]{1,0:T(8,128)(2,1)S(1)}, u32[]{:S(2)}, u32[]{:S(2)}) collective-permute-start(bf16[64,512]{1,0:T(8,128)(2,1)S(1)} %output.2), channel_id=1, source_target_pairs={{0,24},{1,25},{2,26},{3,27},{4,28},{5,29},{6,30},{7,31},{8,16},{9,... | collective-permute-start | bytes 196616 | tf_op jit(solution)/shard_map/ppermute | solution.py:58
  54.4 5.1 %collective-permute-start.17 = (bf16[64,512]{1,0:T(8,128)(2,1)S(1)}, bf16[64,512]{1,0:T(8,128)(2,1)S(1)}, u32[]{:S(2)}, u32[]{:S(2)}) collective-permute-start(bf16[64,512]{1,0:T(8,128)(2,1)S(1)} %output.2), channel_id=1, source_target_pairs={{0,16},{1,17},{2,18},{3,19},{4,20},{5,21},{6,22},{7,23},{8,24},{9,... | collective-permute-start | bytes 196616 | tf_op jit(solution)/shard_map/ppermute | solution.py:58
  59.5 5.4 %collective-permute-start.18 = (bf16[128,512]{1,0:T(8,128)(2,1)S(1)}, bf16[128,512]{1,0:T(8,128)(2,1)S(1)}, u32[]{:S(2)}, u32[]{:S(2)}) collective-permute-start(bf16[128,512]{1,0:T(8,128)(2,1)S(1)} %constant_dynamic-update-slice_fusion.refs_0_), channel_id=1, source_target_pairs={{0,4},{1,5},{2,6},{3,7},{4,0},{5,1},{6,2},{7,3},{8,12},{9,13},{10,... | collective-permute-start | bytes 393224 | tf_op jit(solution)/shard_map/ppermute | solution.py:32
  61.2 4.3 %collective-permute-start.21 = (bf16[128,512]{1,0:T(8,128)(2,1)S(1)}, bf16[128,512]{1,0:T(8,128)(2,1)S(1)}, u32[]{:S(2)}, u32[]{:S(2)}) collective-permute-start(bf16[128,512]{1,0:T(8,128)(2,1)S(1)} %constant_dynamic-update-slice_fusion.refs_0_), channel_id=1, source_target_pairs={{0,1},{1,0},{2,3},{3,2},{4,5},{5,4},{6,7},{7,6},{8,9},{9,8},{10,11... | collective-permute-start | bytes 393224 | tf_op jit(solution)/shard_map/ppermute | solution.py:32
  61.2 6.3 %collective-permute-start.20 = (bf16[128,512]{1,0:T(8,128)(2,1)S(1)}, bf16[128,512]{1,0:T(8,128)(2,1)S(1)}, u32[]{:S(2)}, u32[]{:S(2)}) collective-permute-start(bf16[128,512]{1,0:T(8,128)(2,1)S(1)} %constant_dynamic-update-slice_fusion.refs_0_), channel_id=1, source_target_pairs={{0,2},{1,3},{2,0},{3,1},{4,6},{5,7},{6,4},{7,5},{8,10},{9,11},{10,... | collective-permute-start | bytes 393224 | tf_op jit(solution)/shard_map/ppermute | solution.py:32
  64.9 5.1 %collective-permute-start.19 = (bf16[128,512]{1,0:T(8,128)(2,1)S(1)}, bf16[128,512]{1,0:T(8,128)(2,1)S(1)}, u32[]{:S(2)}, u32[]{:S(2)}) collective-permute-start(bf16[128,512]{1,0:T(8,128)(2,1)S(1)} %collective-permute-done.18.refs_0_), channel_id=1, source_target_pairs={{0,2},{1,3},{2,0},{3,1},{4,6},{5,7},{6,4},{7,5},{8,10},{9,11},{10,... | collective-permute-start | bytes 393224 | tf_op jit(solution)/shard_map/ppermute | solution.py:32
  68.0 1.9 %collective-permute-start.23 = (bf16[128,512]{1,0:T(8,128)(2,1)S(1)}, bf16[128,512]{1,0:T(8,128)(2,1)S(1)}, u32[]{:S(2)}, u32[]{:S(2)}) collective-permute-start(bf16[128,512]{1,0:T(8,128)(2,1)S(1)} %collective-permute-done.18.refs_0_), channel_id=1, source_target_pairs={{0,1},{1,0},{2,3},{3,2},{4,5},{5,4},{6,7},{7,6},{8,9},{9,8},{10,11... | collective-permute-start | bytes 393224 | tf_op jit(solution)/shard_map/ppermute | solution.py:32
  68.1 1.8 %collective-permute-start.24 = (bf16[128,512]{1,0:T(8,128)(2,1)S(1)}, bf16[128,512]{1,0:T(8,128)(2,1)S(1)}, u32[]{:S(2)}, u32[]{:S(2)}) collective-permute-start(bf16[128,512]{1,0:T(8,128)(2,1)S(1)} %collective-permute-done.20.refs_1_), channel_id=1, source_target_pairs={{0,1},{1,0},{2,3},{3,2},{4,5},{5,4},{6,7},{7,6},{8,9},{9,8},{10,11... | collective-permute-start | bytes 393224 | tf_op jit(solution)/shard_map/ppermute | solution.py:32
  70.0 1.3 %collective-permute-start.22 = (bf16[128,512]{1,0:T(8,128)(2,1)S(1)}, bf16[128,512]{1,0:T(8,128)(2,1)S(1)}, u32[]{:S(2)}, u32[]{:S(2)}) collective-permute-start(bf16[128,512]{1,0:T(8,128)(2,1)S(1)} %collective-permute-done.19.refs_0_), channel_id=1, source_target_pairs={{0,1},{1,0},{2,3},{3,2},{4,5},{5,4},{6,7},{7,6},{8,9},{9,8},{10,11... | collective-permute-start | bytes 393224 | tf_op jit(solution)/shard_map/ppermute | solution.py:32
  82.8 4.9 %collective-permute-start.25 = (bf16[1,4,4096]{2,1,0:T(4,128)(2,1)S(1)}, bf16[1,4,4096]{2,1,0:T(4,128)(2,1)S(1)}, u32[]{:S(2)}, u32[]{:S(2)}) collective-permute-start(bf16[1,4,4096]{2,1,0:T(4,128)(2,1)S(1)} %attend.3), channel_id=1, source_target_pairs={{0,8},{1,9},{2,10},{3,11},{4,12},{5,13},{6,14},{7,15},{8,0},{9,1},... | collective-permute-start | bytes 98312 | tf_op jit(solution)/shard_map/ppermute | solution.py:32
  87.8 5.3 %collective-permute-start.28 = (bf16[2,4,4096]{2,1,0:T(4,128)(2,1)S(1)}, bf16[2,4,4096]{2,1,0:T(4,128)(2,1)S(1)}, u32[]{:S(2)}, u32[]{:S(2)}) collective-permute-start(bf16[2,4,4096]{2,1,0:T(4,128)(2,1)S(1)} %pad_maximum_fusion.3.refs_0_), channel_id=1, source_target_pairs={{0,6},{1,7},{2,4},{3,5},{4,2},{5,3},{6,0},{7,1},{8,14},{9,15},{10,... | collective-permute-start | bytes 196616 | tf_op jit(solution)/shard_map/ppermute | solution.py:32
  88.1 5.1 %collective-permute-start.27 = (bf16[2,4,4096]{2,1,0:T(4,128)(2,1)S(1)}, bf16[2,4,4096]{2,1,0:T(4,128)(2,1)S(1)}, u32[]{:S(2)}, u32[]{:S(2)}) collective-permute-start(bf16[2,4,4096]{2,1,0:T(4,128)(2,1)S(1)} %pad_maximum_fusion.3.refs_0_), channel_id=1, source_target_pairs={{0,2},{1,3},{2,0},{3,1},{4,6},{5,7},{6,4},{7,5},{8,10},{9,11},{10,... | collective-permute-start | bytes 196616 | tf_op jit(solution)/shard_map/ppermute | solution.py:32
  89.5 4.3 %collective-permute-start.26 = (bf16[2,4,4096]{2,1,0:T(4,128)(2,1)S(1)}, bf16[2,4,4096]{2,1,0:T(4,128)(2,1)S(1)}, u32[]{:S(2)}, u32[]{:S(2)}) collective-permute-start(bf16[2,4,4096]{2,1,0:T(4,128)(2,1)S(1)} %pad_maximum_fusion.3.refs_0_), channel_id=1, source_target_pairs={{0,4},{1,5},{2,6},{3,7},{4,0},{5,1},{6,2},{7,3},{8,12},{9,13},{10,... | collective-permute-start | bytes 196616 | tf_op jit(solution)/shard_map/ppermute | solution.py:32
  93.2 1.9 %collective-permute-start.29 = (bf16[4,4,4096]{2,1,0:T(4,128)(2,1)S(1)}, bf16[4,4,4096]{2,1,0:T(4,128)(2,1)S(1)}, u32[]{:S(2)}, u32[]{:S(2)}) collective-permute-start(bf16[4,4,4096]{2,1,0:T(4,128)(2,1)S(1)} %pad_maximum_fusion.1), channel_id=1, source_target_pairs={{0,1},{1,0},{2,3},{3,2},{4,5},{5,4},{6,7},{7,6},{8,9},{9,8},{10,11... | collective-permute-start | bytes 393224 | tf_op jit(solution)/shard_map/ppermute | solution.py:32
  93.3 1.4 %collective-permute-start.30 = (bf16[2,4,4096]{2,1,0:T(4,128)(2,1)S(1)}, bf16[2,4,4096]{2,1,0:T(4,128)(2,1)S(1)}, u32[]{:S(2)}, u32[]{:S(2)}) collective-permute-start(bf16[2,4,4096]{2,1,0:T(4,128)(2,1)S(1)} %collective-permute-done.27.refs_2_), channel_id=1, source_target_pairs={{0,1},{1,0},{2,3},{3,2},{4,5},{5,4},{6,7},{7,6},{8,9},{9,8},{10,11... | collective-permute-start | bytes 196616 | tf_op jit(solution)/shard_map/ppermute | solution.py:32
  96.1 4.3 %collective-permute-start.32 = (bf16[64,512]{1,0:T(8,128)(2,1)S(1)}, bf16[64,512]{1,0:T(8,128)(2,1)S(1)}, u32[]{:S(2)}, u32[]{:S(2)}) collective-permute-start(bf16[64,512]{1,0:T(8,128)(2,1)S(1)} %output.3), channel_id=1, source_target_pairs={{0,16},{1,17},{2,18},{3,19},{4,20},{5,21},{6,22},{7,23},{8,24},{9,... | collective-permute-start | bytes 196616 | tf_op jit(solution)/shard_map/ppermute | solution.py:58
  (14 other events, 135.9 us)

commit v8 on v7

--- a/solution.py
+++ b/solution.py
@@ -320,13 +320,10 @@
         acc = acc + jnp.dot(left.astype(jnp.bfloat16), w_ref[k:k + depth],
                             preferred_element_type=jnp.float32)
     move = arrival_rows(lax.axis_index("slot"), slots, batch, arrivals)
-    moved = None
-    for _ in range(3):
-        part = acc.astype(jnp.bfloat16)
-        acc = acc - part.astype(jnp.float32)
-        part = jnp.dot(move, part, preferred_element_type=jnp.float32)
-        moved = part if moved is None else moved + part
-    out_ref[...] = (now_ref[...].astype(jnp.float32) + moved).astype(jnp.bfloat16)
+    now = lax.dot_general(move, now_ref[...], (((0,), (0,)), ((), ())),
+                          preferred_element_type=jnp.float32)
+    updated = (now + acc).astype(jnp.bfloat16)
+    out_ref[...] = jnp.dot(move, updated, preferred_element_type=jnp.float32).astype(jnp.bfloat16)
 
 
 def output(groups, weight, now, slots):

time: 101 us -> 101 us (level)
  no operation moved by 1% of the time
where the time goes in v8:
time: 101 us
  waiting for transfers between devices  32.2 us (32%)
  starting transfers between devices  27.1 us (27%)
  blocking collectives  25.9 us (26%)
  Pallas kernels  8.55 us (8%)
  local copies, waits for them, and re-layouts  6.52 us (6%)
    all_to_all x2, blocking collectives, shards(): qkv = lax.all_to_all(qkv, 'slot', split_axis=0, concat_axis=0, tiled=True)  25.9 us
    ppermute x30, waiting for transfers between devices, exchange(): return lax.ppermute(block, 'slot', [(i, i ^ mask) for i in range(n)])  24.8 us
    ppermute x30, starting transfers between devices, exchange(): return lax.ppermute(block, 'slot', [(i, i ^ mask) for i in range(n)])  22.7 us
    ppermute x3, waiting for transfers between devices, next_segment(): return lax.ppermute(block, ('segment', 'slot'), route)  7.46 us
    unnamed x28, local copies, waits for them, and re-layouts  6.34 us
    pallas_call x8, Pallas kernels, project(): pl.pallas_call(functools.partial(project_kernel, away=[masks for masks, _...  4.56 us
    ppermute x3, starting transfers between devices, next_segment(): return lax.ppermute(block, ('segment', 'slot'), route)  4.41 us
  transfers between devices with their start and end apart: 33, of which 20 were waited for; matrix products, arithmetic and copies ran while one was open for 0% of the time, Pallas kernels for 4%

profile of v8, /device:TPU:0, one launch (start us, length us, event | category | flops | bytes accessed | tf_op | source)
XLA Modules:
  0.0 101.0 jit_solution(3544915908595646090)
XLA Ops:
  0.0 4.0 %collective-permute-start = (bf16[64,512]{1,0:T(8,128)(2,1)}, bf16[64,512]{1,0:T(8,128)(2,1)S(1)}, u32[]{:S(2)}, u32[]{:S(2)}) collective-permute-start(bf16[64,512]{1,0:T(8,128)(2,1)} %bitcast.33), channel_id=1, source_target_pairs={{0,8},{1,9},{2,10},{3,11},{4,12},{5,13},{6,14},{7,15},{8,0},{9,1},... | collective-permute-start | bytes 196616 | tf_op jit(solution)/shard_map/ppermute | solution.py:32
  4.1 0.9 copy-done.3
  5.7 0.8 copy-done.6
  8.0 0.8 collective-permute-done.1
  8.9 1.6 %collective-permute-start.2 = (bf16[144,512]{1,0:T(8,128)(2,1)S(1)}, bf16[144,512]{1,0:T(8,128)(2,1)S(1)}, u32[]{:S(2)}, u32[]{:S(2)}) collective-permute-start(bf16[144,512]{1,0:T(8,128)(2,1)S(1)} %concatenate.20.refs_0_), channel_id=1, source_target_pairs={{0,4},{1,5},{2,6},{3,7},{4,0},{5,1},{6,2},{7,3},{8,12},{9,13},{10,... | collective-permute-start | bytes 442376 | tf_op jit(solution)/shard_map/ppermute | solution.py:32
  10.6 1.5 %collective-permute-start.4 = (bf16[144,512]{1,0:T(8,128)(2,1)S(1)}, bf16[144,512]{1,0:T(8,128)(2,1)S(1)}, u32[]{:S(2)}, u32[]{:S(2)}) collective-permute-start(bf16[144,512]{1,0:T(8,128)(2,1)S(1)} %concatenate.20.refs_0_), channel_id=1, source_target_pairs={{0,2},{1,3},{2,0},{3,1},{4,6},{5,7},{6,4},{7,5},{8,10},{9,11},{10,... | collective-permute-start | bytes 442376 | tf_op jit(solution)/shard_map/ppermute | solution.py:32
  12.1 2.1 %collective-permute-done.2.refs_0_ = bf16[144,512]{1,0:T(8,128)(2,1)S(1)} collective-permute-done((bf16[144,512]{1,0:T(8,128)(2,1)S(1)}, bf16[144,512]{1,0:T(8,128)(2,1)S(1)}, u32[]{:S(2)}, u32[]{:S(2)}) %collective-permute-start.2) | collective-permute-done | bytes 147488 | tf_op jit(solution)/shard_map/ppermute | solution.py:32
  14.1 1.5 %collective-permute-start.3 = (bf16[144,512]{1,0:T(8,128)(2,1)S(1)}, bf16[144,512]{1,0:T(8,128)(2,1)S(1)}, u32[]{:S(2)}, u32[]{:S(2)}) collective-permute-start(bf16[144,512]{1,0:T(8,128)(2,1)S(1)} %collective-permute-done.2.refs_0_), channel_id=1, source_target_pairs={{0,2},{1,3},{2,0},{3,1},{4,6},{5,7},{6,4},{7,5},{8,10},{9,11},{10,... | collective-permute-start | bytes 442376 | tf_op jit(solution)/shard_map/ppermute | solution.py:32
  15.6 2.5 %copy-done = bf16[1,8192,320]{1,2,0:T(8,128)(2,1)S(1)} copy-done((bf16[1,8192,320]{1,2,0:T(8,128)(2,1)S(1)}, bf16[1,8192,320]{1,2,0:T(8,128)(2,1)}, u32[]{:S(2)}) %copy-start) | copy-done | bytes 5242904
  22.2 15.6 %all_to_all.10.qkv_ref = bf16[16,8,1280]{2,1,0:T(8,128)(2,1)S(1)} all-to-all(bf16[16,8,1280]{2,1,0:T(8,128)(2,1)S(1)} %get-tuple-element.55), channel_id=1, replica_groups=mesh['segment'=2,'slot'=16] {'slot'}, dimensions={0} | all-to-all | bytes 655360 | tf_op jit(solution)/shard_map/all_to_all | solution.py:396
  38.5 1.4 %collective-permute-start.9 = (bf16[1,4,4096]{2,1,0:T(4,128)(2,1)S(1)}, bf16[1,4,4096]{2,1,0:T(4,128)(2,1)S(1)}, u32[]{:S(2)}, u32[]{:S(2)}) collective-permute-start(bf16[1,4,4096]{2,1,0:T(4,128)(2,1)S(1)} %attend.2), channel_id=1, source_target_pairs={{0,8},{1,9},{2,10},{3,11},{4,12},{5,13},{6,14},{7,15},{8,0},{9,1},... | collective-permute-start | bytes 98312 | tf_op jit(solution)/shard_map/ppermute | solution.py:32
  40.0 3.6 %collective-permute-done.9 = bf16[1,4,4096]{2,1,0:T(4,128)(2,1)S(1)} collective-permute-done((bf16[1,4,4096]{2,1,0:T(4,128)(2,1)S(1)}, bf16[1,4,4096]{2,1,0:T(4,128)(2,1)S(1)}, u32[]{:S(2)}, u32[]{:S(2)}) %collective-permute-start.9) | collective-permute-done | bytes 32800 | tf_op jit(solution)/shard_map/ppermute | solution.py:32
  43.6 0.8 collective-permute-start.12
  44.4 0.9 collective-permute-start.11
  45.4 1.8 %collective-permute-start.10 = (bf16[2,4,4096]{2,1,0:T(4,128)(2,1)S(1)}, bf16[2,4,4096]{2,1,0:T(4,128)(2,1)S(1)}, u32[]{:S(2)}, u32[]{:S(2)}) collective-permute-start(bf16[2,4,4096]{2,1,0:T(4,128)(2,1)S(1)} %pad_maximum_fusion.2.refs_0_), channel_id=1, source_target_pairs={{0,4},{1,5},{2,6},{3,7},{4,0},{5,1},{6,2},{7,3},{8,12},{9,13},{10,... | collective-permute-start | bytes 196616 | tf_op jit(solution)/shard_map/ppermute | solution.py:32
  47.2 1.8 %collective-permute-done.12.refs_3_ = bf16[2,4,4096]{2,1,0:T(4,128)(2,1)S(1)} collective-permute-done((bf16[2,4,4096]{2,1,0:T(4,128)(2,1)S(1)}, bf16[2,4,4096]{2,1,0:T(4,128)(2,1)S(1)}, u32[]{:S(2)}, u32[]{:S(2)}) %collective-permute-start.12) | collective-permute-done | bytes 65568 | tf_op jit(solution)/shard_map/ppermute | solution.py:32
  50.9 1.0 output.2
  51.9 2.5 %collective-permute-start.16 = (bf16[64,512]{1,0:T(8,128)(2,1)S(1)}, bf16[64,512]{1,0:T(8,128)(2,1)S(1)}, u32[]{:S(2)}, u32[]{:S(2)}) collective-permute-start(bf16[64,512]{1,0:T(8,128)(2,1)S(1)} %output.2), channel_id=1, source_target_pairs={{0,24},{1,25},{2,26},{3,27},{4,28},{5,29},{6,30},{7,31},{8,16},{9,... | collective-permute-start | bytes 196616 | tf_op jit(solution)/shard_map/ppermute | solution.py:58
  54.9 4.6 %collective-permute-done.16 = bf16[64,512]{1,0:T(8,128)(2,1)S(1)} collective-permute-done((bf16[64,512]{1,0:T(8,128)(2,1)S(1)}, bf16[64,512]{1,0:T(8,128)(2,1)S(1)}, u32[]{:S(2)}, u32[]{:S(2)}) %collective-permute-start.16) | collective-permute-done | bytes 65568 | tf_op jit(solution)/shard_map/ppermute | solution.py:58
  59.4 1.7 %collective-permute-start.18 = (bf16[128,512]{1,0:T(8,128)(2,1)S(1)}, bf16[128,512]{1,0:T(8,128)(2,1)S(1)}, u32[]{:S(2)}, u32[]{:S(2)}) collective-permute-start(bf16[128,512]{1,0:T(8,128)(2,1)S(1)} %constant_dynamic-update-slice_fusion.refs_0_), channel_id=1, source_target_pairs={{0,4},{1,5},{2,6},{3,7},{4,0},{5,1},{6,2},{7,3},{8,12},{9,13},{10,... | collective-permute-start | bytes 393224 | tf_op jit(solution)/shard_map/ppermute | solution.py:32
  61.6 3.3 %collective-permute-done.18.refs_0_ = bf16[128,512]{1,0:T(8,128)(2,1)S(1)} collective-permute-done((bf16[128,512]{1,0:T(8,128)(2,1)S(1)}, bf16[128,512]{1,0:T(8,128)(2,1)S(1)}, u32[]{:S(2)}, u32[]{:S(2)}) %collective-permute-start.18) | collective-permute-done | bytes 131104 | tf_op jit(solution)/shard_map/ppermute | solution.py:32
  66.0 1.5 %collective-permute-done.20.refs_1_ = bf16[128,512]{1,0:T(8,128)(2,1)S(1)} collective-permute-done((bf16[128,512]{1,0:T(8,128)(2,1)S(1)}, bf16[128,512]{1,0:T(8,128)(2,1)S(1)}, u32[]{:S(2)}, u32[]{:S(2)}) %collective-permute-start.20) | collective-permute-done | bytes 131104 | tf_op jit(solution)/shard_map/ppermute | solution.py:32
  68.6 1.3 %collective-permute-done.19.refs_0_ = bf16[128,512]{1,0:T(8,128)(2,1)S(1)} collective-permute-done((bf16[128,512]{1,0:T(8,128)(2,1)S(1)}, bf16[128,512]{1,0:T(8,128)(2,1)S(1)}, u32[]{:S(2)}, u32[]{:S(2)}) %collective-permute-start.19) | collective-permute-done | bytes 131104 | tf_op jit(solution)/shard_map/ppermute | solution.py:32
  71.8 10.4 %all_to_all.11.qkv_ref = bf16[16,4,320]{2,1,0:T(4,128)(2,1)S(1)} all-to-all(bf16[16,4,320]{2,1,0:T(4,128)(2,1)S(1)} %project.15), channel_id=1, replica_groups=mesh['segment'=2,'slot'=16] {'slot'}, dimensions={0} | all-to-all | bytes 81920 | tf_op jit(solution)/shard_map/all_to_all | solution.py:396
  83.2 4.5 %collective-permute-done.25 = bf16[1,4,4096]{2,1,0:T(4,128)(2,1)S(1)} collective-permute-done((bf16[1,4,4096]{2,1,0:T(4,128)(2,1)S(1)}, bf16[1,4,4096]{2,1,0:T(4,128)(2,1)S(1)}, u32[]{:S(2)}, u32[]{:S(2)}) %collective-permute-start.25) | collective-permute-done | bytes 32800 | tf_op jit(solution)/shard_map/ppermute | solution.py:32
  88.1 1.4 %collective-permute-start.27 = (bf16[2,4,4096]{2,1,0:T(4,128)(2,1)S(1)}, bf16[2,4,4096]{2,1,0:T(4,128)(2,1)S(1)}, u32[]{:S(2)}, u32[]{:S(2)}) collective-permute-start(bf16[2,4,4096]{2,1,0:T(4,128)(2,1)S(1)} %pad_maximum_fusion.3.refs_0_), channel_id=1, source_target_pairs={{0,2},{1,3},{2,0},{3,1},{4,6},{5,7},{6,4},{7,5},{8,10},{9,11},{10,... | collective-permute-start | bytes 196616 | tf_op jit(solution)/shard_map/ppermute | solution.py:32
  89.5 1.8 %collective-permute-start.26 = (bf16[2,4,4096]{2,1,0:T(4,128)(2,1)S(1)}, bf16[2,4,4096]{2,1,0:T(4,128)(2,1)S(1)}, u32[]{:S(2)}, u32[]{:S(2)}) collective-permute-start(bf16[2,4,4096]{2,1,0:T(4,128)(2,1)S(1)} %pad_maximum_fusion.3.refs_0_), channel_id=1, source_target_pairs={{0,4},{1,5},{2,6},{3,7},{4,0},{5,1},{6,2},{7,3},{8,12},{9,13},{10,... | collective-permute-start | bytes 196616 | tf_op jit(solution)/shard_map/ppermute | solution.py:32
  91.3 1.8 %collective-permute-done.28.refs_3_ = bf16[2,4,4096]{2,1,0:T(4,128)(2,1)S(1)} collective-permute-done((bf16[2,4,4096]{2,1,0:T(4,128)(2,1)S(1)}, bf16[2,4,4096]{2,1,0:T(4,128)(2,1)S(1)}, u32[]{:S(2)}, u32[]{:S(2)}) %collective-permute-start.28) | collective-permute-done | bytes 65568 | tf_op jit(solution)/shard_map/ppermute | solution.py:32
  93.8 0.8 collective-permute-done.30.refs_5_
  95.0 1.0 output.3
  96.0 1.4 %collective-permute-start.32 = (bf16[64,512]{1,0:T(8,128)(2,1)S(1)}, bf16[64,512]{1,0:T(8,128)(2,1)S(1)}, u32[]{:S(2)}, u32[]{:S(2)}) collective-permute-start(bf16[64,512]{1,0:T(8,128)(2,1)S(1)} %output.3), channel_id=1, source_target_pairs={{0,16},{1,17},{2,18},{3,19},{4,20},{5,21},{6,22},{7,23},{8,24},{9,... | collective-permute-start | bytes 196616 | tf_op jit(solution)/shard_map/ppermute | solution.py:58
  97.5 2.9 %collective-permute-done.32 = bf16[64,512]{1,0:T(8,128)(2,1)S(1)} collective-permute-done((bf16[64,512]{1,0:T(8,128)(2,1)S(1)}, bf16[64,512]{1,0:T(8,128)(2,1)S(1)}, u32[]{:S(2)}, u32[]{:S(2)}) %collective-permute-start.32) | collective-permute-done | bytes 65568 | tf_op jit(solution)/shard_map/ppermute | solution.py:58
  (85 shorter events, 17.0 us)
Async XLA Ops:
  0.0 8.7 %collective-permute-start = (bf16[64,512]{1,0:T(8,128)(2,1)}, bf16[64,512]{1,0:T(8,128)(2,1)S(1)}, u32[]{:S(2)}, u32[]{:S(2)}) collective-permute-start(bf16[64,512]{1,0:T(8,128)(2,1)} %bitcast.33), channel_id=1, source_target_pairs={{0,8},{1,9},{2,10},{3,11},{4,12},{5,13},{6,14},{7,15},{8,0},{9,1},... | collective-permute-start | bytes 196616 | tf_op jit(solution)/shard_map/ppermute | solution.py:32
  4.0 4.7 %collective-permute-start.1 = (bf16[1,512]{1,0:T(2,128)(2,1)}, bf16[1,512]{1,0:T(2,128)(2,1)S(1)}, u32[]{:S(2)}, u32[]{:S(2)}) collective-permute-start(bf16[1,512]{1,0:T(2,128)(2,1)} %gain_ref.1), channel_id=1, source_target_pairs={{0,8},{1,9},{2,10},{3,11},{4,12},{5,13},{6,14},{7,15},{8,0},{9,1},... | collective-permute-start | bytes 3080 | tf_op jit(solution)/shard_map/ppermute | solution.py:32
  8.9 5.2 %collective-permute-start.2 = (bf16[144,512]{1,0:T(8,128)(2,1)S(1)}, bf16[144,512]{1,0:T(8,128)(2,1)S(1)}, u32[]{:S(2)}, u32[]{:S(2)}) collective-permute-start(bf16[144,512]{1,0:T(8,128)(2,1)S(1)} %concatenate.20.refs_0_), channel_id=1, source_target_pairs={{0,4},{1,5},{2,6},{3,7},{4,0},{5,1},{6,2},{7,3},{8,12},{9,13},{10,... | collective-permute-start | bytes 442376 | tf_op jit(solution)/shard_map/ppermute | solution.py:32
  10.6 5.1 %collective-permute-start.5 = (bf16[144,512]{1,0:T(8,128)(2,1)S(1)}, bf16[144,512]{1,0:T(8,128)(2,1)S(1)}, u32[]{:S(2)}, u32[]{:S(2)}) collective-permute-start(bf16[144,512]{1,0:T(8,128)(2,1)S(1)} %concatenate.20.refs_0_), channel_id=1, source_target_pairs={{0,1},{1,0},{2,3},{3,2},{4,5},{5,4},{6,7},{7,6},{8,9},{9,8},{10,11... | collective-permute-start | bytes 442376 | tf_op jit(solution)/shard_map/ppermute | solution.py:32
  10.6 8.1 %collective-permute-start.4 = (bf16[144,512]{1,0:T(8,128)(2,1)S(1)}, bf16[144,512]{1,0:T(8,128)(2,1)S(1)}, u32[]{:S(2)}, u32[]{:S(2)}) collective-permute-start(bf16[144,512]{1,0:T(8,128)(2,1)S(1)} %concatenate.20.refs_0_), channel_id=1, source_target_pairs={{0,2},{1,3},{2,0},{3,1},{4,6},{5,7},{6,4},{7,5},{8,10},{9,11},{10,... | collective-permute-start | bytes 442376 | tf_op jit(solution)/shard_map/ppermute | solution.py:32
  14.1 5.9 %collective-permute-start.3 = (bf16[144,512]{1,0:T(8,128)(2,1)S(1)}, bf16[144,512]{1,0:T(8,128)(2,1)S(1)}, u32[]{:S(2)}, u32[]{:S(2)}) collective-permute-start(bf16[144,512]{1,0:T(8,128)(2,1)S(1)} %collective-permute-done.2.refs_0_), channel_id=1, source_target_pairs={{0,2},{1,3},{2,0},{3,1},{4,6},{5,7},{6,4},{7,5},{8,10},{9,11},{10,... | collective-permute-start | bytes 442376 | tf_op jit(solution)/shard_map/ppermute | solution.py:32
  19.2 1.4 %collective-permute-start.7 = (bf16[144,512]{1,0:T(8,128)(2,1)S(1)}, bf16[144,512]{1,0:T(8,128)(2,1)S(1)}, u32[]{:S(2)}, u32[]{:S(2)}) collective-permute-start(bf16[144,512]{1,0:T(8,128)(2,1)S(1)} %collective-permute-done.2.refs_0_), channel_id=1, source_target_pairs={{0,1},{1,0},{2,3},{3,2},{4,5},{5,4},{6,7},{7,6},{8,9},{9,8},{10,11... | collective-permute-start | bytes 442376 | tf_op jit(solution)/shard_map/ppermute | solution.py:32
  19.3 1.6 %collective-permute-start.8 = (bf16[144,512]{1,0:T(8,128)(2,1)S(1)}, bf16[144,512]{1,0:T(8,128)(2,1)S(1)}, u32[]{:S(2)}, u32[]{:S(2)}) collective-permute-start(bf16[144,512]{1,0:T(8,128)(2,1)S(1)} %collective-permute-done.4.refs_1_), channel_id=1, source_target_pairs={{0,1},{1,0},{2,3},{3,2},{4,5},{5,4},{6,7},{7,6},{8,9},{9,8},{10,11... | collective-permute-start | bytes 442376 | tf_op jit(solution)/shard_map/ppermute | solution.py:32
  20.0 1.6 %collective-permute-start.6 = (bf16[144,512]{1,0:T(8,128)(2,1)S(1)}, bf16[144,512]{1,0:T(8,128)(2,1)S(1)}, u32[]{:S(2)}, u32[]{:S(2)}) collective-permute-start(bf16[144,512]{1,0:T(8,128)(2,1)S(1)} %collective-permute-done.3.refs_0_), channel_id=1, source_target_pairs={{0,1},{1,0},{2,3},{3,2},{4,5},{5,4},{6,7},{7,6},{8,9},{9,8},{10,11... | collective-permute-start | bytes 442376 | tf_op jit(solution)/shard_map/ppermute | solution.py:32
  38.5 5.0 %collective-permute-start.9 = (bf16[1,4,4096]{2,1,0:T(4,128)(2,1)S(1)}, bf16[1,4,4096]{2,1,0:T(4,128)(2,1)S(1)}, u32[]{:S(2)}, u32[]{:S(2)}) collective-permute-start(bf16[1,4,4096]{2,1,0:T(4,128)(2,1)S(1)} %attend.2), channel_id=1, source_target_pairs={{0,8},{1,9},{2,10},{3,11},{4,12},{5,13},{6,14},{7,15},{8,0},{9,1},... | collective-permute-start | bytes 98312 | tf_op jit(solution)/shard_map/ppermute | solution.py:32
  43.6 5.3 %collective-permute-start.12 = (bf16[2,4,4096]{2,1,0:T(4,128)(2,1)S(1)}, bf16[2,4,4096]{2,1,0:T(4,128)(2,1)S(1)}, u32[]{:S(2)}, u32[]{:S(2)}) collective-permute-start(bf16[2,4,4096]{2,1,0:T(4,128)(2,1)S(1)} %pad_maximum_fusion.2.refs_0_), channel_id=1, source_target_pairs={{0,6},{1,7},{2,4},{3,5},{4,2},{5,3},{6,0},{7,1},{8,14},{9,15},{10,... | collective-permute-start | bytes 196616 | tf_op jit(solution)/shard_map/ppermute | solution.py:32
  44.4 5.0 %collective-permute-start.11 = (bf16[2,4,4096]{2,1,0:T(4,128)(2,1)S(1)}, bf16[2,4,4096]{2,1,0:T(4,128)(2,1)S(1)}, u32[]{:S(2)}, u32[]{:S(2)}) collective-permute-start(bf16[2,4,4096]{2,1,0:T(4,128)(2,1)S(1)} %pad_maximum_fusion.2.refs_0_), channel_id=1, source_target_pairs={{0,2},{1,3},{2,0},{3,1},{4,6},{5,7},{6,4},{7,5},{8,10},{9,11},{10,... | collective-permute-start | bytes 196616 | tf_op jit(solution)/shard_map/ppermute | solution.py:32
  45.4 4.3 %collective-permute-start.10 = (bf16[2,4,4096]{2,1,0:T(4,128)(2,1)S(1)}, bf16[2,4,4096]{2,1,0:T(4,128)(2,1)S(1)}, u32[]{:S(2)}, u32[]{:S(2)}) collective-permute-start(bf16[2,4,4096]{2,1,0:T(4,128)(2,1)S(1)} %pad_maximum_fusion.2.refs_0_), channel_id=1, source_target_pairs={{0,4},{1,5},{2,6},{3,7},{4,0},{5,1},{6,2},{7,3},{8,12},{9,13},{10,... | collective-permute-start | bytes 196616 | tf_op jit(solution)/shard_map/ppermute | solution.py:32
  49.0 1.8 %collective-permute-start.13 = (bf16[4,4,4096]{2,1,0:T(4,128)(2,1)S(1)}, bf16[4,4,4096]{2,1,0:T(4,128)(2,1)S(1)}, u32[]{:S(2)}, u32[]{:S(2)}) collective-permute-start(bf16[4,4,4096]{2,1,0:T(4,128)(2,1)S(1)} %pad_maximum_fusion), channel_id=1, source_target_pairs={{0,1},{1,0},{2,3},{3,2},{4,5},{5,4},{6,7},{7,6},{8,9},{9,8},{10,11... | collective-permute-start | bytes 393224 | tf_op jit(solution)/shard_map/ppermute | solution.py:32
  49.4 1.3 %collective-permute-start.14 = (bf16[2,4,4096]{2,1,0:T(4,128)(2,1)S(1)}, bf16[2,4,4096]{2,1,0:T(4,128)(2,1)S(1)}, u32[]{:S(2)}, u32[]{:S(2)}) collective-permute-start(bf16[2,4,4096]{2,1,0:T(4,128)(2,1)S(1)} %collective-permute-done.11.refs_2_), channel_id=1, source_target_pairs={{0,1},{1,0},{2,3},{3,2},{4,5},{5,4},{6,7},{7,6},{8,9},{9,8},{10,11... | collective-permute-start | bytes 196616 | tf_op jit(solution)/shard_map/ppermute | solution.py:32
  49.6 1.3 %collective-permute-start.15 = (bf16[2,4,4096]{2,1,0:T(4,128)(2,1)S(1)}, bf16[2,4,4096]{2,1,0:T(4,128)(2,1)S(1)}, u32[]{:S(2)}, u32[]{:S(2)}) collective-permute-start(bf16[2,4,4096]{2,1,0:T(4,128)(2,1)S(1)} %collective-permute-done.10.refs_1_), channel_id=1, source_target_pairs={{0,1},{1,0},{2,3},{3,2},{4,5},{5,4},{6,7},{7,6},{8,9},{9,8},{10,11... | collective-permute-start | bytes 196616 | tf_op jit(solution)/shard_map/ppermute | solution.py:32
  51.9 7.5 %collective-permute-start.16 = (bf16[64,512]{1,0:T(8,128)(2,1)S(1)}, bf16[64,512]{1,0:T(8,128)(2,1)S(1)}, u32[]{:S(2)}, u32[]{:S(2)}) collective-permute-start(bf16[64,512]{1,0:T(8,128)(2,1)S(1)} %output.2), channel_id=1, source_target_pairs={{0,24},{1,25},{2,26},{3,27},{4,28},{5,29},{6,30},{7,31},{8,16},{9,... | collective-permute-start | bytes 196616 | tf_op jit(solution)/shard_map/ppermute | solution.py:58
  54.3 5.1 %collective-permute-start.17 = (bf16[64,512]{1,0:T(8,128)(2,1)S(1)}, bf16[64,512]{1,0:T(8,128)(2,1)S(1)}, u32[]{:S(2)}, u32[]{:S(2)}) collective-permute-start(bf16[64,512]{1,0:T(8,128)(2,1)S(1)} %output.2), channel_id=1, source_target_pairs={{0,16},{1,17},{2,18},{3,19},{4,20},{5,21},{6,22},{7,23},{8,24},{9,... | collective-permute-start | bytes 196616 | tf_op jit(solution)/shard_map/ppermute | solution.py:58
  59.4 5.4 %collective-permute-start.18 = (bf16[128,512]{1,0:T(8,128)(2,1)S(1)}, bf16[128,512]{1,0:T(8,128)(2,1)S(1)}, u32[]{:S(2)}, u32[]{:S(2)}) collective-permute-start(bf16[128,512]{1,0:T(8,128)(2,1)S(1)} %constant_dynamic-update-slice_fusion.refs_0_), channel_id=1, source_target_pairs={{0,4},{1,5},{2,6},{3,7},{4,0},{5,1},{6,2},{7,3},{8,12},{9,13},{10,... | collective-permute-start | bytes 393224 | tf_op jit(solution)/shard_map/ppermute | solution.py:32
  61.2 4.3 %collective-permute-start.21 = (bf16[128,512]{1,0:T(8,128)(2,1)S(1)}, bf16[128,512]{1,0:T(8,128)(2,1)S(1)}, u32[]{:S(2)}, u32[]{:S(2)}) collective-permute-start(bf16[128,512]{1,0:T(8,128)(2,1)S(1)} %constant_dynamic-update-slice_fusion.refs_0_), channel_id=1, source_target_pairs={{0,1},{1,0},{2,3},{3,2},{4,5},{5,4},{6,7},{7,6},{8,9},{9,8},{10,11... | collective-permute-start | bytes 393224 | tf_op jit(solution)/shard_map/ppermute | solution.py:32
  61.2 6.3 %collective-permute-start.20 = (bf16[128,512]{1,0:T(8,128)(2,1)S(1)}, bf16[128,512]{1,0:T(8,128)(2,1)S(1)}, u32[]{:S(2)}, u32[]{:S(2)}) collective-permute-start(bf16[128,512]{1,0:T(8,128)(2,1)S(1)} %constant_dynamic-update-slice_fusion.refs_0_), channel_id=1, source_target_pairs={{0,2},{1,3},{2,0},{3,1},{4,6},{5,7},{6,4},{7,5},{8,10},{9,11},{10,... | collective-permute-start | bytes 393224 | tf_op jit(solution)/shard_map/ppermute | solution.py:32
  64.9 5.1 %collective-permute-start.19 = (bf16[128,512]{1,0:T(8,128)(2,1)S(1)}, bf16[128,512]{1,0:T(8,128)(2,1)S(1)}, u32[]{:S(2)}, u32[]{:S(2)}) collective-permute-start(bf16[128,512]{1,0:T(8,128)(2,1)S(1)} %collective-permute-done.18.refs_0_), channel_id=1, source_target_pairs={{0,2},{1,3},{2,0},{3,1},{4,6},{5,7},{6,4},{7,5},{8,10},{9,11},{10,... | collective-permute-start | bytes 393224 | tf_op jit(solution)/shard_map/ppermute | solution.py:32
  68.0 1.9 %collective-permute-start.23 = (bf16[128,512]{1,0:T(8,128)(2,1)S(1)}, bf16[128,512]{1,0:T(8,128)(2,1)S(1)}, u32[]{:S(2)}, u32[]{:S(2)}) collective-permute-start(bf16[128,512]{1,0:T(8,128)(2,1)S(1)} %collective-permute-done.18.refs_0_), channel_id=1, source_target_pairs={{0,1},{1,0},{2,3},{3,2},{4,5},{5,4},{6,7},{7,6},{8,9},{9,8},{10,11... | collective-permute-start | bytes 393224 | tf_op jit(solution)/shard_map/ppermute | solution.py:32
  68.1 1.8 %collective-permute-start.24 = (bf16[128,512]{1,0:T(8,128)(2,1)S(1)}, bf16[128,512]{1,0:T(8,128)(2,1)S(1)}, u32[]{:S(2)}, u32[]{:S(2)}) collective-permute-start(bf16[128,512]{1,0:T(8,128)(2,1)S(1)} %collective-permute-done.20.refs_1_), channel_id=1, source_target_pairs={{0,1},{1,0},{2,3},{3,2},{4,5},{5,4},{6,7},{7,6},{8,9},{9,8},{10,11... | collective-permute-start | bytes 393224 | tf_op jit(solution)/shard_map/ppermute | solution.py:32
  69.9 1.3 %collective-permute-start.22 = (bf16[128,512]{1,0:T(8,128)(2,1)S(1)}, bf16[128,512]{1,0:T(8,128)(2,1)S(1)}, u32[]{:S(2)}, u32[]{:S(2)}) collective-permute-start(bf16[128,512]{1,0:T(8,128)(2,1)S(1)} %collective-permute-done.19.refs_0_), channel_id=1, source_target_pairs={{0,1},{1,0},{2,3},{3,2},{4,5},{5,4},{6,7},{7,6},{8,9},{9,8},{10,11... | collective-permute-start | bytes 393224 | tf_op jit(solution)/shard_map/ppermute | solution.py:32
  82.8 4.9 %collective-permute-start.25 = (bf16[1,4,4096]{2,1,0:T(4,128)(2,1)S(1)}, bf16[1,4,4096]{2,1,0:T(4,128)(2,1)S(1)}, u32[]{:S(2)}, u32[]{:S(2)}) collective-permute-start(bf16[1,4,4096]{2,1,0:T(4,128)(2,1)S(1)} %attend.3), channel_id=1, source_target_pairs={{0,8},{1,9},{2,10},{3,11},{4,12},{5,13},{6,14},{7,15},{8,0},{9,1},... | collective-permute-start | bytes 98312 | tf_op jit(solution)/shard_map/ppermute | solution.py:32
  87.7 5.3 %collective-permute-start.28 = (bf16[2,4,4096]{2,1,0:T(4,128)(2,1)S(1)}, bf16[2,4,4096]{2,1,0:T(4,128)(2,1)S(1)}, u32[]{:S(2)}, u32[]{:S(2)}) collective-permute-start(bf16[2,4,4096]{2,1,0:T(4,128)(2,1)S(1)} %pad_maximum_fusion.3.refs_0_), channel_id=1, source_target_pairs={{0,6},{1,7},{2,4},{3,5},{4,2},{5,3},{6,0},{7,1},{8,14},{9,15},{10,... | collective-permute-start | bytes 196616 | tf_op jit(solution)/shard_map/ppermute | solution.py:32
  88.1 5.1 %collective-permute-start.27 = (bf16[2,4,4096]{2,1,0:T(4,128)(2,1)S(1)}, bf16[2,4,4096]{2,1,0:T(4,128)(2,1)S(1)}, u32[]{:S(2)}, u32[]{:S(2)}) collective-permute-start(bf16[2,4,4096]{2,1,0:T(4,128)(2,1)S(1)} %pad_maximum_fusion.3.refs_0_), channel_id=1, source_target_pairs={{0,2},{1,3},{2,0},{3,1},{4,6},{5,7},{6,4},{7,5},{8,10},{9,11},{10,... | collective-permute-start | bytes 196616 | tf_op jit(solution)/shard_map/ppermute | solution.py:32
  89.5 4.3 %collective-permute-start.26 = (bf16[2,4,4096]{2,1,0:T(4,128)(2,1)S(1)}, bf16[2,4,4096]{2,1,0:T(4,128)(2,1)S(1)}, u32[]{:S(2)}, u32[]{:S(2)}) collective-permute-start(bf16[2,4,4096]{2,1,0:T(4,128)(2,1)S(1)} %pad_maximum_fusion.3.refs_0_), channel_id=1, source_target_pairs={{0,4},{1,5},{2,6},{3,7},{4,0},{5,1},{6,2},{7,3},{8,12},{9,13},{10,... | collective-permute-start | bytes 196616 | tf_op jit(solution)/shard_map/ppermute | solution.py:32
  93.2 1.9 %collective-permute-start.29 = (bf16[4,4,4096]{2,1,0:T(4,128)(2,1)S(1)}, bf16[4,4,4096]{2,1,0:T(4,128)(2,1)S(1)}, u32[]{:S(2)}, u32[]{:S(2)}) collective-permute-start(bf16[4,4,4096]{2,1,0:T(4,128)(2,1)S(1)} %pad_maximum_fusion.1), channel_id=1, source_target_pairs={{0,1},{1,0},{2,3},{3,2},{4,5},{5,4},{6,7},{7,6},{8,9},{9,8},{10,11... | collective-permute-start | bytes 393224 | tf_op jit(solution)/shard_map/ppermute | solution.py:32
  93.2 1.4 %collective-permute-start.30 = (bf16[2,4,4096]{2,1,0:T(4,128)(2,1)S(1)}, bf16[2,4,4096]{2,1,0:T(4,128)(2,1)S(1)}, u32[]{:S(2)}, u32[]{:S(2)}) collective-permute-start(bf16[2,4,4096]{2,1,0:T(4,128)(2,1)S(1)} %collective-permute-done.27.refs_2_), channel_id=1, source_target_pairs={{0,1},{1,0},{2,3},{3,2},{4,5},{5,4},{6,7},{7,6},{8,9},{9,8},{10,11... | collective-permute-start | bytes 196616 | tf_op jit(solution)/shard_map/ppermute | solution.py:32
  96.0 4.3 %collective-permute-start.32 = (bf16[64,512]{1,0:T(8,128)(2,1)S(1)}, bf16[64,512]{1,0:T(8,128)(2,1)S(1)}, u32[]{:S(2)}, u32[]{:S(2)}) collective-permute-start(bf16[64,512]{1,0:T(8,128)(2,1)S(1)} %output.3), channel_id=1, source_target_pairs={{0,16},{1,17},{2,18},{3,19},{4,20},{5,21},{6,22},{7,23},{8,24},{9,... | collective-permute-start | bytes 196616 | tf_op jit(solution)/shard_map/ppermute | solution.py:58
  (14 other events, 135.9 us)

commit v9 on v8

--- a/solution.py
+++ b/solution.py
@@ -121,8 +121,7 @@
     x_refs = [refs.pop(0) for _ in away]
     kept = None if carried else refs.pop(0)
     acc_in, square_in = (None, None) if first else (refs.pop(0), refs.pop(0))
-    if packed:
-        refs.pop(0)
+    pages_ref = refs.pop(0) if packed else None
     if carried:
         kept = refs.pop(0)
     blocks, width = len(away[0]), x_refs[0].shape[1]
@@ -159,6 +158,7 @@
         if packed:
             at = refs[0].shape[2] - room_for(columns)
             mine = jnp.concatenate([mine[:, :half], mine[:, half:]], axis=0)
+            refs[0][j] = pages_ref[j]
             refs[0][j, :, at:at + half] = mine.astype(jnp.bfloat16)
         else:
             refs[0][j] = mine.astype(jnp.bfloat16)
@@ -170,13 +170,11 @@
     carried, first, packed = gains is None, state is None, outgoing is not None
     operands = [weight] + [x for _, x in groups] + ([] if carried else [gains])
     operands += [] if first else list(state)
-    aliases = {}
     out_shape = []
     if carried:
         out_shape.append(jax.ShapeDtypeStruct((len(groups), held - blocks * rows, width),
                                               jnp.bfloat16))
     if packed:
-        aliases = {len(operands): len(out_shape)}
         operands.append(outgoing)
         out_shape.append(jax.ShapeDtypeStruct(outgoing.shape, outgoing.dtype))
     elif last:
@@ -192,7 +190,6 @@
         out_shape=out_shape,
         in_specs=[whole] * len(operands),
         out_specs=[whole] * len(out_shape),
-        input_output_aliases=aliases,
         compiler_params=params(),
         cost_estimate=pl.CostEstimate(flops=8 * work, bytes_accessed=2 * work // rows,
                                       transcendentals=0),

time: 101 us -> 101 us (level)
  no operation moved by 1% of the time
where the time goes in v9:
time: 101 us
  waiting for transfers between devices  32.2 us (32%)
  starting transfers between devices  27.1 us (27%)
  blocking collectives  25.9 us (26%)
  Pallas kernels  8.55 us (8%)
  local copies, waits for them, and re-layouts  6.52 us (6%)
    all_to_all x2, blocking collectives, shards(): qkv = lax.all_to_all(qkv, 'slot', split_axis=0, concat_axis=0, tiled=True)  25.9 us
    ppermute x30, waiting for transfers between devices, exchange(): return lax.ppermute(block, 'slot', [(i, i ^ mask) for i in range(n)])  24.8 us
    ppermute x30, starting transfers between devices, exchange(): return lax.ppermute(block, 'slot', [(i, i ^ mask) for i in range(n)])  22.7 us
    ppermute x3, waiting for transfers between devices, next_segment(): return lax.ppermute(block, ('segment', 'slot'), route)  7.46 us
    unnamed x28, local copies, waits for them, and re-layouts  6.34 us
    pallas_call x8, Pallas kernels, project(): pl.pallas_call(functools.partial(project_kernel, away=[masks for masks, _...  4.56 us
    ppermute x3, starting transfers between devices, next_segment(): return lax.ppermute(block, ('segment', 'slot'), route)  4.41 us
  transfers between devices with their start and end apart: 33, of which 20 were waited for; matrix products, arithmetic and copies ran while one was open for 0% of the time, Pallas kernels for 4%

profile of v9, /device:TPU:0, one launch (start us, length us, event | category | flops | bytes accessed | tf_op | source)
XLA Modules:
  0.0 101.0 jit_solution(13053944873698116278)
XLA Ops:
  0.0 4.0 %collective-permute-start = (bf16[64,512]{1,0:T(8,128)(2,1)}, bf16[64,512]{1,0:T(8,128)(2,1)S(1)}, u32[]{:S(2)}, u32[]{:S(2)}) collective-permute-start(bf16[64,512]{1,0:T(8,128)(2,1)} %bitcast.33), channel_id=1, source_target_pairs={{0,8},{1,9},{2,10},{3,11},{4,12},{5,13},{6,14},{7,15},{8,0},{9,1},... | collective-permute-start | bytes 196616 | tf_op jit(solution)/shard_map/ppermute | solution.py:32
  4.1 0.9 copy-done.3
  5.7 0.8 copy-done.6
  8.0 0.8 collective-permute-done.1
  8.9 1.6 %collective-permute-start.2 = (bf16[144,512]{1,0:T(8,128)(2,1)S(1)}, bf16[144,512]{1,0:T(8,128)(2,1)S(1)}, u32[]{:S(2)}, u32[]{:S(2)}) collective-permute-start(bf16[144,512]{1,0:T(8,128)(2,1)S(1)} %concatenate.20.refs_0_), channel_id=1, source_target_pairs={{0,4},{1,5},{2,6},{3,7},{4,0},{5,1},{6,2},{7,3},{8,12},{9,13},{10,... | collective-permute-start | bytes 442376 | tf_op jit(solution)/shard_map/ppermute | solution.py:32
  10.6 1.5 %collective-permute-start.4 = (bf16[144,512]{1,0:T(8,128)(2,1)S(1)}, bf16[144,512]{1,0:T(8,128)(2,1)S(1)}, u32[]{:S(2)}, u32[]{:S(2)}) collective-permute-start(bf16[144,512]{1,0:T(8,128)(2,1)S(1)} %concatenate.20.refs_0_), channel_id=1, source_target_pairs={{0,2},{1,3},{2,0},{3,1},{4,6},{5,7},{6,4},{7,5},{8,10},{9,11},{10,... | collective-permute-start | bytes 442376 | tf_op jit(solution)/shard_map/ppermute | solution.py:32
  12.1 2.1 %collective-permute-done.2.refs_0_ = bf16[144,512]{1,0:T(8,128)(2,1)S(1)} collective-permute-done((bf16[144,512]{1,0:T(8,128)(2,1)S(1)}, bf16[144,512]{1,0:T(8,128)(2,1)S(1)}, u32[]{:S(2)}, u32[]{:S(2)}) %collective-permute-start.2) | collective-permute-done | bytes 147488 | tf_op jit(solution)/shard_map/ppermute | solution.py:32
  14.1 1.5 %collective-permute-start.3 = (bf16[144,512]{1,0:T(8,128)(2,1)S(1)}, bf16[144,512]{1,0:T(8,128)(2,1)S(1)}, u32[]{:S(2)}, u32[]{:S(2)}) collective-permute-start(bf16[144,512]{1,0:T(8,128)(2,1)S(1)} %collective-permute-done.2.refs_0_), channel_id=1, source_target_pairs={{0,2},{1,3},{2,0},{3,1},{4,6},{5,7},{6,4},{7,5},{8,10},{9,11},{10,... | collective-permute-start | bytes 442376 | tf_op jit(solution)/shard_map/ppermute | solution.py:32
  15.6 2.5 %copy-done = bf16[1,8192,320]{1,2,0:T(8,128)(2,1)S(1)} copy-done((bf16[1,8192,320]{1,2,0:T(8,128)(2,1)S(1)}, bf16[1,8192,320]{1,2,0:T(8,128)(2,1)}, u32[]{:S(2)}) %copy-start) | copy-done | bytes 5242904
  22.2 15.6 %all_to_all.10.qkv_ref = bf16[16,8,1280]{2,1,0:T(8,128)(2,1)S(1)} all-to-all(bf16[16,8,1280]{2,1,0:T(8,128)(2,1)S(1)} %get-tuple-element.55), channel_id=1, replica_groups=mesh['segment'=2,'slot'=16] {'slot'}, dimensions={0} | all-to-all | bytes 655360 | tf_op jit(solution)/shard_map/all_to_all | solution.py:393
  38.5 1.4 %collective-permute-start.9 = (bf16[1,4,4096]{2,1,0:T(4,128)(2,1)S(1)}, bf16[1,4,4096]{2,1,0:T(4,128)(2,1)S(1)}, u32[]{:S(2)}, u32[]{:S(2)}) collective-permute-start(bf16[1,4,4096]{2,1,0:T(4,128)(2,1)S(1)} %attend.2), channel_id=1, source_target_pairs={{0,8},{1,9},{2,10},{3,11},{4,12},{5,13},{6,14},{7,15},{8,0},{9,1},... | collective-permute-start | bytes 98312 | tf_op jit(solution)/shard_map/ppermute | solution.py:32
  40.0 3.6 %collective-permute-done.9 = bf16[1,4,4096]{2,1,0:T(4,128)(2,1)S(1)} collective-permute-done((bf16[1,4,4096]{2,1,0:T(4,128)(2,1)S(1)}, bf16[1,4,4096]{2,1,0:T(4,128)(2,1)S(1)}, u32[]{:S(2)}, u32[]{:S(2)}) %collective-permute-start.9) | collective-permute-done | bytes 32800 | tf_op jit(solution)/shard_map/ppermute | solution.py:32
  43.6 0.8 collective-permute-start.12
  44.4 0.9 collective-permute-start.11
  45.4 1.8 %collective-permute-start.10 = (bf16[2,4,4096]{2,1,0:T(4,128)(2,1)S(1)}, bf16[2,4,4096]{2,1,0:T(4,128)(2,1)S(1)}, u32[]{:S(2)}, u32[]{:S(2)}) collective-permute-start(bf16[2,4,4096]{2,1,0:T(4,128)(2,1)S(1)} %pad_maximum_fusion.2.refs_0_), channel_id=1, source_target_pairs={{0,4},{1,5},{2,6},{3,7},{4,0},{5,1},{6,2},{7,3},{8,12},{9,13},{10,... | collective-permute-start | bytes 196616 | tf_op jit(solution)/shard_map/ppermute | solution.py:32
  47.2 1.8 %collective-permute-done.12.refs_3_ = bf16[2,4,4096]{2,1,0:T(4,128)(2,1)S(1)} collective-permute-done((bf16[2,4,4096]{2,1,0:T(4,128)(2,1)S(1)}, bf16[2,4,4096]{2,1,0:T(4,128)(2,1)S(1)}, u32[]{:S(2)}, u32[]{:S(2)}) %collective-permute-start.12) | collective-permute-done | bytes 65568 | tf_op jit(solution)/shard_map/ppermute | solution.py:32
  50.9 1.0 output.2
  51.9 2.5 %collective-permute-start.16 = (bf16[64,512]{1,0:T(8,128)(2,1)S(1)}, bf16[64,512]{1,0:T(8,128)(2,1)S(1)}, u32[]{:S(2)}, u32[]{:S(2)}) collective-permute-start(bf16[64,512]{1,0:T(8,128)(2,1)S(1)} %output.2), channel_id=1, source_target_pairs={{0,24},{1,25},{2,26},{3,27},{4,28},{5,29},{6,30},{7,31},{8,16},{9,... | collective-permute-start | bytes 196616 | tf_op jit(solution)/shard_map/ppermute | solution.py:58
  54.9 4.6 %collective-permute-done.16 = bf16[64,512]{1,0:T(8,128)(2,1)S(1)} collective-permute-done((bf16[64,512]{1,0:T(8,128)(2,1)S(1)}, bf16[64,512]{1,0:T(8,128)(2,1)S(1)}, u32[]{:S(2)}, u32[]{:S(2)}) %collective-permute-start.16) | collective-permute-done | bytes 65568 | tf_op jit(solution)/shard_map/ppermute | solution.py:58
  59.4 1.8 %collective-permute-start.18 = (bf16[128,512]{1,0:T(8,128)(2,1)S(1)}, bf16[128,512]{1,0:T(8,128)(2,1)S(1)}, u32[]{:S(2)}, u32[]{:S(2)}) collective-permute-start(bf16[128,512]{1,0:T(8,128)(2,1)S(1)} %constant_dynamic-update-slice_fusion.refs_0_), channel_id=1, source_target_pairs={{0,4},{1,5},{2,6},{3,7},{4,0},{5,1},{6,2},{7,3},{8,12},{9,13},{10,... | collective-permute-start | bytes 393224 | tf_op jit(solution)/shard_map/ppermute | solution.py:32
  61.6 3.3 %collective-permute-done.18.refs_0_ = bf16[128,512]{1,0:T(8,128)(2,1)S(1)} collective-permute-done((bf16[128,512]{1,0:T(8,128)(2,1)S(1)}, bf16[128,512]{1,0:T(8,128)(2,1)S(1)}, u32[]{:S(2)}, u32[]{:S(2)}) %collective-permute-start.18) | collective-permute-done | bytes 131104 | tf_op jit(solution)/shard_map/ppermute | solution.py:32
  66.0 1.5 %collective-permute-done.20.refs_1_ = bf16[128,512]{1,0:T(8,128)(2,1)S(1)} collective-permute-done((bf16[128,512]{1,0:T(8,128)(2,1)S(1)}, bf16[128,512]{1,0:T(8,128)(2,1)S(1)}, u32[]{:S(2)}, u32[]{:S(2)}) %collective-permute-start.20) | collective-permute-done | bytes 131104 | tf_op jit(solution)/shard_map/ppermute | solution.py:32
  68.6 1.3 %collective-permute-done.19.refs_0_ = bf16[128,512]{1,0:T(8,128)(2,1)S(1)} collective-permute-done((bf16[128,512]{1,0:T(8,128)(2,1)S(1)}, bf16[128,512]{1,0:T(8,128)(2,1)S(1)}, u32[]{:S(2)}, u32[]{:S(2)}) %collective-permute-start.19) | collective-permute-done | bytes 131104 | tf_op jit(solution)/shard_map/ppermute | solution.py:32
  71.8 10.4 %all_to_all.11.qkv_ref = bf16[16,4,320]{2,1,0:T(4,128)(2,1)S(1)} all-to-all(bf16[16,4,320]{2,1,0:T(4,128)(2,1)S(1)} %project.15), channel_id=1, replica_groups=mesh['segment'=2,'slot'=16] {'slot'}, dimensions={0} | all-to-all | bytes 81920 | tf_op jit(solution)/shard_map/all_to_all | solution.py:393
  83.2 4.5 %collective-permute-done.25 = bf16[1,4,4096]{2,1,0:T(4,128)(2,1)S(1)} collective-permute-done((bf16[1,4,4096]{2,1,0:T(4,128)(2,1)S(1)}, bf16[1,4,4096]{2,1,0:T(4,128)(2,1)S(1)}, u32[]{:S(2)}, u32[]{:S(2)}) %collective-permute-start.25) | collective-permute-done | bytes 32800 | tf_op jit(solution)/shard_map/ppermute | solution.py:32
  88.1 1.4 %collective-permute-start.27 = (bf16[2,4,4096]{2,1,0:T(4,128)(2,1)S(1)}, bf16[2,4,4096]{2,1,0:T(4,128)(2,1)S(1)}, u32[]{:S(2)}, u32[]{:S(2)}) collective-permute-start(bf16[2,4,4096]{2,1,0:T(4,128)(2,1)S(1)} %pad_maximum_fusion.3.refs_0_), channel_id=1, source_target_pairs={{0,2},{1,3},{2,0},{3,1},{4,6},{5,7},{6,4},{7,5},{8,10},{9,11},{10,... | collective-permute-start | bytes 196616 | tf_op jit(solution)/shard_map/ppermute | solution.py:32
  89.5 1.8 %collective-permute-start.26 = (bf16[2,4,4096]{2,1,0:T(4,128)(2,1)S(1)}, bf16[2,4,4096]{2,1,0:T(4,128)(2,1)S(1)}, u32[]{:S(2)}, u32[]{:S(2)}) collective-permute-start(bf16[2,4,4096]{2,1,0:T(4,128)(2,1)S(1)} %pad_maximum_fusion.3.refs_0_), channel_id=1, source_target_pairs={{0,4},{1,5},{2,6},{3,7},{4,0},{5,1},{6,2},{7,3},{8,12},{9,13},{10,... | collective-permute-start | bytes 196616 | tf_op jit(solution)/shard_map/ppermute | solution.py:32
  91.3 1.8 %collective-permute-done.28.refs_3_ = bf16[2,4,4096]{2,1,0:T(4,128)(2,1)S(1)} collective-permute-done((bf16[2,4,4096]{2,1,0:T(4,128)(2,1)S(1)}, bf16[2,4,4096]{2,1,0:T(4,128)(2,1)S(1)}, u32[]{:S(2)}, u32[]{:S(2)}) %collective-permute-start.28) | collective-permute-done | bytes 65568 | tf_op jit(solution)/shard_map/ppermute | solution.py:32
  93.8 0.8 collective-permute-done.30.refs_5_
  95.0 1.0 output.3
  96.0 1.4 %collective-permute-start.32 = (bf16[64,512]{1,0:T(8,128)(2,1)S(1)}, bf16[64,512]{1,0:T(8,128)(2,1)S(1)}, u32[]{:S(2)}, u32[]{:S(2)}) collective-permute-start(bf16[64,512]{1,0:T(8,128)(2,1)S(1)} %output.3), channel_id=1, source_target_pairs={{0,16},{1,17},{2,18},{3,19},{4,20},{5,21},{6,22},{7,23},{8,24},{9,... | collective-permute-start | bytes 196616 | tf_op jit(solution)/shard_map/ppermute | solution.py:58
  97.5 2.9 %collective-permute-done.32 = bf16[64,512]{1,0:T(8,128)(2,1)S(1)} collective-permute-done((bf16[64,512]{1,0:T(8,128)(2,1)S(1)}, bf16[64,512]{1,0:T(8,128)(2,1)S(1)}, u32[]{:S(2)}, u32[]{:S(2)}) %collective-permute-start.32) | collective-permute-done | bytes 65568 | tf_op jit(solution)/shard_map/ppermute | solution.py:58
  (85 shorter events, 17.0 us)
Async XLA Ops:
  0.0 8.7 %collective-permute-start = (bf16[64,512]{1,0:T(8,128)(2,1)}, bf16[64,512]{1,0:T(8,128)(2,1)S(1)}, u32[]{:S(2)}, u32[]{:S(2)}) collective-permute-start(bf16[64,512]{1,0:T(8,128)(2,1)} %bitcast.33), channel_id=1, source_target_pairs={{0,8},{1,9},{2,10},{3,11},{4,12},{5,13},{6,14},{7,15},{8,0},{9,1},... | collective-permute-start | bytes 196616 | tf_op jit(solution)/shard_map/ppermute | solution.py:32
  4.0 4.7 %collective-permute-start.1 = (bf16[1,512]{1,0:T(2,128)(2,1)}, bf16[1,512]{1,0:T(2,128)(2,1)S(1)}, u32[]{:S(2)}, u32[]{:S(2)}) collective-permute-start(bf16[1,512]{1,0:T(2,128)(2,1)} %gain_ref.1), channel_id=1, source_target_pairs={{0,8},{1,9},{2,10},{3,11},{4,12},{5,13},{6,14},{7,15},{8,0},{9,1},... | collective-permute-start | bytes 3080 | tf_op jit(solution)/shard_map/ppermute | solution.py:32
  8.9 5.2 %collective-permute-start.2 = (bf16[144,512]{1,0:T(8,128)(2,1)S(1)}, bf16[144,512]{1,0:T(8,128)(2,1)S(1)}, u32[]{:S(2)}, u32[]{:S(2)}) collective-permute-start(bf16[144,512]{1,0:T(8,128)(2,1)S(1)} %concatenate.20.refs_0_), channel_id=1, source_target_pairs={{0,4},{1,5},{2,6},{3,7},{4,0},{5,1},{6,2},{7,3},{8,12},{9,13},{10,... | collective-permute-start | bytes 442376 | tf_op jit(solution)/shard_map/ppermute | solution.py:32
  10.6 5.1 %collective-permute-start.5 = (bf16[144,512]{1,0:T(8,128)(2,1)S(1)}, bf16[144,512]{1,0:T(8,128)(2,1)S(1)}, u32[]{:S(2)}, u32[]{:S(2)}) collective-permute-start(bf16[144,512]{1,0:T(8,128)(2,1)S(1)} %concatenate.20.refs_0_), channel_id=1, source_target_pairs={{0,1},{1,0},{2,3},{3,2},{4,5},{5,4},{6,7},{7,6},{8,9},{9,8},{10,11... | collective-permute-start | bytes 442376 | tf_op jit(solution)/shard_map/ppermute | solution.py:32
  10.6 8.1 %collective-permute-start.4 = (bf16[144,512]{1,0:T(8,128)(2,1)S(1)}, bf16[144,512]{1,0:T(8,128)(2,1)S(1)}, u32[]{:S(2)}, u32[]{:S(2)}) collective-permute-start(bf16[144,512]{1,0:T(8,128)(2,1)S(1)} %concatenate.20.refs_0_), channel_id=1, source_target_pairs={{0,2},{1,3},{2,0},{3,1},{4,6},{5,7},{6,4},{7,5},{8,10},{9,11},{10,... | collective-permute-start | bytes 442376 | tf_op jit(solution)/shard_map/ppermute | solution.py:32
  14.1 5.9 %collective-permute-start.3 = (bf16[144,512]{1,0:T(8,128)(2,1)S(1)}, bf16[144,512]{1,0:T(8,128)(2,1)S(1)}, u32[]{:S(2)}, u32[]{:S(2)}) collective-permute-start(bf16[144,512]{1,0:T(8,128)(2,1)S(1)} %collective-permute-done.2.refs_0_), channel_id=1, source_target_pairs={{0,2},{1,3},{2,0},{3,1},{4,6},{5,7},{6,4},{7,5},{8,10},{9,11},{10,... | collective-permute-start | bytes 442376 | tf_op jit(solution)/shard_map/ppermute | solution.py:32
  19.2 1.4 %collective-permute-start.7 = (bf16[144,512]{1,0:T(8,128)(2,1)S(1)}, bf16[144,512]{1,0:T(8,128)(2,1)S(1)}, u32[]{:S(2)}, u32[]{:S(2)}) collective-permute-start(bf16[144,512]{1,0:T(8,128)(2,1)S(1)} %collective-permute-done.2.refs_0_), channel_id=1, source_target_pairs={{0,1},{1,0},{2,3},{3,2},{4,5},{5,4},{6,7},{7,6},{8,9},{9,8},{10,11... | collective-permute-start | bytes 442376 | tf_op jit(solution)/shard_map/ppermute | solution.py:32
  19.3 1.6 %collective-permute-start.8 = (bf16[144,512]{1,0:T(8,128)(2,1)S(1)}, bf16[144,512]{1,0:T(8,128)(2,1)S(1)}, u32[]{:S(2)}, u32[]{:S(2)}) collective-permute-start(bf16[144,512]{1,0:T(8,128)(2,1)S(1)} %collective-permute-done.4.refs_1_), channel_id=1, source_target_pairs={{0,1},{1,0},{2,3},{3,2},{4,5},{5,4},{6,7},{7,6},{8,9},{9,8},{10,11... | collective-permute-start | bytes 442376 | tf_op jit(solution)/shard_map/ppermute | solution.py:32
  20.0 1.6 %collective-permute-start.6 = (bf16[144,512]{1,0:T(8,128)(2,1)S(1)}, bf16[144,512]{1,0:T(8,128)(2,1)S(1)}, u32[]{:S(2)}, u32[]{:S(2)}) collective-permute-start(bf16[144,512]{1,0:T(8,128)(2,1)S(1)} %collective-permute-done.3.refs_0_), channel_id=1, source_target_pairs={{0,1},{1,0},{2,3},{3,2},{4,5},{5,4},{6,7},{7,6},{8,9},{9,8},{10,11... | collective-permute-start | bytes 442376 | tf_op jit(solution)/shard_map/ppermute | solution.py:32
  38.5 5.0 %collective-permute-start.9 = (bf16[1,4,4096]{2,1,0:T(4,128)(2,1)S(1)}, bf16[1,4,4096]{2,1,0:T(4,128)(2,1)S(1)}, u32[]{:S(2)}, u32[]{:S(2)}) collective-permute-start(bf16[1,4,4096]{2,1,0:T(4,128)(2,1)S(1)} %attend.2), channel_id=1, source_target_pairs={{0,8},{1,9},{2,10},{3,11},{4,12},{5,13},{6,14},{7,15},{8,0},{9,1},... | collective-permute-start | bytes 98312 | tf_op jit(solution)/shard_map/ppermute | solution.py:32
  43.6 5.3 %collective-permute-start.12 = (bf16[2,4,4096]{2,1,0:T(4,128)(2,1)S(1)}, bf16[2,4,4096]{2,1,0:T(4,128)(2,1)S(1)}, u32[]{:S(2)}, u32[]{:S(2)}) collective-permute-start(bf16[2,4,4096]{2,1,0:T(4,128)(2,1)S(1)} %pad_maximum_fusion.2.refs_0_), channel_id=1, source_target_pairs={{0,6},{1,7},{2,4},{3,5},{4,2},{5,3},{6,0},{7,1},{8,14},{9,15},{10,... | collective-permute-start | bytes 196616 | tf_op jit(solution)/shard_map/ppermute | solution.py:32
  44.4 5.0 %collective-permute-start.11 = (bf16[2,4,4096]{2,1,0:T(4,128)(2,1)S(1)}, bf16[2,4,4096]{2,1,0:T(4,128)(2,1)S(1)}, u32[]{:S(2)}, u32[]{:S(2)}) collective-permute-start(bf16[2,4,4096]{2,1,0:T(4,128)(2,1)S(1)} %pad_maximum_fusion.2.refs_0_), channel_id=1, source_target_pairs={{0,2},{1,3},{2,0},{3,1},{4,6},{5,7},{6,4},{7,5},{8,10},{9,11},{10,... | collective-permute-start | bytes 196616 | tf_op jit(solution)/shard_map/ppermute | solution.py:32
  45.4 4.3 %collective-permute-start.10 = (bf16[2,4,4096]{2,1,0:T(4,128)(2,1)S(1)}, bf16[2,4,4096]{2,1,0:T(4,128)(2,1)S(1)}, u32[]{:S(2)}, u32[]{:S(2)}) collective-permute-start(bf16[2,4,4096]{2,1,0:T(4,128)(2,1)S(1)} %pad_maximum_fusion.2.refs_0_), channel_id=1, source_target_pairs={{0,4},{1,5},{2,6},{3,7},{4,0},{5,1},{6,2},{7,3},{8,12},{9,13},{10,... | collective-permute-start | bytes 196616 | tf_op jit(solution)/shard_map/ppermute | solution.py:32
  49.0 1.8 %collective-permute-start.13 = (bf16[4,4,4096]{2,1,0:T(4,128)(2,1)S(1)}, bf16[4,4,4096]{2,1,0:T(4,128)(2,1)S(1)}, u32[]{:S(2)}, u32[]{:S(2)}) collective-permute-start(bf16[4,4,4096]{2,1,0:T(4,128)(2,1)S(1)} %pad_maximum_fusion), channel_id=1, source_target_pairs={{0,1},{1,0},{2,3},{3,2},{4,5},{5,4},{6,7},{7,6},{8,9},{9,8},{10,11... | collective-permute-start | bytes 393224 | tf_op jit(solution)/shard_map/ppermute | solution.py:32
  49.4 1.3 %collective-permute-start.14 = (bf16[2,4,4096]{2,1,0:T(4,128)(2,1)S(1)}, bf16[2,4,4096]{2,1,0:T(4,128)(2,1)S(1)}, u32[]{:S(2)}, u32[]{:S(2)}) collective-permute-start(bf16[2,4,4096]{2,1,0:T(4,128)(2,1)S(1)} %collective-permute-done.11.refs_2_), channel_id=1, source_target_pairs={{0,1},{1,0},{2,3},{3,2},{4,5},{5,4},{6,7},{7,6},{8,9},{9,8},{10,11... | collective-permute-start | bytes 196616 | tf_op jit(solution)/shard_map/ppermute | solution.py:32
  49.6 1.3 %collective-permute-start.15 = (bf16[2,4,4096]{2,1,0:T(4,128)(2,1)S(1)}, bf16[2,4,4096]{2,1,0:T(4,128)(2,1)S(1)}, u32[]{:S(2)}, u32[]{:S(2)}) collective-permute-start(bf16[2,4,4096]{2,1,0:T(4,128)(2,1)S(1)} %collective-permute-done.10.refs_1_), channel_id=1, source_target_pairs={{0,1},{1,0},{2,3},{3,2},{4,5},{5,4},{6,7},{7,6},{8,9},{9,8},{10,11... | collective-permute-start | bytes 196616 | tf_op jit(solution)/shard_map/ppermute | solution.py:32
  51.9 7.5 %collective-permute-start.16 = (bf16[64,512]{1,0:T(8,128)(2,1)S(1)}, bf16[64,512]{1,0:T(8,128)(2,1)S(1)}, u32[]{:S(2)}, u32[]{:S(2)}) collective-permute-start(bf16[64,512]{1,0:T(8,128)(2,1)S(1)} %output.2), channel_id=1, source_target_pairs={{0,24},{1,25},{2,26},{3,27},{4,28},{5,29},{6,30},{7,31},{8,16},{9,... | collective-permute-start | bytes 196616 | tf_op jit(solution)/shard_map/ppermute | solution.py:58
  54.3 5.1 %collective-permute-start.17 = (bf16[64,512]{1,0:T(8,128)(2,1)S(1)}, bf16[64,512]{1,0:T(8,128)(2,1)S(1)}, u32[]{:S(2)}, u32[]{:S(2)}) collective-permute-start(bf16[64,512]{1,0:T(8,128)(2,1)S(1)} %output.2), channel_id=1, source_target_pairs={{0,16},{1,17},{2,18},{3,19},{4,20},{5,21},{6,22},{7,23},{8,24},{9,... | collective-permute-start | bytes 196616 | tf_op jit(solution)/shard_map/ppermute | solution.py:58
  59.4 5.4 %collective-permute-start.18 = (bf16[128,512]{1,0:T(8,128)(2,1)S(1)}, bf16[128,512]{1,0:T(8,128)(2,1)S(1)}, u32[]{:S(2)}, u32[]{:S(2)}) collective-permute-start(bf16[128,512]{1,0:T(8,128)(2,1)S(1)} %constant_dynamic-update-slice_fusion.refs_0_), channel_id=1, source_target_pairs={{0,4},{1,5},{2,6},{3,7},{4,0},{5,1},{6,2},{7,3},{8,12},{9,13},{10,... | collective-permute-start | bytes 393224 | tf_op jit(solution)/shard_map/ppermute | solution.py:32
  61.2 4.3 %collective-permute-start.21 = (bf16[128,512]{1,0:T(8,128)(2,1)S(1)}, bf16[128,512]{1,0:T(8,128)(2,1)S(1)}, u32[]{:S(2)}, u32[]{:S(2)}) collective-permute-start(bf16[128,512]{1,0:T(8,128)(2,1)S(1)} %constant_dynamic-update-slice_fusion.refs_0_), channel_id=1, source_target_pairs={{0,1},{1,0},{2,3},{3,2},{4,5},{5,4},{6,7},{7,6},{8,9},{9,8},{10,11... | collective-permute-start | bytes 393224 | tf_op jit(solution)/shard_map/ppermute | solution.py:32
  61.2 6.3 %collective-permute-start.20 = (bf16[128,512]{1,0:T(8,128)(2,1)S(1)}, bf16[128,512]{1,0:T(8,128)(2,1)S(1)}, u32[]{:S(2)}, u32[]{:S(2)}) collective-permute-start(bf16[128,512]{1,0:T(8,128)(2,1)S(1)} %constant_dynamic-update-slice_fusion.refs_0_), channel_id=1, source_target_pairs={{0,2},{1,3},{2,0},{3,1},{4,6},{5,7},{6,4},{7,5},{8,10},{9,11},{10,... | collective-permute-start | bytes 393224 | tf_op jit(solution)/shard_map/ppermute | solution.py:32
  64.9 5.1 %collective-permute-start.19 = (bf16[128,512]{1,0:T(8,128)(2,1)S(1)}, bf16[128,512]{1,0:T(8,128)(2,1)S(1)}, u32[]{:S(2)}, u32[]{:S(2)}) collective-permute-start(bf16[128,512]{1,0:T(8,128)(2,1)S(1)} %collective-permute-done.18.refs_0_), channel_id=1, source_target_pairs={{0,2},{1,3},{2,0},{3,1},{4,6},{5,7},{6,4},{7,5},{8,10},{9,11},{10,... | collective-permute-start | bytes 393224 | tf_op jit(solution)/shard_map/ppermute | solution.py:32
  68.0 1.9 %collective-permute-start.23 = (bf16[128,512]{1,0:T(8,128)(2,1)S(1)}, bf16[128,512]{1,0:T(8,128)(2,1)S(1)}, u32[]{:S(2)}, u32[]{:S(2)}) collective-permute-start(bf16[128,512]{1,0:T(8,128)(2,1)S(1)} %collective-permute-done.18.refs_0_), channel_id=1, source_target_pairs={{0,1},{1,0},{2,3},{3,2},{4,5},{5,4},{6,7},{7,6},{8,9},{9,8},{10,11... | collective-permute-start | bytes 393224 | tf_op jit(solution)/shard_map/ppermute | solution.py:32
  68.1 1.8 %collective-permute-start.24 = (bf16[128,512]{1,0:T(8,128)(2,1)S(1)}, bf16[128,512]{1,0:T(8,128)(2,1)S(1)}, u32[]{:S(2)}, u32[]{:S(2)}) collective-permute-start(bf16[128,512]{1,0:T(8,128)(2,1)S(1)} %collective-permute-done.20.refs_1_), channel_id=1, source_target_pairs={{0,1},{1,0},{2,3},{3,2},{4,5},{5,4},{6,7},{7,6},{8,9},{9,8},{10,11... | collective-permute-start | bytes 393224 | tf_op jit(solution)/shard_map/ppermute | solution.py:32
  69.9 1.3 %collective-permute-start.22 = (bf16[128,512]{1,0:T(8,128)(2,1)S(1)}, bf16[128,512]{1,0:T(8,128)(2,1)S(1)}, u32[]{:S(2)}, u32[]{:S(2)}) collective-permute-start(bf16[128,512]{1,0:T(8,128)(2,1)S(1)} %collective-permute-done.19.refs_0_), channel_id=1, source_target_pairs={{0,1},{1,0},{2,3},{3,2},{4,5},{5,4},{6,7},{7,6},{8,9},{9,8},{10,11... | collective-permute-start | bytes 393224 | tf_op jit(solution)/shard_map/ppermute | solution.py:32
  82.8 4.9 %collective-permute-start.25 = (bf16[1,4,4096]{2,1,0:T(4,128)(2,1)S(1)}, bf16[1,4,4096]{2,1,0:T(4,128)(2,1)S(1)}, u32[]{:S(2)}, u32[]{:S(2)}) collective-permute-start(bf16[1,4,4096]{2,1,0:T(4,128)(2,1)S(1)} %attend.3), channel_id=1, source_target_pairs={{0,8},{1,9},{2,10},{3,11},{4,12},{5,13},{6,14},{7,15},{8,0},{9,1},... | collective-permute-start | bytes 98312 | tf_op jit(solution)/shard_map/ppermute | solution.py:32
  87.7 5.3 %collective-permute-start.28 = (bf16[2,4,4096]{2,1,0:T(4,128)(2,1)S(1)}, bf16[2,4,4096]{2,1,0:T(4,128)(2,1)S(1)}, u32[]{:S(2)}, u32[]{:S(2)}) collective-permute-start(bf16[2,4,4096]{2,1,0:T(4,128)(2,1)S(1)} %pad_maximum_fusion.3.refs_0_), channel_id=1, source_target_pairs={{0,6},{1,7},{2,4},{3,5},{4,2},{5,3},{6,0},{7,1},{8,14},{9,15},{10,... | collective-permute-start | bytes 196616 | tf_op jit(solution)/shard_map/ppermute | solution.py:32
  88.1 5.1 %collective-permute-start.27 = (bf16[2,4,4096]{2,1,0:T(4,128)(2,1)S(1)}, bf16[2,4,4096]{2,1,0:T(4,128)(2,1)S(1)}, u32[]{:S(2)}, u32[]{:S(2)}) collective-permute-start(bf16[2,4,4096]{2,1,0:T(4,128)(2,1)S(1)} %pad_maximum_fusion.3.refs_0_), channel_id=1, source_target_pairs={{0,2},{1,3},{2,0},{3,1},{4,6},{5,7},{6,4},{7,5},{8,10},{9,11},{10,... | collective-permute-start | bytes 196616 | tf_op jit(solution)/shard_map/ppermute | solution.py:32
  89.5 4.3 %collective-permute-start.26 = (bf16[2,4,4096]{2,1,0:T(4,128)(2,1)S(1)}, bf16[2,4,4096]{2,1,0:T(4,128)(2,1)S(1)}, u32[]{:S(2)}, u32[]{:S(2)}) collective-permute-start(bf16[2,4,4096]{2,1,0:T(4,128)(2,1)S(1)} %pad_maximum_fusion.3.refs_0_), channel_id=1, source_target_pairs={{0,4},{1,5},{2,6},{3,7},{4,0},{5,1},{6,2},{7,3},{8,12},{9,13},{10,... | collective-permute-start | bytes 196616 | tf_op jit(solution)/shard_map/ppermute | solution.py:32
  93.2 1.9 %collective-permute-start.29 = (bf16[4,4,4096]{2,1,0:T(4,128)(2,1)S(1)}, bf16[4,4,4096]{2,1,0:T(4,128)(2,1)S(1)}, u32[]{:S(2)}, u32[]{:S(2)}) collective-permute-start(bf16[4,4,4096]{2,1,0:T(4,128)(2,1)S(1)} %pad_maximum_fusion.1), channel_id=1, source_target_pairs={{0,1},{1,0},{2,3},{3,2},{4,5},{5,4},{6,7},{7,6},{8,9},{9,8},{10,11... | collective-permute-start | bytes 393224 | tf_op jit(solution)/shard_map/ppermute | solution.py:32
  93.2 1.4 %collective-permute-start.30 = (bf16[2,4,4096]{2,1,0:T(4,128)(2,1)S(1)}, bf16[2,4,4096]{2,1,0:T(4,128)(2,1)S(1)}, u32[]{:S(2)}, u32[]{:S(2)}) collective-permute-start(bf16[2,4,4096]{2,1,0:T(4,128)(2,1)S(1)} %collective-permute-done.27.refs_2_), channel_id=1, source_target_pairs={{0,1},{1,0},{2,3},{3,2},{4,5},{5,4},{6,7},{7,6},{8,9},{9,8},{10,11... | collective-permute-start | bytes 196616 | tf_op jit(solution)/shard_map/ppermute | solution.py:32
  96.0 4.3 %collective-permute-start.32 = (bf16[64,512]{1,0:T(8,128)(2,1)S(1)}, bf16[64,512]{1,0:T(8,128)(2,1)S(1)}, u32[]{:S(2)}, u32[]{:S(2)}) collective-permute-start(bf16[64,512]{1,0:T(8,128)(2,1)S(1)} %output.3), channel_id=1, source_target_pairs={{0,16},{1,17},{2,18},{3,19},{4,20},{5,21},{6,22},{7,23},{8,24},{9,... | collective-permute-start | bytes 196616 | tf_op jit(solution)/shard_map/ppermute | solution.py:58
  (14 other events, 135.9 us)

commit v10 on v9

--- a/solution.py
+++ b/solution.py
@@ -33,22 +33,25 @@
 
 
 def gather(block, phases):
-    held = [([0], block)]
-    for phase in phases:
-        merged = block if len(held) == 1 else jnp.concatenate([b for _, b in held], axis=0)
-        names = [m for n, _ in held for m in n]
-        if phase == phases[-1]:
-            core = phase[0]
-            for some in [[0, 3], [2], [1]]:
-                both = [held[k] for k in some]
-                away = [core ^ m for n, _ in both for m in n]
-                both = [b for _, b in both]
-                both = both[0] if len(both) == 1 else jnp.concatenate(both, axis=0)
-                held = held + [(away, exchange(both, core))]
-            return held
-        if len(held) > 1:
-            held = [(names, merged)]
-        held = held + [([m ^ n for n in names], exchange(merged, m)) for m in phase]
+    core = phases[-1][0]
+    names, merged, crossed = [0], block, exchange(block, core)
+    for phase in phases[:-2]:
+        arrived = exchange(merged, phase[0])
+        if merged is block:
+            arrived, crossed = lax.optimization_barrier((arrived, crossed))
+        names = names + [m ^ phase[0] for m in names]
+        merged = jnp.concatenate([merged, arrived], axis=0)
+    held = [(names, merged)]
+    held += [([m ^ n for n in names], exchange(merged, m)) for m in phases[-2]]
+    across = [([core], crossed)]
+    for some in [[0, 3], [2], [1]]:
+        away = [m ^ core for k in some for m in held[k][0]]
+        parts = [held[k][1] for k in some]
+        if 0 in some:
+            away, parts[0] = away[1:], parts[0][1:]
+        parts = parts[0] if len(parts) == 1 else jnp.concatenate(parts, axis=0)
+        across.append((away, exchange(parts, core)))
+    return held + across
 
 
 def next_segment(block, mask=0):

time: 101 us -> 102 us (level)
  waiting for transfers between devices: 32.2 us -> 33.8 us
    ppermute x30 -> x32, waiting for transfers between devices: 24.8 us -> 25.7 us  [exchange(): return lax.ppermute(block, 'slot', [(i, i ^ mask) for i in range(n)])]
    ppermute x30 -> x32, starting transfers between devices: 22.7 us -> 22.3 us  [exchange(): return lax.ppermute(block, 'slot', [(i, i ^ mask) for i in range(n)])]
  transfers between devices with their start and end apart: 33 -> 35, of which waited for: 20 -> 23; matrix products, arithmetic and copies ran while one was open for 0% -> 0% of each run, Pallas kernels for 4% -> 4%
where the time goes in v10:
time: 102 us; the launch traced here: 101 us
  waiting for transfers between devices  33.8 us (33%)
  starting transfers between devices  26.1 us (26%)
  blocking collectives  25.9 us (25%)
  Pallas kernels  8.55 us (8%)
  local copies, waits for them, and re-layouts  6.52 us (6%)
    all_to_all x2, blocking collectives, shards(): qkv = lax.all_to_all(qkv, 'slot', split_axis=0, concat_axis=0, tiled=True)  25.9 us
    ppermute x32, waiting for transfers between devices, exchange(): return lax.ppermute(block, 'slot', [(i, i ^ mask) for i in range(n)])  25.7 us
    ppermute x32, starting transfers between devices, exchange(): return lax.ppermute(block, 'slot', [(i, i ^ mask) for i in range(n)])  22.3 us
    ppermute x3, waiting for transfers between devices, next_segment(): return lax.ppermute(block, ('segment', 'slot'), route)  8.01 us
    unnamed x28, local copies, waits for them, and re-layouts  6.34 us
    pallas_call x8, Pallas kernels, project(): pl.pallas_call(functools.partial(project_kernel, away=[masks for masks, _...  4.56 us
    ppermute x3, starting transfers between devices, next_segment(): return lax.ppermute(block, ('segment', 'slot'), route)  3.86 us
  transfers between devices with their start and end apart: 35, of which 23 were waited for; matrix products, arithmetic and copies ran while one was open for 0% of the time, Pallas kernels for 4%

profile of v10, /device:TPU:0, one launch (start us, length us, event | category | flops | bytes accessed | tf_op | source)
XLA Modules:
  0.0 101.4 jit_solution(8584332324947106850)
XLA Ops:
  0.0 4.0 %collective-permute-start = (bf16[64,512]{1,0:T(8,128)(2,1)}, bf16[64,512]{1,0:T(8,128)(2,1)S(1)}, u32[]{:S(2)}, u32[]{:S(2)}) collective-permute-start(bf16[64,512]{1,0:T(8,128)(2,1)} %bitcast.33), channel_id=1, source_target_pairs={{0,8},{1,9},{2,10},{3,11},{4,12},{5,13},{6,14},{7,15},{8,0},{9,1},... | collective-permute-start | bytes 196616 | tf_op jit(solution)/shard_map/ppermute | solution.py:32
  4.1 0.9 copy-done.3
  5.7 0.8 copy-done.6
  8.0 0.8 collective-permute-done.1
  8.9 1.6 %collective-permute-start.2 = (bf16[144,512]{1,0:T(8,128)(2,1)S(1)}, bf16[144,512]{1,0:T(8,128)(2,1)S(1)}, u32[]{:S(2)}, u32[]{:S(2)}) collective-permute-start(bf16[144,512]{1,0:T(8,128)(2,1)S(1)} %concatenate.18.refs_0_), channel_id=1, source_target_pairs={{0,4},{1,5},{2,6},{3,7},{4,0},{5,1},{6,2},{7,3},{8,12},{9,13},{10,... | collective-permute-start | bytes 442376 | tf_op jit(solution)/shard_map/ppermute | solution.py:32
  10.6 1.5 %collective-permute-start.4 = (bf16[144,512]{1,0:T(8,128)(2,1)S(1)}, bf16[144,512]{1,0:T(8,128)(2,1)S(1)}, u32[]{:S(2)}, u32[]{:S(2)}) collective-permute-start(bf16[144,512]{1,0:T(8,128)(2,1)S(1)} %concatenate.18.refs_0_), channel_id=1, source_target_pairs={{0,2},{1,3},{2,0},{3,1},{4,6},{5,7},{6,4},{7,5},{8,10},{9,11},{10,... | collective-permute-start | bytes 442376 | tf_op jit(solution)/shard_map/ppermute | solution.py:32
  12.1 2.1 %collective-permute-done.2.refs_0_ = bf16[144,512]{1,0:T(8,128)(2,1)S(1)} collective-permute-done((bf16[144,512]{1,0:T(8,128)(2,1)S(1)}, bf16[144,512]{1,0:T(8,128)(2,1)S(1)}, u32[]{:S(2)}, u32[]{:S(2)}) %collective-permute-start.2) | collective-permute-done | bytes 147488 | tf_op jit(solution)/shard_map/ppermute | solution.py:32
  14.1 1.5 %collective-permute-start.3 = (bf16[144,512]{1,0:T(8,128)(2,1)S(1)}, bf16[144,512]{1,0:T(8,128)(2,1)S(1)}, u32[]{:S(2)}, u32[]{:S(2)}) collective-permute-start(bf16[144,512]{1,0:T(8,128)(2,1)S(1)} %collective-permute-done.2.refs_0_), channel_id=1, source_target_pairs={{0,2},{1,3},{2,0},{3,1},{4,6},{5,7},{6,4},{7,5},{8,10},{9,11},{10,... | collective-permute-start | bytes 442376 | tf_op jit(solution)/shard_map/ppermute | solution.py:32
  15.6 2.5 %copy-done = bf16[1,8192,320]{1,2,0:T(8,128)(2,1)S(1)} copy-done((bf16[1,8192,320]{1,2,0:T(8,128)(2,1)S(1)}, bf16[1,8192,320]{1,2,0:T(8,128)(2,1)}, u32[]{:S(2)}) %copy-start) | copy-done | bytes 5242904
  22.2 15.6 %all_to_all.10.qkv_ref = bf16[16,8,1280]{2,1,0:T(8,128)(2,1)S(1)} all-to-all(bf16[16,8,1280]{2,1,0:T(8,128)(2,1)S(1)} %get-tuple-element.59), channel_id=1, replica_groups=mesh['segment'=2,'slot'=16] {'slot'}, dimensions={0} | all-to-all | bytes 655360 | tf_op jit(solution)/shard_map/all_to_all | solution.py:396
  38.7 1.4 %collective-permute-start.9 = (bf16[1,4,4096]{2,1,0:T(4,128)(2,1)S(1)}, bf16[1,4,4096]{2,1,0:T(4,128)(2,1)S(1)}, u32[]{:S(2)}, u32[]{:S(2)}) collective-permute-start(bf16[1,4,4096]{2,1,0:T(4,128)(2,1)S(1)} %attend.2), channel_id=1, source_target_pairs={{0,8},{1,9},{2,10},{3,11},{4,12},{5,13},{6,14},{7,15},{8,0},{9,1},... | collective-permute-start | bytes 98312 | tf_op jit(solution)/shard_map/ppermute | solution.py:32
  40.0 3.9 %collective-permute-done.9 = bf16[1,4,4096]{2,1,0:T(4,128)(2,1)S(1)} collective-permute-done((bf16[1,4,4096]{2,1,0:T(4,128)(2,1)S(1)}, bf16[1,4,4096]{2,1,0:T(4,128)(2,1)S(1)}, u32[]{:S(2)}, u32[]{:S(2)}) %collective-permute-start.9) | collective-permute-done | bytes 32800 | tf_op jit(solution)/shard_map/ppermute | solution.py:32
  44.7 1.3 %collective-permute-start.12 = (bf16[2,4,4096]{2,1,0:T(4,128)(2,1)S(1)}, bf16[2,4,4096]{2,1,0:T(4,128)(2,1)S(1)}, u32[]{:S(2)}, u32[]{:S(2)}) collective-permute-start(bf16[2,4,4096]{2,1,0:T(4,128)(2,1)S(1)} %pad_maximum_fusion.2.refs_0_), channel_id=1, source_target_pairs={{0,2},{1,3},{2,0},{3,1},{4,6},{5,7},{6,4},{7,5},{8,10},{9,11},{10,... | collective-permute-start | bytes 196616 | tf_op jit(solution)/shard_map/ppermute | solution.py:32
  46.1 1.5 %collective-permute-start.11 = (bf16[2,4,4096]{2,1,0:T(4,128)(2,1)S(1)}, bf16[2,4,4096]{2,1,0:T(4,128)(2,1)S(1)}, u32[]{:S(2)}, u32[]{:S(2)}) collective-permute-start(bf16[2,4,4096]{2,1,0:T(4,128)(2,1)S(1)} %pad_maximum_fusion.2.refs_0_), channel_id=1, source_target_pairs={{0,4},{1,5},{2,6},{3,7},{4,0},{5,1},{6,2},{7,3},{8,12},{9,13},{10,... | collective-permute-start | bytes 196616 | tf_op jit(solution)/shard_map/ppermute | solution.py:32
  47.6 1.8 %collective-permute-done.13.refs_3_ = bf16[2,4,4096]{2,1,0:T(4,128)(2,1)S(1)} collective-permute-done((bf16[2,4,4096]{2,1,0:T(4,128)(2,1)S(1)}, bf16[2,4,4096]{2,1,0:T(4,128)(2,1)S(1)}, u32[]{:S(2)}, u32[]{:S(2)}) %collective-permute-start.13) | collective-permute-done | bytes 65568 | tf_op jit(solution)/shard_map/ppermute | solution.py:32
  51.6 1.0 output.2
  52.6 2.0 %collective-permute-start.17 = (bf16[64,512]{1,0:T(8,128)(2,1)S(1)}, bf16[64,512]{1,0:T(8,128)(2,1)S(1)}, u32[]{:S(2)}, u32[]{:S(2)}) collective-permute-start(bf16[64,512]{1,0:T(8,128)(2,1)S(1)} %output.2), channel_id=1, source_target_pairs={{0,24},{1,25},{2,26},{3,27},{4,28},{5,29},{6,30},{7,31},{8,16},{9,... | collective-permute-start | bytes 196616 | tf_op jit(solution)/shard_map/ppermute | solution.py:61
  55.1 5.0 %collective-permute-done.17 = bf16[64,512]{1,0:T(8,128)(2,1)S(1)} collective-permute-done((bf16[64,512]{1,0:T(8,128)(2,1)S(1)}, bf16[64,512]{1,0:T(8,128)(2,1)S(1)}, u32[]{:S(2)}, u32[]{:S(2)}) %collective-permute-start.17) | collective-permute-done | bytes 65568 | tf_op jit(solution)/shard_map/ppermute | solution.py:61
  60.1 1.1 %collective-permute-start.19 = (bf16[128,512]{1,0:T(8,128)(2,1)S(1)}, bf16[128,512]{1,0:T(8,128)(2,1)S(1)}, u32[]{:S(2)}, u32[]{:S(2)}) collective-permute-start(bf16[128,512]{1,0:T(8,128)(2,1)S(1)} %constant_dynamic-update-slice_fusion.refs_0_), channel_id=1, source_target_pairs={{0,4},{1,5},{2,6},{3,7},{4,0},{5,1},{6,2},{7,3},{8,12},{9,13},{10,... | collective-permute-start | bytes 393224 | tf_op jit(solution)/shard_map/ppermute | solution.py:32
  61.9 3.3 %collective-permute-done.19.refs_0_ = bf16[128,512]{1,0:T(8,128)(2,1)S(1)} collective-permute-done((bf16[128,512]{1,0:T(8,128)(2,1)S(1)}, bf16[128,512]{1,0:T(8,128)(2,1)S(1)}, u32[]{:S(2)}, u32[]{:S(2)}) %collective-permute-start.19) | collective-permute-done | bytes 131104 | tf_op jit(solution)/shard_map/ppermute | solution.py:32
  66.3 1.3 %collective-permute-done.21.refs_1_ = bf16[128,512]{1,0:T(8,128)(2,1)S(1)} collective-permute-done((bf16[128,512]{1,0:T(8,128)(2,1)S(1)}, bf16[128,512]{1,0:T(8,128)(2,1)S(1)}, u32[]{:S(2)}, u32[]{:S(2)}) %collective-permute-start.21) | collective-permute-done | bytes 131104 | tf_op jit(solution)/shard_map/ppermute | solution.py:32
  68.7 1.5 %collective-permute-done.20.refs_0_ = bf16[128,512]{1,0:T(8,128)(2,1)S(1)} collective-permute-done((bf16[128,512]{1,0:T(8,128)(2,1)S(1)}, bf16[128,512]{1,0:T(8,128)(2,1)S(1)}, u32[]{:S(2)}, u32[]{:S(2)}) %collective-permute-start.20) | collective-permute-done | bytes 131104 | tf_op jit(solution)/shard_map/ppermute | solution.py:32
  72.0 10.3 %all_to_all.11.qkv_ref = bf16[16,4,320]{2,1,0:T(4,128)(2,1)S(1)} all-to-all(bf16[16,4,320]{2,1,0:T(4,128)(2,1)S(1)} %project.15), channel_id=1, replica_groups=mesh['segment'=2,'slot'=16] {'slot'}, dimensions={0} | all-to-all | bytes 81920 | tf_op jit(solution)/shard_map/all_to_all | solution.py:396
  83.5 0.8 collective-permute-done.27.refs_4_
  84.2 3.9 %collective-permute-done.26 = bf16[1,4,4096]{2,1,0:T(4,128)(2,1)S(1)} collective-permute-done((bf16[1,4,4096]{2,1,0:T(4,128)(2,1)S(1)}, bf16[1,4,4096]{2,1,0:T(4,128)(2,1)S(1)}, u32[]{:S(2)}, u32[]{:S(2)}) %collective-permute-start.26) | collective-permute-done | bytes 32800 | tf_op jit(solution)/shard_map/ppermute | solution.py:32
  88.4 1.5 %collective-permute-start.29 = (bf16[2,4,4096]{2,1,0:T(4,128)(2,1)S(1)}, bf16[2,4,4096]{2,1,0:T(4,128)(2,1)S(1)}, u32[]{:S(2)}, u32[]{:S(2)}) collective-permute-start(bf16[2,4,4096]{2,1,0:T(4,128)(2,1)S(1)} %pad_maximum_fusion.3.refs_0_), channel_id=1, source_target_pairs={{0,2},{1,3},{2,0},{3,1},{4,6},{5,7},{6,4},{7,5},{8,10},{9,11},{10,... | collective-permute-start | bytes 196616 | tf_op jit(solution)/shard_map/ppermute | solution.py:32
  89.9 1.8 %collective-permute-start.28 = (bf16[2,4,4096]{2,1,0:T(4,128)(2,1)S(1)}, bf16[2,4,4096]{2,1,0:T(4,128)(2,1)S(1)}, u32[]{:S(2)}, u32[]{:S(2)}) collective-permute-start(bf16[2,4,4096]{2,1,0:T(4,128)(2,1)S(1)} %pad_maximum_fusion.3.refs_0_), channel_id=1, source_target_pairs={{0,4},{1,5},{2,6},{3,7},{4,0},{5,1},{6,2},{7,3},{8,12},{9,13},{10,... | collective-permute-start | bytes 196616 | tf_op jit(solution)/shard_map/ppermute | solution.py:32
  91.7 1.7 %collective-permute-done.30.refs_3_ = bf16[2,4,4096]{2,1,0:T(4,128)(2,1)S(1)} collective-permute-done((bf16[2,4,4096]{2,1,0:T(4,128)(2,1)S(1)}, bf16[2,4,4096]{2,1,0:T(4,128)(2,1)S(1)}, u32[]{:S(2)}, u32[]{:S(2)}) %collective-permute-start.30) | collective-permute-done | bytes 65568 | tf_op jit(solution)/shard_map/ppermute | solution.py:32
  94.2 0.8 collective-permute-done.32.refs_6_
  95.4 1.0 output.3
  96.4 1.3 %collective-permute-start.34 = (bf16[64,512]{1,0:T(8,128)(2,1)S(1)}, bf16[64,512]{1,0:T(8,128)(2,1)S(1)}, u32[]{:S(2)}, u32[]{:S(2)}) collective-permute-start(bf16[64,512]{1,0:T(8,128)(2,1)S(1)} %output.3), channel_id=1, source_target_pairs={{0,16},{1,17},{2,18},{3,19},{4,20},{5,21},{6,22},{7,23},{8,24},{9,... | collective-permute-start | bytes 196616 | tf_op jit(solution)/shard_map/ppermute | solution.py:61
  97.7 3.0 %collective-permute-done.34 = bf16[64,512]{1,0:T(8,128)(2,1)S(1)} collective-permute-done((bf16[64,512]{1,0:T(8,128)(2,1)S(1)}, bf16[64,512]{1,0:T(8,128)(2,1)S(1)}, u32[]{:S(2)}, u32[]{:S(2)}) %collective-permute-start.34) | collective-permute-done | bytes 65568 | tf_op jit(solution)/shard_map/ppermute | solution.py:61
  (89 shorter events, 18.5 us)
Async XLA Ops:
  0.0 8.7 %collective-permute-start = (bf16[64,512]{1,0:T(8,128)(2,1)}, bf16[64,512]{1,0:T(8,128)(2,1)S(1)}, u32[]{:S(2)}, u32[]{:S(2)}) collective-permute-start(bf16[64,512]{1,0:T(8,128)(2,1)} %bitcast.33), channel_id=1, source_target_pairs={{0,8},{1,9},{2,10},{3,11},{4,12},{5,13},{6,14},{7,15},{8,0},{9,1},... | collective-permute-start | bytes 196616 | tf_op jit(solution)/shard_map/ppermute | solution.py:32
  4.0 4.7 %collective-permute-start.1 = (bf16[1,512]{1,0:T(2,128)(2,1)}, bf16[1,512]{1,0:T(2,128)(2,1)S(1)}, u32[]{:S(2)}, u32[]{:S(2)}) collective-permute-start(bf16[1,512]{1,0:T(2,128)(2,1)} %gain_ref.1), channel_id=1, source_target_pairs={{0,8},{1,9},{2,10},{3,11},{4,12},{5,13},{6,14},{7,15},{8,0},{9,1},... | collective-permute-start | bytes 3080 | tf_op jit(solution)/shard_map/ppermute | solution.py:32
  8.9 5.2 %collective-permute-start.2 = (bf16[144,512]{1,0:T(8,128)(2,1)S(1)}, bf16[144,512]{1,0:T(8,128)(2,1)S(1)}, u32[]{:S(2)}, u32[]{:S(2)}) collective-permute-start(bf16[144,512]{1,0:T(8,128)(2,1)S(1)} %concatenate.18.refs_0_), channel_id=1, source_target_pairs={{0,4},{1,5},{2,6},{3,7},{4,0},{5,1},{6,2},{7,3},{8,12},{9,13},{10,... | collective-permute-start | bytes 442376 | tf_op jit(solution)/shard_map/ppermute | solution.py:32
  10.6 5.1 %collective-permute-start.5 = (bf16[144,512]{1,0:T(8,128)(2,1)S(1)}, bf16[144,512]{1,0:T(8,128)(2,1)S(1)}, u32[]{:S(2)}, u32[]{:S(2)}) collective-permute-start(bf16[144,512]{1,0:T(8,128)(2,1)S(1)} %concatenate.18.refs_0_), channel_id=1, source_target_pairs={{0,1},{1,0},{2,3},{3,2},{4,5},{5,4},{6,7},{7,6},{8,9},{9,8},{10,11... | collective-permute-start | bytes 442376 | tf_op jit(solution)/shard_map/ppermute | solution.py:32
  10.6 8.1 %collective-permute-start.4 = (bf16[144,512]{1,0:T(8,128)(2,1)S(1)}, bf16[144,512]{1,0:T(8,128)(2,1)S(1)}, u32[]{:S(2)}, u32[]{:S(2)}) collective-permute-start(bf16[144,512]{1,0:T(8,128)(2,1)S(1)} %concatenate.18.refs_0_), channel_id=1, source_target_pairs={{0,2},{1,3},{2,0},{3,1},{4,6},{5,7},{6,4},{7,5},{8,10},{9,11},{10,... | collective-permute-start | bytes 442376 | tf_op jit(solution)/shard_map/ppermute | solution.py:32
  14.1 5.9 %collective-permute-start.3 = (bf16[144,512]{1,0:T(8,128)(2,1)S(1)}, bf16[144,512]{1,0:T(8,128)(2,1)S(1)}, u32[]{:S(2)}, u32[]{:S(2)}) collective-permute-start(bf16[144,512]{1,0:T(8,128)(2,1)S(1)} %collective-permute-done.2.refs_0_), channel_id=1, source_target_pairs={{0,2},{1,3},{2,0},{3,1},{4,6},{5,7},{6,4},{7,5},{8,10},{9,11},{10,... | collective-permute-start | bytes 442376 | tf_op jit(solution)/shard_map/ppermute | solution.py:32
  19.2 1.4 %collective-permute-start.7 = (bf16[144,512]{1,0:T(8,128)(2,1)S(1)}, bf16[144,512]{1,0:T(8,128)(2,1)S(1)}, u32[]{:S(2)}, u32[]{:S(2)}) collective-permute-start(bf16[144,512]{1,0:T(8,128)(2,1)S(1)} %collective-permute-done.2.refs_0_), channel_id=1, source_target_pairs={{0,1},{1,0},{2,3},{3,2},{4,5},{5,4},{6,7},{7,6},{8,9},{9,8},{10,11... | collective-permute-start | bytes 442376 | tf_op jit(solution)/shard_map/ppermute | solution.py:32
  19.3 1.6 %collective-permute-start.8 = (bf16[144,512]{1,0:T(8,128)(2,1)S(1)}, bf16[144,512]{1,0:T(8,128)(2,1)S(1)}, u32[]{:S(2)}, u32[]{:S(2)}) collective-permute-start(bf16[144,512]{1,0:T(8,128)(2,1)S(1)} %collective-permute-done.4.refs_1_), channel_id=1, source_target_pairs={{0,1},{1,0},{2,3},{3,2},{4,5},{5,4},{6,7},{7,6},{8,9},{9,8},{10,11... | collective-permute-start | bytes 442376 | tf_op jit(solution)/shard_map/ppermute | solution.py:32
  20.0 1.6 %collective-permute-start.6 = (bf16[144,512]{1,0:T(8,128)(2,1)S(1)}, bf16[144,512]{1,0:T(8,128)(2,1)S(1)}, u32[]{:S(2)}, u32[]{:S(2)}) collective-permute-start(bf16[144,512]{1,0:T(8,128)(2,1)S(1)} %collective-permute-done.3.refs_0_), channel_id=1, source_target_pairs={{0,1},{1,0},{2,3},{3,2},{4,5},{5,4},{6,7},{7,6},{8,9},{9,8},{10,11... | collective-permute-start | bytes 442376 | tf_op jit(solution)/shard_map/ppermute | solution.py:32
  38.5 1.5 %collective-permute-start.10 = (bf16[1,4,4096]{2,1,0:T(4,128)(2,1)S(1)}, bf16[1,4,4096]{2,1,0:T(4,128)(2,1)S(1)}, u32[]{:S(2)}, u32[]{:S(2)}) collective-permute-start(bf16[1,4,4096]{2,1,0:T(4,128)(2,1)S(1)} %attend.2), channel_id=1, source_target_pairs={{0,1},{1,0},{2,3},{3,2},{4,5},{5,4},{6,7},{7,6},{8,9},{9,8},{10,11... | collective-permute-start | bytes 98312 | tf_op jit(solution)/shard_map/ppermute | solution.py:32
  38.7 5.3 %collective-permute-start.9 = (bf16[1,4,4096]{2,1,0:T(4,128)(2,1)S(1)}, bf16[1,4,4096]{2,1,0:T(4,128)(2,1)S(1)}, u32[]{:S(2)}, u32[]{:S(2)}) collective-permute-start(bf16[1,4,4096]{2,1,0:T(4,128)(2,1)S(1)} %attend.2), channel_id=1, source_target_pairs={{0,8},{1,9},{2,10},{3,11},{4,12},{5,13},{6,14},{7,15},{8,0},{9,1},... | collective-permute-start | bytes 98312 | tf_op jit(solution)/shard_map/ppermute | solution.py:32
  44.0 5.3 %collective-permute-start.13 = (bf16[2,4,4096]{2,1,0:T(4,128)(2,1)S(1)}, bf16[2,4,4096]{2,1,0:T(4,128)(2,1)S(1)}, u32[]{:S(2)}, u32[]{:S(2)}) collective-permute-start(bf16[2,4,4096]{2,1,0:T(4,128)(2,1)S(1)} %pad_maximum_fusion.2.refs_0_), channel_id=1, source_target_pairs={{0,6},{1,7},{2,4},{3,5},{4,2},{5,3},{6,0},{7,1},{8,14},{9,15},{10,... | collective-permute-start | bytes 196616 | tf_op jit(solution)/shard_map/ppermute | solution.py:32
  44.7 5.0 %collective-permute-start.12 = (bf16[2,4,4096]{2,1,0:T(4,128)(2,1)S(1)}, bf16[2,4,4096]{2,1,0:T(4,128)(2,1)S(1)}, u32[]{:S(2)}, u32[]{:S(2)}) collective-permute-start(bf16[2,4,4096]{2,1,0:T(4,128)(2,1)S(1)} %pad_maximum_fusion.2.refs_0_), channel_id=1, source_target_pairs={{0,2},{1,3},{2,0},{3,1},{4,6},{5,7},{6,4},{7,5},{8,10},{9,11},{10,... | collective-permute-start | bytes 196616 | tf_op jit(solution)/shard_map/ppermute | solution.py:32
  46.1 4.3 %collective-permute-start.11 = (bf16[2,4,4096]{2,1,0:T(4,128)(2,1)S(1)}, bf16[2,4,4096]{2,1,0:T(4,128)(2,1)S(1)}, u32[]{:S(2)}, u32[]{:S(2)}) collective-permute-start(bf16[2,4,4096]{2,1,0:T(4,128)(2,1)S(1)} %pad_maximum_fusion.2.refs_0_), channel_id=1, source_target_pairs={{0,4},{1,5},{2,6},{3,7},{4,0},{5,1},{6,2},{7,3},{8,12},{9,13},{10,... | collective-permute-start | bytes 196616 | tf_op jit(solution)/shard_map/ppermute | solution.py:32
  49.4 2.1 %collective-permute-start.14 = (bf16[3,4,4096]{2,1,0:T(4,128)(2,1)S(1)}, bf16[3,4,4096]{2,1,0:T(4,128)(2,1)S(1)}, u32[]{:S(2)}, u32[]{:S(2)}) collective-permute-start(bf16[3,4,4096]{2,1,0:T(4,128)(2,1)S(1)} %pad_maximum_fusion), channel_id=1, source_target_pairs={{0,1},{1,0},{2,3},{3,2},{4,5},{5,4},{6,7},{7,6},{8,9},{9,8},{10,11... | collective-permute-start | bytes 294920 | tf_op jit(solution)/shard_map/ppermute | solution.py:32
  52.6 7.5 %collective-permute-start.17 = (bf16[64,512]{1,0:T(8,128)(2,1)S(1)}, bf16[64,512]{1,0:T(8,128)(2,1)S(1)}, u32[]{:S(2)}, u32[]{:S(2)}) collective-permute-start(bf16[64,512]{1,0:T(8,128)(2,1)S(1)} %output.2), channel_id=1, source_target_pairs={{0,24},{1,25},{2,26},{3,27},{4,28},{5,29},{6,30},{7,31},{8,16},{9,... | collective-permute-start | bytes 196616 | tf_op jit(solution)/shard_map/ppermute | solution.py:61
  54.6 5.5 %collective-permute-start.18 = (bf16[64,512]{1,0:T(8,128)(2,1)S(1)}, bf16[64,512]{1,0:T(8,128)(2,1)S(1)}, u32[]{:S(2)}, u32[]{:S(2)}) collective-permute-start(bf16[64,512]{1,0:T(8,128)(2,1)S(1)} %output.2), channel_id=1, source_target_pairs={{0,16},{1,17},{2,18},{3,19},{4,20},{5,21},{6,22},{7,23},{8,24},{9,... | collective-permute-start | bytes 196616 | tf_op jit(solution)/shard_map/ppermute | solution.py:61
  60.1 5.0 %collective-permute-start.19 = (bf16[128,512]{1,0:T(8,128)(2,1)S(1)}, bf16[128,512]{1,0:T(8,128)(2,1)S(1)}, u32[]{:S(2)}, u32[]{:S(2)}) collective-permute-start(bf16[128,512]{1,0:T(8,128)(2,1)S(1)} %constant_dynamic-update-slice_fusion.refs_0_), channel_id=1, source_target_pairs={{0,4},{1,5},{2,6},{3,7},{4,0},{5,1},{6,2},{7,3},{8,12},{9,13},{10,... | collective-permute-start | bytes 393224 | tf_op jit(solution)/shard_map/ppermute | solution.py:32
  61.3 4.5 %collective-permute-start.22 = (bf16[128,512]{1,0:T(8,128)(2,1)S(1)}, bf16[128,512]{1,0:T(8,128)(2,1)S(1)}, u32[]{:S(2)}, u32[]{:S(2)}) collective-permute-start(bf16[128,512]{1,0:T(8,128)(2,1)S(1)} %constant_dynamic-update-slice_fusion.refs_0_), channel_id=1, source_target_pairs={{0,1},{1,0},{2,3},{3,2},{4,5},{5,4},{6,7},{7,6},{8,9},{9,8},{10,11... | collective-permute-start | bytes 393224 | tf_op jit(solution)/shard_map/ppermute | solution.py:32
  61.3 6.3 %collective-permute-start.21 = (bf16[128,512]{1,0:T(8,128)(2,1)S(1)}, bf16[128,512]{1,0:T(8,128)(2,1)S(1)}, u32[]{:S(2)}, u32[]{:S(2)}) collective-permute-start(bf16[128,512]{1,0:T(8,128)(2,1)S(1)} %constant_dynamic-update-slice_fusion.refs_0_), channel_id=1, source_target_pairs={{0,2},{1,3},{2,0},{3,1},{4,6},{5,7},{6,4},{7,5},{8,10},{9,11},{10,... | collective-permute-start | bytes 393224 | tf_op jit(solution)/shard_map/ppermute | solution.py:32
  65.2 5.0 %collective-permute-start.20 = (bf16[128,512]{1,0:T(8,128)(2,1)S(1)}, bf16[128,512]{1,0:T(8,128)(2,1)S(1)}, u32[]{:S(2)}, u32[]{:S(2)}) collective-permute-start(bf16[128,512]{1,0:T(8,128)(2,1)S(1)} %collective-permute-done.19.refs_0_), channel_id=1, source_target_pairs={{0,2},{1,3},{2,0},{3,1},{4,6},{5,7},{6,4},{7,5},{8,10},{9,11},{10,... | collective-permute-start | bytes 393224 | tf_op jit(solution)/shard_map/ppermute | solution.py:32
  68.1 2.1 %collective-permute-start.24 = (bf16[128,512]{1,0:T(8,128)(2,1)S(1)}, bf16[128,512]{1,0:T(8,128)(2,1)S(1)}, u32[]{:S(2)}, u32[]{:S(2)}) collective-permute-start(bf16[128,512]{1,0:T(8,128)(2,1)S(1)} %collective-permute-done.19.refs_0_), channel_id=1, source_target_pairs={{0,1},{1,0},{2,3},{3,2},{4,5},{5,4},{6,7},{7,6},{8,9},{9,8},{10,11... | collective-permute-start | bytes 393224 | tf_op jit(solution)/shard_map/ppermute | solution.py:32
  68.2 2.0 %collective-permute-start.25 = (bf16[128,512]{1,0:T(8,128)(2,1)S(1)}, bf16[128,512]{1,0:T(8,128)(2,1)S(1)}, u32[]{:S(2)}, u32[]{:S(2)}) collective-permute-start(bf16[128,512]{1,0:T(8,128)(2,1)S(1)} %collective-permute-done.21.refs_1_), channel_id=1, source_target_pairs={{0,1},{1,0},{2,3},{3,2},{4,5},{5,4},{6,7},{7,6},{8,9},{9,8},{10,11... | collective-permute-start | bytes 393224 | tf_op jit(solution)/shard_map/ppermute | solution.py:32
  70.1 1.3 %collective-permute-start.23 = (bf16[128,512]{1,0:T(8,128)(2,1)S(1)}, bf16[128,512]{1,0:T(8,128)(2,1)S(1)}, u32[]{:S(2)}, u32[]{:S(2)}) collective-permute-start(bf16[128,512]{1,0:T(8,128)(2,1)S(1)} %collective-permute-done.20.refs_0_), channel_id=1, source_target_pairs={{0,1},{1,0},{2,3},{3,2},{4,5},{5,4},{6,7},{7,6},{8,9},{9,8},{10,11... | collective-permute-start | bytes 393224 | tf_op jit(solution)/shard_map/ppermute | solution.py:32
  83.0 1.3 %collective-permute-start.27 = (bf16[1,4,4096]{2,1,0:T(4,128)(2,1)S(1)}, bf16[1,4,4096]{2,1,0:T(4,128)(2,1)S(1)}, u32[]{:S(2)}, u32[]{:S(2)}) collective-permute-start(bf16[1,4,4096]{2,1,0:T(4,128)(2,1)S(1)} %attend.3), channel_id=1, source_target_pairs={{0,1},{1,0},{2,3},{3,2},{4,5},{5,4},{6,7},{7,6},{8,9},{9,8},{10,11... | collective-permute-start | bytes 98312 | tf_op jit(solution)/shard_map/ppermute | solution.py:32
  83.0 5.1 %collective-permute-start.26 = (bf16[1,4,4096]{2,1,0:T(4,128)(2,1)S(1)}, bf16[1,4,4096]{2,1,0:T(4,128)(2,1)S(1)}, u32[]{:S(2)}, u32[]{:S(2)}) collective-permute-start(bf16[1,4,4096]{2,1,0:T(4,128)(2,1)S(1)} %attend.3), channel_id=1, source_target_pairs={{0,8},{1,9},{2,10},{3,11},{4,12},{5,13},{6,14},{7,15},{8,0},{9,1},... | collective-permute-start | bytes 98312 | tf_op jit(solution)/shard_map/ppermute | solution.py:32
  88.1 5.2 %collective-permute-start.30 = (bf16[2,4,4096]{2,1,0:T(4,128)(2,1)S(1)}, bf16[2,4,4096]{2,1,0:T(4,128)(2,1)S(1)}, u32[]{:S(2)}, u32[]{:S(2)}) collective-permute-start(bf16[2,4,4096]{2,1,0:T(4,128)(2,1)S(1)} %pad_maximum_fusion.3.refs_0_), channel_id=1, source_target_pairs={{0,6},{1,7},{2,4},{3,5},{4,2},{5,3},{6,0},{7,1},{8,14},{9,15},{10,... | collective-permute-start | bytes 196616 | tf_op jit(solution)/shard_map/ppermute | solution.py:32
  88.4 5.1 %collective-permute-start.29 = (bf16[2,4,4096]{2,1,0:T(4,128)(2,1)S(1)}, bf16[2,4,4096]{2,1,0:T(4,128)(2,1)S(1)}, u32[]{:S(2)}, u32[]{:S(2)}) collective-permute-start(bf16[2,4,4096]{2,1,0:T(4,128)(2,1)S(1)} %pad_maximum_fusion.3.refs_0_), channel_id=1, source_target_pairs={{0,2},{1,3},{2,0},{3,1},{4,6},{5,7},{6,4},{7,5},{8,10},{9,11},{10,... | collective-permute-start | bytes 196616 | tf_op jit(solution)/shard_map/ppermute | solution.py:32
  89.9 4.3 %collective-permute-start.28 = (bf16[2,4,4096]{2,1,0:T(4,128)(2,1)S(1)}, bf16[2,4,4096]{2,1,0:T(4,128)(2,1)S(1)}, u32[]{:S(2)}, u32[]{:S(2)}) collective-permute-start(bf16[2,4,4096]{2,1,0:T(4,128)(2,1)S(1)} %pad_maximum_fusion.3.refs_0_), channel_id=1, source_target_pairs={{0,4},{1,5},{2,6},{3,7},{4,0},{5,1},{6,2},{7,3},{8,12},{9,13},{10,... | collective-permute-start | bytes 196616 | tf_op jit(solution)/shard_map/ppermute | solution.py:32
  93.4 2.0 %collective-permute-start.31 = (bf16[3,4,4096]{2,1,0:T(4,128)(2,1)S(1)}, bf16[3,4,4096]{2,1,0:T(4,128)(2,1)S(1)}, u32[]{:S(2)}, u32[]{:S(2)}) collective-permute-start(bf16[3,4,4096]{2,1,0:T(4,128)(2,1)S(1)} %pad_maximum_fusion.1), channel_id=1, source_target_pairs={{0,1},{1,0},{2,3},{3,2},{4,5},{5,4},{6,7},{7,6},{8,9},{9,8},{10,11... | collective-permute-start | bytes 294920 | tf_op jit(solution)/shard_map/ppermute | solution.py:32
  93.5 1.4 %collective-permute-start.32 = (bf16[2,4,4096]{2,1,0:T(4,128)(2,1)S(1)}, bf16[2,4,4096]{2,1,0:T(4,128)(2,1)S(1)}, u32[]{:S(2)}, u32[]{:S(2)}) collective-permute-start(bf16[2,4,4096]{2,1,0:T(4,128)(2,1)S(1)} %collective-permute-done.29.refs_2_), channel_id=1, source_target_pairs={{0,1},{1,0},{2,3},{3,2},{4,5},{5,4},{6,7},{7,6},{8,9},{9,8},{10,11... | collective-permute-start | bytes 196616 | tf_op jit(solution)/shard_map/ppermute | solution.py:32
  96.4 4.3 %collective-permute-start.34 = (bf16[64,512]{1,0:T(8,128)(2,1)S(1)}, bf16[64,512]{1,0:T(8,128)(2,1)S(1)}, u32[]{:S(2)}, u32[]{:S(2)}) collective-permute-start(bf16[64,512]{1,0:T(8,128)(2,1)S(1)} %output.3), channel_id=1, source_target_pairs={{0,16},{1,17},{2,18},{3,19},{4,20},{5,21},{6,22},{7,23},{8,24},{9,... | collective-permute-start | bytes 196616 | tf_op jit(solution)/shard_map/ppermute | solution.py:61
  (16 other events, 139.1 us)

commit v11 on v9

--- a/solution.py
+++ b/solution.py
@@ -385,9 +385,9 @@
         gains[1], state = run([(away[1], second), (away[2], third)], gains[1], state)
         second, third, state = lax.optimization_barrier((second, third, state))
         others = [exchange(x, core) for x in (second, third)]
-        fourth, state = lax.optimization_barrier((fourth, state))
+        gains[2], state = run(list(zip(away[5:7], others)), gains[2], state)
         corner = exchange(fourth, core)
-        gains[3], state = run([(away[3], fourth), *zip(away[5:7], others)], gains[3], state)
+        gains[3], state = run([(away[3], fourth)], gains[3], state)
         gains[4], qkv = run([(away[7], corner)], gains[4], state, last=True,
                              outgoing=None if visit else outgoing)
         qkv = lax.all_to_all(qkv, "slot", split_axis=0, concat_axis=0, tiled=True)

time: 101 us -> 101 us (level)
    pallas_call x8 -> x10, Pallas kernels: 4.56 us -> 4.84 us  [project(): pl.pallas_call(functools.partial(project_kernel, away=[masks for masks, _...]
where the time goes in v11:
time: 101 us
  waiting for transfers between devices  32.1 us (32%)
  starting transfers between devices  27.1 us (27%)
  blocking collectives  25.9 us (26%)
  Pallas kernels  8.83 us (9%)
  local copies, waits for them, and re-layouts  6.52 us (6%)
    all_to_all x2, blocking collectives, shards(): qkv = lax.all_to_all(qkv, 'slot', split_axis=0, concat_axis=0, tiled=True)  25.9 us
    ppermute x30, waiting for transfers between devices, exchange(): return lax.ppermute(block, 'slot', [(i, i ^ mask) for i in range(n)])  24.6 us
    ppermute x30, starting transfers between devices, exchange(): return lax.ppermute(block, 'slot', [(i, i ^ mask) for i in range(n)])  22.7 us
    ppermute x3, waiting for transfers between devices, next_segment(): return lax.ppermute(block, ('segment', 'slot'), route)  7.46 us
    unnamed x28, local copies, waits for them, and re-layouts  6.34 us
    pallas_call x10, Pallas kernels, project(): pl.pallas_call(functools.partial(project_kernel, away=[masks for masks, _...  4.84 us
    ppermute x3, starting transfers between devices, next_segment(): return lax.ppermute(block, ('segment', 'slot'), route)  4.41 us
  transfers between devices with their start and end apart: 33, of which 20 were waited for; matrix products, arithmetic and copies ran while one was open for 0% of the time, Pallas kernels for 4%

profile of v11, /device:TPU:0, one launch (start us, length us, event | category | flops | bytes accessed | tf_op | source)
XLA Modules:
  0.0 101.1 jit_solution(12610816755934228839)
XLA Ops:
  0.0 4.0 %collective-permute-start = (bf16[64,512]{1,0:T(8,128)(2,1)}, bf16[64,512]{1,0:T(8,128)(2,1)S(1)}, u32[]{:S(2)}, u32[]{:S(2)}) collective-permute-start(bf16[64,512]{1,0:T(8,128)(2,1)} %bitcast.35), channel_id=1, source_target_pairs={{0,8},{1,9},{2,10},{3,11},{4,12},{5,13},{6,14},{7,15},{8,0},{9,1},... | collective-permute-start | bytes 196616 | tf_op jit(solution)/shard_map/ppermute | solution.py:32
  4.1 0.9 copy-done.3
  5.7 0.8 copy-done.6
  8.0 0.8 collective-permute-done.1
  8.9 1.6 %collective-permute-start.2 = (bf16[144,512]{1,0:T(8,128)(2,1)S(1)}, bf16[144,512]{1,0:T(8,128)(2,1)S(1)}, u32[]{:S(2)}, u32[]{:S(2)}) collective-permute-start(bf16[144,512]{1,0:T(8,128)(2,1)S(1)} %concatenate.20.refs_0_), channel_id=1, source_target_pairs={{0,4},{1,5},{2,6},{3,7},{4,0},{5,1},{6,2},{7,3},{8,12},{9,13},{10,... | collective-permute-start | bytes 442376 | tf_op jit(solution)/shard_map/ppermute | solution.py:32
  10.6 1.5 %collective-permute-start.5 = (bf16[144,512]{1,0:T(8,128)(2,1)S(1)}, bf16[144,512]{1,0:T(8,128)(2,1)S(1)}, u32[]{:S(2)}, u32[]{:S(2)}) collective-permute-start(bf16[144,512]{1,0:T(8,128)(2,1)S(1)} %concatenate.20.refs_0_), channel_id=1, source_target_pairs={{0,2},{1,3},{2,0},{3,1},{4,6},{5,7},{6,4},{7,5},{8,10},{9,11},{10,... | collective-permute-start | bytes 442376 | tf_op jit(solution)/shard_map/ppermute | solution.py:32
  12.1 2.1 %collective-permute-done.2.refs_0_ = bf16[144,512]{1,0:T(8,128)(2,1)S(1)} collective-permute-done((bf16[144,512]{1,0:T(8,128)(2,1)S(1)}, bf16[144,512]{1,0:T(8,128)(2,1)S(1)}, u32[]{:S(2)}, u32[]{:S(2)}) %collective-permute-start.2) | collective-permute-done | bytes 147488 | tf_op jit(solution)/shard_map/ppermute | solution.py:32
  14.1 1.5 %collective-permute-start.3 = (bf16[144,512]{1,0:T(8,128)(2,1)S(1)}, bf16[144,512]{1,0:T(8,128)(2,1)S(1)}, u32[]{:S(2)}, u32[]{:S(2)}) collective-permute-start(bf16[144,512]{1,0:T(8,128)(2,1)S(1)} %collective-permute-done.2.refs_0_), channel_id=1, source_target_pairs={{0,2},{1,3},{2,0},{3,1},{4,6},{5,7},{6,4},{7,5},{8,10},{9,11},{10,... | collective-permute-start | bytes 442376 | tf_op jit(solution)/shard_map/ppermute | solution.py:32
  15.6 2.5 %copy-done = bf16[1,8192,320]{1,2,0:T(8,128)(2,1)S(1)} copy-done((bf16[1,8192,320]{1,2,0:T(8,128)(2,1)S(1)}, bf16[1,8192,320]{1,2,0:T(8,128)(2,1)}, u32[]{:S(2)}) %copy-start) | copy-done | bytes 5242904
  22.4 15.6 %all_to_all.10.qkv_ref = bf16[16,8,1280]{2,1,0:T(8,128)(2,1)S(1)} all-to-all(bf16[16,8,1280]{2,1,0:T(8,128)(2,1)S(1)} %get-tuple-element.53), channel_id=1, replica_groups=mesh['segment'=2,'slot'=16] {'slot'}, dimensions={0} | all-to-all | bytes 655360 | tf_op jit(solution)/shard_map/all_to_all | solution.py:393
  38.7 1.4 %collective-permute-start.9 = (bf16[1,4,4096]{2,1,0:T(4,128)(2,1)S(1)}, bf16[1,4,4096]{2,1,0:T(4,128)(2,1)S(1)}, u32[]{:S(2)}, u32[]{:S(2)}) collective-permute-start(bf16[1,4,4096]{2,1,0:T(4,128)(2,1)S(1)} %attend.2), channel_id=1, source_target_pairs={{0,8},{1,9},{2,10},{3,11},{4,12},{5,13},{6,14},{7,15},{8,0},{9,1},... | collective-permute-start | bytes 98312 | tf_op jit(solution)/shard_map/ppermute | solution.py:32
  40.1 3.6 %collective-permute-done.9 = bf16[1,4,4096]{2,1,0:T(4,128)(2,1)S(1)} collective-permute-done((bf16[1,4,4096]{2,1,0:T(4,128)(2,1)S(1)}, bf16[1,4,4096]{2,1,0:T(4,128)(2,1)S(1)}, u32[]{:S(2)}, u32[]{:S(2)}) %collective-permute-start.9) | collective-permute-done | bytes 32800 | tf_op jit(solution)/shard_map/ppermute | solution.py:32
  43.8 0.8 collective-permute-start.12
  44.6 0.9 collective-permute-start.11
  45.5 1.8 %collective-permute-start.10 = (bf16[2,4,4096]{2,1,0:T(4,128)(2,1)S(1)}, bf16[2,4,4096]{2,1,0:T(4,128)(2,1)S(1)}, u32[]{:S(2)}, u32[]{:S(2)}) collective-permute-start(bf16[2,4,4096]{2,1,0:T(4,128)(2,1)S(1)} %pad_maximum_fusion.2.refs_0_), channel_id=1, source_target_pairs={{0,4},{1,5},{2,6},{3,7},{4,0},{5,1},{6,2},{7,3},{8,12},{9,13},{10,... | collective-permute-start | bytes 196616 | tf_op jit(solution)/shard_map/ppermute | solution.py:32
  47.3 1.8 %collective-permute-done.12.refs_3_ = bf16[2,4,4096]{2,1,0:T(4,128)(2,1)S(1)} collective-permute-done((bf16[2,4,4096]{2,1,0:T(4,128)(2,1)S(1)}, bf16[2,4,4096]{2,1,0:T(4,128)(2,1)S(1)}, u32[]{:S(2)}, u32[]{:S(2)}) %collective-permute-start.12) | collective-permute-done | bytes 65568 | tf_op jit(solution)/shard_map/ppermute | solution.py:32
  51.0 1.0 output.2
  52.0 2.5 %collective-permute-start.16 = (bf16[64,512]{1,0:T(8,128)(2,1)S(1)}, bf16[64,512]{1,0:T(8,128)(2,1)S(1)}, u32[]{:S(2)}, u32[]{:S(2)}) collective-permute-start(bf16[64,512]{1,0:T(8,128)(2,1)S(1)} %output.2), channel_id=1, source_target_pairs={{0,24},{1,25},{2,26},{3,27},{4,28},{5,29},{6,30},{7,31},{8,16},{9,... | collective-permute-start | bytes 196616 | tf_op jit(solution)/shard_map/ppermute | solution.py:58
  55.0 4.6 %collective-permute-done.16 = bf16[64,512]{1,0:T(8,128)(2,1)S(1)} collective-permute-done((bf16[64,512]{1,0:T(8,128)(2,1)S(1)}, bf16[64,512]{1,0:T(8,128)(2,1)S(1)}, u32[]{:S(2)}, u32[]{:S(2)}) %collective-permute-start.16) | collective-permute-done | bytes 65568 | tf_op jit(solution)/shard_map/ppermute | solution.py:58
  59.6 1.7 %collective-permute-start.18 = (bf16[128,512]{1,0:T(8,128)(2,1)S(1)}, bf16[128,512]{1,0:T(8,128)(2,1)S(1)}, u32[]{:S(2)}, u32[]{:S(2)}) collective-permute-start(bf16[128,512]{1,0:T(8,128)(2,1)S(1)} %constant_dynamic-update-slice_fusion.refs_0_), channel_id=1, source_target_pairs={{0,4},{1,5},{2,6},{3,7},{4,0},{5,1},{6,2},{7,3},{8,12},{9,13},{10,... | collective-permute-start | bytes 393224 | tf_op jit(solution)/shard_map/ppermute | solution.py:32
  61.7 3.3 %collective-permute-done.18.refs_0_ = bf16[128,512]{1,0:T(8,128)(2,1)S(1)} collective-permute-done((bf16[128,512]{1,0:T(8,128)(2,1)S(1)}, bf16[128,512]{1,0:T(8,128)(2,1)S(1)}, u32[]{:S(2)}, u32[]{:S(2)}) %collective-permute-start.18) | collective-permute-done | bytes 131104 | tf_op jit(solution)/shard_map/ppermute | solution.py:32
  66.2 1.5 %collective-permute-done.21.refs_1_ = bf16[128,512]{1,0:T(8,128)(2,1)S(1)} collective-permute-done((bf16[128,512]{1,0:T(8,128)(2,1)S(1)}, bf16[128,512]{1,0:T(8,128)(2,1)S(1)}, u32[]{:S(2)}, u32[]{:S(2)}) %collective-permute-start.21) | collective-permute-done | bytes 131104 | tf_op jit(solution)/shard_map/ppermute | solution.py:32
  68.7 1.3 %collective-permute-done.19.refs_0_ = bf16[128,512]{1,0:T(8,128)(2,1)S(1)} collective-permute-done((bf16[128,512]{1,0:T(8,128)(2,1)S(1)}, bf16[128,512]{1,0:T(8,128)(2,1)S(1)}, u32[]{:S(2)}, u32[]{:S(2)}) %collective-permute-start.19) | collective-permute-done | bytes 131104 | tf_op jit(solution)/shard_map/ppermute | solution.py:32
  71.9 10.4 %all_to_all.11.qkv_ref = bf16[16,4,320]{2,1,0:T(4,128)(2,1)S(1)} all-to-all(bf16[16,4,320]{2,1,0:T(4,128)(2,1)S(1)} %project.19), channel_id=1, replica_groups=mesh['segment'=2,'slot'=16] {'slot'}, dimensions={0} | all-to-all | bytes 81920 | tf_op jit(solution)/shard_map/all_to_all | solution.py:393
  83.3 4.5 %collective-permute-done.25 = bf16[1,4,4096]{2,1,0:T(4,128)(2,1)S(1)} collective-permute-done((bf16[1,4,4096]{2,1,0:T(4,128)(2,1)S(1)}, bf16[1,4,4096]{2,1,0:T(4,128)(2,1)S(1)}, u32[]{:S(2)}, u32[]{:S(2)}) %collective-permute-start.25) | collective-permute-done | bytes 32800 | tf_op jit(solution)/shard_map/ppermute | solution.py:32
  88.2 1.4 %collective-permute-start.27 = (bf16[2,4,4096]{2,1,0:T(4,128)(2,1)S(1)}, bf16[2,4,4096]{2,1,0:T(4,128)(2,1)S(1)}, u32[]{:S(2)}, u32[]{:S(2)}) collective-permute-start(bf16[2,4,4096]{2,1,0:T(4,128)(2,1)S(1)} %pad_maximum_fusion.3.refs_0_), channel_id=1, source_target_pairs={{0,2},{1,3},{2,0},{3,1},{4,6},{5,7},{6,4},{7,5},{8,10},{9,11},{10,... | collective-permute-start | bytes 196616 | tf_op jit(solution)/shard_map/ppermute | solution.py:32
  89.6 1.8 %collective-permute-start.26 = (bf16[2,4,4096]{2,1,0:T(4,128)(2,1)S(1)}, bf16[2,4,4096]{2,1,0:T(4,128)(2,1)S(1)}, u32[]{:S(2)}, u32[]{:S(2)}) collective-permute-start(bf16[2,4,4096]{2,1,0:T(4,128)(2,1)S(1)} %pad_maximum_fusion.3.refs_0_), channel_id=1, source_target_pairs={{0,4},{1,5},{2,6},{3,7},{4,0},{5,1},{6,2},{7,3},{8,12},{9,13},{10,... | collective-permute-start | bytes 196616 | tf_op jit(solution)/shard_map/ppermute | solution.py:32
  91.5 1.8 %collective-permute-done.28.refs_3_ = bf16[2,4,4096]{2,1,0:T(4,128)(2,1)S(1)} collective-permute-done((bf16[2,4,4096]{2,1,0:T(4,128)(2,1)S(1)}, bf16[2,4,4096]{2,1,0:T(4,128)(2,1)S(1)}, u32[]{:S(2)}, u32[]{:S(2)}) %collective-permute-start.28) | collective-permute-done | bytes 65568 | tf_op jit(solution)/shard_map/ppermute | solution.py:32
  94.0 0.8 collective-permute-done.30.refs_5_
  95.2 1.0 output.3
  96.2 1.4 %collective-permute-start.32 = (bf16[64,512]{1,0:T(8,128)(2,1)S(1)}, bf16[64,512]{1,0:T(8,128)(2,1)S(1)}, u32[]{:S(2)}, u32[]{:S(2)}) collective-permute-start(bf16[64,512]{1,0:T(8,128)(2,1)S(1)} %output.3), channel_id=1, source_target_pairs={{0,16},{1,17},{2,18},{3,19},{4,20},{5,21},{6,22},{7,23},{8,24},{9,... | collective-permute-start | bytes 196616 | tf_op jit(solution)/shard_map/ppermute | solution.py:58
  97.6 2.9 %collective-permute-done.32 = bf16[64,512]{1,0:T(8,128)(2,1)S(1)} collective-permute-done((bf16[64,512]{1,0:T(8,128)(2,1)S(1)}, bf16[64,512]{1,0:T(8,128)(2,1)S(1)}, u32[]{:S(2)}, u32[]{:S(2)}) %collective-permute-start.32) | collective-permute-done | bytes 65568 | tf_op jit(solution)/shard_map/ppermute | solution.py:58
  (87 shorter events, 17.2 us)
Async XLA Ops:
  0.0 8.7 %collective-permute-start = (bf16[64,512]{1,0:T(8,128)(2,1)}, bf16[64,512]{1,0:T(8,128)(2,1)S(1)}, u32[]{:S(2)}, u32[]{:S(2)}) collective-permute-start(bf16[64,512]{1,0:T(8,128)(2,1)} %bitcast.35), channel_id=1, source_target_pairs={{0,8},{1,9},{2,10},{3,11},{4,12},{5,13},{6,14},{7,15},{8,0},{9,1},... | collective-permute-start | bytes 196616 | tf_op jit(solution)/shard_map/ppermute | solution.py:32
  4.0 4.7 %collective-permute-start.1 = (bf16[1,512]{1,0:T(2,128)(2,1)}, bf16[1,512]{1,0:T(2,128)(2,1)S(1)}, u32[]{:S(2)}, u32[]{:S(2)}) collective-permute-start(bf16[1,512]{1,0:T(2,128)(2,1)} %gain_ref.1), channel_id=1, source_target_pairs={{0,8},{1,9},{2,10},{3,11},{4,12},{5,13},{6,14},{7,15},{8,0},{9,1},... | collective-permute-start | bytes 3080 | tf_op jit(solution)/shard_map/ppermute | solution.py:32
  8.9 5.2 %collective-permute-start.2 = (bf16[144,512]{1,0:T(8,128)(2,1)S(1)}, bf16[144,512]{1,0:T(8,128)(2,1)S(1)}, u32[]{:S(2)}, u32[]{:S(2)}) collective-permute-start(bf16[144,512]{1,0:T(8,128)(2,1)S(1)} %concatenate.20.refs_0_), channel_id=1, source_target_pairs={{0,4},{1,5},{2,6},{3,7},{4,0},{5,1},{6,2},{7,3},{8,12},{9,13},{10,... | collective-permute-start | bytes 442376 | tf_op jit(solution)/shard_map/ppermute | solution.py:32
  10.6 5.1 %collective-permute-start.6 = (bf16[144,512]{1,0:T(8,128)(2,1)S(1)}, bf16[144,512]{1,0:T(8,128)(2,1)S(1)}, u32[]{:S(2)}, u32[]{:S(2)}) collective-permute-start(bf16[144,512]{1,0:T(8,128)(2,1)S(1)} %concatenate.20.refs_0_), channel_id=1, source_target_pairs={{0,1},{1,0},{2,3},{3,2},{4,5},{5,4},{6,7},{7,6},{8,9},{9,8},{10,11... | collective-permute-start | bytes 442376 | tf_op jit(solution)/shard_map/ppermute | solution.py:32
  10.6 8.1 %collective-permute-start.5 = (bf16[144,512]{1,0:T(8,128)(2,1)S(1)}, bf16[144,512]{1,0:T(8,128)(2,1)S(1)}, u32[]{:S(2)}, u32[]{:S(2)}) collective-permute-start(bf16[144,512]{1,0:T(8,128)(2,1)S(1)} %concatenate.20.refs_0_), channel_id=1, source_target_pairs={{0,2},{1,3},{2,0},{3,1},{4,6},{5,7},{6,4},{7,5},{8,10},{9,11},{10,... | collective-permute-start | bytes 442376 | tf_op jit(solution)/shard_map/ppermute | solution.py:32
  14.1 5.9 %collective-permute-start.3 = (bf16[144,512]{1,0:T(8,128)(2,1)S(1)}, bf16[144,512]{1,0:T(8,128)(2,1)S(1)}, u32[]{:S(2)}, u32[]{:S(2)}) collective-permute-start(bf16[144,512]{1,0:T(8,128)(2,1)S(1)} %collective-permute-done.2.refs_0_), channel_id=1, source_target_pairs={{0,2},{1,3},{2,0},{3,1},{4,6},{5,7},{6,4},{7,5},{8,10},{9,11},{10,... | collective-permute-start | bytes 442376 | tf_op jit(solution)/shard_map/ppermute | solution.py:32
  19.2 1.4 %collective-permute-start.7 = (bf16[144,512]{1,0:T(8,128)(2,1)S(1)}, bf16[144,512]{1,0:T(8,128)(2,1)S(1)}, u32[]{:S(2)}, u32[]{:S(2)}) collective-permute-start(bf16[144,512]{1,0:T(8,128)(2,1)S(1)} %collective-permute-done.2.refs_0_), channel_id=1, source_target_pairs={{0,1},{1,0},{2,3},{3,2},{4,5},{5,4},{6,7},{7,6},{8,9},{9,8},{10,11... | collective-permute-start | bytes 442376 | tf_op jit(solution)/shard_map/ppermute | solution.py:32
  19.3 1.6 %collective-permute-start.8 = (bf16[144,512]{1,0:T(8,128)(2,1)S(1)}, bf16[144,512]{1,0:T(8,128)(2,1)S(1)}, u32[]{:S(2)}, u32[]{:S(2)}) collective-permute-start(bf16[144,512]{1,0:T(8,128)(2,1)S(1)} %collective-permute-done.5.refs_1_), channel_id=1, source_target_pairs={{0,1},{1,0},{2,3},{3,2},{4,5},{5,4},{6,7},{7,6},{8,9},{9,8},{10,11... | collective-permute-start | bytes 442376 | tf_op jit(solution)/shard_map/ppermute | solution.py:32
  20.0 1.8 %collective-permute-start.4 = (bf16[144,512]{1,0:T(8,128)(2,1)S(1)}, bf16[144,512]{1,0:T(8,128)(2,1)S(1)}, u32[]{:S(2)}, u32[]{:S(2)}) collective-permute-start(bf16[144,512]{1,0:T(8,128)(2,1)S(1)} %collective-permute-done.3.refs_0_), channel_id=1, source_target_pairs={{0,1},{1,0},{2,3},{3,2},{4,5},{5,4},{6,7},{7,6},{8,9},{9,8},{10,11... | collective-permute-start | bytes 442376 | tf_op jit(solution)/shard_map/ppermute | solution.py:32
  38.7 5.0 %collective-permute-start.9 = (bf16[1,4,4096]{2,1,0:T(4,128)(2,1)S(1)}, bf16[1,4,4096]{2,1,0:T(4,128)(2,1)S(1)}, u32[]{:S(2)}, u32[]{:S(2)}) collective-permute-start(bf16[1,4,4096]{2,1,0:T(4,128)(2,1)S(1)} %attend.2), channel_id=1, source_target_pairs={{0,8},{1,9},{2,10},{3,11},{4,12},{5,13},{6,14},{7,15},{8,0},{9,1},... | collective-permute-start | bytes 98312 | tf_op jit(solution)/shard_map/ppermute | solution.py:32
  43.8 5.3 %collective-permute-start.12 = (bf16[2,4,4096]{2,1,0:T(4,128)(2,1)S(1)}, bf16[2,4,4096]{2,1,0:T(4,128)(2,1)S(1)}, u32[]{:S(2)}, u32[]{:S(2)}) collective-permute-start(bf16[2,4,4096]{2,1,0:T(4,128)(2,1)S(1)} %pad_maximum_fusion.2.refs_0_), channel_id=1, source_target_pairs={{0,6},{1,7},{2,4},{3,5},{4,2},{5,3},{6,0},{7,1},{8,14},{9,15},{10,... | collective-permute-start | bytes 196616 | tf_op jit(solution)/shard_map/ppermute | solution.py:32
  44.6 5.0 %collective-permute-start.11 = (bf16[2,4,4096]{2,1,0:T(4,128)(2,1)S(1)}, bf16[2,4,4096]{2,1,0:T(4,128)(2,1)S(1)}, u32[]{:S(2)}, u32[]{:S(2)}) collective-permute-start(bf16[2,4,4096]{2,1,0:T(4,128)(2,1)S(1)} %pad_maximum_fusion.2.refs_0_), channel_id=1, source_target_pairs={{0,2},{1,3},{2,0},{3,1},{4,6},{5,7},{6,4},{7,5},{8,10},{9,11},{10,... | collective-permute-start | bytes 196616 | tf_op jit(solution)/shard_map/ppermute | solution.py:32
  45.5 4.3 %collective-permute-start.10 = (bf16[2,4,4096]{2,1,0:T(4,128)(2,1)S(1)}, bf16[2,4,4096]{2,1,0:T(4,128)(2,1)S(1)}, u32[]{:S(2)}, u32[]{:S(2)}) collective-permute-start(bf16[2,4,4096]{2,1,0:T(4,128)(2,1)S(1)} %pad_maximum_fusion.2.refs_0_), channel_id=1, source_target_pairs={{0,4},{1,5},{2,6},{3,7},{4,0},{5,1},{6,2},{7,3},{8,12},{9,13},{10,... | collective-permute-start | bytes 196616 | tf_op jit(solution)/shard_map/ppermute | solution.py:32
  49.2 1.8 %collective-permute-start.13 = (bf16[4,4,4096]{2,1,0:T(4,128)(2,1)S(1)}, bf16[4,4,4096]{2,1,0:T(4,128)(2,1)S(1)}, u32[]{:S(2)}, u32[]{:S(2)}) collective-permute-start(bf16[4,4,4096]{2,1,0:T(4,128)(2,1)S(1)} %pad_maximum_fusion), channel_id=1, source_target_pairs={{0,1},{1,0},{2,3},{3,2},{4,5},{5,4},{6,7},{7,6},{8,9},{9,8},{10,11... | collective-permute-start | bytes 393224 | tf_op jit(solution)/shard_map/ppermute | solution.py:32
  49.5 1.3 %collective-permute-start.14 = (bf16[2,4,4096]{2,1,0:T(4,128)(2,1)S(1)}, bf16[2,4,4096]{2,1,0:T(4,128)(2,1)S(1)}, u32[]{:S(2)}, u32[]{:S(2)}) collective-permute-start(bf16[2,4,4096]{2,1,0:T(4,128)(2,1)S(1)} %collective-permute-done.11.refs_2_), channel_id=1, source_target_pairs={{0,1},{1,0},{2,3},{3,2},{4,5},{5,4},{6,7},{7,6},{8,9},{9,8},{10,11... | collective-permute-start | bytes 196616 | tf_op jit(solution)/shard_map/ppermute | solution.py:32
  49.8 1.3 %collective-permute-start.15 = (bf16[2,4,4096]{2,1,0:T(4,128)(2,1)S(1)}, bf16[2,4,4096]{2,1,0:T(4,128)(2,1)S(1)}, u32[]{:S(2)}, u32[]{:S(2)}) collective-permute-start(bf16[2,4,4096]{2,1,0:T(4,128)(2,1)S(1)} %collective-permute-done.10.refs_1_), channel_id=1, source_target_pairs={{0,1},{1,0},{2,3},{3,2},{4,5},{5,4},{6,7},{7,6},{8,9},{9,8},{10,11... | collective-permute-start | bytes 196616 | tf_op jit(solution)/shard_map/ppermute | solution.py:32
  52.0 7.5 %collective-permute-start.16 = (bf16[64,512]{1,0:T(8,128)(2,1)S(1)}, bf16[64,512]{1,0:T(8,128)(2,1)S(1)}, u32[]{:S(2)}, u32[]{:S(2)}) collective-permute-start(bf16[64,512]{1,0:T(8,128)(2,1)S(1)} %output.2), channel_id=1, source_target_pairs={{0,24},{1,25},{2,26},{3,27},{4,28},{5,29},{6,30},{7,31},{8,16},{9,... | collective-permute-start | bytes 196616 | tf_op jit(solution)/shard_map/ppermute | solution.py:58
  54.5 5.1 %collective-permute-start.17 = (bf16[64,512]{1,0:T(8,128)(2,1)S(1)}, bf16[64,512]{1,0:T(8,128)(2,1)S(1)}, u32[]{:S(2)}, u32[]{:S(2)}) collective-permute-start(bf16[64,512]{1,0:T(8,128)(2,1)S(1)} %output.2), channel_id=1, source_target_pairs={{0,16},{1,17},{2,18},{3,19},{4,20},{5,21},{6,22},{7,23},{8,24},{9,... | collective-permute-start | bytes 196616 | tf_op jit(solution)/shard_map/ppermute | solution.py:58
  59.6 5.4 %collective-permute-start.18 = (bf16[128,512]{1,0:T(8,128)(2,1)S(1)}, bf16[128,512]{1,0:T(8,128)(2,1)S(1)}, u32[]{:S(2)}, u32[]{:S(2)}) collective-permute-start(bf16[128,512]{1,0:T(8,128)(2,1)S(1)} %constant_dynamic-update-slice_fusion.refs_0_), channel_id=1, source_target_pairs={{0,4},{1,5},{2,6},{3,7},{4,0},{5,1},{6,2},{7,3},{8,12},{9,13},{10,... | collective-permute-start | bytes 393224 | tf_op jit(solution)/shard_map/ppermute | solution.py:32
  61.4 4.3 %collective-permute-start.22 = (bf16[128,512]{1,0:T(8,128)(2,1)S(1)}, bf16[128,512]{1,0:T(8,128)(2,1)S(1)}, u32[]{:S(2)}, u32[]{:S(2)}) collective-permute-start(bf16[128,512]{1,0:T(8,128)(2,1)S(1)} %constant_dynamic-update-slice_fusion.refs_0_), channel_id=1, source_target_pairs={{0,1},{1,0},{2,3},{3,2},{4,5},{5,4},{6,7},{7,6},{8,9},{9,8},{10,11... | collective-permute-start | bytes 393224 | tf_op jit(solution)/shard_map/ppermute | solution.py:32
  61.4 6.3 %collective-permute-start.21 = (bf16[128,512]{1,0:T(8,128)(2,1)S(1)}, bf16[128,512]{1,0:T(8,128)(2,1)S(1)}, u32[]{:S(2)}, u32[]{:S(2)}) collective-permute-start(bf16[128,512]{1,0:T(8,128)(2,1)S(1)} %constant_dynamic-update-slice_fusion.refs_0_), channel_id=1, source_target_pairs={{0,2},{1,3},{2,0},{3,1},{4,6},{5,7},{6,4},{7,5},{8,10},{9,11},{10,... | collective-permute-start | bytes 393224 | tf_op jit(solution)/shard_map/ppermute | solution.py:32
  65.0 5.1 %collective-permute-start.19 = (bf16[128,512]{1,0:T(8,128)(2,1)S(1)}, bf16[128,512]{1,0:T(8,128)(2,1)S(1)}, u32[]{:S(2)}, u32[]{:S(2)}) collective-permute-start(bf16[128,512]{1,0:T(8,128)(2,1)S(1)} %collective-permute-done.18.refs_0_), channel_id=1, source_target_pairs={{0,2},{1,3},{2,0},{3,1},{4,6},{5,7},{6,4},{7,5},{8,10},{9,11},{10,... | collective-permute-start | bytes 393224 | tf_op jit(solution)/shard_map/ppermute | solution.py:32
  68.2 1.9 %collective-permute-start.23 = (bf16[128,512]{1,0:T(8,128)(2,1)S(1)}, bf16[128,512]{1,0:T(8,128)(2,1)S(1)}, u32[]{:S(2)}, u32[]{:S(2)}) collective-permute-start(bf16[128,512]{1,0:T(8,128)(2,1)S(1)} %collective-permute-done.18.refs_0_), channel_id=1, source_target_pairs={{0,1},{1,0},{2,3},{3,2},{4,5},{5,4},{6,7},{7,6},{8,9},{9,8},{10,11... | collective-permute-start | bytes 393224 | tf_op jit(solution)/shard_map/ppermute | solution.py:32
  68.2 1.8 %collective-permute-start.24 = (bf16[128,512]{1,0:T(8,128)(2,1)S(1)}, bf16[128,512]{1,0:T(8,128)(2,1)S(1)}, u32[]{:S(2)}, u32[]{:S(2)}) collective-permute-start(bf16[128,512]{1,0:T(8,128)(2,1)S(1)} %collective-permute-done.21.refs_1_), channel_id=1, source_target_pairs={{0,1},{1,0},{2,3},{3,2},{4,5},{5,4},{6,7},{7,6},{8,9},{9,8},{10,11... | collective-permute-start | bytes 393224 | tf_op jit(solution)/shard_map/ppermute | solution.py:32
  70.1 1.3 %collective-permute-start.20 = (bf16[128,512]{1,0:T(8,128)(2,1)S(1)}, bf16[128,512]{1,0:T(8,128)(2,1)S(1)}, u32[]{:S(2)}, u32[]{:S(2)}) collective-permute-start(bf16[128,512]{1,0:T(8,128)(2,1)S(1)} %collective-permute-done.19.refs_0_), channel_id=1, source_target_pairs={{0,1},{1,0},{2,3},{3,2},{4,5},{5,4},{6,7},{7,6},{8,9},{9,8},{10,11... | collective-permute-start | bytes 393224 | tf_op jit(solution)/shard_map/ppermute | solution.py:32
  83.0 4.9 %collective-permute-start.25 = (bf16[1,4,4096]{2,1,0:T(4,128)(2,1)S(1)}, bf16[1,4,4096]{2,1,0:T(4,128)(2,1)S(1)}, u32[]{:S(2)}, u32[]{:S(2)}) collective-permute-start(bf16[1,4,4096]{2,1,0:T(4,128)(2,1)S(1)} %attend.3), channel_id=1, source_target_pairs={{0,8},{1,9},{2,10},{3,11},{4,12},{5,13},{6,14},{7,15},{8,0},{9,1},... | collective-permute-start | bytes 98312 | tf_op jit(solution)/shard_map/ppermute | solution.py:32
  87.9 5.3 %collective-permute-start.28 = (bf16[2,4,4096]{2,1,0:T(4,128)(2,1)S(1)}, bf16[2,4,4096]{2,1,0:T(4,128)(2,1)S(1)}, u32[]{:S(2)}, u32[]{:S(2)}) collective-permute-start(bf16[2,4,4096]{2,1,0:T(4,128)(2,1)S(1)} %pad_maximum_fusion.3.refs_0_), channel_id=1, source_target_pairs={{0,6},{1,7},{2,4},{3,5},{4,2},{5,3},{6,0},{7,1},{8,14},{9,15},{10,... | collective-permute-start | bytes 196616 | tf_op jit(solution)/shard_map/ppermute | solution.py:32
  88.2 5.1 %collective-permute-start.27 = (bf16[2,4,4096]{2,1,0:T(4,128)(2,1)S(1)}, bf16[2,4,4096]{2,1,0:T(4,128)(2,1)S(1)}, u32[]{:S(2)}, u32[]{:S(2)}) collective-permute-start(bf16[2,4,4096]{2,1,0:T(4,128)(2,1)S(1)} %pad_maximum_fusion.3.refs_0_), channel_id=1, source_target_pairs={{0,2},{1,3},{2,0},{3,1},{4,6},{5,7},{6,4},{7,5},{8,10},{9,11},{10,... | collective-permute-start | bytes 196616 | tf_op jit(solution)/shard_map/ppermute | solution.py:32
  89.6 4.3 %collective-permute-start.26 = (bf16[2,4,4096]{2,1,0:T(4,128)(2,1)S(1)}, bf16[2,4,4096]{2,1,0:T(4,128)(2,1)S(1)}, u32[]{:S(2)}, u32[]{:S(2)}) collective-permute-start(bf16[2,4,4096]{2,1,0:T(4,128)(2,1)S(1)} %pad_maximum_fusion.3.refs_0_), channel_id=1, source_target_pairs={{0,4},{1,5},{2,6},{3,7},{4,0},{5,1},{6,2},{7,3},{8,12},{9,13},{10,... | collective-permute-start | bytes 196616 | tf_op jit(solution)/shard_map/ppermute | solution.py:32
  93.3 1.9 %collective-permute-start.29 = (bf16[4,4,4096]{2,1,0:T(4,128)(2,1)S(1)}, bf16[4,4,4096]{2,1,0:T(4,128)(2,1)S(1)}, u32[]{:S(2)}, u32[]{:S(2)}) collective-permute-start(bf16[4,4,4096]{2,1,0:T(4,128)(2,1)S(1)} %pad_maximum_fusion.1), channel_id=1, source_target_pairs={{0,1},{1,0},{2,3},{3,2},{4,5},{5,4},{6,7},{7,6},{8,9},{9,8},{10,11... | collective-permute-start | bytes 393224 | tf_op jit(solution)/shard_map/ppermute | solution.py:32
  93.4 1.4 %collective-permute-start.30 = (bf16[2,4,4096]{2,1,0:T(4,128)(2,1)S(1)}, bf16[2,4,4096]{2,1,0:T(4,128)(2,1)S(1)}, u32[]{:S(2)}, u32[]{:S(2)}) collective-permute-start(bf16[2,4,4096]{2,1,0:T(4,128)(2,1)S(1)} %collective-permute-done.27.refs_2_), channel_id=1, source_target_pairs={{0,1},{1,0},{2,3},{3,2},{4,5},{5,4},{6,7},{7,6},{8,9},{9,8},{10,11... | collective-permute-start | bytes 196616 | tf_op jit(solution)/shard_map/ppermute | solution.py:32
  96.2 4.3 %collective-permute-start.32 = (bf16[64,512]{1,0:T(8,128)(2,1)S(1)}, bf16[64,512]{1,0:T(8,128)(2,1)S(1)}, u32[]{:S(2)}, u32[]{:S(2)}) collective-permute-start(bf16[64,512]{1,0:T(8,128)(2,1)S(1)} %output.3), channel_id=1, source_target_pairs={{0,16},{1,17},{2,18},{3,19},{4,20},{5,21},{6,22},{7,23},{8,24},{9,... | collective-permute-start | bytes 196616 | tf_op jit(solution)/shard_map/ppermute | solution.py:58
  (14 other events, 124.5 us)
